TPU v7x, 32 devices: a whole 2x2x4 slice. The times are simulated.
32 devices in a mesh: groups: 2 (over y), lat: 8 (over z, x), lon: 2 (over core).
Axes of the slice: x: 2, y: 2, z: 4, core: 2. Of those that a mesh axis runs over, the one named last changes fastest.
Arguments:
- tokens: bfloat16 [16, 256, 768], P(('groups', 'lat'), 'lon'), parts along dimension 0, may hold values from -5 to 5
- gain_attn: float32 [768], replicated, may hold values from 0.25 to 1.75
- w_qkv: bfloat16 [768, 2304], P('lat'), may hold values from -0.048353085 to 0.048353085
- key_bias: bfloat16 [8, 12, 256], P('lat', None, 'lon'), may hold values from -3 to 250
- w_out: bfloat16 [768, 768], P('lat'), may hold values from -0.21875 to 0.21875
- gain_conv: float32 [768], replicated, may hold values from 0.25 to 1.75
- w_conv: bfloat16 [2, 768, 64], replicated, may hold values from -0.75 to 0.75
- lat_taps: float32 [16, 2], replicated, may hold values from -2 to 2
- lon_half: int32 [8], P('lat'), may hold values from 1 to 128, as said below
- lat_half: int32 [8], P('lat'), may hold values from 0 to 1, as said below
- quad_off: int32 [8], P('lat'), may hold values from 0 to 13
Outputs:
- updated: bfloat16 [16, 256, 768], P(('groups', 'lat'), 'lon'), parts along dimension 0
There are 2 independent parts, one for each index of `groups`. A program takes and returns all parts, laid end to end along the dimension named above; an argument that names none is the same for every part. Nothing has to cross between parts.
Inputs may be any that keep to these rules, and one draw needn't show every extreme that they name: `lon_half`: the bands at either pole reach 128. `lat_half`: both polar bands have 1.
All inputs are finite; a program needn't handle non-finite values.
Results may differ from a plain program's by a relative error of at most 0.008.
Values may be sent and summed in bfloat16 or wider, within the bound.
No kernel may reach another device: no remote copies, remote signals or barrier semaphores. Data moves between devices by JAX's collectives and lax.ppermute only.
A program may use at most 64 MiB of HBM per device.

v0:
```python
import jax
import jax.numpy as jnp
from jax import lax
from jax.sharding import PartitionSpec as P


def padded(cells, sides, width):
    for axis, dim in sides:
        count = lax.axis_size(axis)
        ends = count - 1
        head = lax.slice_in_dim(cells, 0, width, axis=dim)
        tail = lax.slice_in_dim(cells, cells.shape[dim] - width, cells.shape[dim], axis=dim)
        cells = jnp.concatenate(
            [
                lax.ppermute(tail, axis, [(i, (i + 1) % count) for i in range(ends)]),
                cells,
                lax.ppermute(head, axis, [((i + 1) % count, i) for i in range(ends)]),
            ],
            axis=dim,
        )
    return cells


def layer_norm(inputs, gain):
    values = inputs.astype(jnp.float32)
    average = jnp.mean(values, axis=-1, keepdims=True)
    centered = values - average
    variance = jnp.mean(centered * centered, axis=-1, keepdims=True)
    return centered * lax.rsqrt(variance + 1e-05) * gain


def group_mix(inputs, w_conv):
    basis, length, channels = inputs.shape
    group_width = w_conv.shape[2]
    groups = channels // group_width
    mixed_rows = jnp.einsum(
        "kjgc,kgce->kjge",
        inputs.reshape(basis, length, groups, group_width),
        w_conv.reshape(basis, groups, group_width, group_width),
        preferred_element_type=jnp.float32,
    )
    return mixed_rows.reshape(basis, length, channels).astype(jnp.bfloat16)


def lon_weights(row_ids, col_ids, half_width, lon_total):
    offset_lon = (
        jnp.mod(col_ids[None, :] - row_ids[:, None] + lon_total // 2, lon_total) - lon_total // 2
    )
    distance = jnp.abs(offset_lon).astype(jnp.float32)
    span_plus = (half_width + 1).astype(jnp.float32)
    tent_weight = jnp.where(
        distance <= half_width.astype(jnp.float32), (1.0 - distance / span_plus) / span_plus, 0.0
    )
    odd_weight = tent_weight * offset_lon.astype(jnp.float32) / span_plus
    return jnp.stack([tent_weight, odd_weight]).astype(jnp.bfloat16)


def start_state(query_count, head_count, head_dim):
    running_max = jnp.full((head_count, query_count), -jnp.inf, jnp.float32)
    running_sum = jnp.zeros((head_count, query_count), jnp.float32)
    running_out = jnp.zeros((query_count, head_count, head_dim), jnp.float32)
    return (running_max, running_sum, running_out)


def attend_keys(carry_state, queries, key_rows, value_rows, bias_rows, score_scale):
    key_count = key_rows.shape[0]
    for offset in range(0, key_count, 128):
        running_max, running_sum, running_out = carry_state
        key_block = key_rows[offset : offset + 128]
        value_block = value_rows[offset : offset + 128]
        bias_block = bias_rows[offset : offset + 128]
        scores = (
            jnp.einsum("qhd,khd->hqk", queries, key_block, preferred_element_type=jnp.float32)
            * score_scale
        )
        scores = scores + bias_block.T.astype(jnp.float32)[:, None, :]
        new_max = jnp.maximum(running_max, jnp.max(scores, axis=-1))
        rescale = jnp.exp(running_max - new_max)
        exp_scores = jnp.exp(scores - new_max[:, :, None])
        running_sum = running_sum * rescale + jnp.sum(exp_scores, axis=-1)
        running_out = running_out * rescale.T[:, :, None] + jnp.einsum(
            "hqk,khd->qhd",
            exp_scores.astype(jnp.bfloat16),
            value_block,
            preferred_element_type=jnp.float32,
        )
        carry_state = (new_max, running_sum, running_out)
    return carry_state


def finish_state(carry_state):
    running_max, running_sum, running_out = carry_state
    finished = running_out / running_sum.T[:, :, None]
    return finished.reshape(finished.shape[0], -1).astype(jnp.bfloat16)


def lon_conv(blended, half_width, first_col, out_cols):
    lon_total = blended.shape[1]
    block_cols = min(128, lon_total)
    block_count = lon_total // block_cols
    first_block = jnp.floor_divide(first_col - half_width, block_cols)
    last_block = jnp.floor_divide(first_col + out_cols - 1 + half_width, block_cols)
    turn_count = jnp.minimum(block_count, last_block - first_block + 1)
    row_ids = first_col + jnp.arange(out_cols, dtype=jnp.int32)

    def add_block(turn_index, running_out):
        block_at = jnp.mod(first_block + turn_index, block_count)
        lon_block = lax.dynamic_slice_in_dim(blended, block_at * block_cols, block_cols, 1)
        col_ids = block_at * block_cols + jnp.arange(block_cols, dtype=jnp.int32)
        coeffs = lon_weights(row_ids, col_ids, half_width, lon_total)
        return running_out + jnp.einsum(
            "kjc,kcd->jd", coeffs, lon_block, preferred_element_type=jnp.float32
        )

    initial = jnp.zeros((out_cols, blended.shape[2]), jnp.float32)
    return lax.fori_loop(0, turn_count, add_block, initial)


def per_device(
    tokens,
    gain_attn,
    w_qkv,
    key_bias,
    w_out,
    gain_conv,
    w_conv,
    lat_taps,
    lon_half,
    lat_half,
    quad_off,
):
    own_tokens = tokens[0]
    count_lon, model_width = own_tokens.shape
    head_count = key_bias.shape[1]
    head_dim = model_width // head_count
    score_scale = head_dim ** (-0.5)
    lon_place = lax.axis_index("lon")
    normed = layer_norm(own_tokens, gain_attn).astype(jnp.bfloat16)
    bias_rows = key_bias[0].T
    full_qkv, full_out = (
        lax.all_gather(w_qkv, "lat", axis=0, tiled=True),
        lax.all_gather(w_out, "lat", axis=0, tiled=True),
    )
    projected = jnp.dot(normed, full_qkv, preferred_element_type=jnp.float32).astype(jnp.bfloat16)
    queries = projected[:, :model_width].reshape(count_lon, head_count, head_dim)
    key_here = projected[:, model_width : 2 * model_width]
    value_here = projected[:, 2 * model_width :]
    key_piece = lax.all_gather(key_here, "lon", axis=0, tiled=True)
    value_piece = lax.all_gather(value_here, "lon", axis=0, tiled=True)
    bias_piece = lax.all_gather(bias_rows, "lon", axis=0, tiled=True)
    length = key_piece.shape[0]
    carry_state = attend_keys(
        start_state(count_lon, head_count, head_dim),
        queries,
        key_piece.reshape(length, head_count, head_dim),
        value_piece.reshape(length, head_count, head_dim),
        bias_piece,
        score_scale,
    )
    attended = finish_state(carry_state)
    branch_out = jnp.dot(attended, full_out, preferred_element_type=jnp.float32)
    middle = (own_tokens.astype(jnp.float32) + branch_out).astype(jnp.bfloat16)
    conv_in = layer_norm(middle, gain_conv).astype(jnp.bfloat16)
    stacked = padded(conv_in[None], (("lat", 0),), 1)
    lat_row = lax.axis_index("lat")
    last_band = lax.axis_size("lat") - 1
    offsets = jnp.arange(3, dtype=jnp.int32) - 1
    one_hot = (
        (quad_off[0] + offsets + 1)[:, None]
        == jnp.arange(lat_taps.shape[0], dtype=jnp.int32)[None, :]
    ).astype(jnp.float32)
    tap_vals = jnp.dot(one_hot, lat_taps, precision=lax.Precision.HIGHEST)
    tap_vals = jnp.where((jnp.abs(offsets) <= lat_half[0])[:, None], tap_vals, 0.0)
    summed = jnp.einsum(
        "rk,rjd->kjd", tap_vals, stacked.astype(jnp.float32), precision=lax.Precision.HIGHEST
    ).astype(jnp.bfloat16)
    pole_gain = jnp.where(lat_row == 0, tap_vals[0], 0.0) + jnp.where(
        lat_row == last_band, tap_vals[2], 0.0
    )
    first_col = lon_place * count_lon
    pole_rows = (pole_gain[:, None, None] * conv_in.astype(jnp.float32)[None]).astype(jnp.bfloat16)
    mixed_rows = group_mix(summed, w_conv)
    pole_mixed = group_mix(pole_rows, w_conv)
    circle_rows, pole_all = (
        lax.all_gather(mixed_rows, "lon", axis=1, tiled=True),
        lax.all_gather(pole_mixed, "lon", axis=1, tiled=True),
    )
    lon_total = circle_rows.shape[1]
    blended = (
        circle_rows.astype(jnp.float32)
        + jnp.roll(pole_all, -(lon_total // 2), axis=1).astype(jnp.float32)
    ).astype(jnp.bfloat16)
    conv_out = lon_conv(blended, lon_half[0], first_col, count_lon)
    return (middle.astype(jnp.float32) + conv_out).astype(jnp.bfloat16)[None]


def solution(mesh):
    return jax.shard_map(
        per_device,
        mesh=mesh,
        in_specs=(
            P(("groups", "lat"), "lon", None),
            P(),
            P("lat", None),
            P("lat", None, "lon"),
            P("lat", None),
            P(),
            P(),
            P(),
            P("lat"),
            P("lat"),
            P("lat"),
        ),
        out_specs=P(("groups", "lat"), "lon", None),
        check_vma=False,
    )
```

profile of v0, /device:TPU:3, one launch (start us, length us, event | category | flops | bytes accessed | tf_op | source)
XLA Modules:
  0.0 145.0 jit_solution(11945221781708907703)
XLA Ops:
  6.5 0.7 all-gather.3.cloned.1.call-update
  7.3 0.0 all-gather.5.cloned.1.call-start
  7.3 0.7 all-gather.5.cloned.1.call-update
  8.7 1.0 convert_reduce_fusion
  9.7 1.1 fusion.29
  10.9 2.5 %all_gather.23 = bf16[256,12]{0,1:T(8,128)(2,1)S(1)} all-gather(bf16[128,12]{0,1:T(8,128)(2,1)} %bitcast.119), channel_id=1, replica_groups=mesh['groups'=2,'lat'=8,'lon'=2] {'lon'}, dimensions={0}, use_global_device_ids=true | all-gather | bytes 9216 | tf_op jit(solution)/shard_map/all_gather | solution.py:150
  14.7 1.3 reshape.244
  16.0 0.2 convolution_select_fusion
  16.2 0.2 add_reduce_fusion
  16.4 57.7 %all-gather.3.cloned.1.call-done = bf16[768,2304]{1,0:T(8,128)(2,1)} async-done(((bf16[96,2304]{1,0:T(8,128)(2,1)}), bf16[768,2304]{1,0:T(8,128)(2,1)}) %all-gather.3.cloned.1.call-update) | async-done | bytes 3538960 | tf_op jit(solution)/shard_map/all_gather | solution.py:141
  74.1 2.7 %convolution_convert_fusion = bf16[128,2304]{1,0:T(8,128)(2,1)S(1)} fusion(bf16[768,2304]{1,0:T(8,128)(2,1)} %all-gather.3.cloned.1.call-done, bf16[1,128,768]{2,1,0:T(8,128)(2,1)S(1)} %copy-done.1, f32[768]{0:T(1024)S(1)} %copy-done.3, f32[128]{0:T(128)S(1)} %add_rsqrt_fusion.1, f32[128]{0:T(128)S(1)} %broadcast_multiply_fusion.1), kind=kOutput, calls=%fused_computation.20 | convolution fusion | flops 453771264 | bytes 4329472 | tf_op jit(solution)/shard_map/dot_general | solution.py:144
  76.9 3.4 %all_gather.22 = bf16[256,768]{1,0:T(8,128)(2,1)S(1)} all-gather(bf16[128,768]{1,0:T(8,128)(2,1)S(1)} %get-tuple-element.186), channel_id=1, replica_groups=mesh['groups'=2,'lat'=8,'lon'=2] {'lon'}, dimensions={0}, use_global_device_ids=true | all-gather | bytes 589824 | tf_op jit(solution)/shard_map/all_gather | solution.py:148
  80.2 0.2 copy.28
  80.4 0.2 copy.27
  80.6 0.2 copy.31
  80.7 2.1 %all_gather.24 = bf16[256,768]{1,0:T(8,128)(2,1)S(1)} all-gather(bf16[128,768]{1,0:T(8,128)(2,1)S(1)} %get-tuple-element.187), channel_id=1, replica_groups=mesh['groups'=2,'lat'=8,'lon'=2] {'lon'}, dimensions={0}, use_global_device_ids=true | all-gather | bytes 589824 | tf_op jit(solution)/shard_map/all_gather | solution.py:149
  82.9 0.2 copy.29
  83.0 0.2 copy.32
  83.2 0.4 fusion.58
  83.6 0.4 fusion.59
  84.1 0.3 fusion.22
  84.4 0.2 fusion.17
  84.6 0.2 fusion.18
  84.9 30.6 %all-gather.5.cloned.1.call-done = bf16[768,768]{1,0:T(8,128)(2,1)} async-done(((bf16[96,768]{1,0:T(8,128)(2,1)}), bf16[768,768]{1,0:T(8,128)(2,1)}) %all-gather.5.cloned.1.call-update) | async-done | bytes 1179664 | tf_op jit(solution)/shard_map/all_gather | solution.py:142
  115.5 1.7 %fusion.60 = (f32[128]{0:T(128)S(1)}, f32[128,768]{1,0:T(8,128)S(1)}) fusion(bf16[128,768]{0,1:T(8,128)(2,1)S(1)} %bitcast.117, bf16[768,768]{1,0:T(8,128)(2,1)} %all-gather.5.cloned.1.call-done, bf16[1,128,768]{2,1,0:T(8,128)(2,1)S(1)} %copy-done.1), kind=kOutput, calls=%fused_computation.99 | convolution fusion | flops 151486336 | bytes 1966592 | tf_op jit(solution)/shard_map/dot_general | solution.py:161
  117.3 0.2 multiply_reduce_fusion
  117.5 0.1 fusion.51
  117.6 3.9 %collective-permute-start = (bf16[1,128,768]{2,1,0:T(8,128)(2,1)S(1)}, bf16[1,128,768]{2,1,0:T(8,128)(2,1)S(1)}, u32[]{:S(2)}, u32[]{:S(2)}) collective-permute-start(bf16[1,128,768]{2,1,0:T(8,128)(2,1)S(1)} %get-tuple-element.190), channel_id=1, source_target_pairs={{0,2},{2,4},{4,6},{6,8},{8,10},{10,12},{12,14},{1,3},{3,5},{5,7},{... | collective-permute-start | bytes 589832 | tf_op jit(solution)/shard_map/ppermute | solution.py:15
  121.5 1.9 %collective-permute-start.1 = (bf16[1,128,768]{2,1,0:T(8,128)(2,1)S(1)}, bf16[1,128,768]{2,1,0:T(8,128)(2,1)S(1)}, u32[]{:S(2)}, u32[]{:S(2)}) collective-permute-start(bf16[1,128,768]{2,1,0:T(8,128)(2,1)S(1)} %get-tuple-element.190), channel_id=1, source_target_pairs={{2,0},{4,2},{6,4},{8,6},{10,8},{12,10},{14,12},{3,1},{5,3},{7,5},{... | collective-permute-start | bytes 589832 | tf_op jit(solution)/shard_map/ppermute | solution.py:17
  123.4 0.2 copy.38
  123.6 0.3 convolution_convert_fusion.2
  124.0 0.2 copy.40
  124.2 4.0 %all_gather.27 = bf16[2,256,768]{2,1,0:T(8,128)(2,1)S(1)} all-gather(bf16[2,128,768]{2,1,0:T(8,128)(2,1)S(1)} %copy.40), channel_id=1, replica_groups=mesh['groups'=2,'lat'=8,'lon'=2] {'lon'}, dimensions={1}, use_global_device_ids=true | all-gather | bytes 1179648 | tf_op jit(solution)/shard_map/all_gather | solution.py:186
  128.2 0.1 fusion.54
  128.2 0.6 collective-permute-done.1
  128.8 0.1 pad_maximum_fusion
  128.9 1.4 convolution_convert_fusion.1
  130.3 0.5 copy.35
  130.8 0.3 convolution_convert_fusion.3
  131.1 0.2 copy.37
  131.3 5.0 %all_gather.26 = bf16[2,256,768]{2,1,0:T(8,128)(2,1)S(1)} all-gather(bf16[2,128,768]{2,1,0:T(8,128)(2,1)S(1)} %copy.37), channel_id=1, replica_groups=mesh['groups'=2,'lat'=8,'lon'=2] {'lon'}, dimensions={1}, use_global_device_ids=true | all-gather | bytes 1179648 | tf_op jit(solution)/shard_map/all_gather | solution.py:185
  136.3 0.2 add_convert_fusion
  136.5 0.9 while.14
  136.6 0.1 fusion.78
  136.7 0.2 fusion.79
  137.0 0.1 fusion.78
  137.1 0.2 fusion.79
  137.4 0.7 fusion.40
  (25 shorter events, 0.2 us)
Async XLA Ops:
  6.5 9.5 %copy-start = (f32[16,2]{0,1:T(2,128)S(1)}, f32[16,2]{0,1:T(2,128)}, u32[]{:S(2)}) copy-start(f32[16,2]{0,1:T(2,128)} %param.20) | copy-start | bytes 388
  6.5 67.6 %copy-start.1 = (bf16[1,128,768]{2,1,0:T(8,128)(2,1)S(1)}, bf16[1,128,768]{2,1,0:T(8,128)(2,1)}, u32[]{:S(2)}) copy-start(bf16[1,128,768]{2,1,0:T(8,128)(2,1)} %param.13) | copy-start | bytes 589828
  6.5 67.6 %copy-start.3 = (f32[768]{0:T(1024)S(1)}, f32[768]{0:T(1024)}, u32[]{:S(2)}) copy-start(f32[768]{0:T(1024)} %param.14) | copy-start | bytes 9220
  6.5 67.6 %all-gather.3.cloned.1.call-start = ((), (), s32[]{:S(2)}) async-start(), calls=%async_computation | async-start | bytes 3981312 | tf_op jit(solution)/shard_map/all_gather | solution.py:141
  7.3 108.3 %all-gather.5.cloned.1.call-start = ((), (), s32[]{:S(2)}) async-start(), calls=%async_computation.1 | async-start | bytes 1327104 | tf_op jit(solution)/shard_map/all_gather | solution.py:142
  84.9 32.6 %copy-start.2 = (f32[768]{0:T(1024)S(1)}, f32[768]{0:T(1024)}, u32[]{:S(2)}) copy-start(f32[768]{0:T(1024)} %param.18) | copy-start | bytes 9220
  117.6 10.6 %collective-permute-start = (bf16[1,128,768]{2,1,0:T(8,128)(2,1)S(1)}, bf16[1,128,768]{2,1,0:T(8,128)(2,1)S(1)}, u32[]{:S(2)}, u32[]{:S(2)}) collective-permute-start(bf16[1,128,768]{2,1,0:T(8,128)(2,1)S(1)} %get-tuple-element.190), channel_id=1, source_target_pairs={{0,2},{2,4},{4,6},{6,8},{8,10},{10,12},{12,14},{1,3},{3,5},{5,7},{... | collective-permute-start | bytes 589832 | tf_op jit(solution)/shard_map/ppermute | solution.py:15
  121.5 7.3 %collective-permute-start.1 = (bf16[1,128,768]{2,1,0:T(8,128)(2,1)S(1)}, bf16[1,128,768]{2,1,0:T(8,128)(2,1)S(1)}, u32[]{:S(2)}, u32[]{:S(2)}) collective-permute-start(bf16[1,128,768]{2,1,0:T(8,128)(2,1)S(1)} %get-tuple-element.190), channel_id=1, source_target_pairs={{2,0},{4,2},{6,4},{8,6},{10,8},{12,10},{14,12},{3,1},{5,3},{7,5},{... | collective-permute-start | bytes 589832 | tf_op jit(solution)/shard_map/ppermute | solution.py:17
Sparse Core Ops, SparseCore 0:
  9.5 64.5 all-gather.2
  76.3 39.2 all-gather.4
where the time goes:
time: 146 us; the launch traced here: 145 us
  waiting for transfers between devices  90.4 us (62%)
  blocking collectives  16.9 us (12%)
  between operations  15.7 us (11%)
  matrix products  8.42 us (6%)
  starting transfers between devices  5.85 us (4%)
  other arithmetic  4.29 us (3%)
  local copies, waits for them, and re-layouts  3.28 us (2%)
    all_gather x1, waiting for transfers between devices, per_device(): lax.all_gather(w_qkv, 'lat', axis=0, tiled=True)  57.7 us
    all_gather x1, waiting for transfers between devices, per_device(): lax.all_gather(w_out, 'lat', axis=0, tiled=True)  30.6 us
    all_gather x1, blocking collectives, per_device(): lax.all_gather(mixed_rows, 'lon', axis=1, tiled=True)  4.97 us
    all_gather x1, blocking collectives, per_device(): lax.all_gather(pole_mixed, 'lon', axis=1, tiled=True)  4.01 us
    ppermute x1, starting transfers between devices, padded(): lax.ppermute(tail, axis, [(i, (i + 1) % count) for i in range(ends)])  3.89 us
    all_gather x1, blocking collectives, per_device(): key_piece = lax.all_gather(key_here, 'lon', axis=0, tiled=True)  3.36 us
  transfers between devices with their start and end apart: 4, of which 3 were waited for; matrix products, arithmetic and copies ran while one was open for 7% of the time, Pallas kernels for 0%

commit v1 on v0

--- a/solution.py
+++ b/solution.py
@@ -114,6 +114,20 @@
 
     initial = jnp.zeros((out_cols, blended.shape[2]), jnp.float32)
     return lax.fori_loop(0, turn_count, add_block, initial)
+
+
+def gather_weights(w_qkv, w_out, lon_place):
+    lat_count = lax.axis_size("lat")
+    rows = w_qkv.shape[0]
+    half = rows // 2
+    qkv_width = w_qkv.shape[1]
+    both = jnp.concatenate([w_qkv, w_out], axis=1)
+    mine = lax.dynamic_slice_in_dim(both, lon_place * half, half, 0)
+    spread = jnp.broadcast_to(mine[None], (lat_count,) + mine.shape)
+    got = lax.all_to_all(spread, "lat", 0, 0, tiled=False)
+    pair = lax.all_gather(got, "lon", axis=1, tiled=True)
+    full = pair.reshape(lat_count * rows, both.shape[1])
+    return full[:, :qkv_width], full[:, qkv_width:]
 
 
 def per_device(
@@ -137,10 +151,7 @@
     lon_place = lax.axis_index("lon")
     normed = layer_norm(own_tokens, gain_attn).astype(jnp.bfloat16)
     bias_rows = key_bias[0].T
-    full_qkv, full_out = (
-        lax.all_gather(w_qkv, "lat", axis=0, tiled=True),
-        lax.all_gather(w_out, "lat", axis=0, tiled=True),
-    )
+    full_qkv, full_out = gather_weights(w_qkv, w_out, lon_place)
     projected = jnp.dot(normed, full_qkv, preferred_element_type=jnp.float32).astype(jnp.bfloat16)
     queries = projected[:, :model_width].reshape(count_lon, head_count, head_dim)
     key_here = projected[:, model_width : 2 * model_width]

time: 146 us -> 121 us (0.83)
  waiting for transfers between devices: 90.4 us -> 12.2 us
  blocking collectives: 16.9 us -> 72.2 us
    all_gather x2 -> x1, waiting for transfers between devices: 88.4 us -> 9.13 us  [gather_weights(): pair = lax.all_gather(got, 'lon', axis=1, tiled=True)]
    all_to_all x0 -> x1, blocking collectives: none -> 58.4 us  [gather_weights(): got = lax.all_to_all(spread, 'lat', 0, 0, tiled=False)]
    ppermute x1, waiting for transfers between devices: 0.61 us -> 3.03 us  [padded(): lax.ppermute(head, axis, [((i + 1) % count, i) for i in range(ends)])]
  transfers between devices with their start and end apart: 4 -> 3, of which waited for: 3 -> 2; matrix products, arithmetic and copies ran while one was open for 7% -> 1% of each run, Pallas kernels for 0% -> 0%
where the time goes in v1:
time: 121 us; the launch traced here: 120 us
  blocking collectives  72.2 us (60%)
  between operations  15.8 us (13%)
  waiting for transfers between devices  12.2 us (10%)
  matrix products  8.43 us (7%)
  starting transfers between devices  5.29 us (4%)
  other arithmetic  3.47 us (3%)
  local copies, waits for them, and re-layouts  2.63 us (2%)
    all_to_all x1, blocking collectives, gather_weights(): got = lax.all_to_all(spread, 'lat', 0, 0, tiled=False)  58.4 us
    all_gather x1, waiting for transfers between devices, gather_weights(): pair = lax.all_gather(got, 'lon', axis=1, tiled=True)  9.13 us
    all_gather x1, blocking collectives, per_device(): lax.all_gather(mixed_rows, 'lon', axis=1, tiled=True)  3.55 us
    all_gather x1, blocking collectives, per_device(): bias_piece = lax.all_gather(bias_rows, 'lon', axis=0, tiled=True)  3.29 us
    ppermute x1, starting transfers between devices, padded(): lax.ppermute(tail, axis, [(i, (i + 1) % count) for i in range(ends)])  3.04 us
    ppermute x1, waiting for transfers between devices, padded(): lax.ppermute(head, axis, [((i + 1) % count, i) for i in range(ends)])  3.03 us
    all_gather x1, blocking collectives, per_device(): lax.all_gather(pole_mixed, 'lon', axis=1, tiled=True)  2.77 us
    dot_general x1, matrix products, per_device(): jnp.dot(normed, full_qkv, preferred_element_type=jnp.float32)  2.68 us
  transfers between devices with their start and end apart: 3, of which 2 were waited for; matrix products, arithmetic and copies ran while one was open for 1% of the time, Pallas kernels for 0%

profile of v1, /device:TPU:3, one launch (start us, length us, event | category | flops | bytes accessed | tf_op | source)
XLA Modules:
  0.0 120.1 jit_solution(3499747299981955733)
XLA Ops:
  6.5 1.0 fusion.44
  7.6 0.3 broadcast_in_dim.28
  7.8 58.4 %all_to_all.5 = bf16[8,48,3072]{2,1,0:T(8,128)(2,1)} all-to-all(bf16[8,48,3072]{2,1,0:T(8,128)(2,1)S(1)} %broadcast_in_dim.28), channel_id=1, replica_groups=mesh['groups'=2,'lat'=8,'lon'=2] {'lat'}, dimensions={0} | all-to-all | bytes 4718592 | tf_op jit(solution)/shard_map/all_to_all | solution.py:127
  66.3 0.0 all-gather.2.cloned.1.call-update
  68.3 0.3 reshape.249
  68.7 3.3 %all_gather.20 = bf16[256,12]{0,1:T(8,128)(2,1)S(1)} all-gather(bf16[128,12]{0,1:T(8,128)(2,1)S(1)} %bitcast.120), channel_id=1, replica_groups=mesh['groups'=2,'lat'=8,'lon'=2] {'lon'}, dimensions={0}, use_global_device_ids=true | all-gather | bytes 9216 | tf_op jit(solution)/shard_map/all_gather | solution.py:161
  72.0 0.2 convolution_select_fusion
  72.2 0.2 add_reduce_fusion
  72.4 0.1 convert_reduce_fusion
  72.5 0.2 fusion.35
  72.8 9.1 %all-gather.2.cloned.1.call-done = bf16[8,96,3072]{2,1,0:T(8,128)(2,1)} async-done(((bf16[8,48,3072]{2,1,0:T(8,128)(2,1)}), bf16[8,96,3072]{2,1,0:T(8,128)(2,1)}) %all-gather.2.cloned.1.call-update) | async-done | bytes 4718608 | tf_op jit(solution)/shard_map/all_gather | solution.py:128
  81.9 2.7 %convolution_convert_fusion = bf16[128,2304]{1,0:T(8,128)(2,1)S(1)} fusion(bf16[768,3072]{1,0:T(8,128)(2,1)} %bitcast.116, bf16[1,128,768]{2,1,0:T(8,128)(2,1)S(1)} %copy-done.1, f32[768]{0:T(1024)S(1)} %copy-done.5, f32[128]{0:T(128)S(1)} %add_rsqrt_fusion.1, f32[128]{0:T(128)S(1)} %broadcast_multiply_fusion.1), kind=kOutput, calls=%fused_computation.20 | convolution fusion | flops 453771264 | bytes 4329472 | tf_op jit(solution)/shard_map/dot_general | solution.py:155
  84.6 2.1 %all_gather.19 = bf16[256,768]{1,0:T(8,128)(2,1)S(1)} all-gather(bf16[128,768]{1,0:T(8,128)(2,1)S(1)} %get-tuple-element.186), channel_id=1, replica_groups=mesh['groups'=2,'lat'=8,'lon'=2] {'lon'}, dimensions={0}, use_global_device_ids=true | all-gather | bytes 589824 | tf_op jit(solution)/shard_map/all_gather | solution.py:159
  86.7 0.2 copy.28
  86.9 0.2 copy.27
  87.1 0.2 copy.31
  87.2 2.1 %all_gather.21 = bf16[256,768]{1,0:T(8,128)(2,1)S(1)} all-gather(bf16[128,768]{1,0:T(8,128)(2,1)S(1)} %get-tuple-element.187), channel_id=1, replica_groups=mesh['groups'=2,'lat'=8,'lon'=2] {'lon'}, dimensions={0}, use_global_device_ids=true | all-gather | bytes 589824 | tf_op jit(solution)/shard_map/all_gather | solution.py:160
  89.4 0.2 copy.29
  89.5 0.2 copy.32
  89.7 0.4 fusion.65
  90.1 0.4 fusion.66
  90.6 0.3 fusion.28
  90.9 0.2 fusion.18
  91.2 0.2 fusion.20
  91.4 1.7 %fusion.67 = (f32[128]{0:T(128)S(1)}, f32[128,768]{1,0:T(8,128)S(1)}) fusion(bf16[128,768]{0,1:T(8,128)(2,1)S(1)} %bitcast.118, bf16[768,3072]{1,0:T(8,128)(2,1)} %bitcast.117, bf16[1,128,768]{2,1,0:T(8,128)(2,1)S(1)} %copy-done.1), kind=kOutput, calls=%fused_computation.104 | convolution fusion | flops 151486336 | bytes 1966592 | tf_op jit(solution)/shard_map/dot_general | solution.py:172
  93.1 0.2 multiply_reduce_fusion
  93.4 0.1 fusion.58
  93.5 3.0 %collective-permute-start = (bf16[1,128,768]{2,1,0:T(8,128)(2,1)S(1)}, bf16[1,128,768]{2,1,0:T(8,128)(2,1)S(1)}, u32[]{:S(2)}, u32[]{:S(2)}) collective-permute-start(bf16[1,128,768]{2,1,0:T(8,128)(2,1)S(1)} %get-tuple-element.190), channel_id=1, source_target_pairs={{0,2},{2,4},{4,6},{6,8},{8,10},{10,12},{12,14},{1,3},{3,5},{5,7},{... | collective-permute-start | bytes 589832 | tf_op jit(solution)/shard_map/ppermute | solution.py:15
  96.5 2.2 %collective-permute-start.1 = (bf16[1,128,768]{2,1,0:T(8,128)(2,1)S(1)}, bf16[1,128,768]{2,1,0:T(8,128)(2,1)S(1)}, u32[]{:S(2)}, u32[]{:S(2)}) collective-permute-start(bf16[1,128,768]{2,1,0:T(8,128)(2,1)S(1)} %get-tuple-element.190), channel_id=1, source_target_pairs={{2,0},{4,2},{6,4},{8,6},{10,8},{12,10},{14,12},{3,1},{5,3},{7,5},{... | collective-permute-start | bytes 589832 | tf_op jit(solution)/shard_map/ppermute | solution.py:17
  98.8 0.2 copy.38
  99.0 0.3 convolution_convert_fusion.2
  99.3 0.2 copy.40
  99.5 2.8 %all_gather.23 = bf16[2,256,768]{2,1,0:T(8,128)(2,1)S(1)} all-gather(bf16[2,128,768]{2,1,0:T(8,128)(2,1)S(1)} %copy.40), channel_id=1, replica_groups=mesh['groups'=2,'lat'=8,'lon'=2] {'lon'}, dimensions={1}, use_global_device_ids=true | all-gather | bytes 1179648 | tf_op jit(solution)/shard_map/all_gather | solution.py:197
  102.3 0.1 fusion.61
  102.3 3.0 %collective-permute-done.1 = bf16[1,128,768]{2,1,0:T(8,128)(2,1)S(1)} collective-permute-done((bf16[1,128,768]{2,1,0:T(8,128)(2,1)S(1)}, bf16[1,128,768]{2,1,0:T(8,128)(2,1)S(1)}, u32[]{:S(2)}, u32[]{:S(2)}) %collective-permute-start.1) | collective-permute-done | bytes 196640 | tf_op jit(solution)/shard_map/ppermute | solution.py:17
  105.4 0.1 pad_maximum_fusion
  105.4 1.4 %convolution_convert_fusion.1 = bf16[2,128,768]{2,0,1:T(2,128)(2,1)S(1)} fusion(bf16[3,128,768]{2,1,0:T(8,128)(2,1)S(1)} %pad_maximum_fusion, f32[3,2]{0,1:T(2,128)S(1)} %convolution_select_fusion), kind=kOutput, calls=%fused_computation.27 | convolution fusion | flops 7274496 | bytes 983064 | tf_op jit(solution)/shard_map/rk,rjd->kjd/dot_general | solution.py:185
  106.9 0.5 copy.35
  107.4 0.3 convolution_convert_fusion.3
  107.6 0.2 copy.37
  107.8 3.6 %all_gather.22 = bf16[2,256,768]{2,1,0:T(8,128)(2,1)S(1)} all-gather(bf16[2,128,768]{2,1,0:T(8,128)(2,1)S(1)} %copy.37), channel_id=1, replica_groups=mesh['groups'=2,'lat'=8,'lon'=2] {'lon'}, dimensions={1}, use_global_device_ids=true | all-gather | bytes 1179648 | tf_op jit(solution)/shard_map/all_gather | solution.py:196
  111.4 0.2 add_convert_fusion
  111.6 0.9 while.14
  111.7 0.1 fusion.83
  111.8 0.2 fusion.84
  112.1 0.1 fusion.83
  112.3 0.2 fusion.84
  112.5 0.7 fusion.47
  (29 shorter events, 0.2 us)
Async XLA Ops:
  6.5 65.5 %copy-start = (f32[16,2]{0,1:T(2,128)S(1)}, f32[16,2]{0,1:T(2,128)}, u32[]{:S(2)}) copy-start(f32[16,2]{0,1:T(2,128)} %param.20) | copy-start | bytes 388
  6.5 75.3 %all-gather.2.cloned.1.call-start = ((), (), s32[]{:S(2)}) async-start(), calls=%async_computation.1 | async-start | bytes 7077888 | tf_op jit(solution)/shard_map/all_gather | solution.py:128
  66.2 2.1 %copy-start.2 = (bf16[2,768,64]{1,2,0:T(8,128)(2,1)S(1)}, bf16[2,768,64]{1,2,0:T(8,128)(2,1)}, u32[]{:S(2)}) copy-start(bf16[2,768,64]{1,2,0:T(8,128)(2,1)} %param.19) | copy-start | bytes 589828
  66.2 2.5 %copy-start.4 = (bf16[1,12,128]{2,1,0:T(8,128)(2,1)S(1)}, bf16[1,12,128]{2,1,0:T(8,128)(2,1)}, u32[]{:S(2)}) copy-start(bf16[1,12,128]{2,1,0:T(8,128)(2,1)} %param.16) | copy-start | bytes 9220
  66.3 6.2 %copy-start.1 = (bf16[1,128,768]{2,1,0:T(8,128)(2,1)S(1)}, bf16[1,128,768]{2,1,0:T(8,128)(2,1)}, u32[]{:S(2)}) copy-start(bf16[1,128,768]{2,1,0:T(8,128)(2,1)} %param.13) | copy-start | bytes 589828
  66.3 15.6 %copy-start.5 = (f32[768]{0:T(1024)S(1)}, f32[768]{0:T(1024)}, u32[]{:S(2)}) copy-start(f32[768]{0:T(1024)} %param.14) | copy-start | bytes 9220
  91.1 2.2 %copy-start.3 = (f32[768]{0:T(1024)S(1)}, f32[768]{0:T(1024)}, u32[]{:S(2)}) copy-start(f32[768]{0:T(1024)} %param.18) | copy-start | bytes 9220
  93.5 8.8 %collective-permute-start = (bf16[1,128,768]{2,1,0:T(8,128)(2,1)S(1)}, bf16[1,128,768]{2,1,0:T(8,128)(2,1)S(1)}, u32[]{:S(2)}, u32[]{:S(2)}) collective-permute-start(bf16[1,128,768]{2,1,0:T(8,128)(2,1)S(1)} %get-tuple-element.190), channel_id=1, source_target_pairs={{0,2},{2,4},{4,6},{6,8},{8,10},{10,12},{12,14},{1,3},{3,5},{5,7},{... | collective-permute-start | bytes 589832 | tf_op jit(solution)/shard_map/ppermute | solution.py:15
  96.5 8.8 %collective-permute-start.1 = (bf16[1,128,768]{2,1,0:T(8,128)(2,1)S(1)}, bf16[1,128,768]{2,1,0:T(8,128)(2,1)S(1)}, u32[]{:S(2)}, u32[]{:S(2)}) collective-permute-start(bf16[1,128,768]{2,1,0:T(8,128)(2,1)S(1)} %get-tuple-element.190), channel_id=1, source_target_pairs={{2,0},{4,2},{6,4},{8,6},{10,8},{12,10},{14,12},{3,1},{5,3},{7,5},{... | collective-permute-start | bytes 589832 | tf_op jit(solution)/shard_map/ppermute | solution.py:17
Sparse Core Ops, SparseCore 0:
  66.4 15.4 all-gather.1

commit v2 on v0

v2 whole, which is shorter than its diff:
```python
import jax
import jax.numpy as jnp
from jax import lax
from jax.sharding import PartitionSpec as P

AXES = ("groups", "lat", "lon")


def layer_norm(values, gain):
    average = jnp.mean(values, axis=-1, keepdims=True)
    centered = values - average
    variance = jnp.mean(centered * centered, axis=-1, keepdims=True)
    return (centered * lax.rsqrt(variance + 1e-05) * gain).astype(jnp.bfloat16)


def device_pairs(target):
    lat_count = lax.axis_size("lat")
    pairs = []
    for group in range(2):
        for row in range(lat_count):
            for core in range(2):
                to = target(group, row, core)
                if 0 <= to[1] < lat_count:
                    source = (group * lat_count + row) * 2 + core
                    pairs.append((source, (to[0] * lat_count + to[1]) * 2 + to[2]))
    return pairs


def move(values, target):
    return lax.ppermute(values, AXES, device_pairs(target))


def slab_groups():
    lat_count = lax.axis_size("lat")
    return [
        [
            (group * lat_count + 2 * pair + side) * 2 + core
            for group in range(2)
            for side in range(2)
            for core in range(2)
        ]
        for pair in range(lat_count // 2)
    ]


def lon_weights(row_ids, col_ids, half_width, lon_total):
    offset_lon = (
        jnp.mod(col_ids[None, :] - row_ids[:, None] + lon_total // 2, lon_total) - lon_total // 2
    )
    distance = jnp.abs(offset_lon).astype(jnp.float32)
    span_plus = (half_width + 1).astype(jnp.float32)
    tent_weight = jnp.where(
        distance <= half_width.astype(jnp.float32), (1.0 - distance / span_plus) / span_plus, 0.0
    )
    odd_weight = tent_weight * offset_lon.astype(jnp.float32) / span_plus
    return tent_weight.astype(jnp.bfloat16), odd_weight.astype(jnp.bfloat16)


def per_device(
    tokens,
    gain_attn,
    w_qkv,
    key_bias,
    w_out,
    gain_conv,
    w_conv,
    lat_taps,
    lon_half,
    lat_half,
    quad_off,
):
    own_tokens = tokens[0]
    count_lon, width = own_tokens.shape
    head_count = key_bias.shape[1]
    head_dim = width // head_count
    lat_count = lax.axis_size("lat")
    group, lat_row, core = (lax.axis_index(name) for name in AXES)
    side = lax.rem(lat_row, 2)
    quarter = width // 4
    heads_here = head_count // 4
    rows = w_qkv.shape[0]
    half = rows // 2

    bias_rows = head_count * count_lon // width
    message = jnp.concatenate(
        [
            own_tokens,
            key_bias[0].reshape(bias_rows, width),
            jnp.zeros((16 - bias_rows, width), jnp.bfloat16),
        ]
    )
    blocks = {}
    for flip_core in range(2):
        for flip_group in range(2):
            blocks[flip_group, flip_core] = move(
                message,
                lambda g, l, c: (g ^ flip_group, l - l % 2 + (c ^ flip_core), l % 2),
            )

    w_half = lax.dynamic_slice_in_dim(w_qkv, core * half, half, 0)
    w_half = w_half.reshape(half, 3, 2, 2, quarter)
    w_half = lax.dynamic_index_in_dim(w_half, group, 3, keepdims=False)
    w_half = w_half.transpose(2, 0, 1, 3).reshape(2, half, 3 * quarter)
    spread = jnp.broadcast_to(w_half[None], (lat_count // 2, 2, half, 3 * quarter))
    spread = spread.reshape(lat_count, half, 3 * quarter)
    got = lax.all_to_all(spread, "lat", 0, 0, tiled=False)
    w_here = lax.all_gather(got, "lon", axis=1, tiled=True).reshape(width, 3 * quarter)

    out_half = lax.dynamic_slice_in_dim(w_out, core * half, half, 0)
    out_rows = lax.all_gather(out_half, "lat", axis=0)
    full_out = lax.all_gather(out_rows, "lon", axis=1).reshape(width, width)

    passed = move(blocks[0, 0][:count_lon], lambda g, l, c: (g, l if c != l % 2 else -1, 1 - c))
    other_tokens = jnp.where(core == side, passed, blocks[0, 1][:count_lon])

    order = [(0, 0), (0, 1), (1, 0), (1, 1)]
    stacked = jnp.concatenate([blocks[key][:count_lon] for key in order])
    normed = layer_norm(stacked.astype(jnp.float32), gain_attn)
    projected = jnp.dot(normed, w_here, preferred_element_type=jnp.float32).astype(jnp.bfloat16)
    projected = projected.reshape(2, 2 * count_lon, 3, heads_here, head_dim)
    head_first = (2 * side + group) * heads_here
    bias = jnp.concatenate(
        [
            lax.dynamic_slice_in_dim(
                blocks[0, flip][count_lon : count_lon + bias_rows].reshape(head_count, count_lon),
                head_first,
                heads_here,
                0,
            )
            for flip in range(2)
        ],
        axis=1,
    ).astype(jnp.float32)
    scores = jnp.einsum(
        "sqhd,skhd->shqk", projected[:, :, 0], projected[:, :, 1], preferred_element_type=jnp.float32
    ) * (head_dim ** (-0.5))
    scores = scores + bias[None, :, None, :]
    expd = jnp.exp(scores - jnp.max(scores, axis=-1, keepdims=True))
    totals = jnp.sum(expd, axis=-1)
    weighted = jnp.einsum(
        "shqk,skhd->sqhd",
        expd.astype(jnp.bfloat16),
        projected[:, :, 2],
        preferred_element_type=jnp.float32,
    )
    attended = weighted / totals.transpose(0, 2, 1)[..., None]
    attended = attended.astype(jnp.bfloat16).reshape(2, 2, count_lon, quarter)
    attended = jnp.where(group == 1, attended[::-1], attended)
    attended = jnp.where(side == 1, attended[:, ::-1], attended)
    pieces = jnp.broadcast_to(attended[:, None], (2, 2, 2, count_lon, quarter))
    pieces = pieces.reshape(8, count_lon, quarter)
    back = lax.all_to_all(pieces, AXES, 0, 0, axis_index_groups=slab_groups())
    back = back.reshape(2, 2, 2, count_lon, quarter).transpose(2, 3, 1, 0, 4)
    back = back.reshape(2 * count_lon, width)

    both_tokens = jnp.where(
        side == 0,
        jnp.concatenate([own_tokens, other_tokens]),
        jnp.concatenate([other_tokens, own_tokens]),
    )
    middle = (
        both_tokens.astype(jnp.float32)
        + jnp.dot(back, full_out, preferred_element_type=jnp.float32)
    ).astype(jnp.bfloat16)
    conv_in = layer_norm(middle.astype(jnp.float32), gain_conv).reshape(2, count_lon, width)
    first, second = conv_in[0], conv_in[1]
    own_in = jnp.where(side == 0, first, second)
    other_in = jnp.where(side == 0, second, first)
    own_middle = lax.dynamic_slice_in_dim(middle, side * count_lon, count_lon, 0)
    halo = move(other_in, lambda g, l, c: (g, l + 2 - 4 * (l % 2), c))

    offsets = jnp.arange(3, dtype=jnp.int32) - 1
    one_hot = (
        (quad_off[0] + offsets + 1)[:, None]
        == jnp.arange(lat_taps.shape[0], dtype=jnp.int32)[None, :]
    ).astype(jnp.float32)
    tap_vals = jnp.sum(one_hot[:, :, None] * lat_taps[None], axis=1)
    tap_vals = jnp.where((jnp.abs(offsets) <= lat_half[0])[:, None], tap_vals, 0.0)
    pole_gain = jnp.where(lat_row == 0, tap_vals[0], 0.0) + jnp.where(
        lat_row == lat_count - 1, tap_vals[2], 0.0
    )
    other_gain = jnp.where(side == 0, tap_vals[2], tap_vals[0])
    halo_gain = jnp.where(side == 0, tap_vals[0], tap_vals[2])
    own_f32 = own_in.astype(jnp.float32)
    group_width = w_conv.shape[2]
    groups = width // group_width
    lon_total = 2 * count_lon
    row_ids = jnp.arange(lon_total, dtype=jnp.int32)
    col_ids = core * count_lon + jnp.arange(count_lon, dtype=jnp.int32)
    coeffs = lon_weights(row_ids, col_ids, lon_half[0], lon_total)
    coeffs = coeffs + lon_weights(row_ids, col_ids + count_lon, lon_half[0], lon_total)
    lines = []
    for basis in range(2):
        lines.append(
            other_gain[basis] * other_in.astype(jnp.float32)
            + tap_vals[1, basis] * own_f32
            + halo_gain[basis] * halo.astype(jnp.float32)
        )
    for basis in range(2):
        lines.append(pole_gain[basis] * own_f32)
    lines = jnp.stack(lines).astype(jnp.bfloat16)
    weights = w_conv.reshape(1, 2, groups, group_width, group_width)
    mixed = jnp.einsum(
        "pkjgc,kgce->pkjge",
        lines.reshape(2, 2, count_lon, groups, group_width),
        weights[0],
        preferred_element_type=jnp.float32,
    ).astype(jnp.bfloat16)
    mixed = mixed.reshape(4 * count_lon, width)
    partial = jnp.dot(
        jnp.concatenate(coeffs, axis=1), mixed, preferred_element_type=jnp.float32
    ).reshape(2, count_lon, width)
    mine = lax.dynamic_index_in_dim(partial, core, 0, keepdims=False)
    yours = lax.dynamic_index_in_dim(partial, 1 - core, 0, keepdims=False).astype(jnp.bfloat16)
    received = lax.ppermute(yours, "lon", [(0, 1), (1, 0)])
    updated = own_middle.astype(jnp.float32) + mine + received.astype(jnp.float32)
    return updated.astype(jnp.bfloat16)[None]


def solution(mesh):
    return jax.shard_map(
        per_device,
        mesh=mesh,
        in_specs=(
            P(("groups", "lat"), "lon", None),
            P(),
            P("lat", None),
            P("lat", None, "lon"),
            P("lat", None),
            P(),
            P(),
            P(),
            P("lat"),
            P("lat"),
            P("lat"),
        ),
        out_specs=P(("groups", "lat"), "lon", None),
        check_vma=False,
    )
```

time: 146 us -> 115 us (0.79)
  waiting for transfers between devices: 90.4 us -> 18.7 us
  starting transfers between devices: 5.85 us -> 23.6 us
  blocking collectives: 16.9 us -> 32.8 us
  local copies, waits for them, and re-layouts: 3.28 us -> 9.3 us
  other arithmetic: 4.29 us -> 9.59 us
  matrix products: 8.42 us -> 4.29 us
    all_gather x2 -> x1, waiting for transfers between devices: 88.4 us -> 0.02 us  [per_device(): full_out = lax.all_gather(out_rows, 'lon', axis=1).reshape(width, width)]
    all_gather x5 -> x2, blocking collectives: 16.9 us -> 32.8 us  [the longest x1 30.3 us: per_device(): out_rows = lax.all_gather(out_half, 'lat', axis=0)]
    all_to_all x0 -> x2, starting transfers between devices: none -> 14.5 us  [the longest x1 8.74 us: per_device(): back = lax.all_to_all(pieces, AXES, 0, 0, axis_index_groups=slab_groups())]
    ppermute x2 -> x7, waiting for transfers between devices: 0.61 us -> 14.7 us  [the longest x6 13.7 us: move(): return lax.ppermute(values, AXES, device_pairs(target))]
    another operation x2 -> x3, other arithmetic: 0.28 us -> 5.5 us  [per_device(): lines = jnp.stack(lines).astype(jnp.bfloat16)]
    dot_general x12 -> x6, matrix products: 8.42 us -> 4.29 us  [the longest x1 1.88 us: per_device(): jnp.dot(back, full_out, preferred_element_type=jnp.float32)]
    all_to_all x0 -> x2, waiting for transfers between devices: none -> 3.98 us  [the longest x1 3.97 us: per_device(): back = lax.all_to_all(pieces, AXES, 0, 0, axis_index_groups=slab_groups())]
    ppermute x2 -> x7, starting transfers between devices: 5.81 us -> 9.12 us  [the longest x6 7.78 us: move(): return lax.ppermute(values, AXES, device_pairs(target))]
  transfers between devices with their start and end apart: 4 -> 10, of which waited for: 3 -> 4; matrix products, arithmetic and copies ran while one was open for 7% -> 9% of each run, Pallas kernels for 0% -> 0%
where the time goes in v2:
time: 115 us; the launch traced here: 114 us
  blocking collectives  32.8 us (29%)
  starting transfers between devices  23.6 us (21%)
  waiting for transfers between devices  18.7 us (16%)
  between operations  15.8 us (14%)
  other arithmetic  9.59 us (8%)
  local copies, waits for them, and re-layouts  9.3 us (8%)
  matrix products  4.29 us (4%)
    all_gather x1, blocking collectives, per_device(): out_rows = lax.all_gather(out_half, 'lat', axis=0)  30.3 us
    ppermute x6, waiting for transfers between devices, move(): return lax.ppermute(values, AXES, device_pairs(target))  13.7 us
    all_to_all x1, starting transfers between devices, per_device(): back = lax.all_to_all(pieces, AXES, 0, 0, axis_index_groups=slab_groups())  8.74 us
    ppermute x6, starting transfers between devices, move(): return lax.ppermute(values, AXES, device_pairs(target))  7.78 us
    all_to_all x1, starting transfers between devices, per_device(): got = lax.all_to_all(spread, 'lat', 0, 0, tiled=False)  5.78 us
    another operation x3, other arithmetic, per_device(): lines = jnp.stack(lines).astype(jnp.bfloat16)  5.5 us
    all_to_all x1, waiting for transfers between devices, per_device(): back = lax.all_to_all(pieces, AXES, 0, 0, axis_index_groups=slab_groups())  3.97 us
    all_gather x1, blocking collectives, per_device(): lax.all_gather(got, 'lon', axis=1, tiled=True).reshape(width, 3 * quarter)  2.51 us
  transfers between devices with their start and end apart: 10, of which 4 were waited for; matrix products, arithmetic and copies ran while one was open for 9% of the time, Pallas kernels for 0%

profile of v2, /device:TPU:3, one launch (start us, length us, event | category | flops | bytes accessed | tf_op | source)
XLA Modules:
  0.0 114.2 jit_solution(7761984744745657535)
XLA Ops:
  6.5 0.8 reshape_squeeze.3
  7.4 1.0 maximum_maximum_fusion
  8.4 0.7 collective-permute-start
  9.1 3.3 %collective-permute-start.2 = (bf16[144,768]{1,0:T(8,128)(2,1)S(1)}, bf16[144,768]{1,0:T(8,128)(2,1)S(1)}, u32[]{:S(2)}, u32[]{:S(2)}) collective-permute-start(bf16[144,768]{1,0:T(8,128)(2,1)S(1)} %maximum_maximum_fusion), channel_id=1, source_target_pairs={{0,2},{1,0},{2,3},{3,1},{4,6},{5,4},{6,7},{7,5},{8,10},{9,8},{10,1... | collective-permute-start | bytes 663560 | tf_op jit(solution)/shard_map/ppermute | solution.py:30
  12.4 1.2 %collective-permute-start.3 = (bf16[144,768]{1,0:T(8,128)(2,1)S(1)}, bf16[144,768]{1,0:T(8,128)(2,1)S(1)}, u32[]{:S(2)}, u32[]{:S(2)}) collective-permute-start(bf16[144,768]{1,0:T(8,128)(2,1)S(1)} %maximum_maximum_fusion), channel_id=1, source_target_pairs={{0,16},{1,18},{2,17},{3,19},{4,20},{5,22},{6,21},{7,23},{8,24},{9,... | collective-permute-start | bytes 663560 | tf_op jit(solution)/shard_map/ppermute | solution.py:30
  13.6 0.3 reshape.200
  14.0 0.3 constant_dynamic-slice_fusion.3
  14.4 0.2 broadcast_in_dim.32
  14.6 0.8 broadcast_in_dim.33
  15.4 5.8 %all-to-all-start = ((bf16[8,48,576]{2,1,0:T(8,128)(2,1)}), bf16[8,48,576]{2,1,0:T(8,128)(2,1)S(1)}, u32[]{:S(2)}, u32[]{:S(2)}) async-start(bf16[8,48,576]{2,1,0:T(8,128)(2,1)} %bitcast.3), calls=%async_computation | async-start | bytes 983040 | tf_op jit(solution)/shard_map/all_to_all | solution.py:106
  21.3 30.3 %all-gather = bf16[384,768]{1,0:T(8,128)(2,1)} all-gather(bf16[48,768]{1,0:T(8,128)(2,1)S(1)} %constant_dynamic-slice_fusion), channel_id=2, replica_groups=mesh['groups'=2,'lat'=8,'lon'=2] {'lat'}, dimensions={0}, use_global_device_ids=true | all-gather | bytes 663552 | tf_op jit(solution)/shard_map/all_gather | solution.py:110
  53.2 1.3 %collective-permute-start.1 = (bf16[128,768]{1,0:T(8,128)(2,1)S(1)}, bf16[128,768]{1,0:T(8,128)(2,1)S(1)}, u32[]{:S(2)}, u32[]{:S(2)}) collective-permute-start(bf16[128,768]{1,0:T(8,128)(2,1)S(1)} %slice.98), channel_id=1, source_target_pairs={{1,0},{2,3},{5,4},{6,7},{9,8},{10,11},{13,12},{14,15},{17,16},{18,... | collective-permute-start | bytes 589832 | tf_op jit(solution)/shard_map/ppermute | solution.py:30
  54.7 7.3 %collective-permute-done.1 = bf16[128,768]{1,0:T(8,128)(2,1)S(1)} collective-permute-done((bf16[128,768]{1,0:T(8,128)(2,1)S(1)}, bf16[128,768]{1,0:T(8,128)(2,1)S(1)}, u32[]{:S(2)}, u32[]{:S(2)}) %collective-permute-start.1) | collective-permute-done | bytes 196640 | tf_op jit(solution)/shard_map/ppermute | solution.py:30
  62.1 0.2 convert_reduce_fusion
  62.3 0.4 fusion.2
  62.7 2.5 %all_gather.15 = bf16[8,96,576]{2,1,0:T(8,128)(2,1)S(1)} all-gather(bf16[8,48,576]{2,1,0:T(8,128)(2,1)S(1)} %all-to-all-done), channel_id=1, replica_groups=mesh['groups'=2,'lat'=8,'lon'=2] {'lon'}, dimensions={1}, use_global_device_ids=true | all-gather | bytes 1327104 | tf_op jit(solution)/shard_map/all_gather | solution.py:107
  65.2 0.9 convolution_convert_fusion.1
  66.2 0.4 fusion.60
  66.6 0.4 fusion.65
  67.0 0.2 fusion.5
  67.3 0.4 fusion.9
  67.7 0.2 broadcast_select_fusion
  67.9 0.9 rev.7
  68.8 0.3 broadcast_select_fusion.1
  69.1 0.8 broadcast_in_dim.34
  70.0 8.7 %all-to-all-start.1 = ((bf16[8,128,192]{1,2,0:T(8,128)(2,1)}), bf16[8,128,192]{1,2,0:T(8,128)(2,1)S(1)}, u32[]{:S(2)}, u32[]{:S(2)}) async-start(bf16[8,128,192]{1,2,0:T(8,128)(2,1)} %bitcast.10), calls=%async_computation.1 | async-start | bytes 786432 | tf_op jit(solution)/shard_map/all_to_all | solution.py:152
  78.7 0.3 squeeze_reshape.3
  79.7 0.6 fusion.64
  80.3 0.7 fusion.61
  81.0 0.6 fusion.62
  81.6 4.0 %all-to-all-done.1 = bf16[8,128,192]{1,2,0:T(8,128)(2,1)S(1)} async-done(((bf16[8,128,192]{1,2,0:T(8,128)(2,1)}), bf16[8,128,192]{1,2,0:T(8,128)(2,1)S(1)}, u32[]{:S(2)}, u32[]{:S(2)}) %all-to-all-start.1) | async-done | bytes 393248 | tf_op jit(solution)/shard_map/all_to_all | solution.py:152
  85.5 0.4 copy.53
  86.0 1.9 %convert_reduce_fusion.1 = (f32[256]{0:T(256)S(1)}, bf16[256,768]{1,0:T(8,128)(2,1)S(1)}) fusion(bf16[128,768]{1,0:T(8,128)(2,1)S(1)} %bitcast.104, bf16[128,768]{1,0:T(8,128)(2,1)S(1)} %get-tuple-element.12, pred[]{:T(512)S(6)} %eq.42, bf16[768,768]{1,0:T(8,128)(2,1)} %bitcast.106, bf16[96,8,2,128]{3,2,1,0:T(2,128)(2,1)S(1)} %bitcast.102), kind=kOutput, calls=%fused_computation.18 | convolution fusion | flops 304742144 | bytes 2360321 | tf_op jit(solution)/shard_map/dot_general | solution.py:163
  87.9 0.2 fusion.12
  88.1 0.2 fusion.14
  88.4 1.3 %collective-permute-start.5 = (bf16[128,768]{1,0:T(8,128)(2,1)S(1)}, bf16[128,768]{1,0:T(8,128)(2,1)S(1)}, u32[]{:S(2)}, u32[]{:S(2)}) collective-permute-start(bf16[128,768]{1,0:T(8,128)(2,1)S(1)} %broadcast_select_fusion.3), channel_id=1, source_target_pairs={{0,4},{1,5},{4,8},{5,9},{6,2},{7,3},{8,12},{9,13},{10,6},{11,7},{1... | collective-permute-start | bytes 589832 | tf_op jit(solution)/shard_map/ppermute | solution.py:30
  89.7 0.3 fusion.56
  90.0 6.3 %collective-permute-done.5 = bf16[128,768]{1,0:T(8,128)(2,1)S(1)} collective-permute-done((bf16[128,768]{1,0:T(8,128)(2,1)S(1)}, bf16[128,768]{1,0:T(8,128)(2,1)S(1)}, u32[]{:S(2)}, u32[]{:S(2)}) %collective-permute-start.5) | collective-permute-done | bytes 196640 | tf_op jit(solution)/shard_map/ppermute | solution.py:30
  96.3 2.1 %fusion.50 = (bf16[1,128,768]{2,1,0:T(8,128)(2,1)S(1)}, bf16[128,768]{1,0:T(8,128)(2,1)S(1)}) fusion(bf16[128,768]{1,0:T(8,128)(2,1)S(1)} %collective-permute-done.5, f32[]{:T(128)} %bitcast.21, f32[]{:T(128)} %bitcast.20, f32[]{:T(128)} %bitcast.19, bf16[256,768]{1,0:T(8,128)(2,1)S(1)} %fusion.14, pred[]{:T(512)S(6)} %eq.42), kind=kLoop, calls=%fused_computation.74 | loop fusion | flops 1081344 | bytes 983053 | tf_op jit(solution)/shard_map/stack | solution.py:201
  98.4 3.3 %fusion.49 = (bf16[1,128,768]{2,1,0:T(8,128)(2,1)S(1)}, bf16[1,128,768]{2,1,0:T(8,128)(2,1)S(1)}, bf16[1,128,768]{2,1,0:T(8,128)(2,1)S(1)}) fusion(bf16[128,768]{1,0:T(8,128)(2,1)S(1)} %collective-permute-done.5, bf16[128,768]{1,0:T(8,128)(2,1)S(1)} %get-tuple-element.6, f32[]{:T(128)} %bitcast.25, f32[]{:T(128)} %bitcast.24, f32[]{:T(128)} %bitcast.23, ...), kind=kLoop, calls=%fused_computation.73 | loop fusion | flops 1376256 | bytes 1376277 | tf_op jit(solution)/shard_map/stack | solution.py:201
  101.8 0.4 copy.54
  102.3 0.4 fusion.7
  102.6 0.8 copy.57
  103.4 0.3 reshape.211
  103.7 0.4 fusion.17
  104.2 1.3 %collective-permute-start.6 = (bf16[128,768]{1,0:T(8,128)(2,1)S(1)}, bf16[128,768]{1,0:T(8,128)(2,1)S(1)}, u32[]{:S(2)}, u32[]{:S(2)}) collective-permute-start(bf16[128,768]{1,0:T(8,128)(2,1)S(1)} %fusion.45), channel_id=1, source_target_pairs={{0,1},{1,0},{2,3},{3,2},{4,5},{5,4},{6,7},{7,6},{8,9},{9,8},{10,11... | collective-permute-start | bytes 589832 | tf_op jit(solution)/shard_map/ppermute | solution.py:215
  105.5 1.1 collective-permute-done.6
  106.6 0.7 fusion.46
  (57 shorter events, 1.2 us)
Async XLA Ops:
  6.5 7.1 %copy-start = (bf16[96,2304]{1,0:T(8,128)(2,1)S(1)}, bf16[96,2304]{1,0:T(8,128)(2,1)}, u32[]{:S(2)}) copy-start(bf16[96,2304]{1,0:T(8,128)(2,1)} %param.13) | copy-start | bytes 1327108
  8.4 44.8 %collective-permute-start = (bf16[144,768]{1,0:T(8,128)(2,1)S(1)}, bf16[144,768]{1,0:T(8,128)(2,1)S(1)}, u32[]{:S(2)}, u32[]{:S(2)}) collective-permute-start(bf16[144,768]{1,0:T(8,128)(2,1)S(1)} %maximum_maximum_fusion), channel_id=1, source_target_pairs={{0,0},{1,2},{2,1},{3,3},{4,4},{5,6},{6,5},{7,7},{8,8},{9,10},{10,9... | collective-permute-start | bytes 663560 | tf_op jit(solution)/shard_map/ppermute | solution.py:30
  9.1 45.5 %collective-permute-start.2 = (bf16[144,768]{1,0:T(8,128)(2,1)S(1)}, bf16[144,768]{1,0:T(8,128)(2,1)S(1)}, u32[]{:S(2)}, u32[]{:S(2)}) collective-permute-start(bf16[144,768]{1,0:T(8,128)(2,1)S(1)} %maximum_maximum_fusion), channel_id=1, source_target_pairs={{0,2},{1,0},{2,3},{3,1},{4,6},{5,4},{6,7},{7,5},{8,10},{9,8},{10,1... | collective-permute-start | bytes 663560 | tf_op jit(solution)/shard_map/ppermute | solution.py:30
  12.4 42.2 %collective-permute-start.3 = (bf16[144,768]{1,0:T(8,128)(2,1)S(1)}, bf16[144,768]{1,0:T(8,128)(2,1)S(1)}, u32[]{:S(2)}, u32[]{:S(2)}) collective-permute-start(bf16[144,768]{1,0:T(8,128)(2,1)S(1)} %maximum_maximum_fusion), channel_id=1, source_target_pairs={{0,16},{1,18},{2,17},{3,19},{4,20},{5,22},{6,21},{7,23},{8,24},{9,... | collective-permute-start | bytes 663560 | tf_op jit(solution)/shard_map/ppermute | solution.py:30
  13.6 41.0 %collective-permute-start.4 = (bf16[144,768]{1,0:T(8,128)(2,1)S(1)}, bf16[144,768]{1,0:T(8,128)(2,1)S(1)}, u32[]{:S(2)}, u32[]{:S(2)}) collective-permute-start(bf16[144,768]{1,0:T(8,128)(2,1)S(1)} %maximum_maximum_fusion), channel_id=1, source_target_pairs={{0,18},{1,16},{2,19},{3,17},{4,22},{5,20},{6,23},{7,21},{8,26},{9,... | collective-permute-start | bytes 663560 | tf_op jit(solution)/shard_map/ppermute | solution.py:30
  13.9 7.3 %copy-start.3 = (bf16[96,768]{1,0:T(8,128)(2,1)S(1)}, bf16[96,768]{1,0:T(8,128)(2,1)}, u32[]{:S(2)}) copy-start(bf16[96,768]{1,0:T(8,128)(2,1)} %param.15) | copy-start | bytes 442372
  14.6 38.4 %copy-start.5 = (f32[16,2]{0,1:T(2,128)S(1)}, f32[16,2]{0,1:T(2,128)}, u32[]{:S(2)}) copy-start(f32[16,2]{0,1:T(2,128)} %param.18) | copy-start | bytes 388
  15.4 47.2 %all-to-all-start = ((bf16[8,48,576]{2,1,0:T(8,128)(2,1)}), bf16[8,48,576]{2,1,0:T(8,128)(2,1)S(1)}, u32[]{:S(2)}, u32[]{:S(2)}) async-start(bf16[8,48,576]{2,1,0:T(8,128)(2,1)} %bitcast.3), calls=%async_computation | async-start | bytes 983040 | tf_op jit(solution)/shard_map/all_to_all | solution.py:106
  21.2 64.7 %all-gather.4.cloned.1.call-start = ((), (), s32[]{:S(2)}) async-start(), calls=%async_computation.2 | async-start | bytes 1769472 | tf_op jit(solution)/shard_map/all_gather | solution.py:111
  53.2 8.8 %collective-permute-start.1 = (bf16[128,768]{1,0:T(8,128)(2,1)S(1)}, bf16[128,768]{1,0:T(8,128)(2,1)S(1)}, u32[]{:S(2)}, u32[]{:S(2)}) collective-permute-start(bf16[128,768]{1,0:T(8,128)(2,1)S(1)} %slice.98), channel_id=1, source_target_pairs={{1,0},{2,3},{5,4},{6,7},{9,8},{10,11},{13,12},{14,15},{17,16},{18,... | collective-permute-start | bytes 589832 | tf_op jit(solution)/shard_map/ppermute | solution.py:30
  62.1 3.1 %copy-start.6 = (f32[768]{0:T(1024)S(1)}, f32[768]{0:T(1024)}, u32[]{:S(2)}) copy-start(f32[768]{0:T(1024)} %param.12) | copy-start | bytes 9220
  67.7 11.0 %copy-start.2 = (bf16[2,768,64]{1,2,0:T(8,128)(2,1)S(1)}, bf16[2,768,64]{1,2,0:T(8,128)(2,1)}, u32[]{:S(2)}) copy-start(bf16[2,768,64]{1,2,0:T(8,128)(2,1)} %param.17) | copy-start | bytes 589828
  69.1 16.9 %copy-start.1 = (bf16[1,128,768]{2,1,0:T(8,128)(2,1)S(1)}, bf16[1,128,768]{2,1,0:T(8,128)(2,1)}, u32[]{:S(2)}) copy-start(bf16[1,128,768]{2,1,0:T(8,128)(2,1)} %param.11) | copy-start | bytes 589828
  70.0 15.6 %all-to-all-start.1 = ((bf16[8,128,192]{1,2,0:T(8,128)(2,1)}), bf16[8,128,192]{1,2,0:T(8,128)(2,1)S(1)}, u32[]{:S(2)}, u32[]{:S(2)}) async-start(bf16[8,128,192]{1,2,0:T(8,128)(2,1)} %bitcast.10), calls=%async_computation.1 | async-start | bytes 786432 | tf_op jit(solution)/shard_map/all_to_all | solution.py:152
  86.0 2.2 %copy-start.4 = (f32[768]{0:T(1024)S(1)}, f32[768]{0:T(1024)}, u32[]{:S(2)}) copy-start(f32[768]{0:T(1024)} %param.16) | copy-start | bytes 9220
  88.4 7.9 %collective-permute-start.5 = (bf16[128,768]{1,0:T(8,128)(2,1)S(1)}, bf16[128,768]{1,0:T(8,128)(2,1)S(1)}, u32[]{:S(2)}, u32[]{:S(2)}) collective-permute-start(bf16[128,768]{1,0:T(8,128)(2,1)S(1)} %broadcast_select_fusion.3), channel_id=1, source_target_pairs={{0,4},{1,5},{4,8},{5,9},{6,2},{7,3},{8,12},{9,13},{10,6},{11,7},{1... | collective-permute-start | bytes 589832 | tf_op jit(solution)/shard_map/ppermute | solution.py:30
  104.2 2.4 %collective-permute-start.6 = (bf16[128,768]{1,0:T(8,128)(2,1)S(1)}, bf16[128,768]{1,0:T(8,128)(2,1)S(1)}, u32[]{:S(2)}, u32[]{:S(2)}) collective-permute-start(bf16[128,768]{1,0:T(8,128)(2,1)S(1)} %fusion.45), channel_id=1, source_target_pairs={{0,1},{1,0},{2,3},{3,2},{4,5},{5,4},{6,7},{7,6},{8,9},{9,8},{10,11... | collective-permute-start | bytes 589832 | tf_op jit(solution)/shard_map/ppermute | solution.py:215
Sparse Core Ops, SparseCore 0:
  51.7 16.8 all-gather.3

commit v3 on v2

v3 whole, which is shorter than its diff:
```python
import functools

import jax
import jax.numpy as jnp
from jax import lax
from jax.experimental import pallas as pl
from jax.experimental.pallas import tpu as pltpu
from jax.sharding import PartitionSpec as P

AXES = ("groups", "lat", "lon")
VMEM = pl.BlockSpec(memory_space=pltpu.VMEM)
SMEM = pl.BlockSpec(memory_space=pltpu.SMEM)
BF16 = jnp.bfloat16
F32 = jnp.float32


def call(body, outs, specs, args, flops, scratch=()):
    outs = tuple(jax.ShapeDtypeStruct(shape, dtype) for shape, dtype in outs)
    moved = sum(a.size * a.dtype.itemsize for a in args)
    return pl.pallas_call(
        body,
        out_shape=outs,
        in_specs=specs,
        out_specs=tuple(VMEM for _ in outs),
        scratch_shapes=list(scratch),
        compiler_params=pltpu.CompilerParams(vmem_limit_bytes=32 * 1024 * 1024),
        cost_estimate=pl.CostEstimate(flops=flops, bytes_accessed=moved, transcendentals=0),
    )(*args)


def device_pairs(target):
    lat_count = lax.axis_size("lat")
    pairs = []
    for group in range(2):
        for row in range(lat_count):
            for core in range(2):
                to = target(group, row, core)
                if 0 <= to[1] < lat_count:
                    source = (group * lat_count + row) * 2 + core
                    pairs.append((source, (to[0] * lat_count + to[1]) * 2 + to[2]))
    return pairs


def move(values, target):
    return lax.ppermute(values, AXES, device_pairs(target))


def swap_cores(values):
    return lax.ppermute(values, "lon", [(0, 1), (1, 0)])


def slab_groups():
    lat_count = lax.axis_size("lat")
    return [
        [
            (group * lat_count + 2 * pair + side) * 2 + core
            for group in range(2)
            for side in range(2)
            for core in range(2)
        ]
        for pair in range(lat_count // 2)
    ]


def norm_rows(values, gain):
    average = jnp.mean(values, axis=-1, keepdims=True)
    centered = values - average
    variance = jnp.mean(centered * centered, axis=-1, keepdims=True)
    return (centered * lax.rsqrt(variance + 1e-05) * gain).astype(BF16)


def pack_body(place, tokens, bias, w_qkv, w_out, message, qkv_pieces, out_pieces):
    count = tokens.shape[0]
    heads, bias_width = bias.shape
    message[:count, :] = tokens[...]
    message[count:, :] = jnp.zeros((16, tokens.shape[1]), BF16)
    message[count : count + heads, :bias_width] = bias[...]
    group, core = place[0], place[2]
    half = qkv_pieces.shape[1]
    width = w_out.shape[1]
    quarter = width // 4
    start = pl.multiple_of(core * half, half)
    rows = w_qkv[pl.ds(start, half), :]
    for side in range(2):
        parts = []
        for kind in range(3):
            first = kind * width + side * 2 * quarter
            parts.append(
                jnp.where(
                    group == 0,
                    rows[:, first : first + quarter],
                    rows[:, first + quarter : first + 2 * quarter],
                )
            )
        piece = jnp.concatenate(parts, axis=1)
        for pair in range(qkv_pieces.shape[0] // 2):
            qkv_pieces[2 * pair + side] = piece
    out_rows = w_out[pl.ds(start, half), :]
    for row in range(out_pieces.shape[0]):
        out_pieces[row] = out_rows


def join_halves(core, mine, other, joined):
    count, half, _ = mine.shape
    for row in range(count):
        joined[pl.ds(pl.multiple_of(row * 2 * half + core * half, half), half), :] = mine[row]
        joined[pl.ds(pl.multiple_of(row * 2 * half + (1 - core) * half, half), half), :] = other[row]


def attend_body(
    place, gain, near0, near1, far0, far1, mine, other, pieces, weights, bias_rows, normed
):
    group, lat_row, core = place[0], place[1], place[2]
    side = lax.rem(lat_row, 2)
    count, quarter = pieces.shape[3], pieces.shape[4]
    heads = 3
    head_dim = quarter // heads
    join_halves(core, mine, other, weights)
    gains = gain[...]
    for slot, block in enumerate((near0, near1, far0, far1)):
        normed[slot * count : (slot + 1) * count, :] = norm_rows(
            block[:count, :].astype(F32), gains
        )
    for slot, block in enumerate((near0, near1)):
        bias_rows[:, slot * count : (slot + 1) * count] = block[count:, :count].astype(F32)
    first_head = (2 * side + group) * heads
    for far in range(2):
        projected = jnp.dot(
            normed[far * 2 * count : (far + 1) * 2 * count, :],
            weights[...],
            preferred_element_type=F32,
        ).astype(BF16)
        outs = []
        for head in range(heads):
            low = head * head_dim
            queries = projected[:, low : low + head_dim]
            keys = projected[:, quarter + low : quarter + low + head_dim]
            values = projected[:, 2 * quarter + low : 2 * quarter + low + head_dim]
            scores = lax.dot_general(
                queries, keys, (((1,), (1,)), ((), ())), preferred_element_type=F32
            ) * (head_dim**-0.5)
            scores = scores + bias_rows[pl.ds(first_head + head, 1), :]
            expd = jnp.exp(scores - jnp.max(scores, axis=-1, keepdims=True))
            totals = jnp.sum(expd, axis=-1, keepdims=True)
            weighted = jnp.dot(expd.astype(BF16), values, preferred_element_type=F32)
            outs.append((weighted / totals).astype(BF16))
        attended = jnp.concatenate(outs, axis=1)
        sample = far + group - 2 * far * group
        for flip in range(2):
            lon_at = flip + side - 2 * flip * side
            part = attended[flip * count : (flip + 1) * count]
            for to_side in range(2):
                pieces[sample, to_side, lon_at] = part


def project_out(band, back, weights, tokens, gain):
    attended = jnp.concatenate(
        [back[part % 2, part // 2, band] for part in range(4)], axis=1
    )
    summed = tokens + jnp.dot(attended, weights[...], preferred_element_type=F32)
    middle = summed.astype(BF16)
    return middle, norm_rows(middle.astype(F32), gain)


def other_body(place, gain, back, mine, other, passed, near1, other_in, full_out):
    lat_row, core = place[1], place[2]
    side = lax.rem(lat_row, 2)
    count = other_in.shape[0]
    join_halves(core, mine, other, full_out)
    tokens = jnp.where(
        core == side, passed[:count, :].astype(F32), near1[:count, :].astype(F32)
    )
    other_in[...] = project_out(1 - side, back, full_out, tokens, gain[...])[1]


def diagonal_body(w_conv, blocks):
    size = w_conv.shape[2]
    blocks[...] = jnp.zeros(blocks.shape, BF16)
    per_block = blocks.shape[2] // size
    for basis in range(blocks.shape[0]):
        for tile in range(blocks.shape[1]):
            for at in range(per_block):
                first = (tile * per_block + at) * size
                low, high = at * size, (at + 1) * size
                blocks[basis, tile, low:high, low:high] = w_conv[basis, first : first + size, :]


def tent_pair(row_count, first_col, col_count, half_width):
    rows = lax.broadcasted_iota(jnp.int32, (row_count, col_count), 0)
    cols = lax.broadcasted_iota(jnp.int32, (row_count, col_count), 1) + first_col
    offset = ((cols - rows + row_count // 2) & (row_count - 1)) - row_count // 2
    distance = jnp.abs(offset).astype(F32)
    span_plus = (half_width + 1).astype(F32)
    tent = jnp.where(
        distance <= half_width.astype(F32), (1.0 - distance / span_plus) / span_plus, 0.0
    )
    odd = tent * offset.astype(F32) / span_plus
    return tent.astype(BF16), odd.astype(BF16)


def mix(lines, blocks, basis):
    size = blocks.shape[2]
    return jnp.concatenate(
        [
            jnp.dot(
                lines[:, tile * size : (tile + 1) * size],
                blocks[basis, tile],
                preferred_element_type=F32,
            ).astype(BF16)
            for tile in range(blocks.shape[1])
        ],
        axis=1,
    )


def tap_gain(taps, quad_off, lat_half, offset, basis):
    value = taps[quad_off[0] + offset + 1, basis]
    if offset == 0:
        return value
    return jnp.where(lat_half[0] >= 1, value, 0.0)


def own_body(
    lat_count,
    place,
    lon_half,
    lat_half,
    quad_off,
    taps,
    gain,
    back,
    mine,
    other,
    tokens,
    other_in,
    blocks,
    middle,
    partial,
    full_out,
):
    lat_row, core = place[1], place[2]
    side = lax.rem(lat_row, 2)
    count = tokens.shape[0]
    join_halves(core, mine, other, full_out)
    own_middle, own_in = project_out(side, back, full_out, tokens[...].astype(F32), gain[...])
    middle[...] = own_middle
    own = own_in.astype(F32)
    neighbour = other_in[...].astype(F32)
    rows = partial.shape[0]
    mixed, coeffs = [], []
    direct = tent_pair(rows, core * count, count, lon_half[0])
    rolled = tent_pair(rows, core * count + count, count, lon_half[0])
    for basis in range(2):
        below = tap_gain(taps, quad_off, lat_half, -1, basis)
        above = tap_gain(taps, quad_off, lat_half, 1, basis)
        centre = tap_gain(taps, quad_off, lat_half, 0, basis)
        other_gain = jnp.where(side == 0, above, below)
        pole_gain = jnp.where(lat_row == 0, below, 0.0) + jnp.where(
            lat_row == lat_count - 1, above, 0.0
        )
        lines = jnp.concatenate(
            [
                (other_gain * neighbour + centre * own).astype(BF16),
                (pole_gain * own).astype(BF16),
            ]
        )
        mixed.append(mix(lines, blocks, basis))
        coeffs += [direct[basis], rolled[basis]]
    partial[...] = jnp.dot(
        jnp.concatenate(coeffs, axis=1),
        jnp.concatenate(mixed, axis=0),
        preferred_element_type=F32,
    )


def halo_body(
    place, lon_half, lat_half, quad_off, taps, halo, blocks, middle, partial, kept, sent, total
):
    lat_row, core = place[1], place[2]
    side = lax.rem(lat_row, 2)
    count = halo.shape[0]
    rows = partial.shape[0]
    values = halo[...].astype(F32)
    mixed = []
    for basis in range(2):
        below = tap_gain(taps, quad_off, lat_half, -1, basis)
        above = tap_gain(taps, quad_off, lat_half, 1, basis)
        gain = jnp.where(side == 0, below, above)
        mixed.append(mix((gain * values).astype(BF16), blocks, basis))
    total[...] = partial[...] + jnp.dot(
        jnp.concatenate(tent_pair(rows, core * count, count, lon_half[0]), axis=1),
        jnp.concatenate(mixed, axis=0),
        preferred_element_type=F32,
    )
    here = pl.multiple_of(core * count, count)
    there = pl.multiple_of((1 - core) * count, count)
    kept[...] = middle[...].astype(F32) + total[pl.ds(here, count), :]
    sent[...] = total[pl.ds(there, count), :].astype(BF16)


def pack_plain(place, tokens, bias, w_qkv, w_out, lat_count):
    count, width = tokens.shape
    quarter = width // 4
    half = w_qkv.shape[0] // 2
    tail = jnp.zeros((16, width), BF16).at[: bias.shape[0], : bias.shape[1]].set(bias)
    rows = lax.dynamic_slice_in_dim(w_qkv, place[2] * half, half, 0)
    rows = rows.reshape(half, 3, 2, 2, quarter)
    rows = lax.dynamic_index_in_dim(rows, place[0], 3, keepdims=False)
    rows = rows.transpose(2, 0, 1, 3).reshape(2, half, 3 * quarter)
    qkv = jnp.broadcast_to(rows[None], (lat_count // 2, 2, half, 3 * quarter))
    out = lax.dynamic_slice_in_dim(w_out, place[2] * half, half, 0)
    return (
        jnp.concatenate([tokens, tail]),
        qkv.reshape(lat_count, half, 3 * quarter),
        jnp.broadcast_to(out[None], (lat_count, half, width)),
    )


def regroup(core, mine, other):
    both = jnp.where(core == 0, jnp.stack([mine, other], 1), jnp.stack([other, mine], 1))
    whole = both.reshape(8, 2, -1, mine.shape[2])
    pick = lambda index: lax.dynamic_index_in_dim(whole, index, 1, keepdims=False)
    return pick(core), pick(1 - core)


def per_device(
    tokens,
    gain_attn,
    w_qkv,
    key_bias,
    w_out,
    gain_conv,
    w_conv,
    lat_taps,
    lon_half,
    lat_half,
    quad_off,
):
    own_tokens = tokens[0]
    count, width = own_tokens.shape
    quarter = width // 4
    lat_count = lax.axis_size("lat")
    place = jnp.stack([lax.axis_index(name) for name in AXES]).astype(jnp.int32)
    core = place[2]
    half = w_qkv.shape[0] // 2
    gain_attn = gain_attn[None]
    gain_conv = gain_conv[None]

    if half % 16 == 0:
        message, qkv_pieces, out_pieces = call(
            pack_body,
            [
                ((count + 16, width), BF16),
                ((lat_count, half, 3 * quarter), BF16),
                ((lat_count, half, width), BF16),
            ],
            [SMEM] + [VMEM] * 4,
            (place, own_tokens, key_bias[0], w_qkv, w_out),
            0,
        )
    else:
        message, qkv_pieces, out_pieces = pack_plain(
            place, own_tokens, key_bias[0], w_qkv, w_out, lat_count
        )
    qkv_mine = lax.all_to_all(qkv_pieces, "lat", 0, 0)
    blocks = {}
    for flip_core in range(2):
        for flip_group in range(2):
            blocks[flip_group, flip_core] = move(
                message,
                lambda g, l, c: (g ^ flip_group, l - l % 2 + (c ^ flip_core), l % 2),
            )
    out_mine = lax.all_to_all(out_pieces, "lat", 0, 0)
    qkv_other = swap_cores(qkv_mine)
    out_other = swap_cores(out_mine)
    passed = move(blocks[0, 0], lambda g, l, c: (g, l if c != l % 2 else -1, 1 - c))
    if half % 16:
        qkv_mine, qkv_other = regroup(core, qkv_mine, qkv_other)
        out_mine, out_other = regroup(core, out_mine, out_other)

    size = 4 * w_conv.shape[2]
    (diagonal,) = call(
        diagonal_body, [((2, width // size, size, size), BF16)], [VMEM], (w_conv,), 0
    )

    (pieces,) = call(
        attend_body,
        [((2, 2, 2, count, quarter), BF16)],
        [SMEM] + [VMEM] * 7,
        (
            place,
            gain_attn,
            blocks[0, 0],
            blocks[0, 1],
            blocks[1, 0],
            blocks[1, 1],
            qkv_mine,
            qkv_other,
        ),
        2 * 512 * 768 * 576 + 4 * 6 * 256 * 256 * 64,
        [
            pltpu.VMEM((width, 3 * quarter), BF16),
            pltpu.VMEM((16, 2 * count), F32),
            pltpu.VMEM((4 * count, width), BF16),
        ],
    )
    back = lax.all_to_all(
        pieces.reshape(8, count, quarter), AXES, 0, 0, axis_index_groups=slab_groups()
    ).reshape(2, 2, 2, count, quarter)

    (other_in,) = call(
        other_body,
        [((count, width), BF16)],
        [SMEM] + [VMEM] * 6,
        (place, gain_conv, back, out_mine, out_other, passed, blocks[0, 1]),
        2 * count * width * width,
        [pltpu.VMEM((width, width), BF16)],
    )
    halo = move(other_in, lambda g, l, c: (g, l + 2 - 4 * (l % 2), c))
    middle, partial = call(
        functools.partial(own_body, lat_count),
        [((count, width), BF16), ((2 * count, width), F32)],
        [SMEM] * 5 + [VMEM] * 7,
        (
            place,
            lon_half,
            lat_half,
            quad_off,
            lat_taps,
            gain_conv,
            back,
            out_mine,
            out_other,
            own_tokens,
            other_in,
            diagonal,
        ),
        2 * count * width * width * 3,
        [pltpu.VMEM((width, width), BF16)],
    )
    kept, sent = call(
        halo_body,
        [((count, width), F32), ((count, width), BF16)],
        [SMEM] * 5 + [VMEM] * 4,
        (place, lon_half, lat_half, quad_off, lat_taps, halo, diagonal, middle, partial),
        2 * 256 * 256 * width,
        [pltpu.VMEM((2 * count, width), F32)],
    )
    received = swap_cores(sent)
    return (kept + received.astype(F32)).astype(BF16)[None]


def solution(mesh):
    return jax.shard_map(
        per_device,
        mesh=mesh,
        in_specs=(
            P(("groups", "lat"), "lon", None),
            P(),
            P("lat", None),
            P("lat", None, "lon"),
            P("lat", None),
            P(),
            P(),
            P(),
            P("lat"),
            P("lat"),
            P("lat"),
        ),
        out_specs=P(("groups", "lat"), "lon", None),
        check_vma=False,
    )
```

time: 115 us -> 78.8 us (0.69)
  the two profiles are of different devices: /device:TPU:3 before, /device:TPU:0 now
where the time goes in v3:
time: 78.8 us; the launch traced here: 78.2 us
  blocking collectives  20.9 us (27%)
  starting transfers between devices  20.5 us (26%)
  waiting for transfers between devices  18 us (23%)
  Pallas kernels  8.81 us (11%)
  local copies, waits for them, and re-layouts  7.07 us (9%)
  between operations  2.14 us (3%)
  other arithmetic  0.79 us (1%)
    all_to_all x1, blocking collectives, per_device(): qkv_mine = lax.all_to_all(qkv_pieces, 'lat', 0, 0)  20.9 us
    ppermute x6, starting transfers between devices, move(): return lax.ppermute(values, AXES, device_pairs(target))  11.8 us
    all_to_all x1, waiting for transfers between devices, per_device(): out_mine = lax.all_to_all(out_pieces, 'lat', 0, 0)  8.95 us
    pallas_call x6, Pallas kernels, call(): pl.pallas_call(body, out_shape=outs, in_specs=specs, out_specs=tuple((VME...  8.81 us
    all_to_all x1, waiting for transfers between devices, per_device(): lax.all_to_all(pieces.reshape(8, count, quarter), AXES, 0, 0, axis_index_...  7.03 us
    unnamed x24, local copies, waits for them, and re-layouts  5.9 us
    all_to_all x1, starting transfers between devices, per_device(): lax.all_to_all(pieces.reshape(8, count, quarter), AXES, 0, 0, axis_index_...  4.85 us
    all_to_all x1, starting transfers between devices, per_device(): out_mine = lax.all_to_all(out_pieces, 'lat', 0, 0)  3.72 us
  transfers between devices with their start and end apart: 11, of which 4 were waited for; matrix products, arithmetic and copies ran while one was open for 2% of the time, Pallas kernels for 6%

profile of v3, /device:TPU:0, one launch (start us, length us, event | category | flops | bytes accessed | tf_op | source)
XLA Modules:
  0.0 78.2 jit_solution(3326395128612839277)
XLA Ops:
  0.0 0.1 pad_add_fusion.place
  0.1 0.6 copy-done.6
  0.7 0.9 %copy-done = bf16[1,128,768]{2,1,0:T(8,128)(2,1)S(1)} copy-done((bf16[1,128,768]{2,1,0:T(8,128)(2,1)S(1)}, bf16[1,128,768]{2,1,0:T(8,128)(2,1)}, u32[]{:S(2)}) %copy-start) | copy-done | bytes 196632
  1.6 1.0 %copy-done.2 = bf16[96,2304]{1,0:T(8,128)(2,1)S(1)} copy-done((bf16[96,2304]{1,0:T(8,128)(2,1)S(1)}, bf16[96,2304]{1,0:T(8,128)(2,1)}, u32[]{:S(2)}) %copy-start.2) | copy-done | bytes 442392
  2.6 0.9 %copy-done.5 = bf16[96,768]{1,0:T(8,128)(2,1)S(1)} copy-done((bf16[96,768]{1,0:T(8,128)(2,1)S(1)}, bf16[96,768]{1,0:T(8,128)(2,1)}, u32[]{:S(2)}) %copy-start.5) | copy-done | bytes 147480
  3.5 1.5 %shard_map.109 = (bf16[144,768]{1,0:T(8,128)(2,1)S(1)}, bf16[8,48,576]{2,1,0:T(8,128)(2,1)S(1)}, bf16[8,48,768]{2,1,0:T(8,128)(2,1)}) custom-call(s32[3]{0:T(128)S(1)} %pad_add_fusion.place, bf16[128,768]{1,0:T(8,128)(2,1)S(1)} %bitcast.12, bf16[12,128]{1,0:T(8,128)(2,1)S(1)} %bitcast.14, bf16[96,2304]{1,0:T(8,128)(2,1)S(1)} %copy-done.2, ...), custom_call_target="tpu_custom_call" | custom-call | bytes 789516 | tf_op jit(solution)/shard_map/pallas_call | solution.py:20
  5.0 20.9 %all_to_all.15.mine = bf16[8,48,576]{2,1,0:T(8,128)(2,1)S(1)} all-to-all(bf16[8,48,576]{2,1,0:T(8,128)(2,1)S(1)} %get-tuple-element.13), channel_id=1, replica_groups=mesh['groups'=2,'lat'=8,'lon'=2] {'lat'}, dimensions={0} | all-to-all | bytes 884736 | tf_op jit(solution)/shard_map/all_to_all | solution.py:365
  25.9 3.7 %all-to-all-start.2 = ((bf16[8,48,768]{2,1,0:T(8,128)(2,1)}), bf16[8,48,768]{2,1,0:T(8,128)(2,1)S(1)}, u32[]{:S(2)}, u32[]{:S(2)}) async-start(bf16[8,48,768]{2,1,0:T(8,128)(2,1)} %get-tuple-element.14), calls=%async_computation.2 | async-start | bytes 1179648 | tf_op jit(solution)/shard_map/all_to_all | solution.py:373
  29.6 0.0 collective-permute-start.4
  29.7 0.7 collective-permute-start
  30.4 3.4 %collective-permute-start.1 = (bf16[144,768]{1,0:T(8,128)(2,1)S(1)}, bf16[144,768]{1,0:T(8,128)(2,1)S(1)}, u32[]{:S(2)}, u32[]{:S(2)}) collective-permute-start(bf16[144,768]{1,0:T(8,128)(2,1)S(1)} %get-tuple-element.12), channel_id=1, source_target_pairs={{0,2},{1,0},{2,3},{3,1},{4,6},{5,4},{6,7},{7,5},{8,10},{9,8},{10,1... | collective-permute-start | bytes 663560 | tf_op jit(solution)/shard_map/ppermute | solution.py:45
  33.7 1.5 %collective-permute-start.2 = (bf16[144,768]{1,0:T(8,128)(2,1)S(1)}, bf16[144,768]{1,0:T(8,128)(2,1)S(1)}, u32[]{:S(2)}, u32[]{:S(2)}) collective-permute-start(bf16[144,768]{1,0:T(8,128)(2,1)S(1)} %get-tuple-element.12), channel_id=1, source_target_pairs={{0,16},{1,18},{2,17},{3,19},{4,20},{5,22},{6,21},{7,23},{8,24},{9,... | collective-permute-start | bytes 663560 | tf_op jit(solution)/shard_map/ppermute | solution.py:45
  35.3 1.0 %collective-permute-start.3 = (bf16[144,768]{1,0:T(8,128)(2,1)S(1)}, bf16[144,768]{1,0:T(8,128)(2,1)S(1)}, u32[]{:S(2)}, u32[]{:S(2)}) collective-permute-start(bf16[144,768]{1,0:T(8,128)(2,1)S(1)} %get-tuple-element.12), channel_id=1, source_target_pairs={{0,18},{1,16},{2,19},{3,17},{4,22},{5,20},{6,23},{7,21},{8,26},{9,... | collective-permute-start | bytes 663560 | tf_op jit(solution)/shard_map/ppermute | solution.py:45
  36.3 0.0 collective-permute-done.near0
  36.3 8.9 %all-to-all-done.2.mine = bf16[8,48,768]{2,1,0:T(8,128)(2,1)S(1)} async-done(((bf16[8,48,768]{2,1,0:T(8,128)(2,1)}), bf16[8,48,768]{2,1,0:T(8,128)(2,1)S(1)}, u32[]{:S(2)}, u32[]{:S(2)}) %all-to-all-start.2) | async-done | bytes 589856 | tf_op jit(solution)/shard_map/all_to_all | solution.py:373
  45.3 0.0 collective-permute-start.5
  45.3 0.0 copy-done.8
  45.3 0.0 collective-permute-done.1.near1
  45.3 0.0 collective-permute-done.2.far0
  45.3 0.6 collective-permute-done.3.far1
  45.9 0.7 copy-done.3
  46.6 0.0 collective-permute-done.4.other
  46.6 0.9 %copy-done.4 = bf16[144,768]{1,0:T(8,128)(2,1)S(1)} copy-done((bf16[144,768]{1,0:T(8,128)(2,1)S(1)}, bf16[144,768]{1,0:T(8,128)(2,1)}, u32[]{:S(2)}) %copy-start.4) | copy-done | bytes 221208
  47.5 2.8 %shard_map.110 = bf16[2,2,2,128,192]{4,3,2,1,0:T(8,128)(2,1)S(1)} custom-call(s32[3]{0:T(128)S(1)} %pad_add_fusion.place, f32[1,768]{1,0:T(1,128)S(1)} %broadcast_in_dim.10.gain, bf16[144,768]{1,0:T(8,128)(2,1)S(1)} %collective-permute-done.near0, bf16[144,768]{1,0:T(8,128)(2,1)S(1)} %collective-permute-done.1.near1, ...), custom_call_target="tpu_custom_call" | custom-call | flops 553648128 | bytes 1772556 | tf_op jit(solution)/shard_map/pallas_call | solution.py:20
  50.3 1.0 %copy.15 = bf16[8,128,192]{1,2,0:T(8,128)(2,1)} copy(bf16[8,128,192]{2,1,0:T(8,128)(2,1)S(1)} %bitcast.11) | data formatting | bytes 786432 | tf_op jit(solution)/shard_map/reshape | solution.py:408
  51.2 4.8 %all-to-all-start.1 = ((bf16[8,128,192]{1,2,0:T(8,128)(2,1)}), bf16[8,128,192]{1,2,0:T(8,128)(2,1)S(1)}, u32[]{:S(2)}, u32[]{:S(2)}) async-start(bf16[8,128,192]{1,2,0:T(8,128)(2,1)} %copy.15), calls=%async_computation.1 | async-start | bytes 786432 | tf_op jit(solution)/shard_map/all_to_all | solution.py:407
  56.1 1.3 %collective-permute-start.6 = (bf16[144,768]{1,0:T(8,128)(2,1)S(1)}, bf16[144,768]{1,0:T(8,128)(2,1)S(1)}, u32[]{:S(2)}, u32[]{:S(2)}) collective-permute-start(bf16[144,768]{1,0:T(8,128)(2,1)S(1)} %collective-permute-done.near0), channel_id=1, source_target_pairs={{1,0},{2,3},{5,4},{6,7},{9,8},{10,11},{13,12},{14,15},{17,16},{18,... | collective-permute-start | bytes 663560 | tf_op jit(solution)/shard_map/ppermute | solution.py:45
  57.4 0.0 copy-done.9
  57.4 7.0 %all-to-all-done.1 = bf16[8,128,192]{1,2,0:T(8,128)(2,1)S(1)} async-done(((bf16[8,128,192]{1,2,0:T(8,128)(2,1)}), bf16[8,128,192]{1,2,0:T(8,128)(2,1)S(1)}, u32[]{:S(2)}, u32[]{:S(2)}) %all-to-all-start.1) | async-done | bytes 393248 | tf_op jit(solution)/shard_map/all_to_all | solution.py:407
  64.4 0.2 copy.16
  64.6 0.0 collective-permute-done.6.passed
  64.7 0.0 collective-permute-done.5.other
  64.7 0.0 copy-start.7
  64.7 1.2 %shard_map.111.other_in = bf16[128,768]{1,0:T(8,128)(2,1)S(1)} custom-call(s32[3]{0:T(128)S(1)} %pad_add_fusion.place, f32[1,768]{1,0:T(1,128)S(1)} %broadcast_in_dim.9.gain, bf16[2,2,2,128,192]{4,3,2,1,0:T(8,128)(2,1)S(1)} %bitcast.9, bf16[8,48,768]{2,1,0:T(8,128)(2,1)S(1)} %all-to-all-done.2.mine, bf16[8,48,768]{2,1,0:T(8,128)(2,1)S(1)} %collective-permute-done.5.other, ...), custom_call_target="tpu_custom_call" | custom-call | flops 150994944 | bytes 2018316 | tf_op jit(solution)/shard_map/pallas_call | solution.py:20
  65.9 3.9 %collective-permute-start.7 = (bf16[128,768]{1,0:T(8,128)(2,1)S(1)}, bf16[128,768]{1,0:T(8,128)(2,1)S(1)}, u32[]{:S(2)}, u32[]{:S(2)}) collective-permute-start(bf16[128,768]{1,0:T(8,128)(2,1)S(1)} %shard_map.111.other_in), channel_id=1, source_target_pairs={{0,4},{1,5},{4,8},{5,9},{6,2},{7,3},{8,12},{9,13},{10,6},{11,7},{1... | collective-permute-start | bytes 589832 | tf_op jit(solution)/shard_map/ppermute | solution.py:45
  69.8 0.0 copy-done.7
  69.8 0.2 copy.17.w_conv
  70.0 0.0 copy-start.10
  70.0 0.0 copy-start.1
  70.1 0.2 shard_map.112.blocks
  70.2 0.5 copy-done.10
  70.7 0.1 copy.19.taps
  72.8 2.0 %shard_map.113 = (bf16[128,768]{1,0:T(8,128)(2,1)S(1)}, f32[256,768]{1,0:T(8,128)S(1)}) custom-call(s32[3]{0:T(128)S(1)} %pad_add_fusion.place, s32[1]{0:T(128)S(6)} %copy.20.lon_half, s32[1]{0:T(128)S(6)} %copy.21.lat_half, s32[1]{0:T(128)S(6)} %copy.22.quad_off, f32[16,2]{1,0:T(8,128)S(1)} %copy.19.taps, f32[1,768]{1,0:T(1,128)S(1)} %broadcast_in_dim.9.gain, ...), custom_call_target="tpu_custom_call" | custom-call | flops 452984832 | bytes 2755736 | tf_op jit(solution)/shard_map/pallas_call | solution.py:20
  74.7 0.0 collective-permute-done.7.halo
  74.7 1.3 %shard_map.114 = (f32[128,768]{1,0:T(8,128)S(1)}, bf16[128,768]{1,0:T(8,128)(2,1)S(1)}) custom-call(s32[3]{0:T(128)S(1)} %pad_add_fusion.place, s32[1]{0:T(128)S(6)} %copy.20.lon_half, s32[1]{0:T(128)S(6)} %copy.21.lat_half, s32[1]{0:T(128)S(6)} %copy.22.quad_off, f32[16,2]{1,0:T(8,128)S(1)} %copy.19.taps, bf16[128,768]{1,0:T(8,128)(2,1)S(1)} %collective-permute-done.7.halo, ...), custom_call_target="tpu_custom_call" | custom-call | flops 100663296 | bytes 1966232 | tf_op jit(solution)/shard_map/pallas_call | solution.py:20
  76.0 0.1 collective-permute-start.8
  76.1 1.4 %collective-permute-done.8 = bf16[128,768]{1,0:T(8,128)(2,1)S(1)} collective-permute-done((bf16[128,768]{1,0:T(8,128)(2,1)S(1)}, bf16[128,768]{1,0:T(8,128)(2,1)S(1)}, u32[]{:S(2)}, u32[]{:S(2)}) %collective-permute-start.8) | collective-permute-done | bytes 196640 | tf_op jit(solution)/shard_map/ppermute | solution.py:49
  77.5 0.7 fusion
  (11 shorter events, 0.0 us)
Async XLA Ops:
  0.0 0.7 copy-start.6
  0.7 0.9 %copy-start = (bf16[1,128,768]{2,1,0:T(8,128)(2,1)S(1)}, bf16[1,128,768]{2,1,0:T(8,128)(2,1)}, u32[]{:S(2)}) copy-start(bf16[1,128,768]{2,1,0:T(8,128)(2,1)} %param.11) | copy-start | bytes 589828
  1.6 1.0 %copy-start.2 = (bf16[96,2304]{1,0:T(8,128)(2,1)S(1)}, bf16[96,2304]{1,0:T(8,128)(2,1)}, u32[]{:S(2)}) copy-start(bf16[96,2304]{1,0:T(8,128)(2,1)} %w_qkv.1) | copy-start | bytes 1327108
  2.6 0.9 %copy-start.5 = (bf16[96,768]{1,0:T(8,128)(2,1)S(1)}, bf16[96,768]{1,0:T(8,128)(2,1)}, u32[]{:S(2)}) copy-start(bf16[96,768]{1,0:T(8,128)(2,1)} %w_out.1) | copy-start | bytes 442372
  25.9 19.3 %copy-start.8 = (f32[768]{0:T(1024)S(1)}, f32[768]{0:T(1024)}, u32[]{:S(2)}) copy-start(f32[768]{0:T(1024)} %param.12) | copy-start | bytes 9220
  25.9 19.3 %all-to-all-start.2 = ((bf16[8,48,768]{2,1,0:T(8,128)(2,1)}), bf16[8,48,768]{2,1,0:T(8,128)(2,1)S(1)}, u32[]{:S(2)}, u32[]{:S(2)}) async-start(bf16[8,48,768]{2,1,0:T(8,128)(2,1)} %get-tuple-element.14), calls=%async_computation.2 | async-start | bytes 1179648 | tf_op jit(solution)/shard_map/all_to_all | solution.py:373
  29.6 16.9 %collective-permute-start.4 = (bf16[8,48,576]{2,1,0:T(8,128)(2,1)S(1)}, bf16[8,48,576]{2,1,0:T(8,128)(2,1)S(1)}, u32[]{:S(2)}, u32[]{:S(2)}) collective-permute-start(bf16[8,48,576]{2,1,0:T(8,128)(2,1)S(1)} %all_to_all.15.mine), channel_id=1, source_target_pairs={{0,1},{1,0},{2,3},{3,2},{4,5},{5,4},{6,7},{7,6},{8,9},{9,8},{10,11... | collective-permute-start | bytes 1327112 | tf_op jit(solution)/shard_map/ppermute | solution.py:49
  29.7 6.6 %collective-permute-start = (bf16[144,768]{1,0:T(8,128)(2,1)S(1)}, bf16[144,768]{1,0:T(8,128)(2,1)S(1)}, u32[]{:S(2)}, u32[]{:S(2)}) collective-permute-start(bf16[144,768]{1,0:T(8,128)(2,1)S(1)} %get-tuple-element.12), channel_id=1, source_target_pairs={{0,0},{1,2},{2,1},{3,3},{4,4},{5,6},{6,5},{7,7},{8,8},{9,10},{10,9... | collective-permute-start | bytes 663560 | tf_op jit(solution)/shard_map/ppermute | solution.py:45
  30.4 14.9 %collective-permute-start.1 = (bf16[144,768]{1,0:T(8,128)(2,1)S(1)}, bf16[144,768]{1,0:T(8,128)(2,1)S(1)}, u32[]{:S(2)}, u32[]{:S(2)}) collective-permute-start(bf16[144,768]{1,0:T(8,128)(2,1)S(1)} %get-tuple-element.12), channel_id=1, source_target_pairs={{0,2},{1,0},{2,3},{3,1},{4,6},{5,4},{6,7},{7,5},{8,10},{9,8},{10,1... | collective-permute-start | bytes 663560 | tf_op jit(solution)/shard_map/ppermute | solution.py:45
  33.7 11.5 %collective-permute-start.2 = (bf16[144,768]{1,0:T(8,128)(2,1)S(1)}, bf16[144,768]{1,0:T(8,128)(2,1)S(1)}, u32[]{:S(2)}, u32[]{:S(2)}) collective-permute-start(bf16[144,768]{1,0:T(8,128)(2,1)S(1)} %get-tuple-element.12), channel_id=1, source_target_pairs={{0,16},{1,18},{2,17},{3,19},{4,20},{5,22},{6,21},{7,23},{8,24},{9,... | collective-permute-start | bytes 663560 | tf_op jit(solution)/shard_map/ppermute | solution.py:45
  35.3 10.6 %collective-permute-start.3 = (bf16[144,768]{1,0:T(8,128)(2,1)S(1)}, bf16[144,768]{1,0:T(8,128)(2,1)S(1)}, u32[]{:S(2)}, u32[]{:S(2)}) collective-permute-start(bf16[144,768]{1,0:T(8,128)(2,1)S(1)} %get-tuple-element.12), channel_id=1, source_target_pairs={{0,18},{1,16},{2,19},{3,17},{4,22},{5,20},{6,23},{7,21},{8,26},{9,... | collective-permute-start | bytes 663560 | tf_op jit(solution)/shard_map/ppermute | solution.py:45
  45.3 19.4 %collective-permute-start.5 = (bf16[8,48,768]{2,1,0:T(8,128)(2,1)S(1)}, bf16[8,48,768]{2,1,0:T(8,128)(2,1)S(1)}, u32[]{:S(2)}, u32[]{:S(2)}) collective-permute-start(bf16[8,48,768]{2,1,0:T(8,128)(2,1)S(1)} %all-to-all-done.2.mine), channel_id=1, source_target_pairs={{0,1},{1,0},{2,3},{3,2},{4,5},{5,4},{6,7},{7,6},{8,9},{9,8},{10,11... | collective-permute-start | bytes 1769480 | tf_op jit(solution)/shard_map/ppermute | solution.py:49
  45.9 0.7 copy-start.3
  46.6 0.9 %copy-start.4 = (bf16[144,768]{1,0:T(8,128)(2,1)S(1)}, bf16[144,768]{1,0:T(8,128)(2,1)}, u32[]{:S(2)}) copy-start(bf16[144,768]{1,0:T(8,128)(2,1)} %copy-done.3) | copy-start | bytes 663556
  51.2 6.1 %copy-start.9 = (f32[768]{0:T(1024)S(1)}, f32[768]{0:T(1024)}, u32[]{:S(2)}) copy-start(f32[768]{0:T(1024)} %param.16) | copy-start | bytes 9220
  51.2 13.2 %all-to-all-start.1 = ((bf16[8,128,192]{1,2,0:T(8,128)(2,1)}), bf16[8,128,192]{1,2,0:T(8,128)(2,1)S(1)}, u32[]{:S(2)}, u32[]{:S(2)}) async-start(bf16[8,128,192]{1,2,0:T(8,128)(2,1)} %copy.15), calls=%async_computation.1 | async-start | bytes 786432 | tf_op jit(solution)/shard_map/all_to_all | solution.py:407
  56.1 8.6 %collective-permute-start.6 = (bf16[144,768]{1,0:T(8,128)(2,1)S(1)}, bf16[144,768]{1,0:T(8,128)(2,1)S(1)}, u32[]{:S(2)}, u32[]{:S(2)}) collective-permute-start(bf16[144,768]{1,0:T(8,128)(2,1)S(1)} %collective-permute-done.near0), channel_id=1, source_target_pairs={{1,0},{2,3},{5,4},{6,7},{9,8},{10,11},{13,12},{14,15},{17,16},{18,... | collective-permute-start | bytes 663560 | tf_op jit(solution)/shard_map/ppermute | solution.py:45
  64.7 5.1 %copy-start.7 = (bf16[2,768,64]{1,2,0:T(8,128)(2,1)S(1)}, bf16[2,768,64]{1,2,0:T(8,128)(2,1)}, u32[]{:S(2)}) copy-start(bf16[2,768,64]{1,2,0:T(8,128)(2,1)} %param.17) | copy-start | bytes 589828
  65.9 8.9 %collective-permute-start.7 = (bf16[128,768]{1,0:T(8,128)(2,1)S(1)}, bf16[128,768]{1,0:T(8,128)(2,1)S(1)}, u32[]{:S(2)}, u32[]{:S(2)}) collective-permute-start(bf16[128,768]{1,0:T(8,128)(2,1)S(1)} %shard_map.111.other_in), channel_id=1, source_target_pairs={{0,4},{1,5},{4,8},{5,9},{6,2},{7,3},{8,12},{9,13},{10,6},{11,7},{1... | collective-permute-start | bytes 589832 | tf_op jit(solution)/shard_map/ppermute | solution.py:45
  70.0 0.7 copy-start.10
  70.0 2.7 %copy-start.1 = (bf16[1,128,768]{2,1,0:T(8,128)(2,1)S(1)}, bf16[1,128,768]{2,1,0:T(8,128)(2,1)}, u32[]{:S(2)}) copy-start(bf16[1,128,768]{2,1,0:T(8,128)(2,1)} %param.11) | copy-start | bytes 589828
  76.0 1.5 %collective-permute-start.8 = (bf16[128,768]{1,0:T(8,128)(2,1)S(1)}, bf16[128,768]{1,0:T(8,128)(2,1)S(1)}, u32[]{:S(2)}, u32[]{:S(2)}) collective-permute-start(bf16[128,768]{1,0:T(8,128)(2,1)S(1)} %get-tuple-element.18), channel_id=1, source_target_pairs={{0,1},{1,0},{2,3},{3,2},{4,5},{5,4},{6,7},{7,6},{8,9},{9,8},{10,11... | collective-permute-start | bytes 589832 | tf_op jit(solution)/shard_map/ppermute | solution.py:49

commit v4 on v3

v4 whole, which is shorter than its diff:
```python
import functools

import jax
import jax.numpy as jnp
from jax import lax
from jax.experimental import pallas as pl
from jax.experimental.pallas import tpu as pltpu
from jax.sharding import PartitionSpec as P

AXES = ("groups", "lat", "lon")
VMEM = pl.BlockSpec(memory_space=pltpu.VMEM)
ANY = pl.BlockSpec(memory_space=pl.ANY)
FLIPS = ((1, 0), (0, 1), (1, 1))
SMEM = pl.BlockSpec(memory_space=pltpu.SMEM)
BF16 = jnp.bfloat16
F32 = jnp.float32


def call(body, outs, specs, args, flops, scratch=()):
    outs = tuple(jax.ShapeDtypeStruct(shape, dtype) for shape, dtype in outs)
    moved = sum(a.size * a.dtype.itemsize for a in args)
    return pl.pallas_call(
        body,
        out_shape=outs,
        in_specs=specs,
        out_specs=tuple(VMEM for _ in outs),
        scratch_shapes=list(scratch),
        compiler_params=pltpu.CompilerParams(vmem_limit_bytes=32 * 1024 * 1024),
        cost_estimate=pl.CostEstimate(flops=flops, bytes_accessed=moved, transcendentals=0),
    )(*args)


def device_pairs(target):
    lat_count = lax.axis_size("lat")
    pairs = []
    for group in range(2):
        for row in range(lat_count):
            for core in range(2):
                to = target(group, row, core)
                if 0 <= to[1] < lat_count:
                    source = (group * lat_count + row) * 2 + core
                    pairs.append((source, (to[0] * lat_count + to[1]) * 2 + to[2]))
    return pairs


def move(values, target):
    return lax.ppermute(values, AXES, device_pairs(target))


def swap_cores(values):
    return lax.ppermute(values, "lon", [(0, 1), (1, 0)])


def flip_chips(values, flip, sample):
    return move(values, lambda g, l, c: (g ^ sample, l ^ flip, c))


def norm_rows(values, gain):
    average = jnp.mean(values, axis=-1, keepdims=True)
    centered = values - average
    variance = jnp.mean(centered * centered, axis=-1, keepdims=True)
    return (centered * lax.rsqrt(variance + 1e-05) * gain).astype(BF16)


def norm_body(tokens, bias, gain, message, raw, sems):
    count = tokens.shape[0]
    heads, bias_width = bias.shape
    fetch = pltpu.make_async_copy(tokens, raw, sems.at[0])
    fetch.start()
    message[count:, :] = jnp.zeros((16, tokens.shape[1]), BF16)
    message[count : count + heads, :bias_width] = bias[...]
    fetch.wait()
    message[:count, :] = norm_rows(raw[...].astype(F32), gain[...])


def pack_qkv_body(w_qkv, message, pieces, rows, sems):
    del message
    group, core = lax.axis_index("groups"), lax.axis_index("lon")
    half = pieces.shape[1]
    quarter = pieces.shape[2] // 3
    start = pl.multiple_of(core * half, half)
    fetch = pltpu.make_async_copy(w_qkv.at[pl.ds(start, half), :], rows, sems.at[0])
    fetch.start()
    fetch.wait()
    for side in range(2):
        parts = []
        for kind in range(3):
            first = (4 * kind + 2 * side) * quarter
            parts.append(
                jnp.where(
                    group == 0,
                    rows[:, first : first + quarter],
                    rows[:, first + quarter : first + 2 * quarter],
                )
            )
        piece = jnp.concatenate(parts, axis=1)
        for pair in range(pieces.shape[0] // 2):
            pieces[2 * pair + side] = piece


def pack_out_body(w_out, qkv_pieces, pieces, sems):
    del qkv_pieces
    core = lax.axis_index("lon")
    count, half, _ = pieces.shape
    start = pl.multiple_of(core * half, half)
    fetches = [
        pltpu.make_async_copy(w_out.at[pl.ds(start, half), :], pieces.at[row], sems.at[row])
        for row in range(count)
    ]
    for fetch in fetches:
        fetch.start()
    for fetch in fetches:
        fetch.wait()


def join_halves(mine, other, joined):
    core = lax.axis_index("lon")
    count, half, _ = mine.shape
    for row in range(count):
        joined[pl.ds(pl.multiple_of(row * 2 * half + core * half, half), half), :] = mine[row]
        joined[pl.ds(pl.multiple_of(row * 2 * half + (1 - core) * half, half), half), :] = other[row]


def attend_body(*refs):
    near, far, (mine, other) = refs[:4], refs[4:8], refs[8:10]
    pieces, (weights, bias_rows, near_rows, far_rows) = refs[10:14], refs[14:]
    group, side = lax.axis_index("groups"), lax.rem(lax.axis_index("lat"), 2)
    _, count, quarter = pieces[0].shape
    heads = 3
    head_dim = quarter // heads
    join_halves(mine, other, weights)
    for slot in range(4):
        near_rows[slot * count : (slot + 1) * count, :] = near[slot][:count, :]
        far_rows[slot * count : (slot + 1) * count, :] = far[slot][:count, :]
    for flip in range(2):
        for at, block in enumerate((near[flip], far[flip])):
            bias_rows[flip, :, at * count : (at + 1) * count] = block[count:, :count].astype(F32)
    first_head = (2 * side + group) * heads
    here = jnp.dot(near_rows[...], weights[...], preferred_element_type=F32).astype(BF16)
    there = jnp.dot(far_rows[...], weights[:, quarter:], preferred_element_type=F32).astype(BF16)
    for slot in range(4):
        flip, sample = slot % 2, slot // 2
        low_row, high_row = slot * count, (slot + 1) * count
        outs = []
        for head in range(heads):
            low = head * head_dim
            queries = here[low_row:high_row, low : low + head_dim]
            keys, values = (
                jnp.concatenate(
                    [
                        here[low_row:high_row, (kind + 1) * quarter + low :][:, :head_dim],
                        there[low_row:high_row, kind * quarter + low :][:, :head_dim],
                    ]
                )
                for kind in range(2)
            )
            scores = lax.dot_general(
                queries, keys, (((1,), (1,)), ((), ())), preferred_element_type=F32
            ) * (head_dim**-0.5)
            scores = scores + bias_rows[flip, pl.ds(first_head + head, 1), :]
            expd = jnp.exp(scores - jnp.max(scores, axis=-1, keepdims=True))
            totals = jnp.sum(expd, axis=-1, keepdims=True)
            weighted = jnp.dot(expd.astype(BF16), values, preferred_element_type=F32)
            outs.append((weighted / totals).astype(BF16))
        attended = jnp.concatenate(outs, axis=1)
        pieces[2 * sample + flip][0] = attended
        pieces[2 * sample + 1 - flip][1] = attended


def project_out(which, pieces, weights, tokens, gain):
    group, side = lax.axis_index("groups"), lax.rem(lax.axis_index("lat"), 2)
    summed = tokens.astype(F32)
    for slot, piece in enumerate(pieces):
        flip, sample = slot % 2, slot // 2
        quarter = piece.shape[2]
        owner = 2 * (side + flip - 2 * side * flip) + (group + sample - 2 * group * sample)
        rows = pl.ds(pl.multiple_of(owner * quarter, quarter), quarter)
        summed = summed + jnp.dot(piece[which], weights[rows, :], preferred_element_type=F32)
    middle = summed.astype(BF16)
    return middle, norm_rows(middle.astype(F32), gain)


def other_body(gain, piece0, piece1, piece2, piece3, weights, tokens, other_in):
    pieces = (piece0, piece1, piece2, piece3)
    other_in[...] = project_out(1, pieces, weights, tokens[...], gain[...])[1]


def diagonal_body(w_conv, blocks):
    size = w_conv.shape[2]
    blocks[...] = jnp.zeros(blocks.shape, BF16)
    per_block = blocks.shape[2] // size
    for basis in range(blocks.shape[0]):
        for tile in range(blocks.shape[1]):
            for at in range(per_block):
                first = (tile * per_block + at) * size
                low, high = at * size, (at + 1) * size
                blocks[basis, tile, low:high, low:high] = w_conv[basis, first : first + size, :]


def tent_pair(row_count, first_col, col_count, half_width):
    rows = lax.broadcasted_iota(jnp.int32, (row_count, col_count), 0)
    cols = lax.broadcasted_iota(jnp.int32, (row_count, col_count), 1) + first_col
    offset = ((cols - rows + row_count // 2) & (row_count - 1)) - row_count // 2
    distance = jnp.abs(offset).astype(F32)
    span_plus = (half_width + 1).astype(F32)
    tent = jnp.where(
        distance <= half_width.astype(F32), (1.0 - distance / span_plus) / span_plus, 0.0
    )
    odd = tent * offset.astype(F32) / span_plus
    return tent.astype(BF16), odd.astype(BF16)


def mix(lines, blocks, basis):
    size = blocks.shape[2]
    return jnp.concatenate(
        [
            jnp.dot(
                lines[:, tile * size : (tile + 1) * size],
                blocks[basis, tile],
                preferred_element_type=F32,
            ).astype(BF16)
            for tile in range(blocks.shape[1])
        ],
        axis=1,
    )


def tap_gain(taps, quad_off, lat_half, offset, basis):
    value = taps[quad_off[0] + offset + 1, basis]
    if offset == 0:
        return value
    return jnp.where(lat_half[0] >= 1, value, 0.0)


def own_body(
    lat_count,
    lon_half,
    lat_half,
    quad_off,
    taps,
    gain,
    piece0,
    piece1,
    piece2,
    piece3,
    weights,
    tokens,
    other_in,
    blocks,
    middle,
    partial,
):
    lat_row, core = lax.axis_index("lat"), lax.axis_index("lon")
    side = lax.rem(lat_row, 2)
    count = tokens.shape[0]
    pieces = (piece0, piece1, piece2, piece3)
    own_middle, own_in = project_out(0, pieces, weights, tokens[...], gain[...])
    middle[...] = own_middle
    own = own_in.astype(F32)
    neighbour = other_in[...].astype(F32)
    rows = partial.shape[0]
    mixed, coeffs = [], []
    direct = tent_pair(rows, core * count, count, lon_half[0])
    rolled = tent_pair(rows, core * count + count, count, lon_half[0])
    for basis in range(2):
        below = tap_gain(taps, quad_off, lat_half, -1, basis)
        above = tap_gain(taps, quad_off, lat_half, 1, basis)
        centre = tap_gain(taps, quad_off, lat_half, 0, basis)
        other_gain = jnp.where(side == 0, above, below)
        pole_gain = jnp.where(lat_row == 0, below, 0.0) + jnp.where(
            lat_row == lat_count - 1, above, 0.0
        )
        lines = jnp.concatenate(
            [
                (other_gain * neighbour + centre * own).astype(BF16),
                (pole_gain * own).astype(BF16),
            ]
        )
        mixed.append(mix(lines, blocks, basis))
        coeffs += [direct[basis], rolled[basis]]
    partial[...] = jnp.dot(
        jnp.concatenate(coeffs, axis=1),
        jnp.concatenate(mixed, axis=0),
        preferred_element_type=F32,
    )


def halo_body(
    lon_half, lat_half, quad_off, taps, halo, blocks, middle, partial, kept, sent, total
):
    lat_row, core = lax.axis_index("lat"), lax.axis_index("lon")
    side = lax.rem(lat_row, 2)
    count = halo.shape[0]
    rows = partial.shape[0]
    values = halo[...].astype(F32)
    mixed = []
    for basis in range(2):
        below = tap_gain(taps, quad_off, lat_half, -1, basis)
        above = tap_gain(taps, quad_off, lat_half, 1, basis)
        gain = jnp.where(side == 0, below, above)
        mixed.append(mix((gain * values).astype(BF16), blocks, basis))
    total[...] = partial[...] + jnp.dot(
        jnp.concatenate(tent_pair(rows, core * count, count, lon_half[0]), axis=1),
        jnp.concatenate(mixed, axis=0),
        preferred_element_type=F32,
    )
    here = pl.multiple_of(core * count, count)
    there = pl.multiple_of((1 - core) * count, count)
    kept[...] = middle[...].astype(F32) + total[pl.ds(here, count), :]
    sent[...] = total[pl.ds(there, count), :].astype(BF16)


def pack_plain(weights, columns):
    core, lat_count = lax.axis_index("lon"), lax.axis_size("lat")
    half, width = weights.shape[0] // 2, weights.shape[1]
    rows = lax.dynamic_slice_in_dim(weights, core * half, half, 0)
    if columns == width:
        return jnp.broadcast_to(rows[None], (lat_count, half, width))
    rows = rows.reshape(half, 3, 2, 2, columns // 3)
    rows = lax.dynamic_index_in_dim(rows, lax.axis_index("groups"), 3, keepdims=False)
    rows = rows.transpose(2, 0, 1, 3).reshape(2, half, columns)
    rows = jnp.broadcast_to(rows[None], (lat_count // 2, 2, half, columns))
    return rows.reshape(lat_count, half, columns)


def regroup(core, mine, other):
    both = jnp.where(core == 0, jnp.stack([mine, other], 1), jnp.stack([other, mine], 1))
    whole = both.reshape(8, 2, -1, mine.shape[2])
    pick = lambda index: lax.dynamic_index_in_dim(whole, index, 1, keepdims=False)
    return pick(core), pick(1 - core)


def per_device(
    tokens,
    gain_attn,
    w_qkv,
    key_bias,
    w_out,
    gain_conv,
    w_conv,
    lat_taps,
    lon_half,
    lat_half,
    quad_off,
):
    own_tokens = tokens[0]
    count, width = own_tokens.shape
    quarter = width // 4
    lat_count = lax.axis_size("lat")
    core = lax.axis_index("lon")
    half = w_qkv.shape[0] // 2
    gain_attn = gain_attn[None]
    gain_conv = gain_conv[None]

    (message,) = call(
        norm_body,
        [((count + 16, width), BF16)],
        [ANY, VMEM, VMEM],
        (own_tokens, key_bias[0], gain_attn),
        10 * count * width,
        [pltpu.VMEM((count, width), BF16), pltpu.SemaphoreType.DMA((1,))],
    )
    near = [message] + [flip_chips(message, flip, sample) for flip, sample in FLIPS]
    far = [swap_cores(block) for block in near]

    if half % 16 == 0:
        (qkv_pieces,) = call(
            pack_qkv_body,
            [((lat_count, half, 3 * quarter), BF16)],
            [ANY] * 2,
            (w_qkv, message),
            0,
            [pltpu.VMEM((half, 3 * width), BF16), pltpu.SemaphoreType.DMA((1,))],
        )
        (out_pieces,) = call(
            pack_out_body,
            [((lat_count, half, width), BF16)],
            [ANY] * 2,
            (w_out, qkv_pieces),
            0,
            [pltpu.SemaphoreType.DMA((lat_count,))],
        )
    else:
        qkv_pieces = pack_plain(w_qkv, 3 * quarter)
        out_pieces = pack_plain(w_out, width)
    qkv_mine = lax.all_to_all(qkv_pieces, "lat", 0, 0)
    qkv_other = swap_cores(qkv_mine)
    out_mine = lax.all_to_all(out_pieces, "lat", 0, 0)
    out_other = swap_cores(out_mine)
    if half % 16:
        qkv_mine, qkv_other = regroup(core, qkv_mine, qkv_other)
        out_mine, out_other = regroup(core, out_mine, out_other)
    other_tokens = flip_chips(own_tokens, 1, 0)

    size = 4 * w_conv.shape[2]
    (diagonal,) = call(
        diagonal_body, [((2, width // size, size, size), BF16)], [VMEM], (w_conv,), 0
    )

    pieces = call(
        attend_body,
        [((2, count, quarter), BF16)] * 4,
        [VMEM] * 10,
        (*near, *far, qkv_mine, qkv_other),
        2 * 1024 * width * 3 * quarter,
        [
            pltpu.VMEM((width, 3 * quarter), BF16),
            pltpu.VMEM((2, 16, 2 * count), F32),
            pltpu.VMEM((4 * count, width), BF16),
            pltpu.VMEM((4 * count, width), BF16),
        ],
    )
    back = [pieces[0]] + [
        flip_chips(piece, flip, sample) for piece, (flip, sample) in zip(pieces[1:], FLIPS)
    ]
    (full_out,) = call(
        join_halves, [((width, width), BF16)], [VMEM] * 2, (out_mine, out_other), 0
    )
    (other_in,) = call(
        other_body,
        [((count, width), BF16)],
        [VMEM] * 7,
        (gain_conv, *back, full_out, other_tokens),
        2 * count * width * width,
    )
    halo = move(other_in, lambda g, l, c: (g, l + 2 - 4 * (l % 2), c))
    middle, partial = call(
        functools.partial(own_body, lat_count),
        [((count, width), BF16), ((2 * count, width), F32)],
        [SMEM] * 4 + [VMEM] * 9,
        (
            lon_half,
            lat_half,
            quad_off,
            lat_taps,
            gain_conv,
            *back,
            full_out,
            own_tokens,
            other_in,
            diagonal,
        ),
        2 * count * width * width * 3,
    )
    kept, sent = call(
        halo_body,
        [((count, width), F32), ((count, width), BF16)],
        [SMEM] * 4 + [VMEM] * 4,
        (lon_half, lat_half, quad_off, lat_taps, halo, diagonal, middle, partial),
        2 * 256 * 256 * width,
        [pltpu.VMEM((2 * count, width), F32)],
    )
    received = swap_cores(sent)
    return (kept + received.astype(F32)).astype(BF16)[None]


def solution(mesh):
    return jax.shard_map(
        per_device,
        mesh=mesh,
        in_specs=(
            P(("groups", "lat"), "lon", None),
            P(),
            P("lat", None),
            P("lat", None, "lon"),
            P("lat", None),
            P(),
            P(),
            P(),
            P("lat"),
            P("lat"),
            P("lat"),
        ),
        out_specs=P(("groups", "lat"), "lon", None),
        check_vma=False,
    )
```

time: 78.8 us -> 77.3 us (0.981)
  blocking collectives: 20.9 us -> 0 us
  waiting for transfers between devices: 18 us -> 35 us
  local copies, waits for them, and re-layouts: 7.07 us -> 3.64 us
  Pallas kernels: 8.81 us -> 11.8 us
  starting transfers between devices: 20.5 us -> 23.4 us
    all_to_all x1 -> x0, blocking collectives: 20.9 us -> none  [per_device(): qkv_mine = lax.all_to_all(qkv_pieces, 'lat', 0, 0)]
    ppermute x6 -> x8, waiting for transfers between devices: 0.61 us -> 19.3 us  [move(): return lax.ppermute(values, AXES, device_pairs(target))]
    all_to_all x1, waiting for transfers between devices: 8.95 us -> 1.21 us  [per_device(): out_mine = lax.all_to_all(out_pieces, 'lat', 0, 0)]
    all_to_all x1, waiting for transfers between devices: 7.03 us -> 12.1 us  [per_device(): qkv_mine = lax.all_to_all(qkv_pieces, 'lat', 0, 0)]
    pallas_call x6 -> x9, Pallas kernels: 8.81 us -> 11.8 us  [call(): pl.pallas_call(body, out_shape=outs, in_specs=specs, out_specs=tuple((VME...]
    unnamed x24 -> x18, local copies, waits for them, and re-layouts: 5.9 us -> 2.95 us
    all_to_all x1, starting transfers between devices: 4.85 us -> 7.26 us  [per_device(): qkv_mine = lax.all_to_all(qkv_pieces, 'lat', 0, 0)]
    ppermute x3 -> x7, starting transfers between devices: 0.12 us -> 1.6 us  [swap_cores(): return lax.ppermute(values, 'lon', [(0, 1), (1, 0)])]
  transfers between devices with their start and end apart: 11 -> 17, of which waited for: 4 -> 10; matrix products, arithmetic and copies ran while one was open for 2% -> 0% of each run, Pallas kernels for 6% -> 11%
where the time goes in v4:
time: 77.3 us; the launch traced here: 76.8 us
  waiting for transfers between devices  35 us (45%)
  starting transfers between devices  23.4 us (30%)
  Pallas kernels  11.8 us (15%)
  local copies, waits for them, and re-layouts  3.64 us (5%)
  between operations  2.12 us (3%)
    ppermute x8, waiting for transfers between devices, move(): return lax.ppermute(values, AXES, device_pairs(target))  19.3 us
    all_to_all x1, waiting for transfers between devices, per_device(): qkv_mine = lax.all_to_all(qkv_pieces, 'lat', 0, 0)  12.1 us
    pallas_call x9, Pallas kernels, call(): pl.pallas_call(body, out_shape=outs, in_specs=specs, out_specs=tuple((VME...  11.8 us
    ppermute x8, starting transfers between devices, move(): return lax.ppermute(values, AXES, device_pairs(target))  10.9 us
    all_to_all x1, starting transfers between devices, per_device(): qkv_mine = lax.all_to_all(qkv_pieces, 'lat', 0, 0)  7.26 us
    all_to_all x1, starting transfers between devices, per_device(): out_mine = lax.all_to_all(out_pieces, 'lat', 0, 0)  3.64 us
    unnamed x18, local copies, waits for them, and re-layouts  2.95 us
    ppermute x7, waiting for transfers between devices, swap_cores(): return lax.ppermute(values, 'lon', [(0, 1), (1, 0)])  2.46 us
  transfers between devices with their start and end apart: 17, of which 10 were waited for; matrix products, arithmetic and copies ran while one was open for 0% of the time, Pallas kernels for 11%

profile of v4, /device:TPU:0, one launch (start us, length us, event | category | flops | bytes accessed | tf_op | source)
XLA Modules:
  0.0 76.8 jit_solution(5185484350096964094)
XLA Ops:
  0.0 0.7 broadcast_in_dim.10.gain
  0.7 0.9 %copy-done = bf16[1,128,768]{2,1,0:T(8,128)(2,1)S(1)} copy-done((bf16[1,128,768]{2,1,0:T(8,128)(2,1)S(1)}, bf16[1,128,768]{2,1,0:T(8,128)(2,1)}, u32[]{:S(2)}) %copy-start) | copy-done | bytes 196632
  1.6 0.7 copy-done.4
  2.3 0.5 shard_map.109.message.refs_0_
  2.8 0.0 copy-start.2
  2.8 1.0 %copy-done.2 = bf16[96,2304]{1,0:T(8,128)(2,1)S(1)} copy-done((bf16[96,2304]{1,0:T(8,128)(2,1)S(1)}, bf16[96,2304]{1,0:T(8,128)(2,1)}, u32[]{:S(2)}) %copy-start.2) | copy-done | bytes 442392
  3.8 1.2 %shard_map.110.qkv_pieces = bf16[8,48,576]{2,1,0:T(8,128)(2,1)} custom-call(bf16[96,2304]{1,0:T(8,128)(2,1)S(1)} %copy-done.2, bf16[144,768]{1,0:T(8,128)(2,1)S(1)} %shard_map.109.message.refs_0_), custom_call_target="tpu_custom_call" | custom-call | bytes 663552 | tf_op jit(solution)/shard_map/pallas_call | solution.py:22
  5.0 7.3 %all-to-all-start = ((bf16[8,48,576]{2,1,0:T(8,128)(2,1)}), bf16[8,48,576]{2,1,0:T(8,128)(2,1)S(1)}, u32[]{:S(2)}, u32[]{:S(2)}) async-start(bf16[8,48,576]{2,1,0:T(8,128)(2,1)} %shard_map.110.qkv_pieces), calls=%async_computation | async-start | bytes 983040 | tf_op jit(solution)/shard_map/all_to_all | solution.py:386
  12.3 0.0 copy-start.1
  12.3 1.7 %shard_map.112 = bf16[8,48,768]{2,1,0:T(8,128)(2,1)} custom-call(bf16[96,768]{1,0:T(8,128)(2,1)S(1)} %copy-done.3, bf16[8,48,576]{2,1,0:T(8,128)(2,1)} %shard_map.110.qkv_pieces), custom_call_target="tpu_custom_call" | custom-call | bytes 589824 | tf_op jit(solution)/shard_map/pallas_call | solution.py:22
  14.0 12.1 %all-to-all-done.refs_8_ = bf16[8,48,576]{2,1,0:T(8,128)(2,1)S(1)} async-done(((bf16[8,48,576]{2,1,0:T(8,128)(2,1)}), bf16[8,48,576]{2,1,0:T(8,128)(2,1)S(1)}, u32[]{:S(2)}, u32[]{:S(2)}) %all-to-all-start) | async-done | bytes 442400 | tf_op jit(solution)/shard_map/all_to_all | solution.py:386
  26.1 3.6 %all-to-all-start.1 = ((bf16[8,48,768]{2,1,0:T(8,128)(2,1)}), bf16[8,48,768]{2,1,0:T(8,128)(2,1)S(1)}, u32[]{:S(2)}, u32[]{:S(2)}) async-start(bf16[8,48,768]{2,1,0:T(8,128)(2,1)} %shard_map.112), calls=%async_computation.1 | async-start | bytes 1179648 | tf_op jit(solution)/shard_map/all_to_all | solution.py:388
  29.7 2.0 %collective-permute-start = (bf16[144,768]{1,0:T(8,128)(2,1)S(1)}, bf16[144,768]{1,0:T(8,128)(2,1)S(1)}, u32[]{:S(2)}, u32[]{:S(2)}) collective-permute-start(bf16[144,768]{1,0:T(8,128)(2,1)S(1)} %shard_map.109.message.refs_0_), channel_id=1, source_target_pairs={{0,2},{1,3},{2,0},{3,1},{4,6},{5,7},{6,4},{7,5},{8,10},{9,11},{10,... | collective-permute-start | bytes 663560 | tf_op jit(solution)/shard_map/ppermute | solution.py:47
  31.7 1.5 %collective-permute-start.1 = (bf16[144,768]{1,0:T(8,128)(2,1)S(1)}, bf16[144,768]{1,0:T(8,128)(2,1)S(1)}, u32[]{:S(2)}, u32[]{:S(2)}) collective-permute-start(bf16[144,768]{1,0:T(8,128)(2,1)S(1)} %shard_map.109.message.refs_0_), channel_id=1, source_target_pairs={{0,16},{1,17},{2,18},{3,19},{4,20},{5,21},{6,22},{7,23},{8,24},{9,... | collective-permute-start | bytes 663560 | tf_op jit(solution)/shard_map/ppermute | solution.py:47
  33.3 0.0 collective-permute-start.2
  33.3 0.5 collective-permute-start.7
  33.8 10.8 %collective-permute-done.refs_1_ = bf16[144,768]{1,0:T(8,128)(2,1)S(1)} collective-permute-done((bf16[144,768]{1,0:T(8,128)(2,1)S(1)}, bf16[144,768]{1,0:T(8,128)(2,1)S(1)}, u32[]{:S(2)}, u32[]{:S(2)}) %collective-permute-start) | collective-permute-done | bytes 221216 | tf_op jit(solution)/shard_map/ppermute | solution.py:47
  44.6 1.2 %all-to-all-done.1.mine = bf16[8,48,768]{2,1,0:T(8,128)(2,1)S(1)} async-done(((bf16[8,48,768]{2,1,0:T(8,128)(2,1)}), bf16[8,48,768]{2,1,0:T(8,128)(2,1)S(1)}, u32[]{:S(2)}, u32[]{:S(2)}) %all-to-all-start.1) | async-done | bytes 589856 | tf_op jit(solution)/shard_map/all_to_all | solution.py:388
  45.8 0.0 collective-permute-start.11
  45.8 0.0 collective-permute-done.1.refs_2_
  45.8 0.5 collective-permute-start.4
  46.3 2.8 %collective-permute-done.2.refs_3_ = bf16[144,768]{1,0:T(8,128)(2,1)} collective-permute-done((bf16[144,768]{1,0:T(8,128)(2,1)S(1)}, bf16[144,768]{1,0:T(8,128)(2,1)}, u32[]{:S(2)}, u32[]{:S(2)}) %collective-permute-start.2) | collective-permute-done | bytes 221216 | tf_op jit(solution)/shard_map/ppermute | solution.py:47
  49.1 0.0 collective-permute-done.3.refs_4_
  49.1 0.5 collective-permute-start.6
  49.6 0.0 collective-permute-done.4.refs_5_
  49.6 0.5 collective-permute-start.12
  50.1 0.7 collective-permute-done.5.refs_6_
  50.8 0.3 collective-permute-done.6.refs_7_
  51.1 4.3 %shard_map.111 = (bf16[2,128,192]{2,1,0:T(8,128)(2,1)S(1)}, bf16[2,128,192]{2,1,0:T(8,128)(2,1)S(1)}, bf16[2,128,192]{2,1,0:T(8,128)(2,1)S(1)}, bf16[2,128,192]{2,1,0:T(8,128)(2,1)S(1)}) custom-call(bf16[144,768]{1,0:T(8,128)(2,1)S(1)} %shard_map.109.message.refs_0_, bf16[144,768]{1,0:T(8,128)(2,1)S(1)} %collective-permute-done.refs_1_, ...), custom_call_target="tpu_custom_call" | custom-call | flops 905969664 | bytes 2654208 | tf_op jit(solution)/shard_map/pallas_call | solution.py:22
  55.4 0.6 collective-permute-start.10
  56.0 1.5 %collective-permute-start.8 = (bf16[2,128,192]{2,1,0:T(8,128)(2,1)S(1)}, bf16[2,128,192]{2,1,0:T(8,128)(2,1)S(1)}, u32[]{:S(2)}, u32[]{:S(2)}) collective-permute-start(bf16[2,128,192]{2,1,0:T(8,128)(2,1)S(1)} %get-tuple-element.14), channel_id=1, source_target_pairs={{0,2},{1,3},{2,0},{3,1},{4,6},{5,7},{6,4},{7,5},{8,10},{9,11},{10,... | collective-permute-start | bytes 294920 | tf_op jit(solution)/shard_map/ppermute | solution.py:47
  57.5 1.5 %collective-permute-start.9 = (bf16[2,128,192]{2,1,0:T(8,128)(2,1)S(1)}, bf16[2,128,192]{2,1,0:T(8,128)(2,1)S(1)}, u32[]{:S(2)}, u32[]{:S(2)}) collective-permute-start(bf16[2,128,192]{2,1,0:T(8,128)(2,1)S(1)} %get-tuple-element.15), channel_id=1, source_target_pairs={{0,16},{1,17},{2,18},{3,19},{4,20},{5,21},{6,22},{7,23},{8,24},{9,... | collective-permute-start | bytes 294920 | tf_op jit(solution)/shard_map/ppermute | solution.py:47
  59.0 0.1 shard_map.113.weights
  59.1 0.0 copy-start.5
  59.1 3.6 %collective-permute-done.10.piece3 = bf16[2,128,192]{2,1,0:T(8,128)(2,1)S(1)} collective-permute-done((bf16[2,128,192]{2,1,0:T(8,128)(2,1)S(1)}, bf16[2,128,192]{2,1,0:T(8,128)(2,1)S(1)}, u32[]{:S(2)}, u32[]{:S(2)}) %collective-permute-start.10) | collective-permute-done | bytes 98336 | tf_op jit(solution)/shard_map/ppermute | solution.py:47
  62.8 1.1 %collective-permute-done.8.piece1 = bf16[2,128,192]{2,1,0:T(8,128)(2,1)S(1)} collective-permute-done((bf16[2,128,192]{2,1,0:T(8,128)(2,1)S(1)}, bf16[2,128,192]{2,1,0:T(8,128)(2,1)S(1)}, u32[]{:S(2)}, u32[]{:S(2)}) %collective-permute-start.8) | collective-permute-done | bytes 98336 | tf_op jit(solution)/shard_map/ppermute | solution.py:47
  63.9 1.0 %collective-permute-done.9.piece2 = bf16[2,128,192]{2,1,0:T(8,128)(2,1)S(1)} collective-permute-done((bf16[2,128,192]{2,1,0:T(8,128)(2,1)S(1)}, bf16[2,128,192]{2,1,0:T(8,128)(2,1)S(1)}, u32[]{:S(2)}, u32[]{:S(2)}) %collective-permute-start.9) | collective-permute-done | bytes 98336 | tf_op jit(solution)/shard_map/ppermute | solution.py:47
  64.8 0.6 shard_map.114.other_in
  65.4 0.0 copy-start.7
  65.4 3.4 %collective-permute-start.13 = (bf16[128,768]{1,0:T(8,128)(2,1)S(1)}, bf16[128,768]{1,0:T(8,128)(2,1)S(1)}, u32[]{:S(2)}, u32[]{:S(2)}) collective-permute-start(bf16[128,768]{1,0:T(8,128)(2,1)S(1)} %shard_map.114.other_in), channel_id=1, source_target_pairs={{0,4},{1,5},{4,8},{5,9},{6,2},{7,3},{8,12},{9,13},{10,6},{11,7},{1... | collective-permute-start | bytes 589832 | tf_op jit(solution)/shard_map/ppermute | solution.py:47
  68.8 0.2 copy.12.w_conv
  69.0 0.2 shard_map.115.blocks
  69.2 0.1 copy.14.taps
  71.2 2.0 %shard_map.116 = (bf16[128,768]{1,0:T(8,128)(2,1)S(1)}, f32[256,768]{1,0:T(8,128)S(1)}) custom-call(s32[1]{0:T(128)S(6)} %copy.15.lon_half, s32[1]{0:T(128)S(6)} %copy.16.lat_half, s32[1]{0:T(128)S(6)} %copy.17.quad_off, f32[16,2]{1,0:T(8,128)S(1)} %copy.14.taps, f32[1,768]{1,0:T(1,128)S(1)} %broadcast_in_dim.9.gain, ...), custom_call_target="tpu_custom_call" | custom-call | flops 452984832 | bytes 2755724 | tf_op jit(solution)/shard_map/pallas_call | solution.py:22
  73.3 1.3 %shard_map.117 = (f32[128,768]{1,0:T(8,128)S(1)}, bf16[128,768]{1,0:T(8,128)(2,1)S(1)}) custom-call(s32[1]{0:T(128)S(6)} %copy.15.lon_half, s32[1]{0:T(128)S(6)} %copy.16.lat_half, s32[1]{0:T(128)S(6)} %copy.17.quad_off, f32[16,2]{1,0:T(8,128)S(1)} %copy.14.taps, bf16[128,768]{1,0:T(8,128)(2,1)S(1)} %collective-permute-done.13.halo, ...), custom_call_target="tpu_custom_call" | custom-call | flops 100663296 | bytes 1966220 | tf_op jit(solution)/shard_map/pallas_call | solution.py:22
  74.6 0.1 collective-permute-start.14
  74.7 1.4 %collective-permute-done.14 = bf16[128,768]{1,0:T(8,128)(2,1)S(1)} collective-permute-done((bf16[128,768]{1,0:T(8,128)(2,1)S(1)}, bf16[128,768]{1,0:T(8,128)(2,1)S(1)}, u32[]{:S(2)}, u32[]{:S(2)}) %collective-permute-start.14) | collective-permute-done | bytes 196640 | tf_op jit(solution)/shard_map/ppermute | solution.py:51
  76.1 0.7 fusion
  (16 shorter events, 0.0 us)
Async XLA Ops:
  0.7 0.9 %copy-start = (bf16[1,128,768]{2,1,0:T(8,128)(2,1)S(1)}, bf16[1,128,768]{2,1,0:T(8,128)(2,1)}, u32[]{:S(2)}) copy-start(bf16[1,128,768]{2,1,0:T(8,128)(2,1)} %param.11) | copy-start | bytes 589828
  1.6 0.7 copy-start.4
  2.3 10.0 %copy-start.3 = (bf16[96,768]{1,0:T(8,128)(2,1)S(1)}, bf16[96,768]{1,0:T(8,128)(2,1)}, u32[]{:S(2)}) copy-start(bf16[96,768]{1,0:T(8,128)(2,1)} %w_out.1) | copy-start | bytes 442372
  2.8 1.0 %copy-start.2 = (bf16[96,2304]{1,0:T(8,128)(2,1)S(1)}, bf16[96,2304]{1,0:T(8,128)(2,1)}, u32[]{:S(2)}) copy-start(bf16[96,2304]{1,0:T(8,128)(2,1)} %w_qkv.1) | copy-start | bytes 1327108
  5.0 21.0 %all-to-all-start = ((bf16[8,48,576]{2,1,0:T(8,128)(2,1)}), bf16[8,48,576]{2,1,0:T(8,128)(2,1)S(1)}, u32[]{:S(2)}, u32[]{:S(2)}) async-start(bf16[8,48,576]{2,1,0:T(8,128)(2,1)} %shard_map.110.qkv_pieces), calls=%async_computation | async-start | bytes 983040 | tf_op jit(solution)/shard_map/all_to_all | solution.py:386
  12.3 37.3 %copy-start.1 = (bf16[1,128,768]{2,1,0:T(8,128)(2,1)S(1)}, bf16[1,128,768]{2,1,0:T(8,128)(2,1)}, u32[]{:S(2)}) copy-start(bf16[1,128,768]{2,1,0:T(8,128)(2,1)} %param.11) | copy-start | bytes 589828
  26.1 19.7 %all-to-all-start.1 = ((bf16[8,48,768]{2,1,0:T(8,128)(2,1)}), bf16[8,48,768]{2,1,0:T(8,128)(2,1)S(1)}, u32[]{:S(2)}, u32[]{:S(2)}) async-start(bf16[8,48,768]{2,1,0:T(8,128)(2,1)} %shard_map.112), calls=%async_computation.1 | async-start | bytes 1179648 | tf_op jit(solution)/shard_map/all_to_all | solution.py:388
  29.7 29.3 %copy-start.6 = (f32[768]{0:T(1024)S(1)}, f32[768]{0:T(1024)}, u32[]{:S(2)}) copy-start(f32[768]{0:T(1024)} %param.16) | copy-start | bytes 9220
  29.7 14.8 %collective-permute-start = (bf16[144,768]{1,0:T(8,128)(2,1)S(1)}, bf16[144,768]{1,0:T(8,128)(2,1)S(1)}, u32[]{:S(2)}, u32[]{:S(2)}) collective-permute-start(bf16[144,768]{1,0:T(8,128)(2,1)S(1)} %shard_map.109.message.refs_0_), channel_id=1, source_target_pairs={{0,2},{1,3},{2,0},{3,1},{4,6},{5,7},{6,4},{7,5},{8,10},{9,11},{10,... | collective-permute-start | bytes 663560 | tf_op jit(solution)/shard_map/ppermute | solution.py:47
  31.7 14.0 %collective-permute-start.1 = (bf16[144,768]{1,0:T(8,128)(2,1)S(1)}, bf16[144,768]{1,0:T(8,128)(2,1)S(1)}, u32[]{:S(2)}, u32[]{:S(2)}) collective-permute-start(bf16[144,768]{1,0:T(8,128)(2,1)S(1)} %shard_map.109.message.refs_0_), channel_id=1, source_target_pairs={{0,16},{1,17},{2,18},{3,19},{4,20},{5,21},{6,22},{7,23},{8,24},{9,... | collective-permute-start | bytes 663560 | tf_op jit(solution)/shard_map/ppermute | solution.py:47
  33.3 15.8 %collective-permute-start.2 = (bf16[144,768]{1,0:T(8,128)(2,1)S(1)}, bf16[144,768]{1,0:T(8,128)(2,1)}, u32[]{:S(2)}, u32[]{:S(2)}) collective-permute-start(bf16[144,768]{1,0:T(8,128)(2,1)S(1)} %shard_map.109.message.refs_0_), channel_id=1, source_target_pairs={{0,18},{1,19},{2,16},{3,17},{4,22},{5,23},{6,20},{7,21},{8,26},{9,... | collective-permute-start | bytes 663560 | tf_op jit(solution)/shard_map/ppermute | solution.py:47
  33.3 15.8 %collective-permute-start.3 = (bf16[144,768]{1,0:T(8,128)(2,1)S(1)}, bf16[144,768]{1,0:T(8,128)(2,1)}, u32[]{:S(2)}, u32[]{:S(2)}) collective-permute-start(bf16[144,768]{1,0:T(8,128)(2,1)S(1)} %shard_map.109.message.refs_0_), channel_id=1, source_target_pairs={{0,1},{1,0},{2,3},{3,2},{4,5},{5,4},{6,7},{7,6},{8,9},{9,8},{10,11... | collective-permute-start | bytes 663560 | tf_op jit(solution)/shard_map/ppermute | solution.py:51
  33.3 17.8 %collective-permute-start.7 = (bf16[8,48,576]{2,1,0:T(8,128)(2,1)S(1)}, bf16[8,48,576]{2,1,0:T(8,128)(2,1)S(1)}, u32[]{:S(2)}, u32[]{:S(2)}) collective-permute-start(bf16[8,48,576]{2,1,0:T(8,128)(2,1)S(1)} %all-to-all-done.refs_8_), channel_id=1, source_target_pairs={{0,1},{1,0},{2,3},{3,2},{4,5},{5,4},{6,7},{7,6},{8,9},{9,8},{10,11... | collective-permute-start | bytes 1327112 | tf_op jit(solution)/shard_map/ppermute | solution.py:51
  45.8 13.2 %collective-permute-start.11 = (bf16[8,48,768]{2,1,0:T(8,128)(2,1)S(1)}, bf16[8,48,768]{2,1,0:T(8,128)(2,1)S(1)}, u32[]{:S(2)}, u32[]{:S(2)}) collective-permute-start(bf16[8,48,768]{2,1,0:T(8,128)(2,1)S(1)} %all-to-all-done.1.mine), channel_id=1, source_target_pairs={{0,1},{1,0},{2,3},{3,2},{4,5},{5,4},{6,7},{7,6},{8,9},{9,8},{10,11... | collective-permute-start | bytes 1769480 | tf_op jit(solution)/shard_map/ppermute | solution.py:51
  45.8 3.8 %collective-permute-start.4 = (bf16[144,768]{1,0:T(8,128)(2,1)S(1)}, bf16[144,768]{1,0:T(8,128)(2,1)S(1)}, u32[]{:S(2)}, u32[]{:S(2)}) collective-permute-start(bf16[144,768]{1,0:T(8,128)(2,1)S(1)} %collective-permute-done.refs_1_), channel_id=1, source_target_pairs={{0,1},{1,0},{2,3},{3,2},{4,5},{5,4},{6,7},{7,6},{8,9},{9,8},{10,11... | collective-permute-start | bytes 663560 | tf_op jit(solution)/shard_map/ppermute | solution.py:51
  49.1 1.7 %collective-permute-start.5 = (bf16[144,768]{1,0:T(8,128)(2,1)S(1)}, bf16[144,768]{1,0:T(8,128)(2,1)S(1)}, u32[]{:S(2)}, u32[]{:S(2)}) collective-permute-start(bf16[144,768]{1,0:T(8,128)(2,1)S(1)} %collective-permute-done.1.refs_2_), channel_id=1, source_target_pairs={{0,1},{1,0},{2,3},{3,2},{4,5},{5,4},{6,7},{7,6},{8,9},{9,8},{10,11... | collective-permute-start | bytes 663560 | tf_op jit(solution)/shard_map/ppermute | solution.py:51
  49.1 2.0 %collective-permute-start.6 = (bf16[144,768]{1,0:T(8,128)(2,1)}, bf16[144,768]{1,0:T(8,128)(2,1)S(1)}, u32[]{:S(2)}, u32[]{:S(2)}) collective-permute-start(bf16[144,768]{1,0:T(8,128)(2,1)} %collective-permute-done.2.refs_3_), channel_id=1, source_target_pairs={{0,1},{1,0},{2,3},{3,2},{4,5},{5,4},{6,7},{7,6},{8,9},{9,8},{10,11... | collective-permute-start | bytes 663560 | tf_op jit(solution)/shard_map/ppermute | solution.py:51
  49.6 9.5 %collective-permute-start.12 = (bf16[128,768]{1,0:T(8,128)(2,1)S(1)}, bf16[128,768]{1,0:T(8,128)(2,1)S(1)}, u32[]{:S(2)}, u32[]{:S(2)}) collective-permute-start(bf16[128,768]{1,0:T(8,128)(2,1)S(1)} %bitcast.5), channel_id=1, source_target_pairs={{0,2},{1,3},{2,0},{3,1},{4,6},{5,7},{6,4},{7,5},{8,10},{9,11},{10,... | collective-permute-start | bytes 589832 | tf_op jit(solution)/shard_map/ppermute | solution.py:47
  55.4 7.3 %collective-permute-start.10 = (bf16[2,128,192]{2,1,0:T(8,128)(2,1)S(1)}, bf16[2,128,192]{2,1,0:T(8,128)(2,1)S(1)}, u32[]{:S(2)}, u32[]{:S(2)}) collective-permute-start(bf16[2,128,192]{2,1,0:T(8,128)(2,1)S(1)} %get-tuple-element.16), channel_id=1, source_target_pairs={{0,18},{1,19},{2,16},{3,17},{4,22},{5,23},{6,20},{7,21},{8,26},{9,... | collective-permute-start | bytes 294920 | tf_op jit(solution)/shard_map/ppermute | solution.py:47
  56.0 7.9 %collective-permute-start.8 = (bf16[2,128,192]{2,1,0:T(8,128)(2,1)S(1)}, bf16[2,128,192]{2,1,0:T(8,128)(2,1)S(1)}, u32[]{:S(2)}, u32[]{:S(2)}) collective-permute-start(bf16[2,128,192]{2,1,0:T(8,128)(2,1)S(1)} %get-tuple-element.14), channel_id=1, source_target_pairs={{0,2},{1,3},{2,0},{3,1},{4,6},{5,7},{6,4},{7,5},{8,10},{9,11},{10,... | collective-permute-start | bytes 294920 | tf_op jit(solution)/shard_map/ppermute | solution.py:47
  57.5 7.3 %collective-permute-start.9 = (bf16[2,128,192]{2,1,0:T(8,128)(2,1)S(1)}, bf16[2,128,192]{2,1,0:T(8,128)(2,1)S(1)}, u32[]{:S(2)}, u32[]{:S(2)}) collective-permute-start(bf16[2,128,192]{2,1,0:T(8,128)(2,1)S(1)} %get-tuple-element.15), channel_id=1, source_target_pairs={{0,16},{1,17},{2,18},{3,19},{4,20},{5,21},{6,22},{7,23},{8,24},{9,... | collective-permute-start | bytes 294920 | tf_op jit(solution)/shard_map/ppermute | solution.py:47
  59.1 9.7 %copy-start.5 = (bf16[2,768,64]{1,2,0:T(8,128)(2,1)S(1)}, bf16[2,768,64]{1,2,0:T(8,128)(2,1)}, u32[]{:S(2)}) copy-start(bf16[2,768,64]{1,2,0:T(8,128)(2,1)} %param.17) | copy-start | bytes 589828
  65.4 3.8 %copy-start.7 = (f32[16,2]{0,1:T(2,128)S(1)}, f32[16,2]{0,1:T(2,128)}, u32[]{:S(2)}) copy-start(f32[16,2]{0,1:T(2,128)} %param.18) | copy-start | bytes 388
  65.4 7.9 %collective-permute-start.13 = (bf16[128,768]{1,0:T(8,128)(2,1)S(1)}, bf16[128,768]{1,0:T(8,128)(2,1)S(1)}, u32[]{:S(2)}, u32[]{:S(2)}) collective-permute-start(bf16[128,768]{1,0:T(8,128)(2,1)S(1)} %shard_map.114.other_in), channel_id=1, source_target_pairs={{0,4},{1,5},{4,8},{5,9},{6,2},{7,3},{8,12},{9,13},{10,6},{11,7},{1... | collective-permute-start | bytes 589832 | tf_op jit(solution)/shard_map/ppermute | solution.py:47
  74.6 1.5 %collective-permute-start.14 = (bf16[128,768]{1,0:T(8,128)(2,1)S(1)}, bf16[128,768]{1,0:T(8,128)(2,1)S(1)}, u32[]{:S(2)}, u32[]{:S(2)}) collective-permute-start(bf16[128,768]{1,0:T(8,128)(2,1)S(1)} %get-tuple-element.20), channel_id=1, source_target_pairs={{0,1},{1,0},{2,3},{3,2},{4,5},{5,4},{6,7},{7,6},{8,9},{9,8},{10,11... | collective-permute-start | bytes 589832 | tf_op jit(solution)/shard_map/ppermute | solution.py:51

commit v5 on v4

--- a/solution.py
+++ b/solution.py
@@ -10,6 +10,7 @@
 AXES = ("groups", "lat", "lon")
 VMEM = pl.BlockSpec(memory_space=pltpu.VMEM)
 ANY = pl.BlockSpec(memory_space=pl.ANY)
+HBM = pl.BlockSpec(memory_space=pltpu.HBM)
 FLIPS = ((1, 0), (0, 1), (1, 1))
 SMEM = pl.BlockSpec(memory_space=pltpu.SMEM)
 BF16 = jnp.bfloat16
@@ -30,6 +31,20 @@
     )(*args)
 
 
+def untouched(*refs):
+    del refs
+
+
+def gate(value, *after):
+    return pl.pallas_call(
+        untouched,
+        out_shape=jax.ShapeDtypeStruct(value.shape, value.dtype),
+        in_specs=[ANY] * (1 + len(after)),
+        out_specs=ANY,
+        input_output_aliases={0: 0},
+    )(value, *after)
+
+
 def device_pairs(target):
     lat_count = lax.axis_size("lat")
     pairs = []
@@ -62,15 +77,37 @@
     return (centered * lax.rsqrt(variance + 1e-05) * gain).astype(BF16)
 
 
-def norm_body(tokens, bias, gain, message, raw, sems):
+def pack_body(tokens, bias, gain, w_out, message, raw, out_pieces, bias_here, gain_here, sems):
     count = tokens.shape[0]
     heads, bias_width = bias.shape
-    fetch = pltpu.make_async_copy(tokens, raw, sems.at[0])
-    fetch.start()
+    group, core = lax.axis_index("groups"), lax.axis_index("lon")
+    fetches = [
+        pltpu.make_async_copy(source, target, sems.at[at])
+        for at, (source, target) in enumerate(
+            ((tokens, raw), (gain, gain_here), (bias, bias_here))
+        )
+    ]
+    if out_pieces is not None:
+        pieces, half, columns = out_pieces.shape
+        rows = pl.ds(pl.multiple_of(core * half, half), half)
+        lanes = pl.ds(pl.multiple_of(group * columns, columns), columns)
+        fetches += [
+            pltpu.make_async_copy(w_out.at[rows, lanes], out_pieces.at[row], sems.at[3 + row])
+            for row in range(pieces)
+        ]
+    for fetch in fetches:
+        fetch.start()
     message[count:, :] = jnp.zeros((16, tokens.shape[1]), BF16)
-    message[count : count + heads, :bias_width] = bias[...]
-    fetch.wait()
-    message[:count, :] = norm_rows(raw[...].astype(F32), gain[...])
+    for fetch in fetches[:3]:
+        fetch.wait()
+    message[count : count + heads, :bias_width] = bias_here[...]
+    message[:count, :] = norm_rows(raw[...].astype(F32), gain_here[...])
+    for fetch in fetches[3:]:
+        fetch.wait()
+
+
+def pack_norm_body(tokens, bias, gain, message, raw, bias_here, gain_here, sems):
+    pack_body(tokens, bias, gain, None, message, raw, None, bias_here, gain_here, sems)
 
 
 def pack_qkv_body(w_qkv, message, pieces, rows, sems):
@@ -98,27 +135,27 @@
             pieces[2 * pair + side] = piece
 
 
-def pack_out_body(w_out, qkv_pieces, pieces, sems):
-    del qkv_pieces
-    core = lax.axis_index("lon")
-    count, half, _ = pieces.shape
-    start = pl.multiple_of(core * half, half)
-    fetches = [
-        pltpu.make_async_copy(w_out.at[pl.ds(start, half), :], pieces.at[row], sems.at[row])
-        for row in range(count)
-    ]
-    for fetch in fetches:
-        fetch.start()
-    for fetch in fetches:
-        fetch.wait()
-
-
 def join_halves(mine, other, joined):
     core = lax.axis_index("lon")
     count, half, _ = mine.shape
     for row in range(count):
         joined[pl.ds(pl.multiple_of(row * 2 * half + core * half, half), half), :] = mine[row]
         joined[pl.ds(pl.multiple_of(row * 2 * half + (1 - core) * half, half), half), :] = other[row]
+
+
+def join_quarters(mine, other, mine_far, other_far, joined):
+    group, core = lax.axis_index("groups"), lax.axis_index("lon")
+    count, half, columns = mine.shape
+    for at_group, at_core, block in (
+        (group, core, mine),
+        (1 - group, core, other),
+        (group, 1 - core, mine_far),
+        (1 - group, 1 - core, other_far),
+    ):
+        lanes = pl.ds(pl.multiple_of(at_group * columns, columns), columns)
+        for row in range(count):
+            first = row * 2 * half + at_core * half
+            joined[pl.ds(pl.multiple_of(first, half), half), lanes] = block[row]
 
 
 def attend_body(*refs):
@@ -185,18 +222,6 @@
     other_in[...] = project_out(1, pieces, weights, tokens[...], gain[...])[1]
 
 
-def diagonal_body(w_conv, blocks):
-    size = w_conv.shape[2]
-    blocks[...] = jnp.zeros(blocks.shape, BF16)
-    per_block = blocks.shape[2] // size
-    for basis in range(blocks.shape[0]):
-        for tile in range(blocks.shape[1]):
-            for at in range(per_block):
-                first = (tile * per_block + at) * size
-                low, high = at * size, (at + 1) * size
-                blocks[basis, tile, low:high, low:high] = w_conv[basis, first : first + size, :]
-
-
 def tent_pair(row_count, first_col, col_count, half_width):
     rows = lax.broadcasted_iota(jnp.int32, (row_count, col_count), 0)
     cols = lax.broadcasted_iota(jnp.int32, (row_count, col_count), 1) + first_col
@@ -225,19 +250,41 @@
     )
 
 
-def tap_gain(taps, quad_off, lat_half, offset, basis):
-    value = taps[quad_off[0] + offset + 1, basis]
-    if offset == 0:
-        return value
-    return jnp.where(lat_half[0] >= 1, value, 0.0)
+def plan_body(
+    lat_count, lon_half, lat_half, quad_off, taps, w_conv, message, blocks, coeffs, gains
+):
+    del message
+    lat_row, core = lax.axis_index("lat"), lax.axis_index("lon")
+    side = lax.rem(lat_row, 2)
+    for basis in range(2):
+        below, centre, above = (taps[quad_off[0] + row, basis] for row in range(3))
+        below = jnp.where(lat_half[0] >= 1, below, 0.0)
+        above = jnp.where(lat_half[0] >= 1, above, 0.0)
+        other = jnp.where(side == 0, above, below)
+        halo = jnp.where(side == 0, below, above)
+        pole = jnp.where(lat_row == 0, below, 0.0) + jnp.where(
+            lat_row == lat_count - 1, above, 0.0
+        )
+        for at, value in enumerate((other, centre, halo, pole)):
+            gains[4 * basis + at : 4 * basis + at + 1, :] = jnp.full((1, 128), value, F32)
+    rows, count = coeffs.shape[0], coeffs.shape[1] // 4
+    direct = tent_pair(rows, core * count, count, lon_half[0])
+    rolled = tent_pair(rows, core * count + count, count, lon_half[0])
+    for at, part in enumerate((direct[0], direct[1], rolled[0], rolled[1])):
+        coeffs[:, at * count : (at + 1) * count] = part
+    size = w_conv.shape[2]
+    blocks[...] = jnp.zeros(blocks.shape, BF16)
+    per_block = blocks.shape[2] // size
+    for basis in range(blocks.shape[0]):
+        for tile in range(blocks.shape[1]):
+            for at in range(per_block):
+                first = (tile * per_block + at) * size
+                low, high = at * size, (at + 1) * size
+                blocks[basis, tile, low:high, low:high] = w_conv[basis, first : first + size, :]
 
 
 def own_body(
-    lat_count,
-    lon_half,
-    lat_half,
-    quad_off,
-    taps,
+    gains,
     gain,
     piece0,
     piece1,
@@ -247,62 +294,40 @@
     tokens,
     other_in,
     blocks,
+    coeffs,
     middle,
     partial,
 ):
-    lat_row, core = lax.axis_index("lat"), lax.axis_index("lon")
-    side = lax.rem(lat_row, 2)
     count = tokens.shape[0]
     pieces = (piece0, piece1, piece2, piece3)
     own_middle, own_in = project_out(0, pieces, weights, tokens[...], gain[...])
     middle[...] = own_middle
     own = own_in.astype(F32)
     neighbour = other_in[...].astype(F32)
-    rows = partial.shape[0]
-    mixed, coeffs = [], []
-    direct = tent_pair(rows, core * count, count, lon_half[0])
-    rolled = tent_pair(rows, core * count + count, count, lon_half[0])
+    direct, rolled = [], []
     for basis in range(2):
-        below = tap_gain(taps, quad_off, lat_half, -1, basis)
-        above = tap_gain(taps, quad_off, lat_half, 1, basis)
-        centre = tap_gain(taps, quad_off, lat_half, 0, basis)
-        other_gain = jnp.where(side == 0, above, below)
-        pole_gain = jnp.where(lat_row == 0, below, 0.0) + jnp.where(
-            lat_row == lat_count - 1, above, 0.0
+        other, centre, _, pole = (gains[4 * basis + at : 4 * basis + at + 1, :1] for at in range(4))
+        lines = jnp.concatenate(
+            [(other * neighbour + centre * own).astype(BF16), (pole * own).astype(BF16)]
         )
-        lines = jnp.concatenate(
-            [
-                (other_gain * neighbour + centre * own).astype(BF16),
-                (pole_gain * own).astype(BF16),
-            ]
-        )
-        mixed.append(mix(lines, blocks, basis))
-        coeffs += [direct[basis], rolled[basis]]
+        mixed = mix(lines, blocks, basis)
+        direct.append(mixed[:count])
+        rolled.append(mixed[count:])
     partial[...] = jnp.dot(
-        jnp.concatenate(coeffs, axis=1),
-        jnp.concatenate(mixed, axis=0),
-        preferred_element_type=F32,
-    )
-
-
-def halo_body(
-    lon_half, lat_half, quad_off, taps, halo, blocks, middle, partial, kept, sent, total
-):
-    lat_row, core = lax.axis_index("lat"), lax.axis_index("lon")
-    side = lax.rem(lat_row, 2)
+        coeffs[...], jnp.concatenate(direct + rolled), preferred_element_type=F32
+    )
+
+
+def halo_body(gains, halo, blocks, coeffs, middle, partial, kept, sent, total):
+    core = lax.axis_index("lon")
     count = halo.shape[0]
-    rows = partial.shape[0]
     values = halo[...].astype(F32)
-    mixed = []
-    for basis in range(2):
-        below = tap_gain(taps, quad_off, lat_half, -1, basis)
-        above = tap_gain(taps, quad_off, lat_half, 1, basis)
-        gain = jnp.where(side == 0, below, above)
-        mixed.append(mix((gain * values).astype(BF16), blocks, basis))
+    mixed = [
+        mix((gains[4 * basis + 2 : 4 * basis + 3, :1] * values).astype(BF16), blocks, basis)
+        for basis in range(2)
+    ]
     total[...] = partial[...] + jnp.dot(
-        jnp.concatenate(tent_pair(rows, core * count, count, lon_half[0]), axis=1),
-        jnp.concatenate(mixed, axis=0),
-        preferred_element_type=F32,
+        coeffs[:, : 2 * count], jnp.concatenate(mixed), preferred_element_type=F32
     )
     here = pl.multiple_of(core * count, count)
     there = pl.multiple_of((1 - core) * count, count)
@@ -314,8 +339,9 @@
     core, lat_count = lax.axis_index("lon"), lax.axis_size("lat")
     half, width = weights.shape[0] // 2, weights.shape[1]
     rows = lax.dynamic_slice_in_dim(weights, core * half, half, 0)
-    if columns == width:
-        return jnp.broadcast_to(rows[None], (lat_count, half, width))
+    if columns == width // 2:
+        rows = lax.dynamic_slice_in_dim(rows, lax.axis_index("groups") * columns, columns, 1)
+        return jnp.broadcast_to(rows[None], (lat_count, half, columns))
     rows = rows.reshape(half, 3, 2, 2, columns // 3)
     rows = lax.dynamic_index_in_dim(rows, lax.axis_index("groups"), 3, keepdims=False)
     rows = rows.transpose(2, 0, 1, 3).reshape(2, half, columns)
@@ -349,53 +375,70 @@
     lat_count = lax.axis_size("lat")
     core = lax.axis_index("lon")
     half = w_qkv.shape[0] // 2
-    gain_attn = gain_attn[None]
     gain_conv = gain_conv[None]
 
-    (message,) = call(
-        norm_body,
-        [((count + 16, width), BF16)],
-        [ANY, VMEM, VMEM],
-        (own_tokens, key_bias[0], gain_attn),
-        10 * count * width,
-        [pltpu.VMEM((count, width), BF16), pltpu.SemaphoreType.DMA((1,))],
-    )
-    near = [message] + [flip_chips(message, flip, sample) for flip, sample in FLIPS]
+    aligned = half % 16 == 0
+    outs = [((count + 16, width), BF16), ((count, width), BF16)]
+    scratch = [
+        pltpu.VMEM(key_bias.shape[1:], BF16),
+        pltpu.VMEM((1, width), F32),
+        pltpu.SemaphoreType.DMA((3 + lat_count,)),
+    ]
+    args = (own_tokens, key_bias[0], gain_attn[None])
+    if aligned:
+        message, raw_tokens, out_pieces = call(
+            pack_body,
+            outs + [((lat_count, half, width // 2), BF16)],
+            [HBM] * 4,
+            (*args, w_out),
+            10 * count * width,
+            scratch,
+        )
+    else:
+        message, raw_tokens = call(
+            pack_norm_body, outs, [HBM] * 3, args, 10 * count * width, scratch
+        )
+        out_pieces = pack_plain(w_out, width // 2)
+    out_mine = lax.all_to_all(out_pieces, "lat", 0, 0)
+
+    near = [message, flip_chips(message, 1, 0), flip_chips(message, 0, 1)]
+    near.append(flip_chips(near[1], 0, 1))
     far = [swap_cores(block) for block in near]
 
-    if half % 16 == 0:
+    size = 4 * w_conv.shape[2]
+    diagonal, coeffs, gains = call(
+        functools.partial(plan_body, lat_count),
+        [
+            ((2, width // size, size, size), BF16),
+            ((2 * count, 4 * count), BF16),
+            ((8, 128), F32),
+        ],
+        [SMEM] * 4 + [VMEM, ANY],
+        (lon_half, lat_half, quad_off, lat_taps, w_conv, message),
+        0,
+    )
+    if aligned:
         (qkv_pieces,) = call(
             pack_qkv_body,
             [((lat_count, half, 3 * quarter), BF16)],
-            [ANY] * 2,
+            [HBM, ANY],
             (w_qkv, message),
             0,
             [pltpu.VMEM((half, 3 * width), BF16), pltpu.SemaphoreType.DMA((1,))],
         )
-        (out_pieces,) = call(
-            pack_out_body,
-            [((lat_count, half, width), BF16)],
-            [ANY] * 2,
-            (w_out, qkv_pieces),
-            0,
-            [pltpu.SemaphoreType.DMA((lat_count,))],
-        )
     else:
         qkv_pieces = pack_plain(w_qkv, 3 * quarter)
-        out_pieces = pack_plain(w_out, width)
+    qkv_pieces = gate(qkv_pieces, near[1], near[2], out_mine, gains)
     qkv_mine = lax.all_to_all(qkv_pieces, "lat", 0, 0)
     qkv_other = swap_cores(qkv_mine)
-    out_mine = lax.all_to_all(out_pieces, "lat", 0, 0)
-    out_other = swap_cores(out_mine)
-    if half % 16:
+    out_other = flip_chips(out_mine, 0, 1)
+    out_far = [swap_cores(out_mine), swap_cores(out_other)]
+    if not aligned:
         qkv_mine, qkv_other = regroup(core, qkv_mine, qkv_other)
-        out_mine, out_other = regroup(core, out_mine, out_other)
-    other_tokens = flip_chips(own_tokens, 1, 0)
-
-    size = 4 * w_conv.shape[2]
-    (diagonal,) = call(
-        diagonal_body, [((2, width // size, size, size), BF16)], [VMEM], (w_conv,), 0
-    )
+        out_mine, out_far[0] = regroup(core, out_mine, out_far[0])
+        out_other, out_far[1] = regroup(core, out_other, out_far[1])
+    raw_tokens = gate(raw_tokens, qkv_mine)
+    other_tokens = flip_chips(raw_tokens, 1, 0)
 
     pieces = call(
         attend_body,
@@ -414,7 +457,7 @@
         flip_chips(piece, flip, sample) for piece, (flip, sample) in zip(pieces[1:], FLIPS)
     ]
     (full_out,) = call(
-        join_halves, [((width, width), BF16)], [VMEM] * 2, (out_mine, out_other), 0
+        join_quarters, [((width, width), BF16)], [VMEM] * 4, (out_mine, out_other, *out_far), 0
     )
     (other_in,) = call(
         other_body,
@@ -425,28 +468,17 @@
     )
     halo = move(other_in, lambda g, l, c: (g, l + 2 - 4 * (l % 2), c))
     middle, partial = call(
-        functools.partial(own_body, lat_count),
+        own_body,
         [((count, width), BF16), ((2 * count, width), F32)],
-        [SMEM] * 4 + [VMEM] * 9,
-        (
-            lon_half,
-            lat_half,
-            quad_off,
-            lat_taps,
-            gain_conv,
-            *back,
-            full_out,
-            own_tokens,
-            other_in,
-            diagonal,
-        ),
+        [VMEM] * 11,
+        (gains, gain_conv, *back, full_out, raw_tokens, other_in, diagonal, coeffs),
         2 * count * width * width * 3,
     )
     kept, sent = call(
         halo_body,
         [((count, width), F32), ((count, width), BF16)],
-        [SMEM] * 4 + [VMEM] * 4,
-        (lon_half, lat_half, quad_off, lat_taps, halo, diagonal, middle, partial),
+        [VMEM] * 6,
+        (gains, halo, diagonal, coeffs, middle, partial),
         2 * 256 * 256 * width,
         [pltpu.VMEM((2 * count, width), F32)],
     )

time: 77.3 us -> 79.5 us (1.028)
  the two profiles are of different devices: /device:TPU:0 before, /device:TPU:3 now
where the time goes in v5:
time: 79.5 us; the launch traced here: 78.6 us
  starting transfers between devices  27.8 us (35%)
  waiting for transfers between devices  27.7 us (35%)
  Pallas kernels  10.2 us (13%)
  local copies, waits for them, and re-layouts  10.1 us (13%)
  between operations  2.18 us (3%)
    ppermute x9, waiting for transfers between devices, move(): return lax.ppermute(values, AXES, device_pairs(target))  17.2 us
    pallas_call x8, Pallas kernels, call(): pl.pallas_call(body, out_shape=outs, in_specs=specs, out_specs=tuple((VME...  10.2 us
    all_to_all x1, waiting for transfers between devices, per_device(): qkv_mine = lax.all_to_all(qkv_pieces, 'lat', 0, 0)  9.35 us
    unnamed x44, local copies, waits for them, and re-layouts  9.32 us
    ppermute x8, starting transfers between devices, swap_cores(): return lax.ppermute(values, 'lon', [(0, 1), (1, 0)])  8.41 us
    ppermute x9, starting transfers between devices, move(): return lax.ppermute(values, AXES, device_pairs(target))  8.14 us
    all_to_all x1, starting transfers between devices, per_device(): out_mine = lax.all_to_all(out_pieces, 'lat', 0, 0)  5.78 us
    all_to_all x1, starting transfers between devices, per_device(): qkv_mine = lax.all_to_all(qkv_pieces, 'lat', 0, 0)  5.43 us
  transfers between devices with their start and end apart: 19, of which 8 were waited for; matrix products, arithmetic and copies ran while one was open for 2% of the time, Pallas kernels for 10%

profile of v5, /device:TPU:3, one launch (start us, length us, event | category | flops | bytes accessed | tf_op | source)
XLA Modules:
  0.0 78.6 jit_solution(15178227300279139223)
XLA Ops:
  0.0 0.7 broadcast_in_dim.9.gain
  0.7 0.9 %copy-done.12 = bf16[1,128,768]{2,1,0:T(8,128)(2,1)S(1)} copy-done((bf16[1,128,768]{2,1,0:T(8,128)(2,1)S(1)}, bf16[1,128,768]{2,1,0:T(8,128)(2,1)}, u32[]{:S(2)}) %copy-start.12) | copy-done | bytes 196632
  1.7 0.9 %copy-done.13 = bf16[96,768]{1,0:T(8,128)(2,1)S(1)} copy-done((bf16[96,768]{1,0:T(8,128)(2,1)S(1)}, bf16[96,768]{1,0:T(8,128)(2,1)}, u32[]{:S(2)}) %copy-start.13) | copy-done | bytes 147480
  2.6 0.7 copy-done.16
  3.3 1.4 %shard_map.109 = (bf16[144,768]{1,0:T(8,128)(2,1)S(1)}, bf16[128,768]{1,0:T(8,128)(2,1)S(1)}, bf16[8,48,384]{2,1,0:T(8,128)(2,1)}) custom-call(bf16[128,768]{1,0:T(8,128)(2,1)S(1)} %bitcast.4, bf16[12,128]{1,0:T(8,128)(2,1)S(1)} %bitcast.5, f32[1,768]{1,0:T(1,128)S(1)} %broadcast_in_dim.9.gain, bf16[96,768]{1,0:T(8,128)(2,1)S(1)} %copy-done.13), custom_call_target="tpu_custom_call" | custom-call | flops 983040 | bytes 350208 | tf_op jit(solution)/shard_map/pallas_call | solution.py:23
  4.7 0.7 copy-done.5
  5.3 5.8 %all-to-all-start = ((bf16[8,48,384]{2,1,0:T(8,128)(2,1)}), bf16[8,48,384]{2,1,0:T(8,128)(2,1)S(1)}, u32[]{:S(2)}, u32[]{:S(2)}) async-start(bf16[8,48,384]{2,1,0:T(8,128)(2,1)} %get-tuple-element.21), calls=%async_computation | async-start | bytes 589824 | tf_op jit(solution)/shard_map/all_to_all | solution.py:402
  11.1 1.2 %collective-permute-start.1 = (bf16[144,768]{1,0:T(8,128)(2,1)S(1)}, bf16[144,768]{1,0:T(8,128)(2,1)S(1)}, u32[]{:S(2)}, u32[]{:S(2)}) collective-permute-start(bf16[144,768]{1,0:T(8,128)(2,1)S(1)} %get-tuple-element.19.message.refs_0_), channel_id=1, source_target_pairs={{0,16},{1,17},{2,18},{3,19},{4,20},{5,21},{6,22},{7,23},{8,24},{9,... | collective-permute-start | bytes 663560 | tf_op jit(solution)/shard_map/ppermute | solution.py:62
  12.4 1.1 %copy.15.w_conv = bf16[2,768,64]{2,1,0:T(8,128)(2,1)S(1)} copy(bf16[2,768,64]{1,2,0:T(8,128)(2,1)} %param.17) | data formatting | bytes 393216 | tf_op args[6]
  13.5 0.1 copy.14.taps
  15.6 0.5 shard_map.111.refs_0_
  16.1 0.8 copy-done
  16.8 1.0 %shard_map.110 = (bf16[2,3,256,256]{3,2,1,0:T(8,128)(2,1)S(1)}, bf16[256,512]{1,0:T(8,128)(2,1)S(1)}, f32[8,128]{1,0:T(8,128)S(1)}) custom-call(s32[1]{0:T(128)S(6)} %copy.18.lon_half, s32[1]{0:T(128)S(6)} %copy.19.lat_half, s32[1]{0:T(128)S(6)} %copy.20.quad_off, f32[16,2]{1,0:T(8,128)S(1)} %copy.14.taps, bf16[2,768,64]{2,1,0:T(8,128)(2,1)S(1)} %copy.15.w_conv, ...), custom_call_target="tpu_custom_call" | custom-call | bytes 417932 | tf_op jit(solution)/shard_map/pallas_call | solution.py:23
  17.9 0.6 copy-done.14
  18.5 1.6 %collective-permute-done.refs_1_ = bf16[144,768]{1,0:T(8,128)(2,1)S(1)} collective-permute-done((bf16[144,768]{1,0:T(8,128)(2,1)S(1)}, bf16[144,768]{1,0:T(8,128)(2,1)S(1)}, u32[]{:S(2)}, u32[]{:S(2)}) %collective-permute-start) | collective-permute-done | bytes 221216 | tf_op jit(solution)/shard_map/ppermute | solution.py:62
  20.1 0.7 copy-done.8
  20.7 0.1 copy-done.10
  20.8 0.1 copy-done.1
  20.9 5.4 %all-to-all-start.1 = ((bf16[8,48,576]{2,1,0:T(8,128)(2,1)}), bf16[8,48,576]{2,1,0:T(8,128)(2,1)S(1)}, u32[]{:S(2)}, u32[]{:S(2)}) async-start(bf16[8,48,576]{2,1,0:T(8,128)(2,1)} %shard_map.112), calls=%async_computation.1 | async-start | bytes 983040 | tf_op jit(solution)/shard_map/all_to_all | solution.py:432
  26.3 1.8 %collective-permute-start.3 = (bf16[144,768]{1,0:T(8,128)(2,1)S(1)}, bf16[144,768]{1,0:T(8,128)(2,1)S(1)}, u32[]{:S(2)}, u32[]{:S(2)}) collective-permute-start(bf16[144,768]{1,0:T(8,128)(2,1)S(1)} %get-tuple-element.19.message.refs_0_), channel_id=1, source_target_pairs={{0,1},{1,0},{2,3},{3,2},{4,5},{5,4},{6,7},{7,6},{8,9},{9,8},{10,11... | collective-permute-start | bytes 663560 | tf_op jit(solution)/shard_map/ppermute | solution.py:66
  28.1 1.2 %collective-permute-start.2 = (bf16[144,768]{1,0:T(8,128)(2,1)}, bf16[144,768]{1,0:T(8,128)(2,1)}, u32[]{:S(2)}, u32[]{:S(2)}) collective-permute-start(bf16[144,768]{1,0:T(8,128)(2,1)} %copy-done.8), channel_id=1, source_target_pairs={{0,16},{1,17},{2,18},{3,19},{4,20},{5,21},{6,22},{7,23},{8,24},{9,... | collective-permute-start | bytes 663560 | tf_op jit(solution)/shard_map/ppermute | solution.py:62
  29.4 9.3 %all-to-all-done.1.refs_8_.refs_1_ = bf16[8,48,576]{2,1,0:T(8,128)(2,1)S(1)} async-done(((bf16[8,48,576]{2,1,0:T(8,128)(2,1)}), bf16[8,48,576]{2,1,0:T(8,128)(2,1)S(1)}, u32[]{:S(2)}, u32[]{:S(2)}) %all-to-all-start.1) | async-done | bytes 442400 | tf_op jit(solution)/shard_map/all_to_all | solution.py:432
  38.7 2.1 %collective-permute-start.7 = (bf16[8,48,576]{2,1,0:T(8,128)(2,1)S(1)}, bf16[8,48,576]{2,1,0:T(8,128)(2,1)}, u32[]{:S(2)}, u32[]{:S(2)}) collective-permute-start(bf16[8,48,576]{2,1,0:T(8,128)(2,1)S(1)} %all-to-all-done.1.refs_8_.refs_1_), channel_id=1, source_target_pairs={{0,1},{1,0},{2,3},{3,2},{4,5},{5,4},{6,7},{7,6},{8,9},{9,8},{10,11... | collective-permute-start | bytes 1327112 | tf_op jit(solution)/shard_map/ppermute | solution.py:66
  40.8 1.2 %collective-permute-start.11 = (bf16[8,48,384]{2,1,0:T(8,128)(2,1)}, bf16[8,48,384]{2,1,0:T(8,128)(2,1)S(1)}, u32[]{:S(2)}, u32[]{:S(2)}) collective-permute-start(bf16[8,48,384]{2,1,0:T(8,128)(2,1)} %copy-done.1), channel_id=1, source_target_pairs={{0,16},{1,17},{2,18},{3,19},{4,20},{5,21},{6,22},{7,23},{8,24},{9,... | collective-permute-start | bytes 884744 | tf_op jit(solution)/shard_map/ppermute | solution.py:62
  42.0 0.8 %collective-permute-start.5 = (bf16[144,768]{1,0:T(8,128)(2,1)}, bf16[144,768]{1,0:T(8,128)(2,1)}, u32[]{:S(2)}, u32[]{:S(2)}) collective-permute-start(bf16[144,768]{1,0:T(8,128)(2,1)} %copy-done.10), channel_id=1, source_target_pairs={{0,1},{1,0},{2,3},{3,2},{4,5},{5,4},{6,7},{7,6},{8,9},{9,8},{10,11... | collective-permute-start | bytes 663560 | tf_op jit(solution)/shard_map/ppermute | solution.py:66
  42.9 0.7 copy-done.17
  43.6 0.4 collective-permute-start.12
  44.1 5.0 %collective-permute-done.11.other = bf16[8,48,384]{2,1,0:T(8,128)(2,1)S(1)} collective-permute-done((bf16[8,48,384]{2,1,0:T(8,128)(2,1)}, bf16[8,48,384]{2,1,0:T(8,128)(2,1)S(1)}, u32[]{:S(2)}, u32[]{:S(2)}) %collective-permute-start.11) | collective-permute-done | bytes 294944 | tf_op jit(solution)/shard_map/ppermute | solution.py:62
  49.1 1.4 %collective-permute-start.13 = (bf16[8,48,384]{2,1,0:T(8,128)(2,1)S(1)}, bf16[8,48,384]{2,1,0:T(8,128)(2,1)S(1)}, u32[]{:S(2)}, u32[]{:S(2)}) collective-permute-start(bf16[8,48,384]{2,1,0:T(8,128)(2,1)S(1)} %collective-permute-done.11.other), channel_id=1, source_target_pairs={{0,1},{1,0},{2,3},{3,2},{4,5},{5,4},{6,7},{7,6},{8,9},{9,8},{10,11... | collective-permute-start | bytes 884744 | tf_op jit(solution)/shard_map/ppermute | solution.py:66
  50.5 0.4 collective-permute-start.14
  50.9 1.0 %copy-done.4 = bf16[8,48,576]{2,1,0:T(8,128)(2,1)S(1)} copy-done((bf16[8,48,576]{2,1,0:T(8,128)(2,1)S(1)}, bf16[8,48,576]{2,1,0:T(8,128)(2,1)}, u32[]{:S(2)}) %copy-start.4) | copy-done | bytes 442392
  51.9 0.9 %copy-done.18 = bf16[144,768]{1,0:T(8,128)(2,1)S(1)} copy-done((bf16[144,768]{1,0:T(8,128)(2,1)S(1)}, bf16[144,768]{1,0:T(8,128)(2,1)}, u32[]{:S(2)}) %copy-start.18) | copy-done | bytes 221208
  52.8 4.6 %shard_map.113 = (bf16[2,128,192]{2,1,0:T(8,128)(2,1)S(1)}, bf16[2,128,192]{2,1,0:T(8,128)(2,1)S(1)}, bf16[2,128,192]{2,1,0:T(8,128)(2,1)S(1)}, bf16[2,128,192]{2,1,0:T(8,128)(2,1)S(1)}) custom-call(bf16[144,768]{1,0:T(8,128)(2,1)S(1)} %get-tuple-element.19.message.refs_0_, bf16[144,768]{1,0:T(8,128)(2,1)S(1)} %copy-done.9, bf16[144,768]{1,0:T(8,128)(2,1)S(1)} %copy-done.11, ...), custom_call_target="tpu_custom_call" | custom-call | flops 905969664 | bytes 2654208 | tf_op jit(solution)/shard_map/pallas_call | solution.py:23
  57.5 2.2 %collective-permute-start.10 = (bf16[2,128,192]{2,1,0:T(8,128)(2,1)S(1)}, bf16[2,128,192]{2,1,0:T(8,128)(2,1)S(1)}, u32[]{:S(2)}, u32[]{:S(2)}) collective-permute-start(bf16[2,128,192]{2,1,0:T(8,128)(2,1)S(1)} %get-tuple-element.25), channel_id=1, source_target_pairs={{0,18},{1,19},{2,16},{3,17},{4,22},{5,23},{6,20},{7,21},{8,26},{9,... | collective-permute-start | bytes 294920 | tf_op jit(solution)/shard_map/ppermute | solution.py:62
  59.6 0.3 collective-permute-start.8
  60.0 0.2 collective-permute-start.9
  60.2 0.1 shard_map.114.weights
  60.4 2.8 %collective-permute-done.10.piece3 = bf16[2,128,192]{2,1,0:T(8,128)(2,1)S(1)} collective-permute-done((bf16[2,128,192]{2,1,0:T(8,128)(2,1)S(1)}, bf16[2,128,192]{2,1,0:T(8,128)(2,1)S(1)}, u32[]{:S(2)}, u32[]{:S(2)}) %collective-permute-start.10) | collective-permute-done | bytes 98336 | tf_op jit(solution)/shard_map/ppermute | solution.py:62
  63.2 2.9 %collective-permute-done.8.piece1 = bf16[2,128,192]{2,1,0:T(8,128)(2,1)S(1)} collective-permute-done((bf16[2,128,192]{2,1,0:T(8,128)(2,1)S(1)}, bf16[2,128,192]{2,1,0:T(8,128)(2,1)S(1)}, u32[]{:S(2)}, u32[]{:S(2)}) %collective-permute-start.8) | collective-permute-done | bytes 98336 | tf_op jit(solution)/shard_map/ppermute | solution.py:62
  66.1 0.2 collective-permute-done.9.piece2
  66.3 0.6 shard_map.116.other_in
  66.9 1.3 %collective-permute-start.15 = (bf16[128,768]{1,0:T(8,128)(2,1)S(1)}, bf16[128,768]{1,0:T(8,128)(2,1)S(1)}, u32[]{:S(2)}, u32[]{:S(2)}) collective-permute-start(bf16[128,768]{1,0:T(8,128)(2,1)S(1)} %shard_map.116.other_in), channel_id=1, source_target_pairs={{0,4},{1,5},{4,8},{5,9},{6,2},{7,3},{8,12},{9,13},{10,6},{11,7},{1... | collective-permute-start | bytes 589832 | tf_op jit(solution)/shard_map/ppermute | solution.py:62
  68.2 1.4 %shard_map.117 = (bf16[128,768]{1,0:T(8,128)(2,1)S(1)}, f32[256,768]{1,0:T(8,128)S(1)}) custom-call(f32[8,128]{1,0:T(8,128)S(1)} %copy-done.15, f32[1,768]{1,0:T(1,128)S(1)} %broadcast_in_dim.10.gain, bf16[2,128,192]{2,1,0:T(8,128)(2,1)S(1)} %get-tuple-element.22.piece0, bf16[2,128,192]{2,1,0:T(8,128)(2,1)S(1)} %collective-permute-done.8.piece1, ...), custom_call_target="tpu_custom_call" | custom-call | flops 452984832 | bytes 3021824 | tf_op jit(solution)/shard_map/pallas_call | solution.py:23
  69.6 4.7 %collective-permute-done.15.halo = bf16[128,768]{1,0:T(8,128)(2,1)S(1)} collective-permute-done((bf16[128,768]{1,0:T(8,128)(2,1)S(1)}, bf16[128,768]{1,0:T(8,128)(2,1)S(1)}, u32[]{:S(2)}, u32[]{:S(2)}) %collective-permute-start.15) | collective-permute-done | bytes 196640 | tf_op jit(solution)/shard_map/ppermute | solution.py:62
  74.3 0.7 shard_map.118
  75.0 1.9 %collective-permute-start.16 = (bf16[128,768]{1,0:T(8,128)(2,1)S(1)}, bf16[128,768]{1,0:T(8,128)(2,1)S(1)}, u32[]{:S(2)}, u32[]{:S(2)}) collective-permute-start(bf16[128,768]{1,0:T(8,128)(2,1)S(1)} %get-tuple-element.32), channel_id=1, source_target_pairs={{0,1},{1,0},{2,3},{3,2},{4,5},{5,4},{6,7},{7,6},{8,9},{9,8},{10,11... | collective-permute-start | bytes 589832 | tf_op jit(solution)/shard_map/ppermute | solution.py:66
  76.8 1.1 %collective-permute-done.16 = bf16[128,768]{1,0:T(8,128)(2,1)S(1)} collective-permute-done((bf16[128,768]{1,0:T(8,128)(2,1)S(1)}, bf16[128,768]{1,0:T(8,128)(2,1)S(1)}, u32[]{:S(2)}, u32[]{:S(2)}) %collective-permute-start.16) | collective-permute-done | bytes 196640 | tf_op jit(solution)/shard_map/ppermute | solution.py:66
  77.9 0.7 fusion
  (47 shorter events, 0.2 us)
Async XLA Ops:
  0.0 15.6 %copy-start.7 = (bf16[96,2304]{1,0:T(8,128)(2,1)S(1)}, bf16[96,2304]{1,0:T(8,128)(2,1)}, u32[]{:S(2)}) copy-start(bf16[96,2304]{1,0:T(8,128)(2,1)} %w_qkv.1) | copy-start | bytes 1327108
  0.7 0.9 %copy-start.12 = (bf16[1,128,768]{2,1,0:T(8,128)(2,1)S(1)}, bf16[1,128,768]{2,1,0:T(8,128)(2,1)}, u32[]{:S(2)}) copy-start(bf16[1,128,768]{2,1,0:T(8,128)(2,1)} %param.11) | copy-start | bytes 589828
  1.7 0.9 %copy-start.13 = (bf16[96,768]{1,0:T(8,128)(2,1)S(1)}, bf16[96,768]{1,0:T(8,128)(2,1)}, u32[]{:S(2)}) copy-start(bf16[96,768]{1,0:T(8,128)(2,1)} %w_out.1) | copy-start | bytes 442372
  2.6 0.7 copy-start.16
  3.3 10.3 %copy-start.20 = (f32[16,2]{0,1:T(2,128)S(1)}, f32[16,2]{0,1:T(2,128)}, u32[]{:S(2)}) copy-start(f32[16,2]{0,1:T(2,128)} %param.18) | copy-start | bytes 388
  4.6 0.7 copy-start.5
  5.3 14.7 %all-to-all-start = ((bf16[8,48,384]{2,1,0:T(8,128)(2,1)}), bf16[8,48,384]{2,1,0:T(8,128)(2,1)S(1)}, u32[]{:S(2)}, u32[]{:S(2)}) async-start(bf16[8,48,384]{2,1,0:T(8,128)(2,1)} %get-tuple-element.21), calls=%async_computation | async-start | bytes 589824 | tf_op jit(solution)/shard_map/all_to_all | solution.py:402
  11.1 8.9 %collective-permute-start = (bf16[144,768]{1,0:T(8,128)(2,1)S(1)}, bf16[144,768]{1,0:T(8,128)(2,1)S(1)}, u32[]{:S(2)}, u32[]{:S(2)}) collective-permute-start(bf16[144,768]{1,0:T(8,128)(2,1)S(1)} %get-tuple-element.19.message.refs_0_), channel_id=1, source_target_pairs={{0,2},{1,3},{2,0},{3,1},{4,6},{5,7},{6,4},{7,5},{8,10},{9,11},{10,... | collective-permute-start | bytes 663560 | tf_op jit(solution)/shard_map/ppermute | solution.py:62
  11.1 8.9 %collective-permute-start.1 = (bf16[144,768]{1,0:T(8,128)(2,1)S(1)}, bf16[144,768]{1,0:T(8,128)(2,1)S(1)}, u32[]{:S(2)}, u32[]{:S(2)}) collective-permute-start(bf16[144,768]{1,0:T(8,128)(2,1)S(1)} %get-tuple-element.19.message.refs_0_), channel_id=1, source_target_pairs={{0,16},{1,17},{2,18},{3,19},{4,20},{5,21},{6,22},{7,23},{8,24},{9,... | collective-permute-start | bytes 663560 | tf_op jit(solution)/shard_map/ppermute | solution.py:62
  16.1 0.8 copy-start
  17.9 0.6 copy-start.14
  20.0 0.7 copy-start.8
  20.0 0.8 copy-start.10
  20.0 0.9 %copy-start.1 = (bf16[8,48,384]{2,1,0:T(8,128)(2,1)}, bf16[8,48,384]{2,1,0:T(8,128)(2,1)S(1)}, u32[]{:S(2)}) copy-start(bf16[8,48,384]{2,1,0:T(8,128)(2,1)S(1)} %all-to-all-done.refs_3_.mine) | copy-start | bytes 884740
  20.9 29.9 %copy-start.9 = (bf16[144,768]{1,0:T(8,128)(2,1)S(1)}, bf16[144,768]{1,0:T(8,128)(2,1)}, u32[]{:S(2)}) copy-start(bf16[144,768]{1,0:T(8,128)(2,1)} %copy-done.8) | copy-start | bytes 663556
  20.9 30.0 %copy-start.11 = (bf16[144,768]{1,0:T(8,128)(2,1)S(1)}, bf16[144,768]{1,0:T(8,128)(2,1)}, u32[]{:S(2)}) copy-start(bf16[144,768]{1,0:T(8,128)(2,1)} %copy-done.10) | copy-start | bytes 663556
  20.9 17.8 %all-to-all-start.1 = ((bf16[8,48,576]{2,1,0:T(8,128)(2,1)}), bf16[8,48,576]{2,1,0:T(8,128)(2,1)S(1)}, u32[]{:S(2)}, u32[]{:S(2)}) async-start(bf16[8,48,576]{2,1,0:T(8,128)(2,1)} %shard_map.112), calls=%async_computation.1 | async-start | bytes 983040 | tf_op jit(solution)/shard_map/all_to_all | solution.py:432
  26.3 15.7 %collective-permute-start.3 = (bf16[144,768]{1,0:T(8,128)(2,1)S(1)}, bf16[144,768]{1,0:T(8,128)(2,1)S(1)}, u32[]{:S(2)}, u32[]{:S(2)}) collective-permute-start(bf16[144,768]{1,0:T(8,128)(2,1)S(1)} %get-tuple-element.19.message.refs_0_), channel_id=1, source_target_pairs={{0,1},{1,0},{2,3},{3,2},{4,5},{5,4},{6,7},{7,6},{8,9},{9,8},{10,11... | collective-permute-start | bytes 663560 | tf_op jit(solution)/shard_map/ppermute | solution.py:66
  28.1 14.7 %collective-permute-start.2 = (bf16[144,768]{1,0:T(8,128)(2,1)}, bf16[144,768]{1,0:T(8,128)(2,1)}, u32[]{:S(2)}, u32[]{:S(2)}) collective-permute-start(bf16[144,768]{1,0:T(8,128)(2,1)} %copy-done.8), channel_id=1, source_target_pairs={{0,16},{1,17},{2,18},{3,19},{4,20},{5,21},{6,22},{7,23},{8,24},{9,... | collective-permute-start | bytes 663560 | tf_op jit(solution)/shard_map/ppermute | solution.py:62
  38.7 11.7 %copy-start.3 = (bf16[8,48,576]{2,1,0:T(8,128)(2,1)}, bf16[8,48,576]{2,1,0:T(8,128)(2,1)S(1)}, u32[]{:S(2)}) copy-start(bf16[8,48,576]{2,1,0:T(8,128)(2,1)S(1)} %all-to-all-done.1.refs_8_.refs_1_) | copy-start | bytes 1327108
  38.7 12.1 %collective-permute-start.7 = (bf16[8,48,576]{2,1,0:T(8,128)(2,1)S(1)}, bf16[8,48,576]{2,1,0:T(8,128)(2,1)}, u32[]{:S(2)}, u32[]{:S(2)}) collective-permute-start(bf16[8,48,576]{2,1,0:T(8,128)(2,1)S(1)} %all-to-all-done.1.refs_8_.refs_1_), channel_id=1, source_target_pairs={{0,1},{1,0},{2,3},{3,2},{4,5},{5,4},{6,7},{7,6},{8,9},{9,8},{10,11... | collective-permute-start | bytes 1327112 | tf_op jit(solution)/shard_map/ppermute | solution.py:66
  40.8 2.1 %collective-permute-start.4 = (bf16[144,768]{1,0:T(8,128)(2,1)}, bf16[144,768]{1,0:T(8,128)(2,1)S(1)}, u32[]{:S(2)}, u32[]{:S(2)}) collective-permute-start(bf16[144,768]{1,0:T(8,128)(2,1)} %copy-done.8), channel_id=1, source_target_pairs={{0,1},{1,0},{2,3},{3,2},{4,5},{5,4},{6,7},{7,6},{8,9},{9,8},{10,11... | collective-permute-start | bytes 663560 | tf_op jit(solution)/shard_map/ppermute | solution.py:66
  40.8 8.3 %collective-permute-start.11 = (bf16[8,48,384]{2,1,0:T(8,128)(2,1)}, bf16[8,48,384]{2,1,0:T(8,128)(2,1)S(1)}, u32[]{:S(2)}, u32[]{:S(2)}) collective-permute-start(bf16[8,48,384]{2,1,0:T(8,128)(2,1)} %copy-done.1), channel_id=1, source_target_pairs={{0,16},{1,17},{2,18},{3,19},{4,20},{5,21},{6,22},{7,23},{8,24},{9,... | collective-permute-start | bytes 884744 | tf_op jit(solution)/shard_map/ppermute | solution.py:62
  42.0 8.4 %collective-permute-start.5 = (bf16[144,768]{1,0:T(8,128)(2,1)}, bf16[144,768]{1,0:T(8,128)(2,1)}, u32[]{:S(2)}, u32[]{:S(2)}) collective-permute-start(bf16[144,768]{1,0:T(8,128)(2,1)} %copy-done.10), channel_id=1, source_target_pairs={{0,1},{1,0},{2,3},{3,2},{4,5},{5,4},{6,7},{7,6},{8,9},{9,8},{10,11... | collective-permute-start | bytes 663560 | tf_op jit(solution)/shard_map/ppermute | solution.py:66
  42.8 8.0 %collective-permute-start.6 = (bf16[144,768]{1,0:T(8,128)(2,1)}, bf16[144,768]{1,0:T(8,128)(2,1)}, u32[]{:S(2)}, u32[]{:S(2)}) collective-permute-start(bf16[144,768]{1,0:T(8,128)(2,1)} %collective-permute-done.2.refs_3_), channel_id=1, source_target_pairs={{0,1},{1,0},{2,3},{3,2},{4,5},{5,4},{6,7},{7,6},{8,9},{9,8},{10,11... | collective-permute-start | bytes 663560 | tf_op jit(solution)/shard_map/ppermute | solution.py:66
  42.9 0.7 copy-start.17
  43.6 16.4 %collective-permute-start.12 = (bf16[8,48,384]{2,1,0:T(8,128)(2,1)}, bf16[8,48,384]{2,1,0:T(8,128)(2,1)S(1)}, u32[]{:S(2)}, u32[]{:S(2)}) collective-permute-start(bf16[8,48,384]{2,1,0:T(8,128)(2,1)} %copy-done.1), channel_id=1, source_target_pairs={{0,1},{1,0},{2,3},{3,2},{4,5},{5,4},{6,7},{7,6},{8,9},{9,8},{10,11... | collective-permute-start | bytes 884744 | tf_op jit(solution)/shard_map/ppermute | solution.py:66
  49.1 11.1 %collective-permute-start.13 = (bf16[8,48,384]{2,1,0:T(8,128)(2,1)S(1)}, bf16[8,48,384]{2,1,0:T(8,128)(2,1)S(1)}, u32[]{:S(2)}, u32[]{:S(2)}) collective-permute-start(bf16[8,48,384]{2,1,0:T(8,128)(2,1)S(1)} %collective-permute-done.11.other), channel_id=1, source_target_pairs={{0,1},{1,0},{2,3},{3,2},{4,5},{5,4},{6,7},{7,6},{8,9},{9,8},{10,11... | collective-permute-start | bytes 884744 | tf_op jit(solution)/shard_map/ppermute | solution.py:66
  50.4 9.8 %copy-start.19 = (f32[768]{0:T(1024)S(1)}, f32[768]{0:T(1024)}, u32[]{:S(2)}) copy-start(f32[768]{0:T(1024)} %param.16) | copy-start | bytes 9220
  50.4 9.8 %copy-start.2 = (bf16[8,48,384]{2,1,0:T(8,128)(2,1)S(1)}, bf16[8,48,384]{2,1,0:T(8,128)(2,1)}, u32[]{:S(2)}) copy-start(bf16[8,48,384]{2,1,0:T(8,128)(2,1)} %copy-done.1) | copy-start | bytes 884740
  50.5 9.9 %collective-permute-start.14 = (bf16[128,768]{1,0:T(8,128)(2,1)}, bf16[128,768]{1,0:T(8,128)(2,1)S(1)}, u32[]{:S(2)}, u32[]{:S(2)}) collective-permute-start(bf16[128,768]{1,0:T(8,128)(2,1)} %shard_map.115.tokens), channel_id=1, source_target_pairs={{0,2},{1,3},{2,0},{3,1},{4,6},{5,7},{6,4},{7,5},{8,10},{9,11},{10,... | collective-permute-start | bytes 589832 | tf_op jit(solution)/shard_map/ppermute | solution.py:62
  50.9 1.0 %copy-start.4 = (bf16[8,48,576]{2,1,0:T(8,128)(2,1)S(1)}, bf16[8,48,576]{2,1,0:T(8,128)(2,1)}, u32[]{:S(2)}) copy-start(bf16[8,48,576]{2,1,0:T(8,128)(2,1)} %copy-done.3) | copy-start | bytes 1327108
  51.9 0.9 %copy-start.18 = (bf16[144,768]{1,0:T(8,128)(2,1)S(1)}, bf16[144,768]{1,0:T(8,128)(2,1)}, u32[]{:S(2)}) copy-start(bf16[144,768]{1,0:T(8,128)(2,1)} %copy-done.17) | copy-start | bytes 663556
  57.5 5.7 %collective-permute-start.10 = (bf16[2,128,192]{2,1,0:T(8,128)(2,1)S(1)}, bf16[2,128,192]{2,1,0:T(8,128)(2,1)S(1)}, u32[]{:S(2)}, u32[]{:S(2)}) collective-permute-start(bf16[2,128,192]{2,1,0:T(8,128)(2,1)S(1)} %get-tuple-element.25), channel_id=1, source_target_pairs={{0,18},{1,19},{2,16},{3,17},{4,22},{5,23},{6,20},{7,21},{8,26},{9,... | collective-permute-start | bytes 294920 | tf_op jit(solution)/shard_map/ppermute | solution.py:62
  59.6 6.5 %collective-permute-start.8 = (bf16[2,128,192]{2,1,0:T(8,128)(2,1)S(1)}, bf16[2,128,192]{2,1,0:T(8,128)(2,1)S(1)}, u32[]{:S(2)}, u32[]{:S(2)}) collective-permute-start(bf16[2,128,192]{2,1,0:T(8,128)(2,1)S(1)} %get-tuple-element.23), channel_id=1, source_target_pairs={{0,2},{1,3},{2,0},{3,1},{4,6},{5,7},{6,4},{7,5},{8,10},{9,11},{10,... | collective-permute-start | bytes 294920 | tf_op jit(solution)/shard_map/ppermute | solution.py:62
  60.0 6.4 %collective-permute-start.9 = (bf16[2,128,192]{2,1,0:T(8,128)(2,1)S(1)}, bf16[2,128,192]{2,1,0:T(8,128)(2,1)S(1)}, u32[]{:S(2)}, u32[]{:S(2)}) collective-permute-start(bf16[2,128,192]{2,1,0:T(8,128)(2,1)S(1)} %get-tuple-element.24), channel_id=1, source_target_pairs={{0,16},{1,17},{2,18},{3,19},{4,20},{5,21},{6,22},{7,23},{8,24},{9,... | collective-permute-start | bytes 294920 | tf_op jit(solution)/shard_map/ppermute | solution.py:62
  60.4 7.8 %copy-start.6 = (bf16[128,768]{1,0:T(8,128)(2,1)S(1)}, bf16[128,768]{1,0:T(8,128)(2,1)}, u32[]{:S(2)}) copy-start(bf16[128,768]{1,0:T(8,128)(2,1)} %shard_map.115.tokens) | copy-start | bytes 589828
  60.4 7.8 %copy-start.15 = (f32[8,128]{1,0:T(8,128)S(1)}, f32[8,128]{1,0:T(8,128)}, u32[]{:S(2)}) copy-start(f32[8,128]{1,0:T(8,128)} %copy-done.14) | copy-start | bytes 12292
  66.9 7.4 %collective-permute-start.15 = (bf16[128,768]{1,0:T(8,128)(2,1)S(1)}, bf16[128,768]{1,0:T(8,128)(2,1)S(1)}, u32[]{:S(2)}, u32[]{:S(2)}) collective-permute-start(bf16[128,768]{1,0:T(8,128)(2,1)S(1)} %shard_map.116.other_in), channel_id=1, source_target_pairs={{0,4},{1,5},{4,8},{5,9},{6,2},{7,3},{8,12},{9,13},{10,6},{11,7},{1... | collective-permute-start | bytes 589832 | tf_op jit(solution)/shard_map/ppermute | solution.py:62
  75.0 2.9 %collective-permute-start.16 = (bf16[128,768]{1,0:T(8,128)(2,1)S(1)}, bf16[128,768]{1,0:T(8,128)(2,1)S(1)}, u32[]{:S(2)}, u32[]{:S(2)}) collective-permute-start(bf16[128,768]{1,0:T(8,128)(2,1)S(1)} %get-tuple-element.32), channel_id=1, source_target_pairs={{0,1},{1,0},{2,3},{3,2},{4,5},{5,4},{6,7},{7,6},{8,9},{9,8},{10,11... | collective-permute-start | bytes 589832 | tf_op jit(solution)/shard_map/ppermute | solution.py:66

commit v6 on v5

--- a/solution.py
+++ b/solution.py
@@ -17,7 +17,7 @@
 F32 = jnp.float32
 
 
-def call(body, outs, specs, args, flops, scratch=()):
+def call(body, outs, specs, args, flops, scratch=(), limit=32):
     outs = tuple(jax.ShapeDtypeStruct(shape, dtype) for shape, dtype in outs)
     moved = sum(a.size * a.dtype.itemsize for a in args)
     return pl.pallas_call(
@@ -26,23 +26,18 @@
         in_specs=specs,
         out_specs=tuple(VMEM for _ in outs),
         scratch_shapes=list(scratch),
-        compiler_params=pltpu.CompilerParams(vmem_limit_bytes=32 * 1024 * 1024),
+        compiler_params=pltpu.CompilerParams(vmem_limit_bytes=limit * 1024 * 1024),
         cost_estimate=pl.CostEstimate(flops=flops, bytes_accessed=moved, transcendentals=0),
     )(*args)
 
 
-def untouched(*refs):
-    del refs
+def copy_body(*refs):
+    refs[-1][...] = refs[0][...]
 
 
 def gate(value, *after):
-    return pl.pallas_call(
-        untouched,
-        out_shape=jax.ShapeDtypeStruct(value.shape, value.dtype),
-        in_specs=[ANY] * (1 + len(after)),
-        out_specs=ANY,
-        input_output_aliases={0: 0},
-    )(value, *after)
+    specs = [VMEM] * (1 + len(after))
+    return call(copy_body, [(value.shape, value.dtype)], specs, (value, *after), 0)[0]
 
 
 def device_pairs(target):
@@ -77,24 +72,25 @@
     return (centered * lax.rsqrt(variance + 1e-05) * gain).astype(BF16)
 
 
-def pack_body(tokens, bias, gain, w_out, message, raw, out_pieces, bias_here, gain_here, sems):
+def pack_body(*refs, weights):
+    tokens, bias, gain, message, raw = *refs[:3], *refs[-9:-7]
     count = tokens.shape[0]
     heads, bias_width = bias.shape
     group, core = lax.axis_index("groups"), lax.axis_index("lon")
+    side = lax.rem(lax.axis_index("lat"), 2)
+    if weights:
+        w_qkv, w_out = refs[3:5]
+    qkv_own, qkv_cross, out_own, bias_here, gain_here, rows, sems = refs[-7:]
+    half = rows.shape[0]
+    quarter = qkv_own.shape[1] // 3
+    copies = [(gain, gain_here), (bias, bias_here), (tokens, raw)]
+    if weights:
+        picked = pl.ds(pl.multiple_of(core * half, half), half)
+        copies += [(w_qkv.at[picked, :], rows), (w_out.at[picked, :], out_own)]
     fetches = [
         pltpu.make_async_copy(source, target, sems.at[at])
-        for at, (source, target) in enumerate(
-            ((tokens, raw), (gain, gain_here), (bias, bias_here))
-        )
+        for at, (source, target) in enumerate(copies)
     ]
-    if out_pieces is not None:
-        pieces, half, columns = out_pieces.shape
-        rows = pl.ds(pl.multiple_of(core * half, half), half)
-        lanes = pl.ds(pl.multiple_of(group * columns, columns), columns)
-        fetches += [
-            pltpu.make_async_copy(w_out.at[rows, lanes], out_pieces.at[row], sems.at[3 + row])
-            for row in range(pieces)
-        ]
     for fetch in fetches:
         fetch.start()
     message[count:, :] = jnp.zeros((16, tokens.shape[1]), BF16)
@@ -104,68 +100,48 @@
     message[:count, :] = norm_rows(raw[...].astype(F32), gain_here[...])
     for fetch in fetches[3:]:
         fetch.wait()
-
-
-def pack_norm_body(tokens, bias, gain, message, raw, bias_here, gain_here, sems):
-    pack_body(tokens, bias, gain, None, message, raw, None, bias_here, gain_here, sems)
-
-
-def pack_qkv_body(w_qkv, message, pieces, rows, sems):
-    del message
-    group, core = lax.axis_index("groups"), lax.axis_index("lon")
-    half = pieces.shape[1]
-    quarter = pieces.shape[2] // 3
-    start = pl.multiple_of(core * half, half)
-    fetch = pltpu.make_async_copy(w_qkv.at[pl.ds(start, half), :], rows, sems.at[0])
-    fetch.start()
-    fetch.wait()
-    for side in range(2):
-        parts = []
-        for kind in range(3):
-            first = (4 * kind + 2 * side) * quarter
-            parts.append(
-                jnp.where(
-                    group == 0,
-                    rows[:, first : first + quarter],
-                    rows[:, first + quarter : first + 2 * quarter],
-                )
-            )
-        piece = jnp.concatenate(parts, axis=1)
-        for pair in range(pieces.shape[0] // 2):
-            pieces[2 * pair + side] = piece
-
-
-def join_halves(mine, other, joined):
+    if not weights:
+        return
+    for kind in range(3):
+        low = 4 * kind * quarter
+        block = [rows[:, low + at * quarter : low + (at + 1) * quarter] for at in range(4)]
+        sides = [jnp.where(group == 0, block[2 * at], block[2 * at + 1]) for at in range(2)]
+        columns = slice(kind * quarter, (kind + 1) * quarter)
+        qkv_own[:, columns] = jnp.where(side == 0, sides[0], sides[1])
+        qkv_cross[:, columns] = jnp.where(side == 0, sides[1], sides[0])
+
+
+def bundle_body(own, cross, bundle):
+    side = lax.rem(lax.axis_index("lat"), 2)
+    bundle[side] = own[...]
+    bundle[1 - side] = cross[...]
+
+
+def join_bundles(mine, other, joined):
     core = lax.axis_index("lon")
-    count, half, _ = mine.shape
-    for row in range(count):
-        joined[pl.ds(pl.multiple_of(row * 2 * half + core * half, half), half), :] = mine[row]
-        joined[pl.ds(pl.multiple_of(row * 2 * half + (1 - core) * half, half), half), :] = other[row]
-
-
-def join_quarters(mine, other, mine_far, other_far, joined):
-    group, core = lax.axis_index("groups"), lax.axis_index("lon")
-    count, half, columns = mine.shape
-    for at_group, at_core, block in (
-        (group, core, mine),
-        (1 - group, core, other),
-        (group, 1 - core, mine_far),
-        (1 - group, 1 - core, other_far),
-    ):
-        lanes = pl.ds(pl.multiple_of(at_group * columns, columns), columns)
-        for row in range(count):
-            first = row * 2 * half + at_core * half
-            joined[pl.ds(pl.multiple_of(first, half), half), lanes] = block[row]
+    pair = lax.rem(lax.axis_index("lat") // 2, 4)
+    for flip, blocks in enumerate(zip(mine, other)):
+        away = (pair // 2 + flip // 2 - 2 * (pair // 2) * (flip // 2)) * 2
+        away = away + (pair % 2 + flip % 2 - 2 * (pair % 2) * (flip % 2))
+        for block, at in zip(blocks, (core, 1 - core)):
+            half = block.shape[1]
+            for row in range(2):
+                first = pl.multiple_of(((away * 2 + row) * 2 + at) * half, half)
+                joined[pl.ds(first, half), :] = block[row]
+
+
+def join_body(*refs):
+    join_bundles(refs[:4], refs[4:8], refs[8])
 
 
 def attend_body(*refs):
-    near, far, (mine, other) = refs[:4], refs[4:8], refs[8:10]
-    pieces, (weights, bias_rows, near_rows, far_rows) = refs[10:14], refs[14:]
+    near, far, mine, other = refs[:4], refs[4:8], refs[8:12], refs[12:16]
+    pieces, (weights, bias_rows, near_rows, far_rows) = refs[17:21], refs[21:]
     group, side = lax.axis_index("groups"), lax.rem(lax.axis_index("lat"), 2)
     _, count, quarter = pieces[0].shape
     heads = 3
     head_dim = quarter // heads
-    join_halves(mine, other, weights)
+    join_bundles(mine, other, weights)
     for slot in range(4):
         near_rows[slot * count : (slot + 1) * count, :] = near[slot][:count, :]
         far_rows[slot * count : (slot + 1) * count, :] = far[slot][:count, :]
@@ -339,8 +315,7 @@
     core, lat_count = lax.axis_index("lon"), lax.axis_size("lat")
     half, width = weights.shape[0] // 2, weights.shape[1]
     rows = lax.dynamic_slice_in_dim(weights, core * half, half, 0)
-    if columns == width // 2:
-        rows = lax.dynamic_slice_in_dim(rows, lax.axis_index("groups") * columns, columns, 1)
+    if columns == width:
         return jnp.broadcast_to(rows[None], (lat_count, half, columns))
     rows = rows.reshape(half, 3, 2, 2, columns // 3)
     rows = lax.dynamic_index_in_dim(rows, lax.axis_index("groups"), 3, keepdims=False)
@@ -349,11 +324,35 @@
     return rows.reshape(lat_count, half, columns)
 
 
-def regroup(core, mine, other):
+def gather_plain(weights, columns):
+    core = lax.axis_index("lon")
+    mine = lax.all_to_all(pack_plain(weights, columns), "lat", 0, 0)
+    other = swap_cores(mine)
     both = jnp.where(core == 0, jnp.stack([mine, other], 1), jnp.stack([other, mine], 1))
-    whole = both.reshape(8, 2, -1, mine.shape[2])
-    pick = lambda index: lax.dynamic_index_in_dim(whole, index, 1, keepdims=False)
-    return pick(core), pick(1 - core)
+    whole = both.reshape(4, 2, 2, -1, columns)
+    pair = lax.rem(lax.axis_index("lat") // 2, 4)
+    return [
+        [
+            lax.dynamic_index_in_dim(
+                lax.dynamic_index_in_dim(whole, pair ^ flip, 0, keepdims=False),
+                at,
+                1,
+                keepdims=False,
+            )
+            for flip in range(4)
+        ]
+        for at in (core, 1 - core)
+    ]
+
+
+def bundled(own, cross):
+    return call(
+        bundle_body, [((2, *own.shape), BF16)], [VMEM] * 2, (own, flip_chips(cross, 1, 0)), 0
+    )[0]
+
+
+def flip_levels(bundle):
+    return [move(bundle, lambda g, l, c: (g, l ^ (2 * flip), c)) for flip in (1, 2, 3)]
 
 
 def per_device(
@@ -373,33 +372,33 @@
     count, width = own_tokens.shape
     quarter = width // 4
     lat_count = lax.axis_size("lat")
-    core = lax.axis_index("lon")
     half = w_qkv.shape[0] // 2
     gain_conv = gain_conv[None]
 
-    aligned = half % 16 == 0
-    outs = [((count + 16, width), BF16), ((count, width), BF16)]
+    direct = half % 16 == 0 and lat_count == 8
+    outs = [
+        ((count + 16, width), BF16),
+        ((count, width), BF16),
+        ((half, 3 * quarter), BF16),
+        ((half, 3 * quarter), BF16),
+        ((half, width), BF16),
+    ]
     scratch = [
         pltpu.VMEM(key_bias.shape[1:], BF16),
         pltpu.VMEM((1, width), F32),
-        pltpu.SemaphoreType.DMA((3 + lat_count,)),
+        pltpu.VMEM((half, 3 * width), BF16),
+        pltpu.SemaphoreType.DMA((5,)),
     ]
-    args = (own_tokens, key_bias[0], gain_attn[None])
-    if aligned:
-        message, raw_tokens, out_pieces = call(
-            pack_body,
-            outs + [((lat_count, half, width // 2), BF16)],
-            [HBM] * 4,
-            (*args, w_out),
-            10 * count * width,
-            scratch,
-        )
-    else:
-        message, raw_tokens = call(
-            pack_norm_body, outs, [HBM] * 3, args, 10 * count * width, scratch
-        )
-        out_pieces = pack_plain(w_out, width // 2)
-    out_mine = lax.all_to_all(out_pieces, "lat", 0, 0)
+    args = (own_tokens, key_bias[0], gain_attn[None]) + ((w_qkv, w_out) if direct else ())
+    message, raw_tokens, qkv_own, qkv_cross, out_own = call(
+        functools.partial(pack_body, weights=direct),
+        outs,
+        [HBM] * len(args),
+        args,
+        10 * count * width,
+        scratch,
+        limit=56,
+    )
 
     near = [message, flip_chips(message, 1, 0), flip_chips(message, 0, 1)]
     near.append(flip_chips(near[1], 0, 1))
@@ -417,34 +416,23 @@
         (lon_half, lat_half, quad_off, lat_taps, w_conv, message),
         0,
     )
-    if aligned:
-        (qkv_pieces,) = call(
-            pack_qkv_body,
-            [((lat_count, half, 3 * quarter), BF16)],
-            [HBM, ANY],
-            (w_qkv, message),
-            0,
-            [pltpu.VMEM((half, 3 * width), BF16), pltpu.SemaphoreType.DMA((1,))],
-        )
+    if direct:
+        qkv_bundle = bundled(qkv_own, qkv_cross)
+        out_bundle = bundled(out_own, out_own)
+        qkv_mine = [qkv_bundle] + flip_levels(qkv_bundle)
+        qkv_other = [swap_cores(block) for block in qkv_mine]
+        out_bundle = gate(out_bundle, *qkv_mine[1:])
+        out_mine = [out_bundle] + flip_levels(out_bundle)
     else:
-        qkv_pieces = pack_plain(w_qkv, 3 * quarter)
-    qkv_pieces = gate(qkv_pieces, near[1], near[2], out_mine, gains)
-    qkv_mine = lax.all_to_all(qkv_pieces, "lat", 0, 0)
-    qkv_other = swap_cores(qkv_mine)
-    out_other = flip_chips(out_mine, 0, 1)
-    out_far = [swap_cores(out_mine), swap_cores(out_other)]
-    if not aligned:
-        qkv_mine, qkv_other = regroup(core, qkv_mine, qkv_other)
-        out_mine, out_far[0] = regroup(core, out_mine, out_far[0])
-        out_other, out_far[1] = regroup(core, out_other, out_far[1])
-    raw_tokens = gate(raw_tokens, qkv_mine)
+        qkv_mine, qkv_other = gather_plain(w_qkv, 3 * quarter)
+    raw_tokens = gate(raw_tokens, *qkv_mine[1:])
     other_tokens = flip_chips(raw_tokens, 1, 0)
 
     pieces = call(
         attend_body,
         [((2, count, quarter), BF16)] * 4,
-        [VMEM] * 10,
-        (*near, *far, qkv_mine, qkv_other),
+        [VMEM] * 17,
+        (*near, *far, *qkv_mine, *qkv_other, gains),
         2 * 1024 * width * 3 * quarter,
         [
             pltpu.VMEM((width, 3 * quarter), BF16),
@@ -456,8 +444,13 @@
     back = [pieces[0]] + [
         flip_chips(piece, flip, sample) for piece, (flip, sample) in zip(pieces[1:], FLIPS)
     ]
+    if direct:
+        out_mine = [gate(block, back[1]) for block in out_mine]
+        out_other = [swap_cores(block) for block in out_mine]
+    else:
+        out_mine, out_other = gather_plain(w_out, width)
     (full_out,) = call(
-        join_quarters, [((width, width), BF16)], [VMEM] * 4, (out_mine, out_other, *out_far), 0
+        join_body, [((width, width), BF16)], [VMEM] * 8, (*out_mine, *out_other), 0
     )
     (other_in,) = call(
         other_body,

time: 79.5 us -> 77.2 us (0.971)
  waiting for transfers between devices: 27.7 us -> 35.5 us
  local copies, waits for them, and re-layouts: 10.1 us -> 3.42 us
  starting transfers between devices: 27.8 us -> 26 us
  Pallas kernels: 10.2 us -> 9.18 us
    ppermute x9 -> x16, waiting for transfers between devices: 17.2 us -> 34.4 us  [move(): return lax.ppermute(values, AXES, device_pairs(target))]
    all_to_all x2 -> x0, starting transfers between devices: 11.2 us -> none  [the longest x1 5.78 us: per_device(): out_mine = lax.all_to_all(out_pieces, 'lat', 0, 0)]
    all_to_all x2 -> x0, waiting for transfers between devices: 9.35 us -> none  [the longest x1 9.35 us: per_device(): qkv_mine = lax.all_to_all(qkv_pieces, 'lat', 0, 0)]
    unnamed x44 -> x18, local copies, waits for them, and re-layouts: 9.32 us -> 2.09 us
    ppermute x9 -> x16, starting transfers between devices: 8.14 us -> 14.8 us  [move(): return lax.ppermute(values, AXES, device_pairs(target))]
    ppermute x8 -> x13, starting transfers between devices: 8.41 us -> 11.1 us  [swap_cores(): return lax.ppermute(values, 'lon', [(0, 1), (1, 0)])]
    pallas_call x8 -> x15, Pallas kernels: 10.2 us -> 9.18 us  [call(): pl.pallas_call(body, out_shape=outs, in_specs=specs, out_specs=tuple((VME...]
  transfers between devices with their start and end apart: 19 -> 29, of which waited for: 8 -> 9; matrix products, arithmetic and copies ran while one was open for 2% -> 0% of each run, Pallas kernels for 10% -> 8%
where the time goes in v6:
time: 77.2 us; the launch traced here: 77 us
  waiting for transfers between devices  35.5 us (46%)
  starting transfers between devices  26 us (34%)
  Pallas kernels  9.18 us (12%)
  local copies, waits for them, and re-layouts  3.42 us (4%)
  between operations  2.19 us (3%)
    ppermute x16, waiting for transfers between devices, move(): return lax.ppermute(values, AXES, device_pairs(target))  34.4 us
    ppermute x16, starting transfers between devices, move(): return lax.ppermute(values, AXES, device_pairs(target))  14.8 us
    ppermute x13, starting transfers between devices, swap_cores(): return lax.ppermute(values, 'lon', [(0, 1), (1, 0)])  11.1 us
    pallas_call x15, Pallas kernels, call(): pl.pallas_call(body, out_shape=outs, in_specs=specs, out_specs=tuple((VME...  9.18 us
    unnamed x18, local copies, waits for them, and re-layouts  2.09 us
  transfers between devices with their start and end apart: 29, of which 9 were waited for; matrix products, arithmetic and copies ran while one was open for 0% of the time, Pallas kernels for 8%

profile of v6, /device:TPU:3, one launch (start us, length us, event | category | flops | bytes accessed | tf_op | source)
XLA Modules:
  0.0 77.0 jit_solution(1187829524116911926)
XLA Ops:
  0.0 1.3 %broadcast_in_dim.9.refs_2_ = f32[1,768]{1,0:T(1,128)} reshape(f32[768]{0:T(1024)} %param.12) | data formatting | bytes 6144 | tf_op jit(solution)/shard_map/broadcast_in_dim | solution.py:392
  1.3 2.1 %shard_map.109 = (bf16[144,768]{1,0:T(8,128)(2,1)}, bf16[128,768]{1,0:T(8,128)(2,1)}, bf16[48,576]{1,0:T(8,128)(2,1)}, bf16[48,576]{1,0:T(8,128)(2,1)}, bf16[48,768]{1,0:T(8,128)(2,1)}) custom-call(bf16[128,768]{1,0:T(8,128)(2,1)} %bitcast.4, bf16[12,128]{1,0:T(8,128)(2,1)} %bitcast.5, f32[1,768]{1,0:T(1,128)} %broadcast_in_dim.9.refs_2_, ...), custom_call_target="tpu_custom_call" | custom-call | flops 983040 | bytes 792576 | tf_op jit(solution)/shard_map/pallas_call | solution.py:23
  3.4 0.1 collective-permute-start
  3.5 1.5 %collective-permute-start.7 = (bf16[48,576]{1,0:T(8,128)(2,1)}, bf16[48,576]{1,0:T(8,128)(2,1)S(1)}, u32[]{:S(2)}, u32[]{:S(2)}) collective-permute-start(bf16[48,576]{1,0:T(8,128)(2,1)} %get-tuple-element.24), channel_id=1, source_target_pairs={{0,2},{1,3},{2,0},{3,1},{4,6},{5,7},{6,4},{7,5},{8,10},{9,11},{10,... | collective-permute-start | bytes 165896 | tf_op jit(solution)/shard_map/ppermute | solution.py:57
  4.9 6.4 %collective-permute-done.7.cross = bf16[48,576]{1,0:T(8,128)(2,1)S(1)} collective-permute-done((bf16[48,576]{1,0:T(8,128)(2,1)}, bf16[48,576]{1,0:T(8,128)(2,1)S(1)}, u32[]{:S(2)}, u32[]{:S(2)}) %collective-permute-start.7) | collective-permute-done | bytes 55328 | tf_op jit(solution)/shard_map/ppermute | solution.py:57
  11.3 0.8 %copy-done.4 = bf16[48,576]{1,0:T(8,128)(2,1)S(1)} copy-done((bf16[48,576]{1,0:T(8,128)(2,1)S(1)}, bf16[48,576]{1,0:T(8,128)(2,1)}, u32[]{:S(2)}) %copy-start.4) | copy-done | bytes 55320
  12.1 1.4 %collective-permute-start.8 = (bf16[2,48,576]{2,1,0:T(8,128)(2,1)S(1)}, bf16[2,48,576]{2,1,0:T(8,128)(2,1)S(1)}, u32[]{:S(2)}, u32[]{:S(2)}) collective-permute-start(bf16[2,48,576]{2,1,0:T(8,128)(2,1)S(1)} %shard_map.111.refs_8_), channel_id=1, source_target_pairs={{0,4},{1,5},{2,6},{3,7},{4,0},{5,1},{6,2},{7,3},{8,12},{9,13},{10,... | collective-permute-start | bytes 331784 | tf_op jit(solution)/shard_map/ppermute | solution.py:57
  13.5 2.3 %collective-permute-start.9 = (bf16[2,48,576]{2,1,0:T(8,128)(2,1)S(1)}, bf16[2,48,576]{2,1,0:T(8,128)(2,1)S(1)}, u32[]{:S(2)}, u32[]{:S(2)}) collective-permute-start(bf16[2,48,576]{2,1,0:T(8,128)(2,1)S(1)} %shard_map.111.refs_8_), channel_id=1, source_target_pairs={{0,8},{1,9},{2,10},{3,11},{4,12},{5,13},{6,14},{7,15},{8,0},{9,1},... | collective-permute-start | bytes 331784 | tf_op jit(solution)/shard_map/ppermute | solution.py:57
  15.8 1.2 %collective-permute-start.1 = (bf16[144,768]{1,0:T(8,128)(2,1)}, bf16[144,768]{1,0:T(8,128)(2,1)S(1)}, u32[]{:S(2)}, u32[]{:S(2)}) collective-permute-start(bf16[144,768]{1,0:T(8,128)(2,1)} %get-tuple-element.21.message.refs_0_), channel_id=1, source_target_pairs={{0,16},{1,17},{2,18},{3,19},{4,20},{5,21},{6,22},{7,23},{8,24},{9,... | collective-permute-start | bytes 663560 | tf_op jit(solution)/shard_map/ppermute | solution.py:57
  17.1 0.2 collective-permute-start.2
  17.3 0.3 collective-permute-start.18
  17.5 3.5 %collective-permute-done.18.cross = bf16[48,768]{1,0:T(8,128)(2,1)S(1)} collective-permute-done((bf16[48,768]{1,0:T(8,128)(2,1)}, bf16[48,768]{1,0:T(8,128)(2,1)S(1)}, u32[]{:S(2)}, u32[]{:S(2)}) %collective-permute-start.18) | collective-permute-done | bytes 73760 | tf_op jit(solution)/shard_map/ppermute | solution.py:57
  21.0 3.5 %collective-permute-start.3 = (bf16[144,768]{1,0:T(8,128)(2,1)}, bf16[144,768]{1,0:T(8,128)(2,1)S(1)}, u32[]{:S(2)}, u32[]{:S(2)}) collective-permute-start(bf16[144,768]{1,0:T(8,128)(2,1)} %get-tuple-element.21.message.refs_0_), channel_id=1, source_target_pairs={{0,1},{1,0},{2,3},{3,2},{4,5},{5,4},{6,7},{7,6},{8,9},{9,8},{10,11... | collective-permute-start | bytes 663560 | tf_op jit(solution)/shard_map/ppermute | solution.py:61
  24.5 0.2 collective-permute-start.11
  24.8 6.6 %collective-permute-done.10.refs_11_.refs_3_ = bf16[2,48,576]{2,1,0:T(8,128)(2,1)S(1)} collective-permute-done((bf16[2,48,576]{2,1,0:T(8,128)(2,1)S(1)}, bf16[2,48,576]{2,1,0:T(8,128)(2,1)S(1)}, u32[]{:S(2)}, u32[]{:S(2)}) %collective-permute-start.10) | collective-permute-done | bytes 110624 | tf_op jit(solution)/shard_map/ppermute | solution.py:57
  31.3 0.8 %collective-permute-start.12 = (bf16[2,48,576]{2,1,0:T(8,128)(2,1)S(1)}, bf16[2,48,576]{2,1,0:T(8,128)(2,1)S(1)}, u32[]{:S(2)}, u32[]{:S(2)}) collective-permute-start(bf16[2,48,576]{2,1,0:T(8,128)(2,1)S(1)} %collective-permute-done.8.refs_9_.refs_1_), channel_id=1, source_target_pairs={{0,1},{1,0},{2,3},{3,2},{4,5},{5,4},{6,7},{7,6},{8,9},{9,8},{10,11... | collective-permute-start | bytes 331784 | tf_op jit(solution)/shard_map/ppermute | solution.py:61
  32.2 0.5 collective-permute-start.5
  32.8 0.4 collective-permute-start.13
  33.2 0.3 collective-permute-start.14
  33.5 0.2 copy.13.w_conv
  33.7 0.1 copy.12.taps
  35.8 0.9 %copy-done = bf16[144,768]{1,0:T(8,128)(2,1)S(1)} copy-done((bf16[144,768]{1,0:T(8,128)(2,1)S(1)}, bf16[144,768]{1,0:T(8,128)(2,1)}, u32[]{:S(2)}) %copy-start) | copy-done | bytes 221208
  36.7 1.0 %shard_map.110 = (bf16[2,3,256,256]{3,2,1,0:T(8,128)(2,1)S(1)}, bf16[256,512]{1,0:T(8,128)(2,1)S(1)}, f32[8,128]{1,0:T(8,128)S(1)}) custom-call(s32[1]{0:T(128)S(6)} %copy.14.lon_half, s32[1]{0:T(128)S(6)} %copy.15.lat_half, s32[1]{0:T(128)S(6)} %copy.16.quad_off, f32[16,2]{1,0:T(8,128)S(1)} %copy.12.taps, bf16[2,768,64]{2,1,0:T(8,128)(2,1)S(1)} %copy.13.w_conv, ...), custom_call_target="tpu_custom_call" | custom-call | bytes 417932 | tf_op jit(solution)/shard_map/pallas_call | solution.py:23
  37.8 0.1 collective-permute-start.21
  37.9 2.1 %collective-permute-start.20 = (bf16[2,48,768]{2,1,0:T(8,128)(2,1)S(1)}, bf16[2,48,768]{2,1,0:T(8,128)(2,1)S(1)}, u32[]{:S(2)}, u32[]{:S(2)}) collective-permute-start(bf16[2,48,768]{2,1,0:T(8,128)(2,1)S(1)} %shard_map.114.refs_0_), channel_id=1, source_target_pairs={{0,8},{1,9},{2,10},{3,11},{4,12},{5,13},{6,14},{7,15},{8,0},{9,1},... | collective-permute-start | bytes 442376 | tf_op jit(solution)/shard_map/ppermute | solution.py:57
  40.0 3.3 %shard_map.112 = (bf16[2,128,192]{2,1,0:T(8,128)(2,1)S(1)}, bf16[2,128,192]{2,1,0:T(8,128)(2,1)S(1)}, bf16[2,128,192]{2,1,0:T(8,128)(2,1)S(1)}, bf16[2,128,192]{2,1,0:T(8,128)(2,1)S(1)}) custom-call(bf16[144,768]{1,0:T(8,128)(2,1)S(1)} %copy-done.1, bf16[144,768]{1,0:T(8,128)(2,1)S(1)} %collective-permute-done.refs_1_, ...), custom_call_target="tpu_custom_call" | custom-call | flops 905969664 | bytes 2658304 | tf_op jit(solution)/shard_map/pallas_call | solution.py:23
  43.3 0.3 collective-permute-start.15
  43.6 1.5 %collective-permute-start.19 = (bf16[2,48,768]{2,1,0:T(8,128)(2,1)S(1)}, bf16[2,48,768]{2,1,0:T(8,128)(2,1)S(1)}, u32[]{:S(2)}, u32[]{:S(2)}) collective-permute-start(bf16[2,48,768]{2,1,0:T(8,128)(2,1)S(1)} %shard_map.114.refs_0_), channel_id=1, source_target_pairs={{0,4},{1,5},{2,6},{3,7},{4,0},{5,1},{6,2},{7,3},{8,12},{9,13},{10,... | collective-permute-start | bytes 442376 | tf_op jit(solution)/shard_map/ppermute | solution.py:57
  45.1 2.5 %collective-permute-done.15.refs_1_.piece1 = bf16[2,128,192]{2,1,0:T(8,128)(2,1)S(1)} collective-permute-done((bf16[2,128,192]{2,1,0:T(8,128)(2,1)S(1)}, bf16[2,128,192]{2,1,0:T(8,128)(2,1)S(1)}, u32[]{:S(2)}, u32[]{:S(2)}) %collective-permute-start.15) | collective-permute-done | bytes 98336 | tf_op jit(solution)/shard_map/ppermute | solution.py:57
  47.6 1.7 %collective-permute-start.25 = (bf16[2,48,768]{2,1,0:T(8,128)(2,1)S(1)}, bf16[2,48,768]{2,1,0:T(8,128)(2,1)S(1)}, u32[]{:S(2)}, u32[]{:S(2)}) collective-permute-start(bf16[2,48,768]{2,1,0:T(8,128)(2,1)S(1)} %shard_map.118.refs_3_), channel_id=1, source_target_pairs={{0,1},{1,0},{2,3},{3,2},{4,5},{5,4},{6,7},{7,6},{8,9},{9,8},{10,11... | collective-permute-start | bytes 442376 | tf_op jit(solution)/shard_map/ppermute | solution.py:61
  49.3 3.9 %collective-permute-done.20.refs_0_ = bf16[2,48,768]{2,1,0:T(8,128)(2,1)S(1)} collective-permute-done((bf16[2,48,768]{2,1,0:T(8,128)(2,1)S(1)}, bf16[2,48,768]{2,1,0:T(8,128)(2,1)S(1)}, u32[]{:S(2)}, u32[]{:S(2)}) %collective-permute-start.20) | collective-permute-done | bytes 147488 | tf_op jit(solution)/shard_map/ppermute | solution.py:57
  53.2 1.1 %collective-permute-start.24 = (bf16[2,48,768]{2,1,0:T(8,128)(2,1)S(1)}, bf16[2,48,768]{2,1,0:T(8,128)(2,1)S(1)}, u32[]{:S(2)}, u32[]{:S(2)}) collective-permute-start(bf16[2,48,768]{2,1,0:T(8,128)(2,1)S(1)} %shard_map.117.refs_2_), channel_id=1, source_target_pairs={{0,1},{1,0},{2,3},{3,2},{4,5},{5,4},{6,7},{7,6},{8,9},{9,8},{10,11... | collective-permute-start | bytes 442376 | tf_op jit(solution)/shard_map/ppermute | solution.py:61
  54.3 0.3 collective-permute-start.26
  54.7 0.4 collective-permute-start.23
  55.1 0.3 collective-permute-start.22
  55.3 1.2 %collective-permute-start.16 = (bf16[2,128,192]{2,1,0:T(8,128)(2,1)S(1)}, bf16[2,128,192]{2,1,0:T(8,128)(2,1)S(1)}, u32[]{:S(2)}, u32[]{:S(2)}) collective-permute-start(bf16[2,128,192]{2,1,0:T(8,128)(2,1)S(1)} %get-tuple-element.27), channel_id=1, source_target_pairs={{0,16},{1,17},{2,18},{3,19},{4,20},{5,21},{6,22},{7,23},{8,24},{9,... | collective-permute-start | bytes 294920 | tf_op jit(solution)/shard_map/ppermute | solution.py:57
  56.6 1.2 %collective-permute-start.17 = (bf16[2,128,192]{2,1,0:T(8,128)(2,1)S(1)}, bf16[2,128,192]{2,1,0:T(8,128)(2,1)S(1)}, u32[]{:S(2)}, u32[]{:S(2)}) collective-permute-start(bf16[2,128,192]{2,1,0:T(8,128)(2,1)S(1)} %get-tuple-element.28), channel_id=1, source_target_pairs={{0,18},{1,19},{2,16},{3,17},{4,22},{5,23},{6,20},{7,21},{8,26},{9,... | collective-permute-start | bytes 294920 | tf_op jit(solution)/shard_map/ppermute | solution.py:57
  57.7 0.1 shard_map.119.weights
  57.9 3.0 %collective-permute-done.26.tokens = bf16[128,768]{1,0:T(8,128)(2,1)S(1)} collective-permute-done((bf16[128,768]{1,0:T(8,128)(2,1)S(1)}, bf16[128,768]{1,0:T(8,128)(2,1)S(1)}, u32[]{:S(2)}, u32[]{:S(2)}) %collective-permute-start.26) | collective-permute-done | bytes 196640 | tf_op jit(solution)/shard_map/ppermute | solution.py:57
  60.9 3.8 %collective-permute-done.17.piece3 = bf16[2,128,192]{2,1,0:T(8,128)(2,1)S(1)} collective-permute-done((bf16[2,128,192]{2,1,0:T(8,128)(2,1)S(1)}, bf16[2,128,192]{2,1,0:T(8,128)(2,1)S(1)}, u32[]{:S(2)}, u32[]{:S(2)}) %collective-permute-start.17) | collective-permute-done | bytes 98336 | tf_op jit(solution)/shard_map/ppermute | solution.py:57
  64.7 0.6 shard_map.121.other_in
  65.2 1.3 %collective-permute-start.27 = (bf16[128,768]{1,0:T(8,128)(2,1)S(1)}, bf16[128,768]{1,0:T(8,128)(2,1)S(1)}, u32[]{:S(2)}, u32[]{:S(2)}) collective-permute-start(bf16[128,768]{1,0:T(8,128)(2,1)S(1)} %shard_map.121.other_in), channel_id=1, source_target_pairs={{0,4},{1,5},{4,8},{5,9},{6,2},{7,3},{8,12},{9,13},{10,6},{11,7},{1... | collective-permute-start | bytes 589832 | tf_op jit(solution)/shard_map/ppermute | solution.py:57
  66.5 1.4 %shard_map.122 = (bf16[128,768]{1,0:T(8,128)(2,1)S(1)}, f32[256,768]{1,0:T(8,128)S(1)}) custom-call(f32[8,128]{1,0:T(8,128)S(1)} %get-tuple-element.22.refs_16_.gains, f32[1,768]{1,0:T(1,128)S(1)} %broadcast_in_dim.10.gain, bf16[2,128,192]{2,1,0:T(8,128)(2,1)S(1)} %get-tuple-element.25.piece0, ...), custom_call_target="tpu_custom_call" | custom-call | flops 452984832 | bytes 3021824 | tf_op jit(solution)/shard_map/pallas_call | solution.py:23
  67.9 4.8 %collective-permute-done.27.halo = bf16[128,768]{1,0:T(8,128)(2,1)S(1)} collective-permute-done((bf16[128,768]{1,0:T(8,128)(2,1)S(1)}, bf16[128,768]{1,0:T(8,128)(2,1)S(1)}, u32[]{:S(2)}, u32[]{:S(2)}) %collective-permute-start.27) | collective-permute-done | bytes 196640 | tf_op jit(solution)/shard_map/ppermute | solution.py:57
  72.7 0.7 shard_map.123
  73.4 1.8 %collective-permute-start.28 = (bf16[128,768]{1,0:T(8,128)(2,1)S(1)}, bf16[128,768]{1,0:T(8,128)(2,1)S(1)}, u32[]{:S(2)}, u32[]{:S(2)}) collective-permute-start(bf16[128,768]{1,0:T(8,128)(2,1)S(1)} %get-tuple-element.36), channel_id=1, source_target_pairs={{0,1},{1,0},{2,3},{3,2},{4,5},{5,4},{6,7},{7,6},{8,9},{9,8},{10,11... | collective-permute-start | bytes 589832 | tf_op jit(solution)/shard_map/ppermute | solution.py:61
  75.2 1.1 %collective-permute-done.28 = bf16[128,768]{1,0:T(8,128)(2,1)S(1)} collective-permute-done((bf16[128,768]{1,0:T(8,128)(2,1)S(1)}, bf16[128,768]{1,0:T(8,128)(2,1)S(1)}, u32[]{:S(2)}, u32[]{:S(2)}) %collective-permute-start.28) | collective-permute-done | bytes 196640 | tf_op jit(solution)/shard_map/ppermute | solution.py:61
  76.2 0.7 fusion
  (46 shorter events, 0.3 us)
Async XLA Ops:
  0.0 33.5 %copy-start.5 = (bf16[2,768,64]{1,2,0:T(8,128)(2,1)S(1)}, bf16[2,768,64]{1,2,0:T(8,128)(2,1)}, u32[]{:S(2)}) copy-start(bf16[2,768,64]{1,2,0:T(8,128)(2,1)} %param.17) | copy-start | bytes 589828
  0.0 33.7 %copy-start.7 = (f32[16,2]{0,1:T(2,128)S(1)}, f32[16,2]{0,1:T(2,128)}, u32[]{:S(2)}) copy-start(f32[16,2]{0,1:T(2,128)} %param.18) | copy-start | bytes 388
  3.4 34.3 %copy-start.3 = (bf16[48,768]{1,0:T(8,128)(2,1)S(1)}, bf16[48,768]{1,0:T(8,128)(2,1)}, u32[]{:S(2)}) copy-start(bf16[48,768]{1,0:T(8,128)(2,1)} %get-tuple-element.29.own) | copy-start | bytes 221188
  3.4 13.7 %collective-permute-start = (bf16[144,768]{1,0:T(8,128)(2,1)}, bf16[144,768]{1,0:T(8,128)(2,1)S(1)}, u32[]{:S(2)}, u32[]{:S(2)}) collective-permute-start(bf16[144,768]{1,0:T(8,128)(2,1)} %get-tuple-element.21.message.refs_0_), channel_id=1, source_target_pairs={{0,2},{1,3},{2,0},{3,1},{4,6},{5,7},{6,4},{7,5},{8,10},{9,11},{10,... | collective-permute-start | bytes 663560 | tf_op jit(solution)/shard_map/ppermute | solution.py:57
  3.5 7.8 %collective-permute-start.7 = (bf16[48,576]{1,0:T(8,128)(2,1)}, bf16[48,576]{1,0:T(8,128)(2,1)S(1)}, u32[]{:S(2)}, u32[]{:S(2)}) collective-permute-start(bf16[48,576]{1,0:T(8,128)(2,1)} %get-tuple-element.24), channel_id=1, source_target_pairs={{0,2},{1,3},{2,0},{3,1},{4,6},{5,7},{6,4},{7,5},{8,10},{9,11},{10,... | collective-permute-start | bytes 165896 | tf_op jit(solution)/shard_map/ppermute | solution.py:57
  11.3 0.8 %copy-start.4 = (bf16[48,576]{1,0:T(8,128)(2,1)S(1)}, bf16[48,576]{1,0:T(8,128)(2,1)}, u32[]{:S(2)}) copy-start(bf16[48,576]{1,0:T(8,128)(2,1)} %get-tuple-element.23.own) | copy-start | bytes 165892
  12.1 27.8 %copy-start.1 = (bf16[144,768]{1,0:T(8,128)(2,1)S(1)}, bf16[144,768]{1,0:T(8,128)(2,1)}, u32[]{:S(2)}) copy-start(bf16[144,768]{1,0:T(8,128)(2,1)} %get-tuple-element.21.message.refs_0_) | copy-start | bytes 663556
  12.1 12.4 %collective-permute-start.8 = (bf16[2,48,576]{2,1,0:T(8,128)(2,1)S(1)}, bf16[2,48,576]{2,1,0:T(8,128)(2,1)S(1)}, u32[]{:S(2)}, u32[]{:S(2)}) collective-permute-start(bf16[2,48,576]{2,1,0:T(8,128)(2,1)S(1)} %shard_map.111.refs_8_), channel_id=1, source_target_pairs={{0,4},{1,5},{2,6},{3,7},{4,0},{5,1},{6,2},{7,3},{8,12},{9,13},{10,... | collective-permute-start | bytes 331784 | tf_op jit(solution)/shard_map/ppermute | solution.py:57
  13.5 11.0 %collective-permute-start.9 = (bf16[2,48,576]{2,1,0:T(8,128)(2,1)S(1)}, bf16[2,48,576]{2,1,0:T(8,128)(2,1)S(1)}, u32[]{:S(2)}, u32[]{:S(2)}) collective-permute-start(bf16[2,48,576]{2,1,0:T(8,128)(2,1)S(1)} %shard_map.111.refs_8_), channel_id=1, source_target_pairs={{0,8},{1,9},{2,10},{3,11},{4,12},{5,13},{6,14},{7,15},{8,0},{9,1},... | collective-permute-start | bytes 331784 | tf_op jit(solution)/shard_map/ppermute | solution.py:57
  15.8 16.4 %collective-permute-start.1 = (bf16[144,768]{1,0:T(8,128)(2,1)}, bf16[144,768]{1,0:T(8,128)(2,1)S(1)}, u32[]{:S(2)}, u32[]{:S(2)}) collective-permute-start(bf16[144,768]{1,0:T(8,128)(2,1)} %get-tuple-element.21.message.refs_0_), channel_id=1, source_target_pairs={{0,16},{1,17},{2,18},{3,19},{4,20},{5,21},{6,22},{7,23},{8,24},{9,... | collective-permute-start | bytes 663560 | tf_op jit(solution)/shard_map/ppermute | solution.py:57
  17.1 15.6 %collective-permute-start.2 = (bf16[144,768]{1,0:T(8,128)(2,1)S(1)}, bf16[144,768]{1,0:T(8,128)(2,1)S(1)}, u32[]{:S(2)}, u32[]{:S(2)}) collective-permute-start(bf16[144,768]{1,0:T(8,128)(2,1)S(1)} %collective-permute-done.refs_1_), channel_id=1, source_target_pairs={{0,16},{1,17},{2,18},{3,19},{4,20},{5,21},{6,22},{7,23},{8,24},{9,... | collective-permute-start | bytes 663560 | tf_op jit(solution)/shard_map/ppermute | solution.py:57
  17.3 3.7 %collective-permute-start.18 = (bf16[48,768]{1,0:T(8,128)(2,1)}, bf16[48,768]{1,0:T(8,128)(2,1)S(1)}, u32[]{:S(2)}, u32[]{:S(2)}) collective-permute-start(bf16[48,768]{1,0:T(8,128)(2,1)} %get-tuple-element.29.own), channel_id=1, source_target_pairs={{0,2},{1,3},{2,0},{3,1},{4,6},{5,7},{6,4},{7,5},{8,10},{9,11},{10,... | collective-permute-start | bytes 221192 | tf_op jit(solution)/shard_map/ppermute | solution.py:57
  21.0 11.8 %collective-permute-start.3 = (bf16[144,768]{1,0:T(8,128)(2,1)}, bf16[144,768]{1,0:T(8,128)(2,1)S(1)}, u32[]{:S(2)}, u32[]{:S(2)}) collective-permute-start(bf16[144,768]{1,0:T(8,128)(2,1)} %get-tuple-element.21.message.refs_0_), channel_id=1, source_target_pairs={{0,1},{1,0},{2,3},{3,2},{4,5},{5,4},{6,7},{7,6},{8,9},{9,8},{10,11... | collective-permute-start | bytes 663560 | tf_op jit(solution)/shard_map/ppermute | solution.py:61
  24.5 6.8 %collective-permute-start.10 = (bf16[2,48,576]{2,1,0:T(8,128)(2,1)S(1)}, bf16[2,48,576]{2,1,0:T(8,128)(2,1)S(1)}, u32[]{:S(2)}, u32[]{:S(2)}) collective-permute-start(bf16[2,48,576]{2,1,0:T(8,128)(2,1)S(1)} %shard_map.111.refs_8_), channel_id=1, source_target_pairs={{0,12},{1,13},{2,14},{3,15},{4,8},{5,9},{6,10},{7,11},{8,4},{9,5},... | collective-permute-start | bytes 331784 | tf_op jit(solution)/shard_map/ppermute | solution.py:57
  24.5 7.6 %collective-permute-start.11 = (bf16[2,48,576]{2,1,0:T(8,128)(2,1)S(1)}, bf16[2,48,576]{2,1,0:T(8,128)(2,1)S(1)}, u32[]{:S(2)}, u32[]{:S(2)}) collective-permute-start(bf16[2,48,576]{2,1,0:T(8,128)(2,1)S(1)} %shard_map.111.refs_8_), channel_id=1, source_target_pairs={{0,1},{1,0},{2,3},{3,2},{4,5},{5,4},{6,7},{7,6},{8,9},{9,8},{10,11... | collective-permute-start | bytes 331784 | tf_op jit(solution)/shard_map/ppermute | solution.py:61
  31.3 1.9 %collective-permute-start.12 = (bf16[2,48,576]{2,1,0:T(8,128)(2,1)S(1)}, bf16[2,48,576]{2,1,0:T(8,128)(2,1)S(1)}, u32[]{:S(2)}, u32[]{:S(2)}) collective-permute-start(bf16[2,48,576]{2,1,0:T(8,128)(2,1)S(1)} %collective-permute-done.8.refs_9_.refs_1_), channel_id=1, source_target_pairs={{0,1},{1,0},{2,3},{3,2},{4,5},{5,4},{6,7},{7,6},{8,9},{9,8},{10,11... | collective-permute-start | bytes 331784 | tf_op jit(solution)/shard_map/ppermute | solution.py:61
  32.2 7.8 %collective-permute-start.4 = (bf16[144,768]{1,0:T(8,128)(2,1)S(1)}, bf16[144,768]{1,0:T(8,128)(2,1)S(1)}, u32[]{:S(2)}, u32[]{:S(2)}) collective-permute-start(bf16[144,768]{1,0:T(8,128)(2,1)S(1)} %collective-permute-done.refs_1_), channel_id=1, source_target_pairs={{0,1},{1,0},{2,3},{3,2},{4,5},{5,4},{6,7},{7,6},{8,9},{9,8},{10,11... | collective-permute-start | bytes 663560 | tf_op jit(solution)/shard_map/ppermute | solution.py:61
  32.2 7.8 %collective-permute-start.5 = (bf16[144,768]{1,0:T(8,128)(2,1)S(1)}, bf16[144,768]{1,0:T(8,128)(2,1)S(1)}, u32[]{:S(2)}, u32[]{:S(2)}) collective-permute-start(bf16[144,768]{1,0:T(8,128)(2,1)S(1)} %collective-permute-done.1.refs_2_), channel_id=1, source_target_pairs={{0,1},{1,0},{2,3},{3,2},{4,5},{5,4},{6,7},{7,6},{8,9},{9,8},{10,11... | collective-permute-start | bytes 663560 | tf_op jit(solution)/shard_map/ppermute | solution.py:61
  32.7 7.3 %collective-permute-start.6 = (bf16[144,768]{1,0:T(8,128)(2,1)S(1)}, bf16[144,768]{1,0:T(8,128)(2,1)S(1)}, u32[]{:S(2)}, u32[]{:S(2)}) collective-permute-start(bf16[144,768]{1,0:T(8,128)(2,1)S(1)} %collective-permute-done.2.refs_3_), channel_id=1, source_target_pairs={{0,1},{1,0},{2,3},{3,2},{4,5},{5,4},{6,7},{7,6},{8,9},{9,8},{10,11... | collective-permute-start | bytes 663560 | tf_op jit(solution)/shard_map/ppermute | solution.py:61
  32.8 5.0 %collective-permute-start.13 = (bf16[2,48,576]{2,1,0:T(8,128)(2,1)S(1)}, bf16[2,48,576]{2,1,0:T(8,128)(2,1)S(1)}, u32[]{:S(2)}, u32[]{:S(2)}) collective-permute-start(bf16[2,48,576]{2,1,0:T(8,128)(2,1)S(1)} %collective-permute-done.9.refs_10_.refs_2_), channel_id=1, source_target_pairs={{0,1},{1,0},{2,3},{3,2},{4,5},{5,4},{6,7},{7,6},{8,9},{9,8},{10,11... | collective-permute-start | bytes 331784 | tf_op jit(solution)/shard_map/ppermute | solution.py:61
  33.2 4.7 %collective-permute-start.14 = (bf16[2,48,576]{2,1,0:T(8,128)(2,1)S(1)}, bf16[2,48,576]{2,1,0:T(8,128)(2,1)S(1)}, u32[]{:S(2)}, u32[]{:S(2)}) collective-permute-start(bf16[2,48,576]{2,1,0:T(8,128)(2,1)S(1)} %collective-permute-done.10.refs_11_.refs_3_), channel_id=1, source_target_pairs={{0,1},{1,0},{2,3},{3,2},{4,5},{5,4},{6,7},{7,6},{8,9},{9,8},{10,11... | collective-permute-start | bytes 331784 | tf_op jit(solution)/shard_map/ppermute | solution.py:61
  35.8 0.9 %copy-start = (bf16[144,768]{1,0:T(8,128)(2,1)S(1)}, bf16[144,768]{1,0:T(8,128)(2,1)}, u32[]{:S(2)}) copy-start(bf16[144,768]{1,0:T(8,128)(2,1)} %get-tuple-element.21.message.refs_0_) | copy-start | bytes 663556
  37.8 7.3 %collective-permute-start.21 = (bf16[2,48,768]{2,1,0:T(8,128)(2,1)S(1)}, bf16[2,48,768]{2,1,0:T(8,128)(2,1)S(1)}, u32[]{:S(2)}, u32[]{:S(2)}) collective-permute-start(bf16[2,48,768]{2,1,0:T(8,128)(2,1)S(1)} %shard_map.114.refs_0_), channel_id=1, source_target_pairs={{0,12},{1,13},{2,14},{3,15},{4,8},{5,9},{6,10},{7,11},{8,4},{9,5},... | collective-permute-start | bytes 442376 | tf_op jit(solution)/shard_map/ppermute | solution.py:57
  37.9 15.3 %collective-permute-start.20 = (bf16[2,48,768]{2,1,0:T(8,128)(2,1)S(1)}, bf16[2,48,768]{2,1,0:T(8,128)(2,1)S(1)}, u32[]{:S(2)}, u32[]{:S(2)}) collective-permute-start(bf16[2,48,768]{2,1,0:T(8,128)(2,1)S(1)} %shard_map.114.refs_0_), channel_id=1, source_target_pairs={{0,8},{1,9},{2,10},{3,11},{4,12},{5,13},{6,14},{7,15},{8,0},{9,1},... | collective-permute-start | bytes 442376 | tf_op jit(solution)/shard_map/ppermute | solution.py:57
  40.0 14.3 %copy-start.2 = (bf16[128,768]{1,0:T(8,128)(2,1)S(1)}, bf16[128,768]{1,0:T(8,128)(2,1)}, u32[]{:S(2)}) copy-start(bf16[128,768]{1,0:T(8,128)(2,1)} %get-tuple-element.30.refs_0_) | copy-start | bytes 589828
  43.3 14.4 %copy-start.6 = (f32[768]{0:T(1024)S(1)}, f32[768]{0:T(1024)}, u32[]{:S(2)}) copy-start(f32[768]{0:T(1024)} %param.16) | copy-start | bytes 9220
  43.3 4.3 %collective-permute-start.15 = (bf16[2,128,192]{2,1,0:T(8,128)(2,1)S(1)}, bf16[2,128,192]{2,1,0:T(8,128)(2,1)S(1)}, u32[]{:S(2)}, u32[]{:S(2)}) collective-permute-start(bf16[2,128,192]{2,1,0:T(8,128)(2,1)S(1)} %get-tuple-element.26), channel_id=1, source_target_pairs={{0,2},{1,3},{2,0},{3,1},{4,6},{5,7},{6,4},{7,5},{8,10},{9,11},{10,... | collective-permute-start | bytes 294920 | tf_op jit(solution)/shard_map/ppermute | solution.py:57
  43.6 11.0 %collective-permute-start.19 = (bf16[2,48,768]{2,1,0:T(8,128)(2,1)S(1)}, bf16[2,48,768]{2,1,0:T(8,128)(2,1)S(1)}, u32[]{:S(2)}, u32[]{:S(2)}) collective-permute-start(bf16[2,48,768]{2,1,0:T(8,128)(2,1)S(1)} %shard_map.114.refs_0_), channel_id=1, source_target_pairs={{0,4},{1,5},{2,6},{3,7},{4,0},{5,1},{6,2},{7,3},{8,12},{9,13},{10,... | collective-permute-start | bytes 442376 | tf_op jit(solution)/shard_map/ppermute | solution.py:57
  47.6 7.7 %collective-permute-start.25 = (bf16[2,48,768]{2,1,0:T(8,128)(2,1)S(1)}, bf16[2,48,768]{2,1,0:T(8,128)(2,1)S(1)}, u32[]{:S(2)}, u32[]{:S(2)}) collective-permute-start(bf16[2,48,768]{2,1,0:T(8,128)(2,1)S(1)} %shard_map.118.refs_3_), channel_id=1, source_target_pairs={{0,1},{1,0},{2,3},{3,2},{4,5},{5,4},{6,7},{7,6},{8,9},{9,8},{10,11... | collective-permute-start | bytes 442376 | tf_op jit(solution)/shard_map/ppermute | solution.py:61
  53.2 3.3 %collective-permute-start.24 = (bf16[2,48,768]{2,1,0:T(8,128)(2,1)S(1)}, bf16[2,48,768]{2,1,0:T(8,128)(2,1)S(1)}, u32[]{:S(2)}, u32[]{:S(2)}) collective-permute-start(bf16[2,48,768]{2,1,0:T(8,128)(2,1)S(1)} %shard_map.117.refs_2_), channel_id=1, source_target_pairs={{0,1},{1,0},{2,3},{3,2},{4,5},{5,4},{6,7},{7,6},{8,9},{9,8},{10,11... | collective-permute-start | bytes 442376 | tf_op jit(solution)/shard_map/ppermute | solution.py:61
  54.3 6.6 %collective-permute-start.26 = (bf16[128,768]{1,0:T(8,128)(2,1)S(1)}, bf16[128,768]{1,0:T(8,128)(2,1)S(1)}, u32[]{:S(2)}, u32[]{:S(2)}) collective-permute-start(bf16[128,768]{1,0:T(8,128)(2,1)S(1)} %shard_map.120.tokens), channel_id=1, source_target_pairs={{0,2},{1,3},{2,0},{3,1},{4,6},{5,7},{6,4},{7,5},{8,10},{9,11},{10,... | collective-permute-start | bytes 589832 | tf_op jit(solution)/shard_map/ppermute | solution.py:57
  54.7 3.1 %collective-permute-start.23 = (bf16[2,48,768]{2,1,0:T(8,128)(2,1)S(1)}, bf16[2,48,768]{2,1,0:T(8,128)(2,1)S(1)}, u32[]{:S(2)}, u32[]{:S(2)}) collective-permute-start(bf16[2,48,768]{2,1,0:T(8,128)(2,1)S(1)} %shard_map.116.refs_1_), channel_id=1, source_target_pairs={{0,1},{1,0},{2,3},{3,2},{4,5},{5,4},{6,7},{7,6},{8,9},{9,8},{10,11... | collective-permute-start | bytes 442376 | tf_op jit(solution)/shard_map/ppermute | solution.py:61
  55.1 2.7 %collective-permute-start.22 = (bf16[2,48,768]{2,1,0:T(8,128)(2,1)S(1)}, bf16[2,48,768]{2,1,0:T(8,128)(2,1)S(1)}, u32[]{:S(2)}, u32[]{:S(2)}) collective-permute-start(bf16[2,48,768]{2,1,0:T(8,128)(2,1)S(1)} %shard_map.115.refs_0_), channel_id=1, source_target_pairs={{0,1},{1,0},{2,3},{3,2},{4,5},{5,4},{6,7},{7,6},{8,9},{9,8},{10,11... | collective-permute-start | bytes 442376 | tf_op jit(solution)/shard_map/ppermute | solution.py:61
  55.3 5.6 %collective-permute-start.16 = (bf16[2,128,192]{2,1,0:T(8,128)(2,1)S(1)}, bf16[2,128,192]{2,1,0:T(8,128)(2,1)S(1)}, u32[]{:S(2)}, u32[]{:S(2)}) collective-permute-start(bf16[2,128,192]{2,1,0:T(8,128)(2,1)S(1)} %get-tuple-element.27), channel_id=1, source_target_pairs={{0,16},{1,17},{2,18},{3,19},{4,20},{5,21},{6,22},{7,23},{8,24},{9,... | collective-permute-start | bytes 294920 | tf_op jit(solution)/shard_map/ppermute | solution.py:57
  56.6 8.1 %collective-permute-start.17 = (bf16[2,128,192]{2,1,0:T(8,128)(2,1)S(1)}, bf16[2,128,192]{2,1,0:T(8,128)(2,1)S(1)}, u32[]{:S(2)}, u32[]{:S(2)}) collective-permute-start(bf16[2,128,192]{2,1,0:T(8,128)(2,1)S(1)} %get-tuple-element.28), channel_id=1, source_target_pairs={{0,18},{1,19},{2,16},{3,17},{4,22},{5,23},{6,20},{7,21},{8,26},{9,... | collective-permute-start | bytes 294920 | tf_op jit(solution)/shard_map/ppermute | solution.py:57
  65.2 7.5 %collective-permute-start.27 = (bf16[128,768]{1,0:T(8,128)(2,1)S(1)}, bf16[128,768]{1,0:T(8,128)(2,1)S(1)}, u32[]{:S(2)}, u32[]{:S(2)}) collective-permute-start(bf16[128,768]{1,0:T(8,128)(2,1)S(1)} %shard_map.121.other_in), channel_id=1, source_target_pairs={{0,4},{1,5},{4,8},{5,9},{6,2},{7,3},{8,12},{9,13},{10,6},{11,7},{1... | collective-permute-start | bytes 589832 | tf_op jit(solution)/shard_map/ppermute | solution.py:57
  73.4 2.8 %collective-permute-start.28 = (bf16[128,768]{1,0:T(8,128)(2,1)S(1)}, bf16[128,768]{1,0:T(8,128)(2,1)S(1)}, u32[]{:S(2)}, u32[]{:S(2)}) collective-permute-start(bf16[128,768]{1,0:T(8,128)(2,1)S(1)} %get-tuple-element.36), channel_id=1, source_target_pairs={{0,1},{1,0},{2,3},{3,2},{4,5},{5,4},{6,7},{7,6},{8,9},{9,8},{10,11... | collective-permute-start | bytes 589832 | tf_op jit(solution)/shard_map/ppermute | solution.py:61

commit v7 on v6

--- a/solution.py
+++ b/solution.py
@@ -72,19 +72,27 @@
     return (centered * lax.rsqrt(variance + 1e-05) * gain).astype(BF16)
 
 
+def pick_columns(rows, side, quarter):
+    group = lax.axis_index("groups")
+    parts = []
+    for kind in range(3):
+        low = 4 * kind * quarter
+        block = [rows[:, low + at * quarter : low + (at + 1) * quarter] for at in range(4)]
+        sides = [jnp.where(group == 0, block[2 * at], block[2 * at + 1]) for at in range(2)]
+        parts.append(jnp.where(side == 0, sides[0], sides[1]))
+    return jnp.concatenate(parts, axis=1)
+
+
 def pack_body(*refs, weights):
-    tokens, bias, gain, message, raw = *refs[:3], *refs[-9:-7]
+    tokens, bias, gain = refs[:3]
+    message, raw, out_own, bias_here, gain_here, rows, sems = refs[-7:]
     count = tokens.shape[0]
     heads, bias_width = bias.shape
-    group, core = lax.axis_index("groups"), lax.axis_index("lon")
-    side = lax.rem(lax.axis_index("lat"), 2)
+    core = lax.axis_index("lon")
+    half = rows.shape[0]
+    copies = [(gain, gain_here), (bias, bias_here), (tokens, raw)]
     if weights:
         w_qkv, w_out = refs[3:5]
-    qkv_own, qkv_cross, out_own, bias_here, gain_here, rows, sems = refs[-7:]
-    half = rows.shape[0]
-    quarter = qkv_own.shape[1] // 3
-    copies = [(gain, gain_here), (bias, bias_here), (tokens, raw)]
-    if weights:
         picked = pl.ds(pl.multiple_of(core * half, half), half)
         copies += [(w_qkv.at[picked, :], rows), (w_out.at[picked, :], out_own)]
     fetches = [
@@ -93,61 +101,96 @@
     ]
     for fetch in fetches:
         fetch.start()
-    message[count:, :] = jnp.zeros((16, tokens.shape[1]), BF16)
+    message[count:, :] = jnp.zeros((message.shape[0] - count, tokens.shape[1]), BF16)
     for fetch in fetches[:3]:
         fetch.wait()
     message[count : count + heads, :bias_width] = bias_here[...]
-    message[:count, :] = norm_rows(raw[...].astype(F32), gain_here[...])
+    message[:count, :] = norm_rows(raw[...].astype(F32), gain_here[...][None])
     for fetch in fetches[3:]:
         fetch.wait()
-    if not weights:
-        return
-    for kind in range(3):
-        low = 4 * kind * quarter
-        block = [rows[:, low + at * quarter : low + (at + 1) * quarter] for at in range(4)]
-        sides = [jnp.where(group == 0, block[2 * at], block[2 * at + 1]) for at in range(2)]
-        columns = slice(kind * quarter, (kind + 1) * quarter)
-        qkv_own[:, columns] = jnp.where(side == 0, sides[0], sides[1])
-        qkv_cross[:, columns] = jnp.where(side == 0, sides[1], sides[0])
-
-
-def bundle_body(own, cross, bundle):
+    if weights:
+        side = lax.rem(lax.axis_index("lat"), 2)
+        cross = pick_columns(rows, 1 - side, tokens.shape[1] // 4)
+        message[count + 16 :, : cross.shape[1]] = cross
+
+
+def columns_body(w_qkv, gains, own):
+    del gains
+    half = own.shape[0]
+    start = pl.multiple_of(lax.axis_index("lon") * half, half)
+    rows = w_qkv[pl.ds(start, half), :]
+    own[...] = pick_columns(rows, lax.rem(lax.axis_index("lat"), 2), own.shape[1] // 3)
+
+
+def arrived_body(
+    own, by_x, by_y, out_own, out1, out2, out3, gains, bundle, x_block, outs
+):
+    del by_y, gains
     side = lax.rem(lax.axis_index("lat"), 2)
+    rows, width = x_block.shape[0], own.shape[1]
     bundle[side] = own[...]
-    bundle[1 - side] = cross[...]
+    bundle[1 - side] = by_x[rows:, :width]
+    x_block[...] = by_x[:rows, :]
+    for at, block in enumerate((out_own, out1, out2, out3)):
+        outs[at] = block[...]
+
+
+def complete_body(
+    bundle, level1, level2, level3, message, x_block, by_y, by_xy, outs, crossed, weights, near, both
+):
+    rows = x_block.shape[0]
+    for at, block in enumerate((bundle, level1, level2, level3)):
+        weights[at] = block[...]
+    for at, block in enumerate((message, x_block, by_y, by_xy)):
+        near[at] = block[:rows, :]
+    both[0] = outs[...]
+    both[1] = crossed[...]
+
+
+def pair_away(flip):
+    pair = lax.rem(lax.axis_index("lat") // 2, 4)
+    high, low = pair // 2, pair % 2
+    high = 1 - high if flip // 2 else high
+    low = 1 - low if flip % 2 else low
+    return 2 * high + low
 
 
 def join_bundles(mine, other, joined):
     core = lax.axis_index("lon")
-    pair = lax.rem(lax.axis_index("lat") // 2, 4)
-    for flip, blocks in enumerate(zip(mine, other)):
-        away = (pair // 2 + flip // 2 - 2 * (pair // 2) * (flip // 2)) * 2
-        away = away + (pair % 2 + flip % 2 - 2 * (pair % 2) * (flip % 2))
-        for block, at in zip(blocks, (core, 1 - core)):
-            half = block.shape[1]
+    half = mine.shape[2]
+    for flip in range(4):
+        for block, at in ((mine, core), (other, 1 - core)):
             for row in range(2):
-                first = pl.multiple_of(((away * 2 + row) * 2 + at) * half, half)
-                joined[pl.ds(first, half), :] = block[row]
-
-
-def join_body(*refs):
-    join_bundles(refs[:4], refs[4:8], refs[8])
+                first = pl.multiple_of(((pair_away(flip) * 2 + row) * 2 + at) * half, half)
+                joined[pl.ds(first, half), :] = block[flip, row]
+
+
+def join_columns(mine, other, joined):
+    core, side = lax.axis_index("lon"), lax.rem(lax.axis_index("lat"), 2)
+    half = mine.shape[2]
+    for flip in range(4):
+        for block, at in ((mine, core), (other, 1 - core)):
+            for cross, row in enumerate((side, 1 - side)):
+                first = pl.multiple_of(((pair_away(flip) * 2 + row) * 2 + at) * half, half)
+                joined[pl.ds(first, half), :] = block[cross, flip]
 
 
 def attend_body(*refs):
-    near, far, mine, other = refs[:4], refs[4:8], refs[8:12], refs[12:16]
-    pieces, (weights, bias_rows, near_rows, far_rows) = refs[17:21], refs[21:]
+    (near, far, mine, other), pieces = refs[:4], refs[4:8]
+    weights, bias_rows, near_rows, far_rows = refs[8:]
     group, side = lax.axis_index("groups"), lax.rem(lax.axis_index("lat"), 2)
     _, count, quarter = pieces[0].shape
     heads = 3
     head_dim = quarter // heads
     join_bundles(mine, other, weights)
     for slot in range(4):
-        near_rows[slot * count : (slot + 1) * count, :] = near[slot][:count, :]
-        far_rows[slot * count : (slot + 1) * count, :] = far[slot][:count, :]
+        near_rows[slot * count : (slot + 1) * count, :] = near[slot, :count, :]
+        far_rows[slot * count : (slot + 1) * count, :] = far[slot, :count, :]
     for flip in range(2):
-        for at, block in enumerate((near[flip], far[flip])):
-            bias_rows[flip, :, at * count : (at + 1) * count] = block[count:, :count].astype(F32)
+        for at, block in enumerate((near, far)):
+            bias_rows[flip, :, at * count : (at + 1) * count] = block[flip, count:, :count].astype(
+                F32
+            )
     first_head = (2 * side + group) * heads
     here = jnp.dot(near_rows[...], weights[...], preferred_element_type=F32).astype(BF16)
     there = jnp.dot(far_rows[...], weights[:, quarter:], preferred_element_type=F32).astype(BF16)
@@ -331,24 +374,12 @@
     both = jnp.where(core == 0, jnp.stack([mine, other], 1), jnp.stack([other, mine], 1))
     whole = both.reshape(4, 2, 2, -1, columns)
     pair = lax.rem(lax.axis_index("lat") // 2, 4)
+    whole = jnp.stack(
+        [lax.dynamic_index_in_dim(whole, pair ^ flip, 0, keepdims=False) for flip in range(4)]
+    )
     return [
-        [
-            lax.dynamic_index_in_dim(
-                lax.dynamic_index_in_dim(whole, pair ^ flip, 0, keepdims=False),
-                at,
-                1,
-                keepdims=False,
-            )
-            for flip in range(4)
-        ]
-        for at in (core, 1 - core)
+        lax.dynamic_index_in_dim(whole, at, 2, keepdims=False) for at in (core, 1 - core)
     ]
-
-
-def bundled(own, cross):
-    return call(
-        bundle_body, [((2, *own.shape), BF16)], [VMEM] * 2, (own, flip_chips(cross, 1, 0)), 0
-    )[0]
 
 
 def flip_levels(bundle):
@@ -376,33 +407,25 @@
     gain_conv = gain_conv[None]
 
     direct = half % 16 == 0 and lat_count == 8
-    outs = [
-        ((count + 16, width), BF16),
-        ((count, width), BF16),
-        ((half, 3 * quarter), BF16),
-        ((half, 3 * quarter), BF16),
-        ((half, width), BF16),
-    ]
-    scratch = [
-        pltpu.VMEM(key_bias.shape[1:], BF16),
-        pltpu.VMEM((1, width), F32),
-        pltpu.VMEM((half, 3 * width), BF16),
-        pltpu.SemaphoreType.DMA((5,)),
-    ]
-    args = (own_tokens, key_bias[0], gain_attn[None]) + ((w_qkv, w_out) if direct else ())
-    message, raw_tokens, qkv_own, qkv_cross, out_own = call(
+    rows = count + 16
+    message, raw_tokens, out_own = call(
         functools.partial(pack_body, weights=direct),
-        outs,
-        [HBM] * len(args),
-        args,
+        [
+            ((rows + (half if direct else 0), width), BF16),
+            ((count, width), BF16),
+            ((half, width), BF16),
+        ],
+        [HBM] * (5 if direct else 3),
+        (own_tokens, key_bias[0], gain_attn) + ((w_qkv, w_out) if direct else ()),
         10 * count * width,
-        scratch,
+        [
+            pltpu.VMEM(key_bias.shape[1:], BF16),
+            pltpu.VMEM((width,), F32),
+            pltpu.VMEM((half, 3 * width), BF16),
+            pltpu.SemaphoreType.DMA((5,)),
+        ],
         limit=56,
     )
-
-    near = [message, flip_chips(message, 1, 0), flip_chips(message, 0, 1)]
-    near.append(flip_chips(near[1], 0, 1))
-    far = [swap_cores(block) for block in near]
 
     size = 4 * w_conv.shape[2]
     diagonal, coeffs, gains = call(
@@ -416,23 +439,58 @@
         (lon_half, lat_half, quad_off, lat_taps, w_conv, message),
         0,
     )
+    by_x, by_y = flip_chips(message, 1, 0), flip_chips(message, 0, 1)
     if direct:
-        qkv_bundle = bundled(qkv_own, qkv_cross)
-        out_bundle = bundled(out_own, out_own)
-        qkv_mine = [qkv_bundle] + flip_levels(qkv_bundle)
-        qkv_other = [swap_cores(block) for block in qkv_mine]
-        out_bundle = gate(out_bundle, *qkv_mine[1:])
-        out_mine = [out_bundle] + flip_levels(out_bundle)
+        (qkv_own,) = call(
+            columns_body, [((half, 3 * quarter), BF16)], [VMEM] * 2, (w_qkv, gains), 0
+        )
+        bundle, x_block, outs = call(
+            arrived_body,
+            [
+                ((2, half, 3 * quarter), BF16),
+                ((rows, width), BF16),
+                ((4, half, width), BF16),
+            ],
+            [VMEM] * 8,
+            (qkv_own, by_x, by_y, out_own, *flip_levels(out_own), gains),
+            0,
+        )
+        qkv_mine, near, out_mine = call(
+            complete_body,
+            [
+                ((4, 2, half, 3 * quarter), BF16),
+                ((4, rows, width), BF16),
+                ((2, 4, half, width), BF16),
+            ],
+            [VMEM] * 10,
+            (
+                bundle,
+                *flip_levels(bundle),
+                message,
+                x_block,
+                by_y,
+                flip_chips(x_block, 0, 1),
+                outs,
+                flip_chips(outs, 1, 0),
+            ),
+            0,
+        )
+        qkv_other, out_other = swap_cores(qkv_mine), swap_cores(out_mine)
+        join = join_columns
     else:
+        near = jnp.stack([message, by_x, by_y, flip_chips(by_x, 0, 1)])
         qkv_mine, qkv_other = gather_plain(w_qkv, 3 * quarter)
-    raw_tokens = gate(raw_tokens, *qkv_mine[1:])
+        out_mine, out_other = gather_plain(w_out, width)
+        join = join_bundles
+    far = swap_cores(near)
+    raw_tokens = gate(raw_tokens, qkv_mine)
     other_tokens = flip_chips(raw_tokens, 1, 0)
 
     pieces = call(
         attend_body,
         [((2, count, quarter), BF16)] * 4,
-        [VMEM] * 17,
-        (*near, *far, *qkv_mine, *qkv_other, gains),
+        [VMEM] * 4,
+        (near, far, qkv_mine, qkv_other),
         2 * 1024 * width * 3 * quarter,
         [
             pltpu.VMEM((width, 3 * quarter), BF16),
@@ -444,13 +502,8 @@
     back = [pieces[0]] + [
         flip_chips(piece, flip, sample) for piece, (flip, sample) in zip(pieces[1:], FLIPS)
     ]
-    if direct:
-        out_mine = [gate(block, back[1]) for block in out_mine]
-        out_other = [swap_cores(block) for block in out_mine]
-    else:
-        out_mine, out_other = gather_plain(w_out, width)
     (full_out,) = call(
-        join_body, [((width, width), BF16)], [VMEM] * 8, (*out_mine, *out_other), 0
+        join, [((width, width), BF16)], [VMEM] * 2, (out_mine, out_other), 0
     )
     (other_in,) = call(
         other_body,

time: 77.2 us -> 57.1 us (0.74)
  waiting for transfers between devices: 35.5 us -> 20.2 us
  starting transfers between devices: 26 us -> 21.2 us
    ppermute x16 -> x15, waiting for transfers between devices: 34.4 us -> 17.2 us  [move(): return lax.ppermute(values, AXES, device_pairs(target))]
    ppermute x13 -> x4, starting transfers between devices: 11.1 us -> 6.67 us  [swap_cores(): return lax.ppermute(values, 'lon', [(0, 1), (1, 0)])]
    ppermute x13 -> x4, waiting for transfers between devices: 1.1 us -> 2.95 us  [swap_cores(): return lax.ppermute(values, 'lon', [(0, 1), (1, 0)])]
    broadcast_in_dim x1 -> x0, local copies, waits for them, and re-layouts: 1.32 us -> none  [per_device(): gain_attn[None]]
    unnamed x18 -> x14, local copies, waits for them, and re-layouts: 2.09 us -> 2.89 us
    pallas_call x15 -> x11, Pallas kernels: 9.18 us -> 9.52 us  [call(): pl.pallas_call(body, out_shape=outs, in_specs=specs, out_specs=tuple((VME...]
    ppermute x16 -> x15, starting transfers between devices: 14.8 us -> 14.5 us  [move(): return lax.ppermute(values, AXES, device_pairs(target))]
  transfers between devices with their start and end apart: 29 -> 19, of which waited for: 9 -> 8; matrix products, arithmetic and copies ran while one was open for 0% -> 3% of each run, Pallas kernels for 8% -> 11%
where the time goes in v7:
time: 57.1 us; the launch traced here: 56.7 us
  starting transfers between devices  21.2 us (37%)
  waiting for transfers between devices  20.2 us (35%)
  Pallas kernels  9.52 us (17%)
  local copies, waits for them, and re-layouts  2.89 us (5%)
  between operations  2.16 us (4%)
  other arithmetic  0.71 us (1%)
    ppermute x15, waiting for transfers between devices, move(): return lax.ppermute(values, AXES, device_pairs(target))  17.2 us
    ppermute x15, starting transfers between devices, move(): return lax.ppermute(values, AXES, device_pairs(target))  14.5 us
    pallas_call x11, Pallas kernels, call(): pl.pallas_call(body, out_shape=outs, in_specs=specs, out_specs=tuple((VME...  9.52 us
    ppermute x4, starting transfers between devices, swap_cores(): return lax.ppermute(values, 'lon', [(0, 1), (1, 0)])  6.67 us
    ppermute x4, waiting for transfers between devices, swap_cores(): return lax.ppermute(values, 'lon', [(0, 1), (1, 0)])  2.95 us
    unnamed x14, local copies, waits for them, and re-layouts  2.89 us
  transfers between devices with their start and end apart: 19, of which 8 were waited for; matrix products, arithmetic and copies ran while one was open for 3% of the time, Pallas kernels for 11%

profile of v7, /device:TPU:3, one launch (start us, length us, event | category | flops | bytes accessed | tf_op | source)
XLA Modules:
  0.0 56.7 jit_solution(13673308695038113579)
XLA Ops:
  0.0 2.1 %shard_map.109 = (bf16[192,768]{1,0:T(8,128)(2,1)}, bf16[128,768]{1,0:T(8,128)(2,1)}, bf16[48,768]{1,0:T(8,128)(2,1)}) custom-call(bf16[128,768]{1,0:T(8,128)(2,1)} %bitcast.4, bf16[12,128]{1,0:T(8,128)(2,1)} %bitcast.5, f32[768]{0:T(1024)} %refs_2_.1, bf16[96,2304]{1,0:T(8,128)(2,1)} %w_qkv.1, bf16[96,768]{1,0:T(8,128)(2,1)} %refs_4_.1), custom_call_target="tpu_custom_call" | custom-call | flops 983040 | bytes 792576 | tf_op jit(solution)/shard_map/pallas_call | solution.py:23
  2.2 0.1 collective-permute-start
  2.2 1.5 %collective-permute-start.1 = (bf16[192,768]{1,0:T(8,128)(2,1)}, bf16[192,768]{1,0:T(8,128)(2,1)S(1)}, u32[]{:S(2)}, u32[]{:S(2)}) collective-permute-start(bf16[192,768]{1,0:T(8,128)(2,1)} %get-tuple-element.25.message), channel_id=1, source_target_pairs={{0,16},{1,17},{2,18},{3,19},{4,20},{5,21},{6,22},{7,23},{8,24},{9,... | collective-permute-start | bytes 884744 | tf_op jit(solution)/shard_map/ppermute | solution.py:57
  3.7 1.3 %collective-permute-start.2 = (bf16[48,768]{1,0:T(8,128)(2,1)}, bf16[48,768]{1,0:T(8,128)(2,1)S(1)}, u32[]{:S(2)}, u32[]{:S(2)}) collective-permute-start(bf16[48,768]{1,0:T(8,128)(2,1)} %get-tuple-element.27.out_own), channel_id=1, source_target_pairs={{0,4},{1,5},{2,6},{3,7},{4,0},{5,1},{6,2},{7,3},{8,12},{9,13},{10,... | collective-permute-start | bytes 221192 | tf_op jit(solution)/shard_map/ppermute | solution.py:57
  5.0 2.3 %collective-permute-start.3 = (bf16[48,768]{1,0:T(8,128)(2,1)}, bf16[48,768]{1,0:T(8,128)(2,1)S(1)}, u32[]{:S(2)}, u32[]{:S(2)}) collective-permute-start(bf16[48,768]{1,0:T(8,128)(2,1)} %get-tuple-element.27.out_own), channel_id=1, source_target_pairs={{0,8},{1,9},{2,10},{3,11},{4,12},{5,13},{6,14},{7,15},{8,0},{9,1},... | collective-permute-start | bytes 221192 | tf_op jit(solution)/shard_map/ppermute | solution.py:57
  9.3 0.8 %copy.12.taps = f32[16,2]{1,0:T(8,128)S(1)} copy(f32[16,2]{0,1:T(2,128)} %param.18) | data formatting | bytes 256 | tf_op args[7]
  10.0 1.1 %copy.13.w_conv = bf16[2,768,64]{2,1,0:T(8,128)(2,1)S(1)} copy(bf16[2,768,64]{1,2,0:T(8,128)(2,1)} %param.17) | data formatting | bytes 393216 | tf_op args[6]
  11.2 1.0 %copy-done.1 = bf16[192,768]{1,0:T(8,128)(2,1)S(1)} copy-done((bf16[192,768]{1,0:T(8,128)(2,1)S(1)}, bf16[192,768]{1,0:T(8,128)(2,1)}, u32[]{:S(2)}) %copy-start.1) | copy-done | bytes 294936
  12.2 1.0 %shard_map.110 = (bf16[2,3,256,256]{3,2,1,0:T(8,128)(2,1)S(1)}, bf16[256,512]{1,0:T(8,128)(2,1)S(1)}, f32[8,128]{1,0:T(8,128)S(1)}) custom-call(s32[1]{0:T(128)S(6)} %copy.14.lon_half, s32[1]{0:T(128)S(6)} %copy.15.lat_half, s32[1]{0:T(128)S(6)} %copy.16.quad_off, f32[16,2]{1,0:T(8,128)S(1)} %copy.12.taps, bf16[2,768,64]{2,1,0:T(8,128)(2,1)S(1)} %copy.13.w_conv, ...), custom_call_target="tpu_custom_call" | custom-call | bytes 491660 | tf_op jit(solution)/shard_map/pallas_call | solution.py:23
  13.2 0.2 shard_map.111.own
  13.4 0.0 collective-permute-done.2.out1
  13.4 0.0 collective-permute-done.4.out3
  13.4 0.0 collective-permute-done.by_x
  13.4 0.1 shard_map.112
  13.5 0.0 copy-start.3
  13.5 1.3 %collective-permute-start.9 = (bf16[4,48,768]{2,1,0:T(8,128)(2,1)S(1)}, bf16[4,48,768]{2,1,0:T(8,128)(2,1)S(1)}, u32[]{:S(2)}, u32[]{:S(2)}) collective-permute-start(bf16[4,48,768]{2,1,0:T(8,128)(2,1)S(1)} %get-tuple-element.30.outs), channel_id=1, source_target_pairs={{0,2},{1,3},{2,0},{3,1},{4,6},{5,7},{6,4},{7,5},{8,10},{9,11},{10,... | collective-permute-start | bytes 884744 | tf_op jit(solution)/shard_map/ppermute | solution.py:57
  14.8 0.2 collective-permute-start.8
  15.0 0.3 collective-permute-start.5
  15.3 3.2 %collective-permute-start.6 = (bf16[2,48,576]{2,1,0:T(8,128)(2,1)S(1)}, bf16[2,48,576]{2,1,0:T(8,128)(2,1)S(1)}, u32[]{:S(2)}, u32[]{:S(2)}) collective-permute-start(bf16[2,48,576]{2,1,0:T(8,128)(2,1)S(1)} %get-tuple-element.28.bundle), channel_id=1, source_target_pairs={{0,8},{1,9},{2,10},{3,11},{4,12},{5,13},{6,14},{7,15},{8,0},{9,1},... | collective-permute-start | bytes 331784 | tf_op jit(solution)/shard_map/ppermute | solution.py:57
  18.5 0.5 collective-permute-done.5.level1
  19.0 3.1 %collective-permute-done.6.level2 = bf16[2,48,576]{2,1,0:T(8,128)(2,1)S(1)} collective-permute-done((bf16[2,48,576]{2,1,0:T(8,128)(2,1)S(1)}, bf16[2,48,576]{2,1,0:T(8,128)(2,1)S(1)}, u32[]{:S(2)}, u32[]{:S(2)}) %collective-permute-start.6) | collective-permute-done | bytes 110624 | tf_op jit(solution)/shard_map/ppermute | solution.py:57
  22.1 3.2 %collective-permute-done.7.level3 = bf16[2,48,576]{2,1,0:T(8,128)(2,1)S(1)} collective-permute-done((bf16[2,48,576]{2,1,0:T(8,128)(2,1)S(1)}, bf16[2,48,576]{2,1,0:T(8,128)(2,1)S(1)}, u32[]{:S(2)}, u32[]{:S(2)}) %collective-permute-start.7) | collective-permute-done | bytes 110624 | tf_op jit(solution)/shard_map/ppermute | solution.py:57
  25.4 0.0 collective-permute-done.9.crossed
  25.4 0.1 shard_map.113
  25.5 4.1 %collective-permute-start.10 = (bf16[4,144,768]{2,1,0:T(8,128)(2,1)S(1)}, bf16[4,144,768]{2,1,0:T(8,128)(2,1)S(1)}, u32[]{:S(2)}, u32[]{:S(2)}) collective-permute-start(bf16[4,144,768]{2,1,0:T(8,128)(2,1)S(1)} %get-tuple-element.31.refs_0_), channel_id=1, source_target_pairs={{0,1},{1,0},{2,3},{3,2},{4,5},{5,4},{6,7},{7,6},{8,9},{9,8},{10,11... | collective-permute-start | bytes 2654216 | tf_op jit(solution)/shard_map/ppermute | solution.py:61
  29.6 0.1 collective-permute-start.11
  29.7 0.4 collective-permute-start.15
  30.2 0.0 copy-start.5
  30.2 0.3 collective-permute-start.16
  30.5 1.9 %collective-permute-done.11.refs_3_ = bf16[4,2,48,576]{3,2,1,0:T(8,128)(2,1)S(1)} collective-permute-done((bf16[4,2,48,576]{3,2,1,0:T(8,128)(2,1)S(1)}, bf16[4,2,48,576]{3,2,1,0:T(8,128)(2,1)S(1)}, u32[]{:S(2)}, u32[]{:S(2)}) %collective-permute-start.11) | collective-permute-done | bytes 442400 | tf_op jit(solution)/shard_map/ppermute | solution.py:61
  32.4 3.3 %shard_map.114 = (bf16[2,128,192]{2,1,0:T(8,128)(2,1)S(1)}, bf16[2,128,192]{2,1,0:T(8,128)(2,1)S(1)}, bf16[2,128,192]{2,1,0:T(8,128)(2,1)S(1)}, bf16[2,128,192]{2,1,0:T(8,128)(2,1)S(1)}) custom-call(bf16[4,144,768]{2,1,0:T(8,128)(2,1)S(1)} %get-tuple-element.31.refs_0_, bf16[4,144,768]{2,1,0:T(8,128)(2,1)S(1)} %collective-permute-done.10.refs_1_, ...), custom_call_target="tpu_custom_call" | custom-call | flops 905969664 | bytes 2654208 | tf_op jit(solution)/shard_map/pallas_call | solution.py:23
  35.7 0.3 collective-permute-start.12
  36.0 1.2 %collective-permute-start.13 = (bf16[2,128,192]{2,1,0:T(8,128)(2,1)S(1)}, bf16[2,128,192]{2,1,0:T(8,128)(2,1)S(1)}, u32[]{:S(2)}, u32[]{:S(2)}) collective-permute-start(bf16[2,128,192]{2,1,0:T(8,128)(2,1)S(1)} %get-tuple-element.35), channel_id=1, source_target_pairs={{0,16},{1,17},{2,18},{3,19},{4,20},{5,21},{6,22},{7,23},{8,24},{9,... | collective-permute-start | bytes 294920 | tf_op jit(solution)/shard_map/ppermute | solution.py:57
  37.2 1.2 %collective-permute-start.14 = (bf16[2,128,192]{2,1,0:T(8,128)(2,1)S(1)}, bf16[2,128,192]{2,1,0:T(8,128)(2,1)S(1)}, u32[]{:S(2)}, u32[]{:S(2)}) collective-permute-start(bf16[2,128,192]{2,1,0:T(8,128)(2,1)S(1)} %get-tuple-element.36), channel_id=1, source_target_pairs={{0,18},{1,19},{2,16},{3,17},{4,22},{5,23},{6,20},{7,21},{8,26},{9,... | collective-permute-start | bytes 294920 | tf_op jit(solution)/shard_map/ppermute | solution.py:57
  38.4 0.0 collective-permute-done.15.other
  38.4 0.1 shard_map.115.weights
  38.5 0.0 collective-permute-done.16.tokens
  38.5 1.9 %collective-permute-done.12.piece1 = bf16[2,128,192]{2,1,0:T(8,128)(2,1)S(1)} collective-permute-done((bf16[2,128,192]{2,1,0:T(8,128)(2,1)S(1)}, bf16[2,128,192]{2,1,0:T(8,128)(2,1)S(1)}, u32[]{:S(2)}, u32[]{:S(2)}) %collective-permute-start.12) | collective-permute-done | bytes 98336 | tf_op jit(solution)/shard_map/ppermute | solution.py:57
  40.4 0.0 collective-permute-done.13.piece2
  40.5 3.8 %collective-permute-done.14.piece3 = bf16[2,128,192]{2,1,0:T(8,128)(2,1)S(1)} collective-permute-done((bf16[2,128,192]{2,1,0:T(8,128)(2,1)S(1)}, bf16[2,128,192]{2,1,0:T(8,128)(2,1)S(1)}, u32[]{:S(2)}, u32[]{:S(2)}) %collective-permute-start.14) | collective-permute-done | bytes 98336 | tf_op jit(solution)/shard_map/ppermute | solution.py:57
  44.2 0.6 shard_map.117.other_in
  44.8 1.3 %collective-permute-start.17 = (bf16[128,768]{1,0:T(8,128)(2,1)S(1)}, bf16[128,768]{1,0:T(8,128)(2,1)S(1)}, u32[]{:S(2)}, u32[]{:S(2)}) collective-permute-start(bf16[128,768]{1,0:T(8,128)(2,1)S(1)} %shard_map.117.other_in), channel_id=1, source_target_pairs={{0,4},{1,5},{4,8},{5,9},{6,2},{7,3},{8,12},{9,13},{10,6},{11,7},{1... | collective-permute-start | bytes 589832 | tf_op jit(solution)/shard_map/ppermute | solution.py:57
  46.1 1.4 %shard_map.118 = (bf16[128,768]{1,0:T(8,128)(2,1)S(1)}, f32[256,768]{1,0:T(8,128)S(1)}) custom-call(f32[8,128]{1,0:T(8,128)S(1)} %get-tuple-element.26.gains, f32[1,768]{1,0:T(1,128)S(1)} %broadcast_in_dim.6.gain, bf16[2,128,192]{2,1,0:T(8,128)(2,1)S(1)} %get-tuple-element.33.piece0, bf16[2,128,192]{2,1,0:T(8,128)(2,1)S(1)} %collective-permute-done.12.piece1, ...), custom_call_target="tpu_custom_call" | custom-call | flops 452984832 | bytes 3021824 | tf_op jit(solution)/shard_map/pallas_call | solution.py:23
  47.5 4.7 %collective-permute-done.17.halo = bf16[128,768]{1,0:T(8,128)(2,1)S(1)} collective-permute-done((bf16[128,768]{1,0:T(8,128)(2,1)S(1)}, bf16[128,768]{1,0:T(8,128)(2,1)S(1)}, u32[]{:S(2)}, u32[]{:S(2)}) %collective-permute-start.17) | collective-permute-done | bytes 196640 | tf_op jit(solution)/shard_map/ppermute | solution.py:57
  52.2 0.7 %shard_map.119 = (f32[128,768]{1,0:T(8,128)S(1)}, bf16[128,768]{1,0:T(8,128)(2,1)S(1)}) custom-call(f32[8,128]{1,0:T(8,128)S(1)} %get-tuple-element.26.gains, bf16[128,768]{1,0:T(8,128)(2,1)S(1)} %collective-permute-done.17.halo, bf16[2,3,256,256]{3,2,1,0:T(8,128)(2,1)S(1)} %get-tuple-element.39.blocks, bf16[256,512]{1,0:T(8,128)(2,1)S(1)} %get-tuple-element.40.coeffs, ...), custom_call_target="tpu_custom_call" | custom-call | flops 100663296 | bytes 2232320 | tf_op jit(solution)/shard_map/pallas_call | solution.py:23
  52.8 2.0 %collective-permute-start.18 = (bf16[128,768]{1,0:T(8,128)(2,1)S(1)}, bf16[128,768]{1,0:T(8,128)(2,1)S(1)}, u32[]{:S(2)}, u32[]{:S(2)}) collective-permute-start(bf16[128,768]{1,0:T(8,128)(2,1)S(1)} %get-tuple-element.44), channel_id=1, source_target_pairs={{0,1},{1,0},{2,3},{3,2},{4,5},{5,4},{6,7},{7,6},{8,9},{9,8},{10,11... | collective-permute-start | bytes 589832 | tf_op jit(solution)/shard_map/ppermute | solution.py:61
  54.9 1.1 %collective-permute-done.18 = bf16[128,768]{1,0:T(8,128)(2,1)S(1)} collective-permute-done((bf16[128,768]{1,0:T(8,128)(2,1)S(1)}, bf16[128,768]{1,0:T(8,128)(2,1)S(1)}, u32[]{:S(2)}, u32[]{:S(2)}) %collective-permute-start.18) | collective-permute-done | bytes 196640 | tf_op jit(solution)/shard_map/ppermute | solution.py:61
  55.9 0.7 %fusion = bf16[1,128,768]{2,1,0:T(8,128)(2,1)} fusion(f32[128,768]{1,0:T(8,128)S(1)} %get-tuple-element.43, bf16[128,768]{1,0:T(8,128)(2,1)S(1)} %collective-permute-done.18), kind=kLoop, calls=%fused_computation.1 | loop fusion | flops 294912 | bytes 786432 | tf_op jit(solution)/shard_map/broadcast_in_dim | solution.py:532
  (17 shorter events, 0.1 us)
Async XLA Ops:
  0.0 13.2 %copy-start = (bf16[96,2304]{1,0:T(8,128)(2,1)S(1)}, bf16[96,2304]{1,0:T(8,128)(2,1)}, u32[]{:S(2)}) copy-start(bf16[96,2304]{1,0:T(8,128)(2,1)} %w_qkv.1) | copy-start | bytes 1327108
  2.2 11.3 %copy-start.4 = (bf16[48,768]{1,0:T(8,128)(2,1)S(1)}, bf16[48,768]{1,0:T(8,128)(2,1)}, u32[]{:S(2)}) copy-start(bf16[48,768]{1,0:T(8,128)(2,1)} %get-tuple-element.27.out_own) | copy-start | bytes 221188
  2.2 11.2 %collective-permute-start = (bf16[192,768]{1,0:T(8,128)(2,1)}, bf16[192,768]{1,0:T(8,128)(2,1)S(1)}, u32[]{:S(2)}, u32[]{:S(2)}) collective-permute-start(bf16[192,768]{1,0:T(8,128)(2,1)} %get-tuple-element.25.message), channel_id=1, source_target_pairs={{0,2},{1,3},{2,0},{3,1},{4,6},{5,7},{6,4},{7,5},{8,10},{9,11},{10,... | collective-permute-start | bytes 884744 | tf_op jit(solution)/shard_map/ppermute | solution.py:57
  2.2 11.2 %collective-permute-start.1 = (bf16[192,768]{1,0:T(8,128)(2,1)}, bf16[192,768]{1,0:T(8,128)(2,1)S(1)}, u32[]{:S(2)}, u32[]{:S(2)}) collective-permute-start(bf16[192,768]{1,0:T(8,128)(2,1)} %get-tuple-element.25.message), channel_id=1, source_target_pairs={{0,16},{1,17},{2,18},{3,19},{4,20},{5,21},{6,22},{7,23},{8,24},{9,... | collective-permute-start | bytes 884744 | tf_op jit(solution)/shard_map/ppermute | solution.py:57
  3.7 9.6 %collective-permute-start.2 = (bf16[48,768]{1,0:T(8,128)(2,1)}, bf16[48,768]{1,0:T(8,128)(2,1)S(1)}, u32[]{:S(2)}, u32[]{:S(2)}) collective-permute-start(bf16[48,768]{1,0:T(8,128)(2,1)} %get-tuple-element.27.out_own), channel_id=1, source_target_pairs={{0,4},{1,5},{2,6},{3,7},{4,0},{5,1},{6,2},{7,3},{8,12},{9,13},{10,... | collective-permute-start | bytes 221192 | tf_op jit(solution)/shard_map/ppermute | solution.py:57
  5.0 8.3 %collective-permute-start.3 = (bf16[48,768]{1,0:T(8,128)(2,1)}, bf16[48,768]{1,0:T(8,128)(2,1)S(1)}, u32[]{:S(2)}, u32[]{:S(2)}) collective-permute-start(bf16[48,768]{1,0:T(8,128)(2,1)} %get-tuple-element.27.out_own), channel_id=1, source_target_pairs={{0,8},{1,9},{2,10},{3,11},{4,12},{5,13},{6,14},{7,15},{8,0},{9,1},... | collective-permute-start | bytes 221192 | tf_op jit(solution)/shard_map/ppermute | solution.py:57
  7.3 6.0 %collective-permute-start.4 = (bf16[48,768]{1,0:T(8,128)(2,1)}, bf16[48,768]{1,0:T(8,128)(2,1)S(1)}, u32[]{:S(2)}, u32[]{:S(2)}) collective-permute-start(bf16[48,768]{1,0:T(8,128)(2,1)} %get-tuple-element.27.out_own), channel_id=1, source_target_pairs={{0,12},{1,13},{2,14},{3,15},{4,8},{5,9},{6,10},{7,11},{8,4},{9,5},... | collective-permute-start | bytes 221192 | tf_op jit(solution)/shard_map/ppermute | solution.py:57
  11.2 1.0 %copy-start.1 = (bf16[192,768]{1,0:T(8,128)(2,1)S(1)}, bf16[192,768]{1,0:T(8,128)(2,1)}, u32[]{:S(2)}) copy-start(bf16[192,768]{1,0:T(8,128)(2,1)} %get-tuple-element.25.message) | copy-start | bytes 884740
  12.2 13.2 %copy-start.2 = (bf16[192,768]{1,0:T(8,128)(2,1)S(1)}, bf16[192,768]{1,0:T(8,128)(2,1)}, u32[]{:S(2)}) copy-start(bf16[192,768]{1,0:T(8,128)(2,1)} %get-tuple-element.25.message) | copy-start | bytes 884740
  13.5 16.7 %copy-start.3 = (bf16[128,768]{1,0:T(8,128)(2,1)S(1)}, bf16[128,768]{1,0:T(8,128)(2,1)}, u32[]{:S(2)}) copy-start(bf16[128,768]{1,0:T(8,128)(2,1)} %get-tuple-element.38.refs_0_) | copy-start | bytes 589828
  13.5 11.9 %collective-permute-start.9 = (bf16[4,48,768]{2,1,0:T(8,128)(2,1)S(1)}, bf16[4,48,768]{2,1,0:T(8,128)(2,1)S(1)}, u32[]{:S(2)}, u32[]{:S(2)}) collective-permute-start(bf16[4,48,768]{2,1,0:T(8,128)(2,1)S(1)} %get-tuple-element.30.outs), channel_id=1, source_target_pairs={{0,2},{1,3},{2,0},{3,1},{4,6},{5,7},{6,4},{7,5},{8,10},{9,11},{10,... | collective-permute-start | bytes 884744 | tf_op jit(solution)/shard_map/ppermute | solution.py:57
  14.8 10.6 %collective-permute-start.8 = (bf16[144,768]{1,0:T(8,128)(2,1)S(1)}, bf16[144,768]{1,0:T(8,128)(2,1)S(1)}, u32[]{:S(2)}, u32[]{:S(2)}) collective-permute-start(bf16[144,768]{1,0:T(8,128)(2,1)S(1)} %get-tuple-element.29.x_block), channel_id=1, source_target_pairs={{0,16},{1,17},{2,18},{3,19},{4,20},{5,21},{6,22},{7,23},{8,24},{9,... | collective-permute-start | bytes 663560 | tf_op jit(solution)/shard_map/ppermute | solution.py:57
  15.0 4.0 %collective-permute-start.5 = (bf16[2,48,576]{2,1,0:T(8,128)(2,1)S(1)}, bf16[2,48,576]{2,1,0:T(8,128)(2,1)S(1)}, u32[]{:S(2)}, u32[]{:S(2)}) collective-permute-start(bf16[2,48,576]{2,1,0:T(8,128)(2,1)S(1)} %get-tuple-element.28.bundle), channel_id=1, source_target_pairs={{0,4},{1,5},{2,6},{3,7},{4,0},{5,1},{6,2},{7,3},{8,12},{9,13},{10,... | collective-permute-start | bytes 331784 | tf_op jit(solution)/shard_map/ppermute | solution.py:57
  15.3 6.8 %collective-permute-start.6 = (bf16[2,48,576]{2,1,0:T(8,128)(2,1)S(1)}, bf16[2,48,576]{2,1,0:T(8,128)(2,1)S(1)}, u32[]{:S(2)}, u32[]{:S(2)}) collective-permute-start(bf16[2,48,576]{2,1,0:T(8,128)(2,1)S(1)} %get-tuple-element.28.bundle), channel_id=1, source_target_pairs={{0,8},{1,9},{2,10},{3,11},{4,12},{5,13},{6,14},{7,15},{8,0},{9,1},... | collective-permute-start | bytes 331784 | tf_op jit(solution)/shard_map/ppermute | solution.py:57
  18.5 6.8 %collective-permute-start.7 = (bf16[2,48,576]{2,1,0:T(8,128)(2,1)S(1)}, bf16[2,48,576]{2,1,0:T(8,128)(2,1)S(1)}, u32[]{:S(2)}, u32[]{:S(2)}) collective-permute-start(bf16[2,48,576]{2,1,0:T(8,128)(2,1)S(1)} %get-tuple-element.28.bundle), channel_id=1, source_target_pairs={{0,12},{1,13},{2,14},{3,15},{4,8},{5,9},{6,10},{7,11},{8,4},{9,5},... | collective-permute-start | bytes 331784 | tf_op jit(solution)/shard_map/ppermute | solution.py:57
  25.5 6.9 %collective-permute-start.10 = (bf16[4,144,768]{2,1,0:T(8,128)(2,1)S(1)}, bf16[4,144,768]{2,1,0:T(8,128)(2,1)S(1)}, u32[]{:S(2)}, u32[]{:S(2)}) collective-permute-start(bf16[4,144,768]{2,1,0:T(8,128)(2,1)S(1)} %get-tuple-element.31.refs_0_), channel_id=1, source_target_pairs={{0,1},{1,0},{2,3},{3,2},{4,5},{5,4},{6,7},{7,6},{8,9},{9,8},{10,11... | collective-permute-start | bytes 2654216 | tf_op jit(solution)/shard_map/ppermute | solution.py:61
  29.6 2.8 %collective-permute-start.11 = (bf16[4,2,48,576]{3,2,1,0:T(8,128)(2,1)S(1)}, bf16[4,2,48,576]{3,2,1,0:T(8,128)(2,1)S(1)}, u32[]{:S(2)}, u32[]{:S(2)}) collective-permute-start(bf16[4,2,48,576]{3,2,1,0:T(8,128)(2,1)S(1)} %get-tuple-element.32.refs_2_.refs_1_), channel_id=1, source_target_pairs={{0,1},{1,0},{2,3},{3,2},{4,5},{5,4},{6,7},{7,6},{8,9},{9,8},{10,11... | collective-permute-start | bytes 1327112 | tf_op jit(solution)/shard_map/ppermute | solution.py:61
  29.7 8.7 %collective-permute-start.15 = (bf16[2,4,48,768]{3,2,1,0:T(8,128)(2,1)S(1)}, bf16[2,4,48,768]{3,2,1,0:T(8,128)(2,1)S(1)}, u32[]{:S(2)}, u32[]{:S(2)}) collective-permute-start(bf16[2,4,48,768]{3,2,1,0:T(8,128)(2,1)S(1)} %get-tuple-element.37.mine), channel_id=1, source_target_pairs={{0,1},{1,0},{2,3},{3,2},{4,5},{5,4},{6,7},{7,6},{8,9},{9,8},{10,11... | collective-permute-start | bytes 1769480 | tf_op jit(solution)/shard_map/ppermute | solution.py:61
  30.2 8.2 %copy-start.5 = (f32[768]{0:T(1024)S(1)}, f32[768]{0:T(1024)}, u32[]{:S(2)}) copy-start(f32[768]{0:T(1024)} %param.16) | copy-start | bytes 9220
  30.2 8.3 %collective-permute-start.16 = (bf16[128,768]{1,0:T(8,128)(2,1)S(1)}, bf16[128,768]{1,0:T(8,128)(2,1)S(1)}, u32[]{:S(2)}, u32[]{:S(2)}) collective-permute-start(bf16[128,768]{1,0:T(8,128)(2,1)S(1)} %shard_map.116.tokens), channel_id=1, source_target_pairs={{0,2},{1,3},{2,0},{3,1},{4,6},{5,7},{6,4},{7,5},{8,10},{9,11},{10,... | collective-permute-start | bytes 589832 | tf_op jit(solution)/shard_map/ppermute | solution.py:57
  35.7 4.8 %collective-permute-start.12 = (bf16[2,128,192]{2,1,0:T(8,128)(2,1)S(1)}, bf16[2,128,192]{2,1,0:T(8,128)(2,1)S(1)}, u32[]{:S(2)}, u32[]{:S(2)}) collective-permute-start(bf16[2,128,192]{2,1,0:T(8,128)(2,1)S(1)} %get-tuple-element.34), channel_id=1, source_target_pairs={{0,2},{1,3},{2,0},{3,1},{4,6},{5,7},{6,4},{7,5},{8,10},{9,11},{10,... | collective-permute-start | bytes 294920 | tf_op jit(solution)/shard_map/ppermute | solution.py:57
  36.0 4.5 %collective-permute-start.13 = (bf16[2,128,192]{2,1,0:T(8,128)(2,1)S(1)}, bf16[2,128,192]{2,1,0:T(8,128)(2,1)S(1)}, u32[]{:S(2)}, u32[]{:S(2)}) collective-permute-start(bf16[2,128,192]{2,1,0:T(8,128)(2,1)S(1)} %get-tuple-element.35), channel_id=1, source_target_pairs={{0,16},{1,17},{2,18},{3,19},{4,20},{5,21},{6,22},{7,23},{8,24},{9,... | collective-permute-start | bytes 294920 | tf_op jit(solution)/shard_map/ppermute | solution.py:57
  37.2 7.0 %collective-permute-start.14 = (bf16[2,128,192]{2,1,0:T(8,128)(2,1)S(1)}, bf16[2,128,192]{2,1,0:T(8,128)(2,1)S(1)}, u32[]{:S(2)}, u32[]{:S(2)}) collective-permute-start(bf16[2,128,192]{2,1,0:T(8,128)(2,1)S(1)} %get-tuple-element.36), channel_id=1, source_target_pairs={{0,18},{1,19},{2,16},{3,17},{4,22},{5,23},{6,20},{7,21},{8,26},{9,... | collective-permute-start | bytes 294920 | tf_op jit(solution)/shard_map/ppermute | solution.py:57
  44.8 7.4 %collective-permute-start.17 = (bf16[128,768]{1,0:T(8,128)(2,1)S(1)}, bf16[128,768]{1,0:T(8,128)(2,1)S(1)}, u32[]{:S(2)}, u32[]{:S(2)}) collective-permute-start(bf16[128,768]{1,0:T(8,128)(2,1)S(1)} %shard_map.117.other_in), channel_id=1, source_target_pairs={{0,4},{1,5},{4,8},{5,9},{6,2},{7,3},{8,12},{9,13},{10,6},{11,7},{1... | collective-permute-start | bytes 589832 | tf_op jit(solution)/shard_map/ppermute | solution.py:57
  52.8 3.1 %collective-permute-start.18 = (bf16[128,768]{1,0:T(8,128)(2,1)S(1)}, bf16[128,768]{1,0:T(8,128)(2,1)S(1)}, u32[]{:S(2)}, u32[]{:S(2)}) collective-permute-start(bf16[128,768]{1,0:T(8,128)(2,1)S(1)} %get-tuple-element.44), channel_id=1, source_target_pairs={{0,1},{1,0},{2,3},{3,2},{4,5},{5,4},{6,7},{7,6},{8,9},{9,8},{10,11... | collective-permute-start | bytes 589832 | tf_op jit(solution)/shard_map/ppermute | solution.py:61

commit v8 on v7

--- a/solution.py
+++ b/solution.py
@@ -31,15 +31,6 @@
     )(*args)
 
 
-def copy_body(*refs):
-    refs[-1][...] = refs[0][...]
-
-
-def gate(value, *after):
-    specs = [VMEM] * (1 + len(after))
-    return call(copy_body, [(value.shape, value.dtype)], specs, (value, *after), 0)[0]
-
-
 def device_pairs(target):
     lat_count = lax.axis_size("lat")
     pairs = []
@@ -85,7 +76,7 @@
 
 def pack_body(*refs, weights):
     tokens, bias, gain = refs[:3]
-    message, raw, out_own, bias_here, gain_here, rows, sems = refs[-7:]
+    message, with_raw, raw, qkv_both, out_own, bias_here, gain_here, rows, sems = refs[-9:]
     count = tokens.shape[0]
     heads, bias_width = bias.shape
     core = lax.axis_index("lon")
@@ -106,44 +97,45 @@
         fetch.wait()
     message[count : count + heads, :bias_width] = bias_here[...]
     message[:count, :] = norm_rows(raw[...].astype(F32), gain_here[...][None])
+    with_raw[: count + 16, :] = message[...]
+    with_raw[count + 16 :, :] = raw[...]
     for fetch in fetches[3:]:
         fetch.wait()
     if weights:
         side = lax.rem(lax.axis_index("lat"), 2)
-        cross = pick_columns(rows, 1 - side, tokens.shape[1] // 4)
-        message[count + 16 :, : cross.shape[1]] = cross
-
-
-def columns_body(w_qkv, gains, own):
-    del gains
-    half = own.shape[0]
-    start = pl.multiple_of(lax.axis_index("lon") * half, half)
-    rows = w_qkv[pl.ds(start, half), :]
-    own[...] = pick_columns(rows, lax.rem(lax.axis_index("lat"), 2), own.shape[1] // 3)
+        columns = qkv_both.shape[1] // 2
+        qkv_both[:, :columns] = pick_columns(rows, side, columns // 3)
+        qkv_both[:, columns:] = pick_columns(rows, 1 - side, columns // 3)
 
 
 def arrived_body(
-    own, by_x, by_y, out_own, out1, out2, out3, gains, bundle, x_block, outs
+    own, level1, level2, level3, by_x, by_y, out_own, gains, mine, cross, x_block, raw_x, outs
 ):
     del by_y, gains
-    side = lax.rem(lax.axis_index("lat"), 2)
-    rows, width = x_block.shape[0], own.shape[1]
-    bundle[side] = own[...]
-    bundle[1 - side] = by_x[rows:, :width]
+    columns = mine.shape[2]
+    rows = x_block.shape[0]
+    for at, block in enumerate((own, level1, level2, level3)):
+        mine[at] = block[:, :columns]
+        cross[at] = block[:, columns:]
     x_block[...] = by_x[:rows, :]
-    for at, block in enumerate((out_own, out1, out2, out3)):
+    raw_x[...] = by_x[rows:, :]
+    outs[...] = out_own[...]
+
+
+def complete_body(
+    mine, crossed, message, x_block, by_y, by_xy, own, level1, level2, level3, weights, near, outs
+):
+    weights[0] = mine[...]
+    weights[1] = crossed[...]
+    for at, block in enumerate((message, x_block, by_y, by_xy)):
+        near[at] = block[...]
+    for at, block in enumerate((own, level1, level2, level3)):
         outs[at] = block[...]
 
 
-def complete_body(
-    bundle, level1, level2, level3, message, x_block, by_y, by_xy, outs, crossed, weights, near, both
-):
-    rows = x_block.shape[0]
-    for at, block in enumerate((bundle, level1, level2, level3)):
-        weights[at] = block[...]
-    for at, block in enumerate((message, x_block, by_y, by_xy)):
-        near[at] = block[:rows, :]
-    both[0] = outs[...]
+def pair_body(mine, crossed, after, both):
+    del after
+    both[0] = mine[...]
     both[1] = crossed[...]
 
 
@@ -175,14 +167,14 @@
                 joined[pl.ds(first, half), :] = block[cross, flip]
 
 
-def attend_body(*refs):
-    (near, far, mine, other), pieces = refs[:4], refs[4:8]
-    weights, bias_rows, near_rows, far_rows = refs[8:]
+def attend_body(join, *refs):
+    near, far, mine, other = refs[:4]
+    pieces, (weights, bias_rows, near_rows, far_rows) = refs[4:8], refs[8:]
     group, side = lax.axis_index("groups"), lax.rem(lax.axis_index("lat"), 2)
     _, count, quarter = pieces[0].shape
     heads = 3
     head_dim = quarter // heads
-    join_bundles(mine, other, weights)
+    join(mine, other, weights)
     for slot in range(4):
         near_rows[slot * count : (slot + 1) * count, :] = near[slot, :count, :]
         far_rows[slot * count : (slot + 1) * count, :] = far[slot, :count, :]
@@ -408,11 +400,13 @@
 
     direct = half % 16 == 0 and lat_count == 8
     rows = count + 16
-    message, raw_tokens, out_own = call(
+    message, with_raw, raw_tokens, qkv_both, out_own = call(
         functools.partial(pack_body, weights=direct),
         [
-            ((rows + (half if direct else 0), width), BF16),
+            ((rows, width), BF16),
+            ((rows + count, width), BF16),
             ((count, width), BF16),
+            ((half, 6 * quarter), BF16),
             ((half, width), BF16),
         ],
         [HBM] * (5 if direct else 3),
@@ -439,55 +433,53 @@
         (lon_half, lat_half, quad_off, lat_taps, w_conv, message),
         0,
     )
-    by_x, by_y = flip_chips(message, 1, 0), flip_chips(message, 0, 1)
+    by_x, by_y = flip_chips(with_raw, 1, 0), flip_chips(message, 0, 1)
     if direct:
-        (qkv_own,) = call(
-            columns_body, [((half, 3 * quarter), BF16)], [VMEM] * 2, (w_qkv, gains), 0
-        )
-        bundle, x_block, outs = call(
+        mine, cross, x_block, other_tokens, outs = call(
             arrived_body,
             [
-                ((2, half, 3 * quarter), BF16),
+                ((4, half, 3 * quarter), BF16),
+                ((4, half, 3 * quarter), BF16),
                 ((rows, width), BF16),
-                ((4, half, width), BF16),
+                ((count, width), BF16),
+                ((half, width), BF16),
             ],
             [VMEM] * 8,
-            (qkv_own, by_x, by_y, out_own, *flip_levels(out_own), gains),
+            (qkv_both, *flip_levels(qkv_both), by_x, by_y, out_own, gains),
             0,
         )
-        qkv_mine, near, out_mine = call(
+        qkv_mine, near, outs = call(
             complete_body,
             [
-                ((4, 2, half, 3 * quarter), BF16),
+                ((2, 4, half, 3 * quarter), BF16),
                 ((4, rows, width), BF16),
-                ((2, 4, half, width), BF16),
+                ((4, half, width), BF16),
             ],
             [VMEM] * 10,
             (
-                bundle,
-                *flip_levels(bundle),
+                mine,
+                flip_chips(cross, 1, 0),
                 message,
                 x_block,
                 by_y,
                 flip_chips(x_block, 0, 1),
                 outs,
-                flip_chips(outs, 1, 0),
+                *flip_levels(outs),
             ),
             0,
         )
-        qkv_other, out_other = swap_cores(qkv_mine), swap_cores(out_mine)
+        qkv_other = swap_cores(qkv_mine)
         join = join_columns
     else:
-        near = jnp.stack([message, by_x, by_y, flip_chips(by_x, 0, 1)])
+        x_block, other_tokens = by_x[:rows], by_x[rows:]
+        near = jnp.stack([message, x_block, by_y, flip_chips(x_block, 0, 1)])
         qkv_mine, qkv_other = gather_plain(w_qkv, 3 * quarter)
-        out_mine, out_other = gather_plain(w_out, width)
+        outs, out_other = gather_plain(w_out, width)
         join = join_bundles
     far = swap_cores(near)
-    raw_tokens = gate(raw_tokens, qkv_mine)
-    other_tokens = flip_chips(raw_tokens, 1, 0)
 
     pieces = call(
-        attend_body,
+        functools.partial(attend_body, join),
         [((2, count, quarter), BF16)] * 4,
         [VMEM] * 4,
         (near, far, qkv_mine, qkv_other),
@@ -502,9 +494,16 @@
     back = [pieces[0]] + [
         flip_chips(piece, flip, sample) for piece, (flip, sample) in zip(pieces[1:], FLIPS)
     ]
-    (full_out,) = call(
-        join, [((width, width), BF16)], [VMEM] * 2, (out_mine, out_other), 0
-    )
+    if direct:
+        (outs,) = call(
+            pair_body,
+            [((2, 4, half, width), BF16)],
+            [VMEM] * 3,
+            (outs, flip_chips(outs, 1, 0), pieces[0]),
+            0,
+        )
+        out_other = swap_cores(outs)
+    (full_out,) = call(join, [((width, width), BF16)], [VMEM] * 2, (outs, out_other), 0)
     (other_in,) = call(
         other_body,
         [((count, width), BF16)],

time: 57.1 us -> 60.5 us (1.060)
  starting transfers between devices: 21.2 us -> 23.6 us
  waiting for transfers between devices: 20.2 us -> 22 us
  local copies, waits for them, and re-layouts: 2.89 us -> 2.19 us
    ppermute x15, waiting for transfers between devices: 17.2 us -> 18.5 us  [move(): return lax.ppermute(values, AXES, device_pairs(target))]
    ppermute x15, starting transfers between devices: 14.5 us -> 15.8 us  [move(): return lax.ppermute(values, AXES, device_pairs(target))]
    ppermute x4, starting transfers between devices: 6.67 us -> 7.79 us  [swap_cores(): return lax.ppermute(values, 'lon', [(0, 1), (1, 0)])]
    unnamed x14 -> x16, local copies, waits for them, and re-layouts: 2.89 us -> 2.19 us
    pallas_call x11 -> x10, Pallas kernels: 9.52 us -> 9.65 us  [call(): pl.pallas_call(body, out_shape=outs, in_specs=specs, out_specs=tuple((VME...]
  transfers between devices with their start and end apart: 19 -> 19, of which waited for: 8 -> 9; matrix products, arithmetic and copies ran while one was open for 3% -> 2% of each run, Pallas kernels for 11% -> 10%
where the time goes in v8:
time: 60.5 us; the launch traced here: 60.3 us
  starting transfers between devices  23.6 us (39%)
  waiting for transfers between devices  22 us (36%)
  Pallas kernels  9.65 us (16%)
  local copies, waits for them, and re-layouts  2.19 us (4%)
  between operations  2.15 us (4%)
  other arithmetic  0.71 us (1%)
    ppermute x15, waiting for transfers between devices, move(): return lax.ppermute(values, AXES, device_pairs(target))  18.5 us
    ppermute x15, starting transfers between devices, move(): return lax.ppermute(values, AXES, device_pairs(target))  15.8 us
    pallas_call x10, Pallas kernels, call(): pl.pallas_call(body, out_shape=outs, in_specs=specs, out_specs=tuple((VME...  9.65 us
    ppermute x4, starting transfers between devices, swap_cores(): return lax.ppermute(values, 'lon', [(0, 1), (1, 0)])  7.79 us
    ppermute x4, waiting for transfers between devices, swap_cores(): return lax.ppermute(values, 'lon', [(0, 1), (1, 0)])  3.5 us
    unnamed x16, local copies, waits for them, and re-layouts  2.19 us
  transfers between devices with their start and end apart: 19, of which 9 were waited for; matrix products, arithmetic and copies ran while one was open for 2% of the time, Pallas kernels for 10%

profile of v8, /device:TPU:3, one launch (start us, length us, event | category | flops | bytes accessed | tf_op | source)
XLA Modules:
  0.0 60.3 jit_solution(9758664999200123244)
XLA Ops:
  0.0 2.3 %shard_map.109 = (bf16[144,768]{1,0:T(8,128)(2,1)}, bf16[272,768]{1,0:T(8,128)(2,1)}, bf16[128,768]{1,0:T(8,128)(2,1)}, bf16[48,1152]{1,0:T(8,128)(2,1)}, bf16[48,768]{1,0:T(8,128)(2,1)}) custom-call(bf16[128,768]{1,0:T(8,128)(2,1)} %bitcast.4, bf16[12,128]{1,0:T(8,128)(2,1)} %bitcast.5, f32[768]{0:T(1024)} %refs_2_.1, bf16[96,2304]{1,0:T(8,128)(2,1)} %refs_3_.1, ...), custom_call_target="tpu_custom_call" | custom-call | flops 983040 | bytes 792576 | tf_op jit(solution)/shard_map/pallas_call | solution.py:23
  2.4 0.1 collective-permute-start.3
  2.5 1.5 %collective-permute-start.4 = (bf16[144,768]{1,0:T(8,128)(2,1)}, bf16[144,768]{1,0:T(8,128)(2,1)S(1)}, u32[]{:S(2)}, u32[]{:S(2)}) collective-permute-start(bf16[144,768]{1,0:T(8,128)(2,1)} %get-tuple-element.29.message), channel_id=1, source_target_pairs={{0,16},{1,17},{2,18},{3,19},{4,20},{5,21},{6,22},{7,23},{8,24},{9,... | collective-permute-start | bytes 663560 | tf_op jit(solution)/shard_map/ppermute | solution.py:48
  3.9 1.3 %collective-permute-start = (bf16[48,1152]{1,0:T(8,128)(2,1)}, bf16[48,1152]{1,0:T(8,128)(2,1)S(1)}, u32[]{:S(2)}, u32[]{:S(2)}) collective-permute-start(bf16[48,1152]{1,0:T(8,128)(2,1)} %get-tuple-element.31.own), channel_id=1, source_target_pairs={{0,4},{1,5},{2,6},{3,7},{4,0},{5,1},{6,2},{7,3},{8,12},{9,13},{10,... | collective-permute-start | bytes 331784 | tf_op jit(solution)/shard_map/ppermute | solution.py:48
  5.2 2.3 %collective-permute-start.1 = (bf16[48,1152]{1,0:T(8,128)(2,1)}, bf16[48,1152]{1,0:T(8,128)(2,1)S(1)}, u32[]{:S(2)}, u32[]{:S(2)}) collective-permute-start(bf16[48,1152]{1,0:T(8,128)(2,1)} %get-tuple-element.31.own), channel_id=1, source_target_pairs={{0,8},{1,9},{2,10},{3,11},{4,12},{5,13},{6,14},{7,15},{8,0},{9,1},... | collective-permute-start | bytes 331784 | tf_op jit(solution)/shard_map/ppermute | solution.py:48
  7.6 1.1 %copy.13.w_conv = bf16[2,768,64]{2,1,0:T(8,128)(2,1)S(1)} copy(bf16[2,768,64]{1,2,0:T(8,128)(2,1)} %param.17) | data formatting | bytes 393216 | tf_op args[6]
  8.7 0.1 copy.12.taps
  10.8 0.9 %copy-done = bf16[144,768]{1,0:T(8,128)(2,1)S(1)} copy-done((bf16[144,768]{1,0:T(8,128)(2,1)S(1)}, bf16[144,768]{1,0:T(8,128)(2,1)}, u32[]{:S(2)}) %copy-start) | copy-done | bytes 221208
  11.7 1.0 %shard_map.110 = (bf16[2,3,256,256]{3,2,1,0:T(8,128)(2,1)S(1)}, bf16[256,512]{1,0:T(8,128)(2,1)S(1)}, f32[8,128]{1,0:T(8,128)S(1)}) custom-call(s32[1]{0:T(128)S(6)} %copy.14.lon_half, s32[1]{0:T(128)S(6)} %copy.15.lat_half, s32[1]{0:T(128)S(6)} %copy.16.quad_off, f32[16,2]{1,0:T(8,128)S(1)} %copy.12.taps, bf16[2,768,64]{2,1,0:T(8,128)(2,1)S(1)} %copy.13.w_conv, ...), custom_call_target="tpu_custom_call" | custom-call | bytes 417932 | tf_op jit(solution)/shard_map/pallas_call | solution.py:23
  12.7 0.0 collective-permute-done.level1
  12.7 1.8 %collective-permute-done.2.level3 = bf16[48,1152]{1,0:T(8,128)(2,1)S(1)} collective-permute-done((bf16[48,1152]{1,0:T(8,128)(2,1)}, bf16[48,1152]{1,0:T(8,128)(2,1)S(1)}, u32[]{:S(2)}, u32[]{:S(2)}) %collective-permute-start.2) | collective-permute-done | bytes 110624 | tf_op jit(solution)/shard_map/ppermute | solution.py:48
  14.5 0.0 collective-permute-done.4.by_y
  14.5 0.0 collective-permute-done.3.by_x
  14.5 0.2 shard_map.111
  14.7 0.3 collective-permute-start.6
  15.0 1.2 %collective-permute-start.5 = (bf16[4,48,576]{2,1,0:T(8,128)(2,1)S(1)}, bf16[4,48,576]{2,1,0:T(8,128)(2,1)S(1)}, u32[]{:S(2)}, u32[]{:S(2)}) collective-permute-start(bf16[4,48,576]{2,1,0:T(8,128)(2,1)S(1)} %get-tuple-element.35), channel_id=1, source_target_pairs={{0,2},{1,3},{2,0},{3,1},{4,6},{5,7},{6,4},{7,5},{8,10},{9,11},{10,... | collective-permute-start | bytes 663560 | tf_op jit(solution)/shard_map/ppermute | solution.py:48
  16.2 2.9 %collective-permute-start.7 = (bf16[48,768]{1,0:T(8,128)(2,1)S(1)}, bf16[48,768]{1,0:T(8,128)(2,1)S(1)}, u32[]{:S(2)}, u32[]{:S(2)}) collective-permute-start(bf16[48,768]{1,0:T(8,128)(2,1)S(1)} %get-tuple-element.37.own), channel_id=1, source_target_pairs={{0,4},{1,5},{2,6},{3,7},{4,0},{5,1},{6,2},{7,3},{8,12},{9,13},{10,... | collective-permute-start | bytes 221192 | tf_op jit(solution)/shard_map/ppermute | solution.py:48
  19.0 0.7 %collective-permute-start.8 = (bf16[48,768]{1,0:T(8,128)(2,1)S(1)}, bf16[48,768]{1,0:T(8,128)(2,1)S(1)}, u32[]{:S(2)}, u32[]{:S(2)}) collective-permute-start(bf16[48,768]{1,0:T(8,128)(2,1)S(1)} %get-tuple-element.37.own), channel_id=1, source_target_pairs={{0,8},{1,9},{2,10},{3,11},{4,12},{5,13},{6,14},{7,15},{8,0},{9,1},... | collective-permute-start | bytes 221192 | tf_op jit(solution)/shard_map/ppermute | solution.py:48
  19.8 1.3 %collective-permute-start.9 = (bf16[48,768]{1,0:T(8,128)(2,1)S(1)}, bf16[48,768]{1,0:T(8,128)(2,1)S(1)}, u32[]{:S(2)}, u32[]{:S(2)}) collective-permute-start(bf16[48,768]{1,0:T(8,128)(2,1)S(1)} %get-tuple-element.37.own), channel_id=1, source_target_pairs={{0,12},{1,13},{2,14},{3,15},{4,8},{5,9},{6,10},{7,11},{8,4},{9,5},... | collective-permute-start | bytes 221192 | tf_op jit(solution)/shard_map/ppermute | solution.py:48
  21.1 0.0 collective-permute-done.7.level1
  21.1 2.9 %collective-permute-done.8.level2 = bf16[48,768]{1,0:T(8,128)(2,1)S(1)} collective-permute-done((bf16[48,768]{1,0:T(8,128)(2,1)S(1)}, bf16[48,768]{1,0:T(8,128)(2,1)S(1)}, u32[]{:S(2)}, u32[]{:S(2)}) %collective-permute-start.8) | collective-permute-done | bytes 73760 | tf_op jit(solution)/shard_map/ppermute | solution.py:48
  24.0 0.8 %collective-permute-done.9.level3 = bf16[48,768]{1,0:T(8,128)(2,1)S(1)} collective-permute-done((bf16[48,768]{1,0:T(8,128)(2,1)S(1)}, bf16[48,768]{1,0:T(8,128)(2,1)S(1)}, u32[]{:S(2)}, u32[]{:S(2)}) %collective-permute-start.9) | collective-permute-done | bytes 73760 | tf_op jit(solution)/shard_map/ppermute | solution.py:48
  24.9 0.1 shard_map.112
  25.0 4.6 %collective-permute-start.10 = (bf16[4,144,768]{2,1,0:T(8,128)(2,1)S(1)}, bf16[4,144,768]{2,1,0:T(8,128)(2,1)S(1)}, u32[]{:S(2)}, u32[]{:S(2)}) collective-permute-start(bf16[4,144,768]{2,1,0:T(8,128)(2,1)S(1)} %get-tuple-element.38.refs_0_), channel_id=1, source_target_pairs={{0,1},{1,0},{2,3},{3,2},{4,5},{5,4},{6,7},{7,6},{8,9},{9,8},{10,11... | collective-permute-start | bytes 2654216 | tf_op jit(solution)/shard_map/ppermute | solution.py:52
  29.6 0.1 collective-permute-start.11
  29.6 0.3 collective-permute-start.15
  29.9 2.4 %collective-permute-done.11.refs_3_ = bf16[2,4,48,576]{3,2,1,0:T(8,128)(2,1)S(1)} collective-permute-done((bf16[2,4,48,576]{3,2,1,0:T(8,128)(2,1)S(1)}, bf16[2,4,48,576]{3,2,1,0:T(8,128)(2,1)S(1)}, u32[]{:S(2)}, u32[]{:S(2)}) %collective-permute-start.11) | collective-permute-done | bytes 442400 | tf_op jit(solution)/shard_map/ppermute | solution.py:52
  32.3 0.0 collective-permute-done.10.refs_1_
  32.3 3.3 %shard_map.113 = (bf16[2,128,192]{2,1,0:T(8,128)(2,1)S(1)}, bf16[2,128,192]{2,1,0:T(8,128)(2,1)S(1)}, bf16[2,128,192]{2,1,0:T(8,128)(2,1)S(1)}, bf16[2,128,192]{2,1,0:T(8,128)(2,1)S(1)}) custom-call(bf16[4,144,768]{2,1,0:T(8,128)(2,1)S(1)} %get-tuple-element.38.refs_0_, bf16[4,144,768]{2,1,0:T(8,128)(2,1)S(1)} %collective-permute-done.10.refs_1_, ...), custom_call_target="tpu_custom_call" | custom-call | flops 905969664 | bytes 2654208 | tf_op jit(solution)/shard_map/pallas_call | solution.py:23
  35.6 0.0 copy-start.5
  35.6 2.2 %collective-permute-done.15.crossed = bf16[4,48,768]{2,1,0:T(8,128)(2,1)S(1)} collective-permute-done((bf16[4,48,768]{2,1,0:T(8,128)(2,1)S(1)}, bf16[4,48,768]{2,1,0:T(8,128)(2,1)S(1)}, u32[]{:S(2)}, u32[]{:S(2)}) %collective-permute-start.15) | collective-permute-done | bytes 294944 | tf_op jit(solution)/shard_map/ppermute | solution.py:48
  37.8 1.3 %collective-permute-start.16 = (bf16[2,4,48,768]{3,2,1,0:T(8,128)(2,1)S(1)}, bf16[2,4,48,768]{3,2,1,0:T(8,128)(2,1)S(1)}, u32[]{:S(2)}, u32[]{:S(2)}) collective-permute-start(bf16[2,4,48,768]{3,2,1,0:T(8,128)(2,1)S(1)} %shard_map.114.mine), channel_id=1, source_target_pairs={{0,1},{1,0},{2,3},{3,2},{4,5},{5,4},{6,7},{7,6},{8,9},{9,8},{10,11... | collective-permute-start | bytes 1769480 | tf_op jit(solution)/shard_map/ppermute | solution.py:52
  39.2 0.3 collective-permute-start.12
  39.4 1.2 %collective-permute-start.13 = (bf16[2,128,192]{2,1,0:T(8,128)(2,1)S(1)}, bf16[2,128,192]{2,1,0:T(8,128)(2,1)S(1)}, u32[]{:S(2)}, u32[]{:S(2)}) collective-permute-start(bf16[2,128,192]{2,1,0:T(8,128)(2,1)S(1)} %get-tuple-element.42), channel_id=1, source_target_pairs={{0,16},{1,17},{2,18},{3,19},{4,20},{5,21},{6,22},{7,23},{8,24},{9,... | collective-permute-start | bytes 294920 | tf_op jit(solution)/shard_map/ppermute | solution.py:48
  40.7 1.2 %collective-permute-start.14 = (bf16[2,128,192]{2,1,0:T(8,128)(2,1)S(1)}, bf16[2,128,192]{2,1,0:T(8,128)(2,1)S(1)}, u32[]{:S(2)}, u32[]{:S(2)}) collective-permute-start(bf16[2,128,192]{2,1,0:T(8,128)(2,1)S(1)} %get-tuple-element.43), channel_id=1, source_target_pairs={{0,18},{1,19},{2,16},{3,17},{4,22},{5,23},{6,20},{7,21},{8,26},{9,... | collective-permute-start | bytes 294920 | tf_op jit(solution)/shard_map/ppermute | solution.py:48
  41.8 0.1 shard_map.115.weights
  42.0 0.0 copy-start.2
  42.0 2.3 %collective-permute-done.12.piece1 = bf16[2,128,192]{2,1,0:T(8,128)(2,1)S(1)} collective-permute-done((bf16[2,128,192]{2,1,0:T(8,128)(2,1)S(1)}, bf16[2,128,192]{2,1,0:T(8,128)(2,1)S(1)}, u32[]{:S(2)}, u32[]{:S(2)}) %collective-permute-start.12) | collective-permute-done | bytes 98336 | tf_op jit(solution)/shard_map/ppermute | solution.py:48
  44.2 0.0 collective-permute-done.13.piece2
  44.2 3.8 %collective-permute-done.14.piece3 = bf16[2,128,192]{2,1,0:T(8,128)(2,1)S(1)} collective-permute-done((bf16[2,128,192]{2,1,0:T(8,128)(2,1)S(1)}, bf16[2,128,192]{2,1,0:T(8,128)(2,1)S(1)}, u32[]{:S(2)}, u32[]{:S(2)}) %collective-permute-start.14) | collective-permute-done | bytes 98336 | tf_op jit(solution)/shard_map/ppermute | solution.py:48
  48.0 0.6 shard_map.116.other_in
  48.6 1.3 %collective-permute-start.17 = (bf16[128,768]{1,0:T(8,128)(2,1)S(1)}, bf16[128,768]{1,0:T(8,128)(2,1)S(1)}, u32[]{:S(2)}, u32[]{:S(2)}) collective-permute-start(bf16[128,768]{1,0:T(8,128)(2,1)S(1)} %shard_map.116.other_in), channel_id=1, source_target_pairs={{0,4},{1,5},{4,8},{5,9},{6,2},{7,3},{8,12},{9,13},{10,6},{11,7},{1... | collective-permute-start | bytes 589832 | tf_op jit(solution)/shard_map/ppermute | solution.py:48
  49.9 1.4 %shard_map.117 = (bf16[128,768]{1,0:T(8,128)(2,1)S(1)}, f32[256,768]{1,0:T(8,128)S(1)}) custom-call(f32[8,128]{1,0:T(8,128)S(1)} %get-tuple-element.30.gains, f32[1,768]{1,0:T(1,128)S(1)} %broadcast_in_dim.6.gain, bf16[2,128,192]{2,1,0:T(8,128)(2,1)S(1)} %get-tuple-element.40.after.piece0, bf16[2,128,192]{2,1,0:T(8,128)(2,1)S(1)} %collective-permute-done.12.piece1, ...), custom_call_target="tpu_custom_call" | custom-call | flops 452984832 | bytes 3021824 | tf_op jit(solution)/shard_map/pallas_call | solution.py:23
  51.3 4.8 %collective-permute-done.17.halo = bf16[128,768]{1,0:T(8,128)(2,1)S(1)} collective-permute-done((bf16[128,768]{1,0:T(8,128)(2,1)S(1)}, bf16[128,768]{1,0:T(8,128)(2,1)S(1)}, u32[]{:S(2)}, u32[]{:S(2)}) %collective-permute-start.17) | collective-permute-done | bytes 196640 | tf_op jit(solution)/shard_map/ppermute | solution.py:48
  56.0 0.7 %shard_map.118 = (f32[128,768]{1,0:T(8,128)S(1)}, bf16[128,768]{1,0:T(8,128)(2,1)S(1)}) custom-call(f32[8,128]{1,0:T(8,128)S(1)} %get-tuple-element.30.gains, bf16[128,768]{1,0:T(8,128)(2,1)S(1)} %collective-permute-done.17.halo, bf16[2,3,256,256]{3,2,1,0:T(8,128)(2,1)S(1)} %get-tuple-element.46.blocks, bf16[256,512]{1,0:T(8,128)(2,1)S(1)} %get-tuple-element.47.coeffs, ...), custom_call_target="tpu_custom_call" | custom-call | flops 100663296 | bytes 2232320 | tf_op jit(solution)/shard_map/pallas_call | solution.py:23
  56.7 1.8 %collective-permute-start.18 = (bf16[128,768]{1,0:T(8,128)(2,1)S(1)}, bf16[128,768]{1,0:T(8,128)(2,1)S(1)}, u32[]{:S(2)}, u32[]{:S(2)}) collective-permute-start(bf16[128,768]{1,0:T(8,128)(2,1)S(1)} %get-tuple-element.52), channel_id=1, source_target_pairs={{0,1},{1,0},{2,3},{3,2},{4,5},{5,4},{6,7},{7,6},{8,9},{9,8},{10,11... | collective-permute-start | bytes 589832 | tf_op jit(solution)/shard_map/ppermute | solution.py:52
  58.5 1.1 %collective-permute-done.18 = bf16[128,768]{1,0:T(8,128)(2,1)S(1)} collective-permute-done((bf16[128,768]{1,0:T(8,128)(2,1)S(1)}, bf16[128,768]{1,0:T(8,128)(2,1)S(1)}, u32[]{:S(2)}, u32[]{:S(2)}) %collective-permute-start.18) | collective-permute-done | bytes 196640 | tf_op jit(solution)/shard_map/ppermute | solution.py:52
  59.6 0.7 %fusion = bf16[1,128,768]{2,1,0:T(8,128)(2,1)} fusion(f32[128,768]{1,0:T(8,128)S(1)} %get-tuple-element.51, bf16[128,768]{1,0:T(8,128)(2,1)S(1)} %collective-permute-done.18), kind=kLoop, calls=%fused_computation.1 | loop fusion | flops 294912 | bytes 786432 | tf_op jit(solution)/shard_map/broadcast_in_dim | solution.py:531
  (18 shorter events, 0.1 us)
Async XLA Ops:
  0.0 8.7 %copy-start.6 = (f32[16,2]{0,1:T(2,128)S(1)}, f32[16,2]{0,1:T(2,128)}, u32[]{:S(2)}) copy-start(f32[16,2]{0,1:T(2,128)} %param.18) | copy-start | bytes 388
  2.4 12.2 %copy-start.3 = (bf16[48,1152]{1,0:T(8,128)(2,1)S(1)}, bf16[48,1152]{1,0:T(8,128)(2,1)}, u32[]{:S(2)}) copy-start(bf16[48,1152]{1,0:T(8,128)(2,1)} %get-tuple-element.31.own) | copy-start | bytes 331780
  2.4 12.1 %copy-start.4 = (bf16[48,768]{1,0:T(8,128)(2,1)S(1)}, bf16[48,768]{1,0:T(8,128)(2,1)}, u32[]{:S(2)}) copy-start(bf16[48,768]{1,0:T(8,128)(2,1)} %get-tuple-element.33.out_own) | copy-start | bytes 221188
  2.4 12.1 %collective-permute-start.3 = (bf16[272,768]{1,0:T(8,128)(2,1)}, bf16[272,768]{1,0:T(8,128)(2,1)S(1)}, u32[]{:S(2)}, u32[]{:S(2)}) collective-permute-start(bf16[272,768]{1,0:T(8,128)(2,1)} %get-tuple-element.32), channel_id=1, source_target_pairs={{0,2},{1,3},{2,0},{3,1},{4,6},{5,7},{6,4},{7,5},{8,10},{9,11},{10,... | collective-permute-start | bytes 1253384 | tf_op jit(solution)/shard_map/ppermute | solution.py:48
  2.5 12.0 %collective-permute-start.4 = (bf16[144,768]{1,0:T(8,128)(2,1)}, bf16[144,768]{1,0:T(8,128)(2,1)S(1)}, u32[]{:S(2)}, u32[]{:S(2)}) collective-permute-start(bf16[144,768]{1,0:T(8,128)(2,1)} %get-tuple-element.29.message), channel_id=1, source_target_pairs={{0,16},{1,17},{2,18},{3,19},{4,20},{5,21},{6,22},{7,23},{8,24},{9,... | collective-permute-start | bytes 663560 | tf_op jit(solution)/shard_map/ppermute | solution.py:48
  3.9 20.9 %copy-start.1 = (bf16[144,768]{1,0:T(8,128)(2,1)S(1)}, bf16[144,768]{1,0:T(8,128)(2,1)}, u32[]{:S(2)}) copy-start(bf16[144,768]{1,0:T(8,128)(2,1)} %get-tuple-element.29.message) | copy-start | bytes 663556
  3.9 8.8 %collective-permute-start = (bf16[48,1152]{1,0:T(8,128)(2,1)}, bf16[48,1152]{1,0:T(8,128)(2,1)S(1)}, u32[]{:S(2)}, u32[]{:S(2)}) collective-permute-start(bf16[48,1152]{1,0:T(8,128)(2,1)} %get-tuple-element.31.own), channel_id=1, source_target_pairs={{0,4},{1,5},{2,6},{3,7},{4,0},{5,1},{6,2},{7,3},{8,12},{9,13},{10,... | collective-permute-start | bytes 331784 | tf_op jit(solution)/shard_map/ppermute | solution.py:48
  5.2 7.5 %collective-permute-start.1 = (bf16[48,1152]{1,0:T(8,128)(2,1)}, bf16[48,1152]{1,0:T(8,128)(2,1)S(1)}, u32[]{:S(2)}, u32[]{:S(2)}) collective-permute-start(bf16[48,1152]{1,0:T(8,128)(2,1)} %get-tuple-element.31.own), channel_id=1, source_target_pairs={{0,8},{1,9},{2,10},{3,11},{4,12},{5,13},{6,14},{7,15},{8,0},{9,1},... | collective-permute-start | bytes 331784 | tf_op jit(solution)/shard_map/ppermute | solution.py:48
  7.5 7.0 %collective-permute-start.2 = (bf16[48,1152]{1,0:T(8,128)(2,1)}, bf16[48,1152]{1,0:T(8,128)(2,1)S(1)}, u32[]{:S(2)}, u32[]{:S(2)}) collective-permute-start(bf16[48,1152]{1,0:T(8,128)(2,1)} %get-tuple-element.31.own), channel_id=1, source_target_pairs={{0,12},{1,13},{2,14},{3,15},{4,8},{5,9},{6,10},{7,11},{8,4},{9,5},... | collective-permute-start | bytes 331784 | tf_op jit(solution)/shard_map/ppermute | solution.py:48
  10.7 0.9 %copy-start = (bf16[144,768]{1,0:T(8,128)(2,1)S(1)}, bf16[144,768]{1,0:T(8,128)(2,1)}, u32[]{:S(2)}) copy-start(bf16[144,768]{1,0:T(8,128)(2,1)} %get-tuple-element.29.message) | copy-start | bytes 663556
  14.7 10.2 %collective-permute-start.6 = (bf16[144,768]{1,0:T(8,128)(2,1)S(1)}, bf16[144,768]{1,0:T(8,128)(2,1)S(1)}, u32[]{:S(2)}, u32[]{:S(2)}) collective-permute-start(bf16[144,768]{1,0:T(8,128)(2,1)S(1)} %get-tuple-element.36.x_block), channel_id=1, source_target_pairs={{0,16},{1,17},{2,18},{3,19},{4,20},{5,21},{6,22},{7,23},{8,24},{9,... | collective-permute-start | bytes 663560 | tf_op jit(solution)/shard_map/ppermute | solution.py:48
  15.0 9.9 %collective-permute-start.5 = (bf16[4,48,576]{2,1,0:T(8,128)(2,1)S(1)}, bf16[4,48,576]{2,1,0:T(8,128)(2,1)S(1)}, u32[]{:S(2)}, u32[]{:S(2)}) collective-permute-start(bf16[4,48,576]{2,1,0:T(8,128)(2,1)S(1)} %get-tuple-element.35), channel_id=1, source_target_pairs={{0,2},{1,3},{2,0},{3,1},{4,6},{5,7},{6,4},{7,5},{8,10},{9,11},{10,... | collective-permute-start | bytes 663560 | tf_op jit(solution)/shard_map/ppermute | solution.py:48
  16.2 4.9 %collective-permute-start.7 = (bf16[48,768]{1,0:T(8,128)(2,1)S(1)}, bf16[48,768]{1,0:T(8,128)(2,1)S(1)}, u32[]{:S(2)}, u32[]{:S(2)}) collective-permute-start(bf16[48,768]{1,0:T(8,128)(2,1)S(1)} %get-tuple-element.37.own), channel_id=1, source_target_pairs={{0,4},{1,5},{2,6},{3,7},{4,0},{5,1},{6,2},{7,3},{8,12},{9,13},{10,... | collective-permute-start | bytes 221192 | tf_op jit(solution)/shard_map/ppermute | solution.py:48
  19.0 5.0 %collective-permute-start.8 = (bf16[48,768]{1,0:T(8,128)(2,1)S(1)}, bf16[48,768]{1,0:T(8,128)(2,1)S(1)}, u32[]{:S(2)}, u32[]{:S(2)}) collective-permute-start(bf16[48,768]{1,0:T(8,128)(2,1)S(1)} %get-tuple-element.37.own), channel_id=1, source_target_pairs={{0,8},{1,9},{2,10},{3,11},{4,12},{5,13},{6,14},{7,15},{8,0},{9,1},... | collective-permute-start | bytes 221192 | tf_op jit(solution)/shard_map/ppermute | solution.py:48
  19.8 5.1 %collective-permute-start.9 = (bf16[48,768]{1,0:T(8,128)(2,1)S(1)}, bf16[48,768]{1,0:T(8,128)(2,1)S(1)}, u32[]{:S(2)}, u32[]{:S(2)}) collective-permute-start(bf16[48,768]{1,0:T(8,128)(2,1)S(1)} %get-tuple-element.37.own), channel_id=1, source_target_pairs={{0,12},{1,13},{2,14},{3,15},{4,8},{5,9},{6,10},{7,11},{8,4},{9,5},... | collective-permute-start | bytes 221192 | tf_op jit(solution)/shard_map/ppermute | solution.py:48
  25.0 7.3 %collective-permute-start.10 = (bf16[4,144,768]{2,1,0:T(8,128)(2,1)S(1)}, bf16[4,144,768]{2,1,0:T(8,128)(2,1)S(1)}, u32[]{:S(2)}, u32[]{:S(2)}) collective-permute-start(bf16[4,144,768]{2,1,0:T(8,128)(2,1)S(1)} %get-tuple-element.38.refs_0_), channel_id=1, source_target_pairs={{0,1},{1,0},{2,3},{3,2},{4,5},{5,4},{6,7},{7,6},{8,9},{9,8},{10,11... | collective-permute-start | bytes 2654216 | tf_op jit(solution)/shard_map/ppermute | solution.py:52
  29.6 2.8 %collective-permute-start.11 = (bf16[2,4,48,576]{3,2,1,0:T(8,128)(2,1)S(1)}, bf16[2,4,48,576]{3,2,1,0:T(8,128)(2,1)S(1)}, u32[]{:S(2)}, u32[]{:S(2)}) collective-permute-start(bf16[2,4,48,576]{3,2,1,0:T(8,128)(2,1)S(1)} %get-tuple-element.39.refs_2_), channel_id=1, source_target_pairs={{0,1},{1,0},{2,3},{3,2},{4,5},{5,4},{6,7},{7,6},{8,9},{9,8},{10,11... | collective-permute-start | bytes 1327112 | tf_op jit(solution)/shard_map/ppermute | solution.py:52
  29.6 8.2 %collective-permute-start.15 = (bf16[4,48,768]{2,1,0:T(8,128)(2,1)S(1)}, bf16[4,48,768]{2,1,0:T(8,128)(2,1)S(1)}, u32[]{:S(2)}, u32[]{:S(2)}) collective-permute-start(bf16[4,48,768]{2,1,0:T(8,128)(2,1)S(1)} %get-tuple-element.44.mine), channel_id=1, source_target_pairs={{0,2},{1,3},{2,0},{3,1},{4,6},{5,7},{6,4},{7,5},{8,10},{9,11},{10,... | collective-permute-start | bytes 884744 | tf_op jit(solution)/shard_map/ppermute | solution.py:48
  35.6 6.2 %copy-start.5 = (f32[768]{0:T(1024)S(1)}, f32[768]{0:T(1024)}, u32[]{:S(2)}) copy-start(f32[768]{0:T(1024)} %param.16) | copy-start | bytes 9220
  37.8 4.0 %collective-permute-start.16 = (bf16[2,4,48,768]{3,2,1,0:T(8,128)(2,1)S(1)}, bf16[2,4,48,768]{3,2,1,0:T(8,128)(2,1)S(1)}, u32[]{:S(2)}, u32[]{:S(2)}) collective-permute-start(bf16[2,4,48,768]{3,2,1,0:T(8,128)(2,1)S(1)} %shard_map.114.mine), channel_id=1, source_target_pairs={{0,1},{1,0},{2,3},{3,2},{4,5},{5,4},{6,7},{7,6},{8,9},{9,8},{10,11... | collective-permute-start | bytes 1769480 | tf_op jit(solution)/shard_map/ppermute | solution.py:52
  39.2 5.1 %collective-permute-start.12 = (bf16[2,128,192]{2,1,0:T(8,128)(2,1)S(1)}, bf16[2,128,192]{2,1,0:T(8,128)(2,1)S(1)}, u32[]{:S(2)}, u32[]{:S(2)}) collective-permute-start(bf16[2,128,192]{2,1,0:T(8,128)(2,1)S(1)} %get-tuple-element.41), channel_id=1, source_target_pairs={{0,2},{1,3},{2,0},{3,1},{4,6},{5,7},{6,4},{7,5},{8,10},{9,11},{10,... | collective-permute-start | bytes 294920 | tf_op jit(solution)/shard_map/ppermute | solution.py:48
  39.4 4.8 %collective-permute-start.13 = (bf16[2,128,192]{2,1,0:T(8,128)(2,1)S(1)}, bf16[2,128,192]{2,1,0:T(8,128)(2,1)S(1)}, u32[]{:S(2)}, u32[]{:S(2)}) collective-permute-start(bf16[2,128,192]{2,1,0:T(8,128)(2,1)S(1)} %get-tuple-element.42), channel_id=1, source_target_pairs={{0,16},{1,17},{2,18},{3,19},{4,20},{5,21},{6,22},{7,23},{8,24},{9,... | collective-permute-start | bytes 294920 | tf_op jit(solution)/shard_map/ppermute | solution.py:48
  40.7 7.3 %collective-permute-start.14 = (bf16[2,128,192]{2,1,0:T(8,128)(2,1)S(1)}, bf16[2,128,192]{2,1,0:T(8,128)(2,1)S(1)}, u32[]{:S(2)}, u32[]{:S(2)}) collective-permute-start(bf16[2,128,192]{2,1,0:T(8,128)(2,1)S(1)} %get-tuple-element.43), channel_id=1, source_target_pairs={{0,18},{1,19},{2,16},{3,17},{4,22},{5,23},{6,20},{7,21},{8,26},{9,... | collective-permute-start | bytes 294920 | tf_op jit(solution)/shard_map/ppermute | solution.py:48
  42.0 7.9 %copy-start.2 = (bf16[128,768]{1,0:T(8,128)(2,1)S(1)}, bf16[128,768]{1,0:T(8,128)(2,1)}, u32[]{:S(2)}) copy-start(bf16[128,768]{1,0:T(8,128)(2,1)} %get-tuple-element.48.tokens) | copy-start | bytes 589828
  48.6 7.5 %collective-permute-start.17 = (bf16[128,768]{1,0:T(8,128)(2,1)S(1)}, bf16[128,768]{1,0:T(8,128)(2,1)S(1)}, u32[]{:S(2)}, u32[]{:S(2)}) collective-permute-start(bf16[128,768]{1,0:T(8,128)(2,1)S(1)} %shard_map.116.other_in), channel_id=1, source_target_pairs={{0,4},{1,5},{4,8},{5,9},{6,2},{7,3},{8,12},{9,13},{10,6},{11,7},{1... | collective-permute-start | bytes 589832 | tf_op jit(solution)/shard_map/ppermute | solution.py:48
  56.7 2.9 %collective-permute-start.18 = (bf16[128,768]{1,0:T(8,128)(2,1)S(1)}, bf16[128,768]{1,0:T(8,128)(2,1)S(1)}, u32[]{:S(2)}, u32[]{:S(2)}) collective-permute-start(bf16[128,768]{1,0:T(8,128)(2,1)S(1)} %get-tuple-element.52), channel_id=1, source_target_pairs={{0,1},{1,0},{2,3},{3,2},{4,5},{5,4},{6,7},{7,6},{8,9},{9,8},{10,11... | collective-permute-start | bytes 589832 | tf_op jit(solution)/shard_map/ppermute | solution.py:52

commit v9 on v7

--- a/solution.py
+++ b/solution.py
@@ -114,18 +114,18 @@
         message[count + 16 :, : cross.shape[1]] = cross
 
 
-def columns_body(w_qkv, gains, own):
-    del gains
+def columns_body(w_qkv, w_out, own, out_own):
     half = own.shape[0]
     start = pl.multiple_of(lax.axis_index("lon") * half, half)
     rows = w_qkv[pl.ds(start, half), :]
     own[...] = pick_columns(rows, lax.rem(lax.axis_index("lat"), 2), own.shape[1] // 3)
+    out_own[...] = w_out[pl.ds(start, half), :]
 
 
 def arrived_body(
-    own, by_x, by_y, out_own, out1, out2, out3, gains, bundle, x_block, outs
+    own, by_x, by_y, out_own, out1, out2, out3, bundle, x_block, outs
 ):
-    del by_y, gains
+    del by_y
     side = lax.rem(lax.axis_index("lat"), 2)
     rows, width = x_block.shape[0], own.shape[1]
     bundle[side] = own[...]
@@ -136,8 +136,10 @@
 
 
 def complete_body(
-    bundle, level1, level2, level3, message, x_block, by_y, by_xy, outs, crossed, weights, near, both
+    bundle, level1, level2, level3, message, x_block, by_y, by_xy, outs, crossed, gains, *results
 ):
+    del gains
+    weights, near, both = results
     rows = x_block.shape[0]
     for at, block in enumerate((bundle, level1, level2, level3)):
         weights[at] = block[...]
@@ -427,6 +429,28 @@
         limit=56,
     )
 
+    by_x, by_y = flip_chips(message, 1, 0), flip_chips(message, 0, 1)
+    x_block = by_x
+    if direct:
+        levels = flip_levels(out_own)
+        qkv_own, out_own = call(
+            columns_body,
+            [((half, 3 * quarter), BF16), ((half, width), BF16)],
+            [VMEM] * 2,
+            (w_qkv, w_out),
+            0,
+        )
+        bundle, x_block, outs = call(
+            arrived_body,
+            [
+                ((2, half, 3 * quarter), BF16),
+                ((rows, width), BF16),
+                ((4, half, width), BF16),
+            ],
+            [VMEM] * 7,
+            (qkv_own, by_x, by_y, out_own, *levels),
+            0,
+        )
     size = 4 * w_conv.shape[2]
     diagonal, coeffs, gains = call(
         functools.partial(plan_body, lat_count),
@@ -436,25 +460,10 @@
             ((8, 128), F32),
         ],
         [SMEM] * 4 + [VMEM, ANY],
-        (lon_half, lat_half, quad_off, lat_taps, w_conv, message),
+        (lon_half, lat_half, quad_off, lat_taps, w_conv, x_block),
         0,
     )
-    by_x, by_y = flip_chips(message, 1, 0), flip_chips(message, 0, 1)
     if direct:
-        (qkv_own,) = call(
-            columns_body, [((half, 3 * quarter), BF16)], [VMEM] * 2, (w_qkv, gains), 0
-        )
-        bundle, x_block, outs = call(
-            arrived_body,
-            [
-                ((2, half, 3 * quarter), BF16),
-                ((rows, width), BF16),
-                ((4, half, width), BF16),
-            ],
-            [VMEM] * 8,
-            (qkv_own, by_x, by_y, out_own, *flip_levels(out_own), gains),
-            0,
-        )
         qkv_mine, near, out_mine = call(
             complete_body,
             [
@@ -462,7 +471,7 @@
                 ((4, rows, width), BF16),
                 ((2, 4, half, width), BF16),
             ],
-            [VMEM] * 10,
+            [VMEM] * 11,
             (
                 bundle,
                 *flip_levels(bundle),
@@ -472,6 +481,7 @@
                 flip_chips(x_block, 0, 1),
                 outs,
                 flip_chips(outs, 1, 0),
+                gains,
             ),
             0,
         )

time: 57.1 us -> 56.3 us (0.986)
  waiting for transfers between devices: 20.2 us -> 18.9 us
  starting transfers between devices: 21.2 us -> 22.2 us
  local copies, waits for them, and re-layouts: 2.89 us -> 2.25 us
    ppermute x15, waiting for transfers between devices: 17.2 us -> 15.9 us  [move(): return lax.ppermute(values, AXES, device_pairs(target))]
    ppermute x4, starting transfers between devices: 6.67 us -> 7.54 us  [swap_cores(): return lax.ppermute(values, 'lon', [(0, 1), (1, 0)])]
    unnamed x14 -> x16, local copies, waits for them, and re-layouts: 2.89 us -> 2.25 us
  transfers between devices with their start and end apart: 19 -> 19, of which waited for: 8 -> 8; matrix products, arithmetic and copies ran while one was open for 3% -> 1% of each run, Pallas kernels for 11% -> 11%
where the time goes in v9:
time: 56.3 us; the launch traced here: 55.7 us
  starting transfers between devices  22.2 us (39%)
  waiting for transfers between devices  18.9 us (34%)
  Pallas kernels  9.51 us (17%)
  local copies, waits for them, and re-layouts  2.25 us (4%)
  between operations  2.12 us (4%)
  other arithmetic  0.71 us (1%)
    ppermute x15, waiting for transfers between devices, move(): return lax.ppermute(values, AXES, device_pairs(target))  15.9 us
    ppermute x15, starting transfers between devices, move(): return lax.ppermute(values, AXES, device_pairs(target))  14.7 us
    pallas_call x11, Pallas kernels, call(): pl.pallas_call(body, out_shape=outs, in_specs=specs, out_specs=tuple((VME...  9.51 us
    ppermute x4, starting transfers between devices, swap_cores(): return lax.ppermute(values, 'lon', [(0, 1), (1, 0)])  7.54 us
    ppermute x4, waiting for transfers between devices, swap_cores(): return lax.ppermute(values, 'lon', [(0, 1), (1, 0)])  2.95 us
    unnamed x16, local copies, waits for them, and re-layouts  2.25 us
  transfers between devices with their start and end apart: 19, of which 8 were waited for; matrix products, arithmetic and copies ran while one was open for 1% of the time, Pallas kernels for 11%

profile of v9, /device:TPU:3, one launch (start us, length us, event | category | flops | bytes accessed | tf_op | source)
XLA Modules:
  0.0 55.7 jit_solution(6010208280367575776)
XLA Ops:
  0.0 2.1 %shard_map.110 = (bf16[192,768]{1,0:T(8,128)(2,1)}, bf16[128,768]{1,0:T(8,128)(2,1)}, bf16[48,768]{1,0:T(8,128)(2,1)}) custom-call(bf16[128,768]{1,0:T(8,128)(2,1)} %bitcast.4, bf16[12,128]{1,0:T(8,128)(2,1)} %bitcast.5, f32[768]{0:T(1024)} %refs_2_.1, bf16[96,2304]{1,0:T(8,128)(2,1)} %refs_3_.1, bf16[96,768]{1,0:T(8,128)(2,1)} %refs_4_.1), custom_call_target="tpu_custom_call" | custom-call | flops 983040 | bytes 792576 | tf_op jit(solution)/shard_map/pallas_call | solution.py:23
  2.1 0.1 collective-permute-start
  2.2 1.5 %collective-permute-start.1 = (bf16[192,768]{1,0:T(8,128)(2,1)}, bf16[192,768]{1,0:T(8,128)(2,1)S(1)}, u32[]{:S(2)}, u32[]{:S(2)}) collective-permute-start(bf16[192,768]{1,0:T(8,128)(2,1)} %get-tuple-element.28.message), channel_id=1, source_target_pairs={{0,16},{1,17},{2,18},{3,19},{4,20},{5,21},{6,22},{7,23},{8,24},{9,... | collective-permute-start | bytes 884744 | tf_op jit(solution)/shard_map/ppermute | solution.py:57
  3.7 1.3 %collective-permute-start.2 = (bf16[48,768]{1,0:T(8,128)(2,1)}, bf16[48,768]{1,0:T(8,128)(2,1)S(1)}, u32[]{:S(2)}, u32[]{:S(2)}) collective-permute-start(bf16[48,768]{1,0:T(8,128)(2,1)} %get-tuple-element.30), channel_id=1, source_target_pairs={{0,4},{1,5},{2,6},{3,7},{4,0},{5,1},{6,2},{7,3},{8,12},{9,13},{10,... | collective-permute-start | bytes 221192 | tf_op jit(solution)/shard_map/ppermute | solution.py:57
  5.0 2.3 %collective-permute-start.3 = (bf16[48,768]{1,0:T(8,128)(2,1)}, bf16[48,768]{1,0:T(8,128)(2,1)S(1)}, u32[]{:S(2)}, u32[]{:S(2)}) collective-permute-start(bf16[48,768]{1,0:T(8,128)(2,1)} %get-tuple-element.30), channel_id=1, source_target_pairs={{0,8},{1,9},{2,10},{3,11},{4,12},{5,13},{6,14},{7,15},{8,0},{9,1},... | collective-permute-start | bytes 221192 | tf_op jit(solution)/shard_map/ppermute | solution.py:57
  7.3 0.0 collective-permute-start.4
  7.3 1.0 %copy-done = bf16[96,2304]{1,0:T(8,128)(2,1)S(1)} copy-done((bf16[96,2304]{1,0:T(8,128)(2,1)S(1)}, bf16[96,2304]{1,0:T(8,128)(2,1)}, u32[]{:S(2)}) %copy-start) | copy-done | bytes 442392
  8.3 0.9 %copy-done.1 = bf16[96,768]{1,0:T(8,128)(2,1)S(1)} copy-done((bf16[96,768]{1,0:T(8,128)(2,1)S(1)}, bf16[96,768]{1,0:T(8,128)(2,1)}, u32[]{:S(2)}) %copy-start.1) | copy-done | bytes 147480
  9.2 0.2 shard_map.109
  9.4 0.0 collective-permute-done.2.out1
  9.4 0.7 %collective-permute-done.3.out2 = bf16[48,768]{1,0:T(8,128)(2,1)S(1)} collective-permute-done((bf16[48,768]{1,0:T(8,128)(2,1)}, bf16[48,768]{1,0:T(8,128)(2,1)S(1)}, u32[]{:S(2)}, u32[]{:S(2)}) %collective-permute-start.3) | collective-permute-done | bytes 73760 | tf_op jit(solution)/shard_map/ppermute | solution.py:57
  10.1 2.4 %collective-permute-done.4.out3 = bf16[48,768]{1,0:T(8,128)(2,1)S(1)} collective-permute-done((bf16[48,768]{1,0:T(8,128)(2,1)}, bf16[48,768]{1,0:T(8,128)(2,1)S(1)}, u32[]{:S(2)}, u32[]{:S(2)}) %collective-permute-start.4) | collective-permute-done | bytes 73760 | tf_op jit(solution)/shard_map/ppermute | solution.py:57
  12.5 0.0 collective-permute-done.1.by_y
  12.6 1.3 %collective-permute-start.9 = (bf16[4,48,768]{2,1,0:T(8,128)(2,1)S(1)}, bf16[4,48,768]{2,1,0:T(8,128)(2,1)S(1)}, u32[]{:S(2)}, u32[]{:S(2)}) collective-permute-start(bf16[4,48,768]{2,1,0:T(8,128)(2,1)S(1)} %get-tuple-element.34.outs), channel_id=1, source_target_pairs={{0,2},{1,3},{2,0},{3,1},{4,6},{5,7},{6,4},{7,5},{8,10},{9,11},{10,... | collective-permute-start | bytes 884744 | tf_op jit(solution)/shard_map/ppermute | solution.py:57
  13.9 0.2 collective-permute-start.8
  14.1 0.9 %collective-permute-start.5 = (bf16[2,48,576]{2,1,0:T(8,128)(2,1)S(1)}, bf16[2,48,576]{2,1,0:T(8,128)(2,1)S(1)}, u32[]{:S(2)}, u32[]{:S(2)}) collective-permute-start(bf16[2,48,576]{2,1,0:T(8,128)(2,1)S(1)} %get-tuple-element.33.bundle), channel_id=1, source_target_pairs={{0,4},{1,5},{2,6},{3,7},{4,0},{5,1},{6,2},{7,3},{8,12},{9,13},{10,... | collective-permute-start | bytes 331784 | tf_op jit(solution)/shard_map/ppermute | solution.py:57
  15.0 1.6 %collective-permute-start.6 = (bf16[2,48,576]{2,1,0:T(8,128)(2,1)S(1)}, bf16[2,48,576]{2,1,0:T(8,128)(2,1)S(1)}, u32[]{:S(2)}, u32[]{:S(2)}) collective-permute-start(bf16[2,48,576]{2,1,0:T(8,128)(2,1)S(1)} %get-tuple-element.33.bundle), channel_id=1, source_target_pairs={{0,8},{1,9},{2,10},{3,11},{4,12},{5,13},{6,14},{7,15},{8,0},{9,1},... | collective-permute-start | bytes 331784 | tf_op jit(solution)/shard_map/ppermute | solution.py:57
  16.6 1.2 %collective-permute-start.7 = (bf16[2,48,576]{2,1,0:T(8,128)(2,1)S(1)}, bf16[2,48,576]{2,1,0:T(8,128)(2,1)S(1)}, u32[]{:S(2)}, u32[]{:S(2)}) collective-permute-start(bf16[2,48,576]{2,1,0:T(8,128)(2,1)S(1)} %get-tuple-element.33.bundle), channel_id=1, source_target_pairs={{0,12},{1,13},{2,14},{3,15},{4,8},{5,9},{6,10},{7,11},{8,4},{9,5},... | collective-permute-start | bytes 331784 | tf_op jit(solution)/shard_map/ppermute | solution.py:57
  19.7 0.1 copy.12.taps
  19.8 0.2 copy.13.w_conv
  20.1 1.0 %shard_map.112 = (bf16[2,3,256,256]{3,2,1,0:T(8,128)(2,1)S(1)}, bf16[256,512]{1,0:T(8,128)(2,1)S(1)}, f32[8,128]{1,0:T(8,128)S(1)}) custom-call(s32[1]{0:T(128)S(6)} %copy.14.lon_half, s32[1]{0:T(128)S(6)} %copy.15.lat_half, s32[1]{0:T(128)S(6)} %copy.16.quad_off, f32[16,2]{1,0:T(8,128)S(1)} %copy.12.taps, bf16[2,768,64]{2,1,0:T(8,128)(2,1)S(1)} %copy.13.w_conv, ...), custom_call_target="tpu_custom_call" | custom-call | bytes 417932 | tf_op jit(solution)/shard_map/pallas_call | solution.py:23
  21.1 0.0 copy-start.3
  21.1 0.0 collective-permute-done.6.level2
  21.1 2.6 %collective-permute-done.7.level3 = bf16[2,48,576]{2,1,0:T(8,128)(2,1)S(1)} collective-permute-done((bf16[2,48,576]{2,1,0:T(8,128)(2,1)S(1)}, bf16[2,48,576]{2,1,0:T(8,128)(2,1)S(1)}, u32[]{:S(2)}, u32[]{:S(2)}) %collective-permute-start.7) | collective-permute-done | bytes 110624 | tf_op jit(solution)/shard_map/ppermute | solution.py:57
  23.7 0.0 collective-permute-done.8.by_xy
  23.7 0.0 collective-permute-done.9.crossed
  23.7 0.1 shard_map.113
  23.9 5.0 %collective-permute-start.10 = (bf16[4,144,768]{2,1,0:T(8,128)(2,1)S(1)}, bf16[4,144,768]{2,1,0:T(8,128)(2,1)S(1)}, u32[]{:S(2)}, u32[]{:S(2)}) collective-permute-start(bf16[4,144,768]{2,1,0:T(8,128)(2,1)S(1)} %get-tuple-element.35.refs_0_), channel_id=1, source_target_pairs={{0,1},{1,0},{2,3},{3,2},{4,5},{5,4},{6,7},{7,6},{8,9},{9,8},{10,11... | collective-permute-start | bytes 2654216 | tf_op jit(solution)/shard_map/ppermute | solution.py:61
  28.9 0.1 collective-permute-start.11
  28.9 0.4 collective-permute-start.15
  29.4 0.0 copy-start.5
  29.4 0.3 collective-permute-start.16
  29.7 1.9 %collective-permute-done.11.refs_3_ = bf16[4,2,48,576]{3,2,1,0:T(8,128)(2,1)S(1)} collective-permute-done((bf16[4,2,48,576]{3,2,1,0:T(8,128)(2,1)S(1)}, bf16[4,2,48,576]{3,2,1,0:T(8,128)(2,1)S(1)}, u32[]{:S(2)}, u32[]{:S(2)}) %collective-permute-start.11) | collective-permute-done | bytes 442400 | tf_op jit(solution)/shard_map/ppermute | solution.py:61
  31.6 3.3 %shard_map.114 = (bf16[2,128,192]{2,1,0:T(8,128)(2,1)S(1)}, bf16[2,128,192]{2,1,0:T(8,128)(2,1)S(1)}, bf16[2,128,192]{2,1,0:T(8,128)(2,1)S(1)}, bf16[2,128,192]{2,1,0:T(8,128)(2,1)S(1)}) custom-call(bf16[4,144,768]{2,1,0:T(8,128)(2,1)S(1)} %get-tuple-element.35.refs_0_, bf16[4,144,768]{2,1,0:T(8,128)(2,1)S(1)} %collective-permute-done.10.refs_1_, ...), custom_call_target="tpu_custom_call" | custom-call | flops 905969664 | bytes 2654208 | tf_op jit(solution)/shard_map/pallas_call | solution.py:23
  34.9 0.3 collective-permute-start.12
  35.2 1.0 %collective-permute-start.13 = (bf16[2,128,192]{2,1,0:T(8,128)(2,1)S(1)}, bf16[2,128,192]{2,1,0:T(8,128)(2,1)S(1)}, u32[]{:S(2)}, u32[]{:S(2)}) collective-permute-start(bf16[2,128,192]{2,1,0:T(8,128)(2,1)S(1)} %get-tuple-element.39), channel_id=1, source_target_pairs={{0,16},{1,17},{2,18},{3,19},{4,20},{5,21},{6,22},{7,23},{8,24},{9,... | collective-permute-start | bytes 294920 | tf_op jit(solution)/shard_map/ppermute | solution.py:57
  36.3 1.4 %collective-permute-start.14 = (bf16[2,128,192]{2,1,0:T(8,128)(2,1)S(1)}, bf16[2,128,192]{2,1,0:T(8,128)(2,1)S(1)}, u32[]{:S(2)}, u32[]{:S(2)}) collective-permute-start(bf16[2,128,192]{2,1,0:T(8,128)(2,1)S(1)} %get-tuple-element.40), channel_id=1, source_target_pairs={{0,18},{1,19},{2,16},{3,17},{4,22},{5,23},{6,20},{7,21},{8,26},{9,... | collective-permute-start | bytes 294920 | tf_op jit(solution)/shard_map/ppermute | solution.py:57
  37.6 0.1 shard_map.115.weights
  37.8 1.9 %collective-permute-done.12.piece1 = bf16[2,128,192]{2,1,0:T(8,128)(2,1)S(1)} collective-permute-done((bf16[2,128,192]{2,1,0:T(8,128)(2,1)S(1)}, bf16[2,128,192]{2,1,0:T(8,128)(2,1)S(1)}, u32[]{:S(2)}, u32[]{:S(2)}) %collective-permute-start.12) | collective-permute-done | bytes 98336 | tf_op jit(solution)/shard_map/ppermute | solution.py:57
  39.7 3.5 %collective-permute-done.14.piece3 = bf16[2,128,192]{2,1,0:T(8,128)(2,1)S(1)} collective-permute-done((bf16[2,128,192]{2,1,0:T(8,128)(2,1)S(1)}, bf16[2,128,192]{2,1,0:T(8,128)(2,1)S(1)}, u32[]{:S(2)}, u32[]{:S(2)}) %collective-permute-start.14) | collective-permute-done | bytes 98336 | tf_op jit(solution)/shard_map/ppermute | solution.py:57
  43.2 0.6 shard_map.117.other_in
  43.8 1.3 %collective-permute-start.17 = (bf16[128,768]{1,0:T(8,128)(2,1)S(1)}, bf16[128,768]{1,0:T(8,128)(2,1)S(1)}, u32[]{:S(2)}, u32[]{:S(2)}) collective-permute-start(bf16[128,768]{1,0:T(8,128)(2,1)S(1)} %shard_map.117.other_in), channel_id=1, source_target_pairs={{0,4},{1,5},{4,8},{5,9},{6,2},{7,3},{8,12},{9,13},{10,6},{11,7},{1... | collective-permute-start | bytes 589832 | tf_op jit(solution)/shard_map/ppermute | solution.py:57
  45.1 1.4 %shard_map.118 = (bf16[128,768]{1,0:T(8,128)(2,1)S(1)}, f32[256,768]{1,0:T(8,128)S(1)}) custom-call(f32[8,128]{1,0:T(8,128)S(1)} %get-tuple-element.32.gains, f32[1,768]{1,0:T(1,128)S(1)} %broadcast_in_dim.6.gain, bf16[2,128,192]{2,1,0:T(8,128)(2,1)S(1)} %get-tuple-element.37.piece0, bf16[2,128,192]{2,1,0:T(8,128)(2,1)S(1)} %collective-permute-done.12.piece1, ...), custom_call_target="tpu_custom_call" | custom-call | flops 452984832 | bytes 3021824 | tf_op jit(solution)/shard_map/pallas_call | solution.py:23
  46.5 4.7 %collective-permute-done.17.halo = bf16[128,768]{1,0:T(8,128)(2,1)S(1)} collective-permute-done((bf16[128,768]{1,0:T(8,128)(2,1)S(1)}, bf16[128,768]{1,0:T(8,128)(2,1)S(1)}, u32[]{:S(2)}, u32[]{:S(2)}) %collective-permute-start.17) | collective-permute-done | bytes 196640 | tf_op jit(solution)/shard_map/ppermute | solution.py:57
  51.2 0.7 %shard_map.119 = (f32[128,768]{1,0:T(8,128)S(1)}, bf16[128,768]{1,0:T(8,128)(2,1)S(1)}) custom-call(f32[8,128]{1,0:T(8,128)S(1)} %get-tuple-element.32.gains, bf16[128,768]{1,0:T(8,128)(2,1)S(1)} %collective-permute-done.17.halo, bf16[2,3,256,256]{3,2,1,0:T(8,128)(2,1)S(1)} %get-tuple-element.43.blocks, bf16[256,512]{1,0:T(8,128)(2,1)S(1)} %get-tuple-element.44.coeffs, ...), custom_call_target="tpu_custom_call" | custom-call | flops 100663296 | bytes 2232320 | tf_op jit(solution)/shard_map/pallas_call | solution.py:23
  51.8 2.1 %collective-permute-start.18 = (bf16[128,768]{1,0:T(8,128)(2,1)S(1)}, bf16[128,768]{1,0:T(8,128)(2,1)S(1)}, u32[]{:S(2)}, u32[]{:S(2)}) collective-permute-start(bf16[128,768]{1,0:T(8,128)(2,1)S(1)} %get-tuple-element.48), channel_id=1, source_target_pairs={{0,1},{1,0},{2,3},{3,2},{4,5},{5,4},{6,7},{7,6},{8,9},{9,8},{10,11... | collective-permute-start | bytes 589832 | tf_op jit(solution)/shard_map/ppermute | solution.py:61
  53.9 1.1 %collective-permute-done.18 = bf16[128,768]{1,0:T(8,128)(2,1)S(1)} collective-permute-done((bf16[128,768]{1,0:T(8,128)(2,1)S(1)}, bf16[128,768]{1,0:T(8,128)(2,1)S(1)}, u32[]{:S(2)}, u32[]{:S(2)}) %collective-permute-start.18) | collective-permute-done | bytes 196640 | tf_op jit(solution)/shard_map/ppermute | solution.py:61
  55.0 0.7 %fusion = bf16[1,128,768]{2,1,0:T(8,128)(2,1)} fusion(f32[128,768]{1,0:T(8,128)S(1)} %get-tuple-element.47, bf16[128,768]{1,0:T(8,128)(2,1)S(1)} %collective-permute-done.18), kind=kLoop, calls=%fused_computation.1 | loop fusion | flops 294912 | bytes 786432 | tf_op jit(solution)/shard_map/broadcast_in_dim | solution.py:542
  (19 shorter events, 0.1 us)
Async XLA Ops:
  0.0 19.7 %copy-start.6 = (f32[16,2]{0,1:T(2,128)S(1)}, f32[16,2]{0,1:T(2,128)}, u32[]{:S(2)}) copy-start(f32[16,2]{0,1:T(2,128)} %param.18) | copy-start | bytes 388
  0.0 19.8 %copy-start.4 = (bf16[2,768,64]{1,2,0:T(8,128)(2,1)S(1)}, bf16[2,768,64]{1,2,0:T(8,128)(2,1)}, u32[]{:S(2)}) copy-start(bf16[2,768,64]{1,2,0:T(8,128)(2,1)} %param.17) | copy-start | bytes 589828
  2.1 10.4 %collective-permute-start = (bf16[192,768]{1,0:T(8,128)(2,1)}, bf16[192,768]{1,0:T(8,128)(2,1)S(1)}, u32[]{:S(2)}, u32[]{:S(2)}) collective-permute-start(bf16[192,768]{1,0:T(8,128)(2,1)} %get-tuple-element.28.message), channel_id=1, source_target_pairs={{0,2},{1,3},{2,0},{3,1},{4,6},{5,7},{6,4},{7,5},{8,10},{9,11},{10,... | collective-permute-start | bytes 884744 | tf_op jit(solution)/shard_map/ppermute | solution.py:57
  2.2 10.3 %collective-permute-start.1 = (bf16[192,768]{1,0:T(8,128)(2,1)}, bf16[192,768]{1,0:T(8,128)(2,1)S(1)}, u32[]{:S(2)}, u32[]{:S(2)}) collective-permute-start(bf16[192,768]{1,0:T(8,128)(2,1)} %get-tuple-element.28.message), channel_id=1, source_target_pairs={{0,16},{1,17},{2,18},{3,19},{4,20},{5,21},{6,22},{7,23},{8,24},{9,... | collective-permute-start | bytes 884744 | tf_op jit(solution)/shard_map/ppermute | solution.py:57
  3.7 5.7 %collective-permute-start.2 = (bf16[48,768]{1,0:T(8,128)(2,1)}, bf16[48,768]{1,0:T(8,128)(2,1)S(1)}, u32[]{:S(2)}, u32[]{:S(2)}) collective-permute-start(bf16[48,768]{1,0:T(8,128)(2,1)} %get-tuple-element.30), channel_id=1, source_target_pairs={{0,4},{1,5},{2,6},{3,7},{4,0},{5,1},{6,2},{7,3},{8,12},{9,13},{10,... | collective-permute-start | bytes 221192 | tf_op jit(solution)/shard_map/ppermute | solution.py:57
  5.0 5.1 %collective-permute-start.3 = (bf16[48,768]{1,0:T(8,128)(2,1)}, bf16[48,768]{1,0:T(8,128)(2,1)S(1)}, u32[]{:S(2)}, u32[]{:S(2)}) collective-permute-start(bf16[48,768]{1,0:T(8,128)(2,1)} %get-tuple-element.30), channel_id=1, source_target_pairs={{0,8},{1,9},{2,10},{3,11},{4,12},{5,13},{6,14},{7,15},{8,0},{9,1},... | collective-permute-start | bytes 221192 | tf_op jit(solution)/shard_map/ppermute | solution.py:57
  7.3 5.2 %collective-permute-start.4 = (bf16[48,768]{1,0:T(8,128)(2,1)}, bf16[48,768]{1,0:T(8,128)(2,1)S(1)}, u32[]{:S(2)}, u32[]{:S(2)}) collective-permute-start(bf16[48,768]{1,0:T(8,128)(2,1)} %get-tuple-element.30), channel_id=1, source_target_pairs={{0,12},{1,13},{2,14},{3,15},{4,8},{5,9},{6,10},{7,11},{8,4},{9,5},... | collective-permute-start | bytes 221192 | tf_op jit(solution)/shard_map/ppermute | solution.py:57
  7.3 1.0 %copy-start = (bf16[96,2304]{1,0:T(8,128)(2,1)S(1)}, bf16[96,2304]{1,0:T(8,128)(2,1)}, u32[]{:S(2)}) copy-start(bf16[96,2304]{1,0:T(8,128)(2,1)} %refs_3_.1) | copy-start | bytes 1327108
  8.3 0.9 %copy-start.1 = (bf16[96,768]{1,0:T(8,128)(2,1)S(1)}, bf16[96,768]{1,0:T(8,128)(2,1)}, u32[]{:S(2)}) copy-start(bf16[96,768]{1,0:T(8,128)(2,1)} %refs_4_.1) | copy-start | bytes 442372
  9.4 14.3 %copy-start.2 = (bf16[192,768]{1,0:T(8,128)(2,1)S(1)}, bf16[192,768]{1,0:T(8,128)(2,1)}, u32[]{:S(2)}) copy-start(bf16[192,768]{1,0:T(8,128)(2,1)} %get-tuple-element.28.message) | copy-start | bytes 884740
  12.6 11.1 %collective-permute-start.9 = (bf16[4,48,768]{2,1,0:T(8,128)(2,1)S(1)}, bf16[4,48,768]{2,1,0:T(8,128)(2,1)S(1)}, u32[]{:S(2)}, u32[]{:S(2)}) collective-permute-start(bf16[4,48,768]{2,1,0:T(8,128)(2,1)S(1)} %get-tuple-element.34.outs), channel_id=1, source_target_pairs={{0,2},{1,3},{2,0},{3,1},{4,6},{5,7},{6,4},{7,5},{8,10},{9,11},{10,... | collective-permute-start | bytes 884744 | tf_op jit(solution)/shard_map/ppermute | solution.py:57
  13.9 9.9 %collective-permute-start.8 = (bf16[144,768]{1,0:T(8,128)(2,1)S(1)}, bf16[144,768]{1,0:T(8,128)(2,1)S(1)}, u32[]{:S(2)}, u32[]{:S(2)}) collective-permute-start(bf16[144,768]{1,0:T(8,128)(2,1)S(1)} %get-tuple-element.31.message.x_block), channel_id=1, source_target_pairs={{0,16},{1,17},{2,18},{3,19},{4,20},{5,21},{6,22},{7,23},{8,24},{9,... | collective-permute-start | bytes 663560 | tf_op jit(solution)/shard_map/ppermute | solution.py:57
  14.1 7.0 %collective-permute-start.5 = (bf16[2,48,576]{2,1,0:T(8,128)(2,1)S(1)}, bf16[2,48,576]{2,1,0:T(8,128)(2,1)S(1)}, u32[]{:S(2)}, u32[]{:S(2)}) collective-permute-start(bf16[2,48,576]{2,1,0:T(8,128)(2,1)S(1)} %get-tuple-element.33.bundle), channel_id=1, source_target_pairs={{0,4},{1,5},{2,6},{3,7},{4,0},{5,1},{6,2},{7,3},{8,12},{9,13},{10,... | collective-permute-start | bytes 331784 | tf_op jit(solution)/shard_map/ppermute | solution.py:57
  15.0 6.1 %collective-permute-start.6 = (bf16[2,48,576]{2,1,0:T(8,128)(2,1)S(1)}, bf16[2,48,576]{2,1,0:T(8,128)(2,1)S(1)}, u32[]{:S(2)}, u32[]{:S(2)}) collective-permute-start(bf16[2,48,576]{2,1,0:T(8,128)(2,1)S(1)} %get-tuple-element.33.bundle), channel_id=1, source_target_pairs={{0,8},{1,9},{2,10},{3,11},{4,12},{5,13},{6,14},{7,15},{8,0},{9,1},... | collective-permute-start | bytes 331784 | tf_op jit(solution)/shard_map/ppermute | solution.py:57
  16.6 7.1 %collective-permute-start.7 = (bf16[2,48,576]{2,1,0:T(8,128)(2,1)S(1)}, bf16[2,48,576]{2,1,0:T(8,128)(2,1)S(1)}, u32[]{:S(2)}, u32[]{:S(2)}) collective-permute-start(bf16[2,48,576]{2,1,0:T(8,128)(2,1)S(1)} %get-tuple-element.33.bundle), channel_id=1, source_target_pairs={{0,12},{1,13},{2,14},{3,15},{4,8},{5,9},{6,10},{7,11},{8,4},{9,5},... | collective-permute-start | bytes 331784 | tf_op jit(solution)/shard_map/ppermute | solution.py:57
  21.1 8.3 %copy-start.3 = (bf16[128,768]{1,0:T(8,128)(2,1)S(1)}, bf16[128,768]{1,0:T(8,128)(2,1)}, u32[]{:S(2)}) copy-start(bf16[128,768]{1,0:T(8,128)(2,1)} %get-tuple-element.42.refs_0_) | copy-start | bytes 589828
  23.9 7.7 %collective-permute-start.10 = (bf16[4,144,768]{2,1,0:T(8,128)(2,1)S(1)}, bf16[4,144,768]{2,1,0:T(8,128)(2,1)S(1)}, u32[]{:S(2)}, u32[]{:S(2)}) collective-permute-start(bf16[4,144,768]{2,1,0:T(8,128)(2,1)S(1)} %get-tuple-element.35.refs_0_), channel_id=1, source_target_pairs={{0,1},{1,0},{2,3},{3,2},{4,5},{5,4},{6,7},{7,6},{8,9},{9,8},{10,11... | collective-permute-start | bytes 2654216 | tf_op jit(solution)/shard_map/ppermute | solution.py:61
  28.9 2.8 %collective-permute-start.11 = (bf16[4,2,48,576]{3,2,1,0:T(8,128)(2,1)S(1)}, bf16[4,2,48,576]{3,2,1,0:T(8,128)(2,1)S(1)}, u32[]{:S(2)}, u32[]{:S(2)}) collective-permute-start(bf16[4,2,48,576]{3,2,1,0:T(8,128)(2,1)S(1)} %get-tuple-element.36.refs_2_.refs_1_), channel_id=1, source_target_pairs={{0,1},{1,0},{2,3},{3,2},{4,5},{5,4},{6,7},{7,6},{8,9},{9,8},{10,11... | collective-permute-start | bytes 1327112 | tf_op jit(solution)/shard_map/ppermute | solution.py:61
  28.9 8.7 %collective-permute-start.15 = (bf16[2,4,48,768]{3,2,1,0:T(8,128)(2,1)S(1)}, bf16[2,4,48,768]{3,2,1,0:T(8,128)(2,1)S(1)}, u32[]{:S(2)}, u32[]{:S(2)}) collective-permute-start(bf16[2,4,48,768]{3,2,1,0:T(8,128)(2,1)S(1)} %get-tuple-element.41.mine), channel_id=1, source_target_pairs={{0,1},{1,0},{2,3},{3,2},{4,5},{5,4},{6,7},{7,6},{8,9},{9,8},{10,11... | collective-permute-start | bytes 1769480 | tf_op jit(solution)/shard_map/ppermute | solution.py:61
  29.4 8.2 %copy-start.5 = (f32[768]{0:T(1024)S(1)}, f32[768]{0:T(1024)}, u32[]{:S(2)}) copy-start(f32[768]{0:T(1024)} %param.16) | copy-start | bytes 9220
  29.4 8.3 %collective-permute-start.16 = (bf16[128,768]{1,0:T(8,128)(2,1)S(1)}, bf16[128,768]{1,0:T(8,128)(2,1)S(1)}, u32[]{:S(2)}, u32[]{:S(2)}) collective-permute-start(bf16[128,768]{1,0:T(8,128)(2,1)S(1)} %shard_map.116.tokens), channel_id=1, source_target_pairs={{0,2},{1,3},{2,0},{3,1},{4,6},{5,7},{6,4},{7,5},{8,10},{9,11},{10,... | collective-permute-start | bytes 589832 | tf_op jit(solution)/shard_map/ppermute | solution.py:57
  34.9 4.8 %collective-permute-start.12 = (bf16[2,128,192]{2,1,0:T(8,128)(2,1)S(1)}, bf16[2,128,192]{2,1,0:T(8,128)(2,1)S(1)}, u32[]{:S(2)}, u32[]{:S(2)}) collective-permute-start(bf16[2,128,192]{2,1,0:T(8,128)(2,1)S(1)} %get-tuple-element.38), channel_id=1, source_target_pairs={{0,2},{1,3},{2,0},{3,1},{4,6},{5,7},{6,4},{7,5},{8,10},{9,11},{10,... | collective-permute-start | bytes 294920 | tf_op jit(solution)/shard_map/ppermute | solution.py:57
  35.2 4.5 %collective-permute-start.13 = (bf16[2,128,192]{2,1,0:T(8,128)(2,1)S(1)}, bf16[2,128,192]{2,1,0:T(8,128)(2,1)S(1)}, u32[]{:S(2)}, u32[]{:S(2)}) collective-permute-start(bf16[2,128,192]{2,1,0:T(8,128)(2,1)S(1)} %get-tuple-element.39), channel_id=1, source_target_pairs={{0,16},{1,17},{2,18},{3,19},{4,20},{5,21},{6,22},{7,23},{8,24},{9,... | collective-permute-start | bytes 294920 | tf_op jit(solution)/shard_map/ppermute | solution.py:57
  36.3 7.0 %collective-permute-start.14 = (bf16[2,128,192]{2,1,0:T(8,128)(2,1)S(1)}, bf16[2,128,192]{2,1,0:T(8,128)(2,1)S(1)}, u32[]{:S(2)}, u32[]{:S(2)}) collective-permute-start(bf16[2,128,192]{2,1,0:T(8,128)(2,1)S(1)} %get-tuple-element.40), channel_id=1, source_target_pairs={{0,18},{1,19},{2,16},{3,17},{4,22},{5,23},{6,20},{7,21},{8,26},{9,... | collective-permute-start | bytes 294920 | tf_op jit(solution)/shard_map/ppermute | solution.py:57
  43.8 7.4 %collective-permute-start.17 = (bf16[128,768]{1,0:T(8,128)(2,1)S(1)}, bf16[128,768]{1,0:T(8,128)(2,1)S(1)}, u32[]{:S(2)}, u32[]{:S(2)}) collective-permute-start(bf16[128,768]{1,0:T(8,128)(2,1)S(1)} %shard_map.117.other_in), channel_id=1, source_target_pairs={{0,4},{1,5},{4,8},{5,9},{6,2},{7,3},{8,12},{9,13},{10,6},{11,7},{1... | collective-permute-start | bytes 589832 | tf_op jit(solution)/shard_map/ppermute | solution.py:57
  51.8 3.1 %collective-permute-start.18 = (bf16[128,768]{1,0:T(8,128)(2,1)S(1)}, bf16[128,768]{1,0:T(8,128)(2,1)S(1)}, u32[]{:S(2)}, u32[]{:S(2)}) collective-permute-start(bf16[128,768]{1,0:T(8,128)(2,1)S(1)} %get-tuple-element.48), channel_id=1, source_target_pairs={{0,1},{1,0},{2,3},{3,2},{4,5},{5,4},{6,7},{7,6},{8,9},{9,8},{10,11... | collective-permute-start | bytes 589832 | tf_op jit(solution)/shard_map/ppermute | solution.py:61

commit v10 on v9

--- a/solution.py
+++ b/solution.py
@@ -177,18 +177,19 @@
                 joined[pl.ds(first, half), :] = block[cross, flip]
 
 
-def attend_body(*refs):
-    (near, far, mine, other), pieces = refs[:4], refs[4:8]
-    weights, bias_rows, near_rows, far_rows = refs[8:]
+def attend_body(join, sample, near, far, mine, other, *rest):
+    piece0, piece1, *scratch = rest[-6:]
+    weights, bias_rows, near_rows, far_rows = scratch
+    pieces = (piece0, piece1)
     group, side = lax.axis_index("groups"), lax.rem(lax.axis_index("lat"), 2)
-    _, count, quarter = pieces[0].shape
+    _, count, quarter = piece0.shape
     heads = 3
     head_dim = quarter // heads
-    join_bundles(mine, other, weights)
-    for slot in range(4):
-        near_rows[slot * count : (slot + 1) * count, :] = near[slot, :count, :]
-        far_rows[slot * count : (slot + 1) * count, :] = far[slot, :count, :]
+    join(mine, other, weights)
     for flip in range(2):
+        rows = slice(flip * count, (flip + 1) * count)
+        near_rows[rows, :] = near[2 * sample + flip, :count, :]
+        far_rows[rows, :] = far[2 * sample + flip, :count, :]
         for at, block in enumerate((near, far)):
             bias_rows[flip, :, at * count : (at + 1) * count] = block[flip, count:, :count].astype(
                 F32
@@ -196,9 +197,8 @@
     first_head = (2 * side + group) * heads
     here = jnp.dot(near_rows[...], weights[...], preferred_element_type=F32).astype(BF16)
     there = jnp.dot(far_rows[...], weights[:, quarter:], preferred_element_type=F32).astype(BF16)
-    for slot in range(4):
-        flip, sample = slot % 2, slot // 2
-        low_row, high_row = slot * count, (slot + 1) * count
+    for flip in range(2):
+        low_row, high_row = flip * count, (flip + 1) * count
         outs = []
         for head in range(heads):
             low = head * head_dim
@@ -221,8 +221,8 @@
             weighted = jnp.dot(expd.astype(BF16), values, preferred_element_type=F32)
             outs.append((weighted / totals).astype(BF16))
         attended = jnp.concatenate(outs, axis=1)
-        pieces[2 * sample + flip][0] = attended
-        pieces[2 * sample + 1 - flip][1] = attended
+        pieces[flip][0] = attended
+        pieces[1 - flip][1] = attended
 
 
 def project_out(which, pieces, weights, tokens, gain):
@@ -496,19 +496,25 @@
     raw_tokens = gate(raw_tokens, qkv_mine)
     other_tokens = flip_chips(raw_tokens, 1, 0)
 
-    pieces = call(
-        attend_body,
-        [((2, count, quarter), BF16)] * 4,
-        [VMEM] * 4,
-        (near, far, qkv_mine, qkv_other),
-        2 * 1024 * width * 3 * quarter,
-        [
-            pltpu.VMEM((width, 3 * quarter), BF16),
-            pltpu.VMEM((2, 16, 2 * count), F32),
-            pltpu.VMEM((4 * count, width), BF16),
-            pltpu.VMEM((4 * count, width), BF16),
-        ],
-    )
+    pieces = ()
+    for sample in (1, 0):
+        after = pieces[:1]
+        pieces = (
+            *call(
+                functools.partial(attend_body, join_bundles, sample),
+                [((2, count, quarter), BF16)] * 2,
+                [VMEM] * (4 + len(after)),
+                (near, far, qkv_mine, qkv_other, *after),
+                512 * width * 3 * quarter,
+                [
+                    pltpu.VMEM((width, 3 * quarter), BF16),
+                    pltpu.VMEM((2, 16, 2 * count), F32),
+                    pltpu.VMEM((2 * count, width), BF16),
+                    pltpu.VMEM((2 * count, width), BF16),
+                ],
+            ),
+            *pieces,
+        )
     back = [pieces[0]] + [
         flip_chips(piece, flip, sample) for piece, (flip, sample) in zip(pieces[1:], FLIPS)
     ]

time: 56.3 us -> 57.5 us (1.021)
    ppermute x4, waiting for transfers between devices: 2.95 us -> 3.81 us  [swap_cores(): return lax.ppermute(values, 'lon', [(0, 1), (1, 0)])]
    pallas_call x11 -> x12, Pallas kernels: 9.51 us -> 9.46 us  [call(): pl.pallas_call(body, out_shape=outs, in_specs=specs, out_specs=tuple((VME...]
  transfers between devices with their start and end apart: 19 -> 19, of which waited for: 8 -> 8; matrix products, arithmetic and copies ran while one was open for 1% -> 1% of each run, Pallas kernels for 11% -> 10%
where the time goes in v10:
time: 57.5 us; the launch traced here: 56.6 us
  starting transfers between devices  22.6 us (39%)
  waiting for transfers between devices  19.4 us (34%)
  Pallas kernels  9.46 us (16%)
  local copies, waits for them, and re-layouts  2.25 us (4%)
  between operations  2.12 us (4%)
  other arithmetic  0.71 us (1%)
    ppermute x15, waiting for transfers between devices, move(): return lax.ppermute(values, AXES, device_pairs(target))  15.6 us
    ppermute x15, starting transfers between devices, move(): return lax.ppermute(values, AXES, device_pairs(target))  14.7 us
    pallas_call x12, Pallas kernels, call(): pl.pallas_call(body, out_shape=outs, in_specs=specs, out_specs=tuple((VME...  9.46 us
    ppermute x4, starting transfers between devices, swap_cores(): return lax.ppermute(values, 'lon', [(0, 1), (1, 0)])  7.89 us
    ppermute x4, waiting for transfers between devices, swap_cores(): return lax.ppermute(values, 'lon', [(0, 1), (1, 0)])  3.81 us
    unnamed x16, local copies, waits for them, and re-layouts  2.25 us
  transfers between devices with their start and end apart: 19, of which 8 were waited for; matrix products, arithmetic and copies ran while one was open for 1% of the time, Pallas kernels for 10%

profile of v10, /device:TPU:3, one launch (start us, length us, event | category | flops | bytes accessed | tf_op | source)
XLA Modules:
  0.0 56.6 jit_solution(4692508284905272277)
XLA Ops:
  0.0 2.1 %shard_map.110 = (bf16[192,768]{1,0:T(8,128)(2,1)}, bf16[128,768]{1,0:T(8,128)(2,1)}, bf16[48,768]{1,0:T(8,128)(2,1)}) custom-call(bf16[128,768]{1,0:T(8,128)(2,1)} %bitcast.4, bf16[12,128]{1,0:T(8,128)(2,1)} %bitcast.5, f32[768]{0:T(1024)} %refs_2_.1, bf16[96,2304]{1,0:T(8,128)(2,1)} %refs_3_.1, bf16[96,768]{1,0:T(8,128)(2,1)} %refs_4_.1), custom_call_target="tpu_custom_call" | custom-call | flops 983040 | bytes 792576 | tf_op jit(solution)/shard_map/pallas_call | solution.py:23
  2.1 0.1 collective-permute-start
  2.2 1.5 %collective-permute-start.1 = (bf16[192,768]{1,0:T(8,128)(2,1)}, bf16[192,768]{1,0:T(8,128)(2,1)S(1)}, u32[]{:S(2)}, u32[]{:S(2)}) collective-permute-start(bf16[192,768]{1,0:T(8,128)(2,1)} %get-tuple-element.28.message), channel_id=1, source_target_pairs={{0,16},{1,17},{2,18},{3,19},{4,20},{5,21},{6,22},{7,23},{8,24},{9,... | collective-permute-start | bytes 884744 | tf_op jit(solution)/shard_map/ppermute | solution.py:57
  3.7 1.3 %collective-permute-start.2 = (bf16[48,768]{1,0:T(8,128)(2,1)}, bf16[48,768]{1,0:T(8,128)(2,1)S(1)}, u32[]{:S(2)}, u32[]{:S(2)}) collective-permute-start(bf16[48,768]{1,0:T(8,128)(2,1)} %get-tuple-element.30), channel_id=1, source_target_pairs={{0,4},{1,5},{2,6},{3,7},{4,0},{5,1},{6,2},{7,3},{8,12},{9,13},{10,... | collective-permute-start | bytes 221192 | tf_op jit(solution)/shard_map/ppermute | solution.py:57
  5.0 2.3 %collective-permute-start.3 = (bf16[48,768]{1,0:T(8,128)(2,1)}, bf16[48,768]{1,0:T(8,128)(2,1)S(1)}, u32[]{:S(2)}, u32[]{:S(2)}) collective-permute-start(bf16[48,768]{1,0:T(8,128)(2,1)} %get-tuple-element.30), channel_id=1, source_target_pairs={{0,8},{1,9},{2,10},{3,11},{4,12},{5,13},{6,14},{7,15},{8,0},{9,1},... | collective-permute-start | bytes 221192 | tf_op jit(solution)/shard_map/ppermute | solution.py:57
  7.3 1.0 %copy-done = bf16[96,2304]{1,0:T(8,128)(2,1)S(1)} copy-done((bf16[96,2304]{1,0:T(8,128)(2,1)S(1)}, bf16[96,2304]{1,0:T(8,128)(2,1)}, u32[]{:S(2)}) %copy-start) | copy-done | bytes 442392
  8.3 0.9 %copy-done.1 = bf16[96,768]{1,0:T(8,128)(2,1)S(1)} copy-done((bf16[96,768]{1,0:T(8,128)(2,1)S(1)}, bf16[96,768]{1,0:T(8,128)(2,1)}, u32[]{:S(2)}) %copy-start.1) | copy-done | bytes 147480
  9.2 0.2 shard_map.109
  9.4 0.0 collective-permute-done.2.out1
  9.4 0.7 %collective-permute-done.3.out2 = bf16[48,768]{1,0:T(8,128)(2,1)S(1)} collective-permute-done((bf16[48,768]{1,0:T(8,128)(2,1)}, bf16[48,768]{1,0:T(8,128)(2,1)S(1)}, u32[]{:S(2)}, u32[]{:S(2)}) %collective-permute-start.3) | collective-permute-done | bytes 73760 | tf_op jit(solution)/shard_map/ppermute | solution.py:57
  10.1 2.4 %collective-permute-done.4.out3 = bf16[48,768]{1,0:T(8,128)(2,1)S(1)} collective-permute-done((bf16[48,768]{1,0:T(8,128)(2,1)}, bf16[48,768]{1,0:T(8,128)(2,1)S(1)}, u32[]{:S(2)}, u32[]{:S(2)}) %collective-permute-start.4) | collective-permute-done | bytes 73760 | tf_op jit(solution)/shard_map/ppermute | solution.py:57
  12.5 0.0 collective-permute-done.by_x
  12.5 0.0 collective-permute-done.1.by_y
  12.6 1.3 %collective-permute-start.9 = (bf16[4,48,768]{2,1,0:T(8,128)(2,1)S(1)}, bf16[4,48,768]{2,1,0:T(8,128)(2,1)S(1)}, u32[]{:S(2)}, u32[]{:S(2)}) collective-permute-start(bf16[4,48,768]{2,1,0:T(8,128)(2,1)S(1)} %get-tuple-element.34.outs), channel_id=1, source_target_pairs={{0,2},{1,3},{2,0},{3,1},{4,6},{5,7},{6,4},{7,5},{8,10},{9,11},{10,... | collective-permute-start | bytes 884744 | tf_op jit(solution)/shard_map/ppermute | solution.py:57
  13.9 0.2 collective-permute-start.8
  14.1 0.9 %collective-permute-start.5 = (bf16[2,48,576]{2,1,0:T(8,128)(2,1)S(1)}, bf16[2,48,576]{2,1,0:T(8,128)(2,1)S(1)}, u32[]{:S(2)}, u32[]{:S(2)}) collective-permute-start(bf16[2,48,576]{2,1,0:T(8,128)(2,1)S(1)} %get-tuple-element.33.bundle), channel_id=1, source_target_pairs={{0,4},{1,5},{2,6},{3,7},{4,0},{5,1},{6,2},{7,3},{8,12},{9,13},{10,... | collective-permute-start | bytes 331784 | tf_op jit(solution)/shard_map/ppermute | solution.py:57
  15.0 1.6 %collective-permute-start.6 = (bf16[2,48,576]{2,1,0:T(8,128)(2,1)S(1)}, bf16[2,48,576]{2,1,0:T(8,128)(2,1)S(1)}, u32[]{:S(2)}, u32[]{:S(2)}) collective-permute-start(bf16[2,48,576]{2,1,0:T(8,128)(2,1)S(1)} %get-tuple-element.33.bundle), channel_id=1, source_target_pairs={{0,8},{1,9},{2,10},{3,11},{4,12},{5,13},{6,14},{7,15},{8,0},{9,1},... | collective-permute-start | bytes 331784 | tf_op jit(solution)/shard_map/ppermute | solution.py:57
  16.6 1.2 %collective-permute-start.7 = (bf16[2,48,576]{2,1,0:T(8,128)(2,1)S(1)}, bf16[2,48,576]{2,1,0:T(8,128)(2,1)S(1)}, u32[]{:S(2)}, u32[]{:S(2)}) collective-permute-start(bf16[2,48,576]{2,1,0:T(8,128)(2,1)S(1)} %get-tuple-element.33.bundle), channel_id=1, source_target_pairs={{0,12},{1,13},{2,14},{3,15},{4,8},{5,9},{6,10},{7,11},{8,4},{9,5},... | collective-permute-start | bytes 331784 | tf_op jit(solution)/shard_map/ppermute | solution.py:57
  19.7 0.1 copy.12.taps
  19.8 0.2 copy.13.w_conv
  20.0 1.0 %shard_map.112 = (bf16[2,3,256,256]{3,2,1,0:T(8,128)(2,1)S(1)}, bf16[256,512]{1,0:T(8,128)(2,1)S(1)}, f32[8,128]{1,0:T(8,128)S(1)}) custom-call(s32[1]{0:T(128)S(6)} %copy.14.lon_half, s32[1]{0:T(128)S(6)} %copy.15.lat_half, s32[1]{0:T(128)S(6)} %copy.16.quad_off, f32[16,2]{1,0:T(8,128)S(1)} %copy.12.taps, bf16[2,768,64]{2,1,0:T(8,128)(2,1)S(1)} %copy.13.w_conv, ...), custom_call_target="tpu_custom_call" | custom-call | bytes 417932 | tf_op jit(solution)/shard_map/pallas_call | solution.py:23
  21.1 0.0 copy-start.3
  21.1 0.0 collective-permute-done.5.level1
  21.1 2.6 %collective-permute-done.7.level3 = bf16[2,48,576]{2,1,0:T(8,128)(2,1)S(1)} collective-permute-done((bf16[2,48,576]{2,1,0:T(8,128)(2,1)S(1)}, bf16[2,48,576]{2,1,0:T(8,128)(2,1)S(1)}, u32[]{:S(2)}, u32[]{:S(2)}) %collective-permute-start.7) | collective-permute-done | bytes 110624 | tf_op jit(solution)/shard_map/ppermute | solution.py:57
  23.7 0.0 collective-permute-done.9.crossed
  23.7 0.1 shard_map.113
  23.9 5.0 %collective-permute-start.10 = (bf16[4,144,768]{2,1,0:T(8,128)(2,1)S(1)}, bf16[4,144,768]{2,1,0:T(8,128)(2,1)S(1)}, u32[]{:S(2)}, u32[]{:S(2)}) collective-permute-start(bf16[4,144,768]{2,1,0:T(8,128)(2,1)S(1)} %get-tuple-element.35.near), channel_id=1, source_target_pairs={{0,1},{1,0},{2,3},{3,2},{4,5},{5,4},{6,7},{7,6},{8,9},{9,8},{10,11... | collective-permute-start | bytes 2654216 | tf_op jit(solution)/shard_map/ppermute | solution.py:61
  28.9 0.1 collective-permute-start.15
  28.9 0.4 collective-permute-start.11
  29.4 0.3 collective-permute-start.16
  29.7 2.7 %collective-permute-done.11.other = bf16[4,2,48,576]{3,2,1,0:T(8,128)(2,1)S(1)} collective-permute-done((bf16[4,2,48,576]{3,2,1,0:T(8,128)(2,1)S(1)}, bf16[4,2,48,576]{3,2,1,0:T(8,128)(2,1)S(1)}, u32[]{:S(2)}, u32[]{:S(2)}) %collective-permute-start.11) | collective-permute-done | bytes 442400 | tf_op jit(solution)/shard_map/ppermute | solution.py:61
  32.5 1.6 %shard_map.114 = (bf16[2,128,192]{2,1,0:T(8,128)(2,1)S(1)}, bf16[2,128,192]{2,1,0:T(8,128)(2,1)S(1)}) custom-call(bf16[4,144,768]{2,1,0:T(8,128)(2,1)S(1)} %get-tuple-element.35.near, bf16[4,144,768]{2,1,0:T(8,128)(2,1)S(1)} %collective-permute-done.10.far, bf16[4,2,48,576]{3,2,1,0:T(8,128)(2,1)S(1)} %get-tuple-element.36.mine.refs_1_, ...), custom_call_target="tpu_custom_call" | custom-call | flops 226492416 | bytes 2654208 | tf_op jit(solution)/shard_map/pallas_call | solution.py:23
  34.1 0.0 copy-start.5
  34.1 1.1 %collective-permute-start.13 = (bf16[2,128,192]{2,1,0:T(8,128)(2,1)S(1)}, bf16[2,128,192]{2,1,0:T(8,128)(2,1)S(1)}, u32[]{:S(2)}, u32[]{:S(2)}) collective-permute-start(bf16[2,128,192]{2,1,0:T(8,128)(2,1)S(1)} %get-tuple-element.37.rest_0_), channel_id=1, source_target_pairs={{0,16},{1,17},{2,18},{3,19},{4,20},{5,21},{6,22},{7,23},{8,24},{9,... | collective-permute-start | bytes 294920 | tf_op jit(solution)/shard_map/ppermute | solution.py:57
  35.2 1.6 %shard_map.115 = (bf16[2,128,192]{2,1,0:T(8,128)(2,1)S(1)}, bf16[2,128,192]{2,1,0:T(8,128)(2,1)S(1)}) custom-call(bf16[4,144,768]{2,1,0:T(8,128)(2,1)S(1)} %get-tuple-element.35.near, bf16[4,144,768]{2,1,0:T(8,128)(2,1)S(1)} %collective-permute-done.10.far, bf16[4,2,48,576]{3,2,1,0:T(8,128)(2,1)S(1)} %get-tuple-element.36.mine.refs_1_, ...), custom_call_target="tpu_custom_call" | custom-call | flops 226492416 | bytes 2752512 | tf_op jit(solution)/shard_map/pallas_call | solution.py:23
  36.8 0.3 collective-permute-start.12
  37.1 1.4 %collective-permute-start.14 = (bf16[2,128,192]{2,1,0:T(8,128)(2,1)S(1)}, bf16[2,128,192]{2,1,0:T(8,128)(2,1)S(1)}, u32[]{:S(2)}, u32[]{:S(2)}) collective-permute-start(bf16[2,128,192]{2,1,0:T(8,128)(2,1)S(1)} %get-tuple-element.40), channel_id=1, source_target_pairs={{0,18},{1,19},{2,16},{3,17},{4,22},{5,23},{6,20},{7,21},{8,26},{9,... | collective-permute-start | bytes 294920 | tf_op jit(solution)/shard_map/ppermute | solution.py:57
  38.5 0.1 shard_map.116.weights
  38.6 2.7 %collective-permute-done.12.piece1 = bf16[2,128,192]{2,1,0:T(8,128)(2,1)S(1)} collective-permute-done((bf16[2,128,192]{2,1,0:T(8,128)(2,1)S(1)}, bf16[2,128,192]{2,1,0:T(8,128)(2,1)S(1)}, u32[]{:S(2)}, u32[]{:S(2)}) %collective-permute-start.12) | collective-permute-done | bytes 98336 | tf_op jit(solution)/shard_map/ppermute | solution.py:57
  41.3 2.9 %collective-permute-done.14.piece3 = bf16[2,128,192]{2,1,0:T(8,128)(2,1)S(1)} collective-permute-done((bf16[2,128,192]{2,1,0:T(8,128)(2,1)S(1)}, bf16[2,128,192]{2,1,0:T(8,128)(2,1)S(1)}, u32[]{:S(2)}, u32[]{:S(2)}) %collective-permute-start.14) | collective-permute-done | bytes 98336 | tf_op jit(solution)/shard_map/ppermute | solution.py:57
  44.2 0.6 shard_map.118.other_in
  44.8 1.3 %collective-permute-start.17 = (bf16[128,768]{1,0:T(8,128)(2,1)S(1)}, bf16[128,768]{1,0:T(8,128)(2,1)S(1)}, u32[]{:S(2)}, u32[]{:S(2)}) collective-permute-start(bf16[128,768]{1,0:T(8,128)(2,1)S(1)} %shard_map.118.other_in), channel_id=1, source_target_pairs={{0,4},{1,5},{4,8},{5,9},{6,2},{7,3},{8,12},{9,13},{10,6},{11,7},{1... | collective-permute-start | bytes 589832 | tf_op jit(solution)/shard_map/ppermute | solution.py:57
  46.1 1.4 %shard_map.119 = (bf16[128,768]{1,0:T(8,128)(2,1)S(1)}, f32[256,768]{1,0:T(8,128)S(1)}) custom-call(f32[8,128]{1,0:T(8,128)S(1)} %get-tuple-element.32.gains, f32[1,768]{1,0:T(1,128)S(1)} %broadcast_in_dim.6.gain, bf16[2,128,192]{2,1,0:T(8,128)(2,1)S(1)} %get-tuple-element.38.piece0, bf16[2,128,192]{2,1,0:T(8,128)(2,1)S(1)} %collective-permute-done.12.piece1, ...), custom_call_target="tpu_custom_call" | custom-call | flops 452984832 | bytes 3021824 | tf_op jit(solution)/shard_map/pallas_call | solution.py:23
  47.5 4.3 %collective-permute-done.17.halo = bf16[128,768]{1,0:T(8,128)(2,1)S(1)} collective-permute-done((bf16[128,768]{1,0:T(8,128)(2,1)S(1)}, bf16[128,768]{1,0:T(8,128)(2,1)S(1)}, u32[]{:S(2)}, u32[]{:S(2)}) %collective-permute-start.17) | collective-permute-done | bytes 196640 | tf_op jit(solution)/shard_map/ppermute | solution.py:57
  51.8 0.7 %shard_map.120 = (f32[128,768]{1,0:T(8,128)S(1)}, bf16[128,768]{1,0:T(8,128)(2,1)S(1)}) custom-call(f32[8,128]{1,0:T(8,128)S(1)} %get-tuple-element.32.gains, bf16[128,768]{1,0:T(8,128)(2,1)S(1)} %collective-permute-done.17.halo, bf16[2,3,256,256]{3,2,1,0:T(8,128)(2,1)S(1)} %get-tuple-element.43.blocks, bf16[256,512]{1,0:T(8,128)(2,1)S(1)} %get-tuple-element.44.coeffs, ...), custom_call_target="tpu_custom_call" | custom-call | flops 100663296 | bytes 2232320 | tf_op jit(solution)/shard_map/pallas_call | solution.py:23
  52.4 2.4 %collective-permute-start.18 = (bf16[128,768]{1,0:T(8,128)(2,1)S(1)}, bf16[128,768]{1,0:T(8,128)(2,1)S(1)}, u32[]{:S(2)}, u32[]{:S(2)}) collective-permute-start(bf16[128,768]{1,0:T(8,128)(2,1)S(1)} %get-tuple-element.48), channel_id=1, source_target_pairs={{0,1},{1,0},{2,3},{3,2},{4,5},{5,4},{6,7},{7,6},{8,9},{9,8},{10,11... | collective-permute-start | bytes 589832 | tf_op jit(solution)/shard_map/ppermute | solution.py:61
  54.8 1.1 %collective-permute-done.18 = bf16[128,768]{1,0:T(8,128)(2,1)S(1)} collective-permute-done((bf16[128,768]{1,0:T(8,128)(2,1)S(1)}, bf16[128,768]{1,0:T(8,128)(2,1)S(1)}, u32[]{:S(2)}, u32[]{:S(2)}) %collective-permute-start.18) | collective-permute-done | bytes 196640 | tf_op jit(solution)/shard_map/ppermute | solution.py:61
  55.9 0.7 %fusion = bf16[1,128,768]{2,1,0:T(8,128)(2,1)} fusion(f32[128,768]{1,0:T(8,128)S(1)} %get-tuple-element.47, bf16[128,768]{1,0:T(8,128)(2,1)S(1)} %collective-permute-done.18), kind=kLoop, calls=%fused_computation.1 | loop fusion | flops 294912 | bytes 786432 | tf_op jit(solution)/shard_map/broadcast_in_dim | solution.py:548
  (20 shorter events, 0.1 us)
Async XLA Ops:
  0.0 19.7 %copy-start.6 = (f32[16,2]{0,1:T(2,128)S(1)}, f32[16,2]{0,1:T(2,128)}, u32[]{:S(2)}) copy-start(f32[16,2]{0,1:T(2,128)} %param.18) | copy-start | bytes 388
  0.0 19.8 %copy-start.4 = (bf16[2,768,64]{1,2,0:T(8,128)(2,1)S(1)}, bf16[2,768,64]{1,2,0:T(8,128)(2,1)}, u32[]{:S(2)}) copy-start(bf16[2,768,64]{1,2,0:T(8,128)(2,1)} %param.17) | copy-start | bytes 589828
  2.1 10.4 %collective-permute-start = (bf16[192,768]{1,0:T(8,128)(2,1)}, bf16[192,768]{1,0:T(8,128)(2,1)S(1)}, u32[]{:S(2)}, u32[]{:S(2)}) collective-permute-start(bf16[192,768]{1,0:T(8,128)(2,1)} %get-tuple-element.28.message), channel_id=1, source_target_pairs={{0,2},{1,3},{2,0},{3,1},{4,6},{5,7},{6,4},{7,5},{8,10},{9,11},{10,... | collective-permute-start | bytes 884744 | tf_op jit(solution)/shard_map/ppermute | solution.py:57
  2.2 10.3 %collective-permute-start.1 = (bf16[192,768]{1,0:T(8,128)(2,1)}, bf16[192,768]{1,0:T(8,128)(2,1)S(1)}, u32[]{:S(2)}, u32[]{:S(2)}) collective-permute-start(bf16[192,768]{1,0:T(8,128)(2,1)} %get-tuple-element.28.message), channel_id=1, source_target_pairs={{0,16},{1,17},{2,18},{3,19},{4,20},{5,21},{6,22},{7,23},{8,24},{9,... | collective-permute-start | bytes 884744 | tf_op jit(solution)/shard_map/ppermute | solution.py:57
  3.7 5.7 %collective-permute-start.2 = (bf16[48,768]{1,0:T(8,128)(2,1)}, bf16[48,768]{1,0:T(8,128)(2,1)S(1)}, u32[]{:S(2)}, u32[]{:S(2)}) collective-permute-start(bf16[48,768]{1,0:T(8,128)(2,1)} %get-tuple-element.30), channel_id=1, source_target_pairs={{0,4},{1,5},{2,6},{3,7},{4,0},{5,1},{6,2},{7,3},{8,12},{9,13},{10,... | collective-permute-start | bytes 221192 | tf_op jit(solution)/shard_map/ppermute | solution.py:57
  5.0 5.1 %collective-permute-start.3 = (bf16[48,768]{1,0:T(8,128)(2,1)}, bf16[48,768]{1,0:T(8,128)(2,1)S(1)}, u32[]{:S(2)}, u32[]{:S(2)}) collective-permute-start(bf16[48,768]{1,0:T(8,128)(2,1)} %get-tuple-element.30), channel_id=1, source_target_pairs={{0,8},{1,9},{2,10},{3,11},{4,12},{5,13},{6,14},{7,15},{8,0},{9,1},... | collective-permute-start | bytes 221192 | tf_op jit(solution)/shard_map/ppermute | solution.py:57
  7.3 5.2 %collective-permute-start.4 = (bf16[48,768]{1,0:T(8,128)(2,1)}, bf16[48,768]{1,0:T(8,128)(2,1)S(1)}, u32[]{:S(2)}, u32[]{:S(2)}) collective-permute-start(bf16[48,768]{1,0:T(8,128)(2,1)} %get-tuple-element.30), channel_id=1, source_target_pairs={{0,12},{1,13},{2,14},{3,15},{4,8},{5,9},{6,10},{7,11},{8,4},{9,5},... | collective-permute-start | bytes 221192 | tf_op jit(solution)/shard_map/ppermute | solution.py:57
  7.3 1.0 %copy-start = (bf16[96,2304]{1,0:T(8,128)(2,1)S(1)}, bf16[96,2304]{1,0:T(8,128)(2,1)}, u32[]{:S(2)}) copy-start(bf16[96,2304]{1,0:T(8,128)(2,1)} %refs_3_.1) | copy-start | bytes 1327108
  8.3 0.9 %copy-start.1 = (bf16[96,768]{1,0:T(8,128)(2,1)S(1)}, bf16[96,768]{1,0:T(8,128)(2,1)}, u32[]{:S(2)}) copy-start(bf16[96,768]{1,0:T(8,128)(2,1)} %refs_4_.1) | copy-start | bytes 442372
  9.4 14.3 %copy-start.2 = (bf16[192,768]{1,0:T(8,128)(2,1)S(1)}, bf16[192,768]{1,0:T(8,128)(2,1)}, u32[]{:S(2)}) copy-start(bf16[192,768]{1,0:T(8,128)(2,1)} %get-tuple-element.28.message) | copy-start | bytes 884740
  12.6 11.1 %collective-permute-start.9 = (bf16[4,48,768]{2,1,0:T(8,128)(2,1)S(1)}, bf16[4,48,768]{2,1,0:T(8,128)(2,1)S(1)}, u32[]{:S(2)}, u32[]{:S(2)}) collective-permute-start(bf16[4,48,768]{2,1,0:T(8,128)(2,1)S(1)} %get-tuple-element.34.outs), channel_id=1, source_target_pairs={{0,2},{1,3},{2,0},{3,1},{4,6},{5,7},{6,4},{7,5},{8,10},{9,11},{10,... | collective-permute-start | bytes 884744 | tf_op jit(solution)/shard_map/ppermute | solution.py:57
  13.9 9.9 %collective-permute-start.8 = (bf16[144,768]{1,0:T(8,128)(2,1)S(1)}, bf16[144,768]{1,0:T(8,128)(2,1)S(1)}, u32[]{:S(2)}, u32[]{:S(2)}) collective-permute-start(bf16[144,768]{1,0:T(8,128)(2,1)S(1)} %get-tuple-element.31.message.x_block), channel_id=1, source_target_pairs={{0,16},{1,17},{2,18},{3,19},{4,20},{5,21},{6,22},{7,23},{8,24},{9,... | collective-permute-start | bytes 663560 | tf_op jit(solution)/shard_map/ppermute | solution.py:57
  14.1 7.0 %collective-permute-start.5 = (bf16[2,48,576]{2,1,0:T(8,128)(2,1)S(1)}, bf16[2,48,576]{2,1,0:T(8,128)(2,1)S(1)}, u32[]{:S(2)}, u32[]{:S(2)}) collective-permute-start(bf16[2,48,576]{2,1,0:T(8,128)(2,1)S(1)} %get-tuple-element.33.bundle), channel_id=1, source_target_pairs={{0,4},{1,5},{2,6},{3,7},{4,0},{5,1},{6,2},{7,3},{8,12},{9,13},{10,... | collective-permute-start | bytes 331784 | tf_op jit(solution)/shard_map/ppermute | solution.py:57
  15.0 6.1 %collective-permute-start.6 = (bf16[2,48,576]{2,1,0:T(8,128)(2,1)S(1)}, bf16[2,48,576]{2,1,0:T(8,128)(2,1)S(1)}, u32[]{:S(2)}, u32[]{:S(2)}) collective-permute-start(bf16[2,48,576]{2,1,0:T(8,128)(2,1)S(1)} %get-tuple-element.33.bundle), channel_id=1, source_target_pairs={{0,8},{1,9},{2,10},{3,11},{4,12},{5,13},{6,14},{7,15},{8,0},{9,1},... | collective-permute-start | bytes 331784 | tf_op jit(solution)/shard_map/ppermute | solution.py:57
  16.6 7.1 %collective-permute-start.7 = (bf16[2,48,576]{2,1,0:T(8,128)(2,1)S(1)}, bf16[2,48,576]{2,1,0:T(8,128)(2,1)S(1)}, u32[]{:S(2)}, u32[]{:S(2)}) collective-permute-start(bf16[2,48,576]{2,1,0:T(8,128)(2,1)S(1)} %get-tuple-element.33.bundle), channel_id=1, source_target_pairs={{0,12},{1,13},{2,14},{3,15},{4,8},{5,9},{6,10},{7,11},{8,4},{9,5},... | collective-permute-start | bytes 331784 | tf_op jit(solution)/shard_map/ppermute | solution.py:57
  21.1 8.3 %copy-start.3 = (bf16[128,768]{1,0:T(8,128)(2,1)S(1)}, bf16[128,768]{1,0:T(8,128)(2,1)}, u32[]{:S(2)}) copy-start(bf16[128,768]{1,0:T(8,128)(2,1)} %get-tuple-element.42.refs_0_) | copy-start | bytes 589828
  23.9 8.6 %collective-permute-start.10 = (bf16[4,144,768]{2,1,0:T(8,128)(2,1)S(1)}, bf16[4,144,768]{2,1,0:T(8,128)(2,1)S(1)}, u32[]{:S(2)}, u32[]{:S(2)}) collective-permute-start(bf16[4,144,768]{2,1,0:T(8,128)(2,1)S(1)} %get-tuple-element.35.near), channel_id=1, source_target_pairs={{0,1},{1,0},{2,3},{3,2},{4,5},{5,4},{6,7},{7,6},{8,9},{9,8},{10,11... | collective-permute-start | bytes 2654216 | tf_op jit(solution)/shard_map/ppermute | solution.py:61
  28.9 9.7 %collective-permute-start.15 = (bf16[2,4,48,768]{3,2,1,0:T(8,128)(2,1)S(1)}, bf16[2,4,48,768]{3,2,1,0:T(8,128)(2,1)S(1)}, u32[]{:S(2)}, u32[]{:S(2)}) collective-permute-start(bf16[2,4,48,768]{3,2,1,0:T(8,128)(2,1)S(1)} %get-tuple-element.41.mine), channel_id=1, source_target_pairs={{0,1},{1,0},{2,3},{3,2},{4,5},{5,4},{6,7},{7,6},{8,9},{9,8},{10,11... | collective-permute-start | bytes 1769480 | tf_op jit(solution)/shard_map/ppermute | solution.py:61
  28.9 3.5 %collective-permute-start.11 = (bf16[4,2,48,576]{3,2,1,0:T(8,128)(2,1)S(1)}, bf16[4,2,48,576]{3,2,1,0:T(8,128)(2,1)S(1)}, u32[]{:S(2)}, u32[]{:S(2)}) collective-permute-start(bf16[4,2,48,576]{3,2,1,0:T(8,128)(2,1)S(1)} %get-tuple-element.36.mine.refs_1_), channel_id=1, source_target_pairs={{0,1},{1,0},{2,3},{3,2},{4,5},{5,4},{6,7},{7,6},{8,9},{9,8},{10,11... | collective-permute-start | bytes 1327112 | tf_op jit(solution)/shard_map/ppermute | solution.py:61
  29.4 9.2 %collective-permute-start.16 = (bf16[128,768]{1,0:T(8,128)(2,1)S(1)}, bf16[128,768]{1,0:T(8,128)(2,1)S(1)}, u32[]{:S(2)}, u32[]{:S(2)}) collective-permute-start(bf16[128,768]{1,0:T(8,128)(2,1)S(1)} %shard_map.117.tokens), channel_id=1, source_target_pairs={{0,2},{1,3},{2,0},{3,1},{4,6},{5,7},{6,4},{7,5},{8,10},{9,11},{10,... | collective-permute-start | bytes 589832 | tf_op jit(solution)/shard_map/ppermute | solution.py:57
  34.1 4.4 %copy-start.5 = (f32[768]{0:T(1024)S(1)}, f32[768]{0:T(1024)}, u32[]{:S(2)}) copy-start(f32[768]{0:T(1024)} %param.16) | copy-start | bytes 9220
  34.1 7.2 %collective-permute-start.13 = (bf16[2,128,192]{2,1,0:T(8,128)(2,1)S(1)}, bf16[2,128,192]{2,1,0:T(8,128)(2,1)S(1)}, u32[]{:S(2)}, u32[]{:S(2)}) collective-permute-start(bf16[2,128,192]{2,1,0:T(8,128)(2,1)S(1)} %get-tuple-element.37.rest_0_), channel_id=1, source_target_pairs={{0,16},{1,17},{2,18},{3,19},{4,20},{5,21},{6,22},{7,23},{8,24},{9,... | collective-permute-start | bytes 294920 | tf_op jit(solution)/shard_map/ppermute | solution.py:57
  36.8 4.5 %collective-permute-start.12 = (bf16[2,128,192]{2,1,0:T(8,128)(2,1)S(1)}, bf16[2,128,192]{2,1,0:T(8,128)(2,1)S(1)}, u32[]{:S(2)}, u32[]{:S(2)}) collective-permute-start(bf16[2,128,192]{2,1,0:T(8,128)(2,1)S(1)} %get-tuple-element.39), channel_id=1, source_target_pairs={{0,2},{1,3},{2,0},{3,1},{4,6},{5,7},{6,4},{7,5},{8,10},{9,11},{10,... | collective-permute-start | bytes 294920 | tf_op jit(solution)/shard_map/ppermute | solution.py:57
  37.1 7.1 %collective-permute-start.14 = (bf16[2,128,192]{2,1,0:T(8,128)(2,1)S(1)}, bf16[2,128,192]{2,1,0:T(8,128)(2,1)S(1)}, u32[]{:S(2)}, u32[]{:S(2)}) collective-permute-start(bf16[2,128,192]{2,1,0:T(8,128)(2,1)S(1)} %get-tuple-element.40), channel_id=1, source_target_pairs={{0,18},{1,19},{2,16},{3,17},{4,22},{5,23},{6,20},{7,21},{8,26},{9,... | collective-permute-start | bytes 294920 | tf_op jit(solution)/shard_map/ppermute | solution.py:57
  44.8 7.0 %collective-permute-start.17 = (bf16[128,768]{1,0:T(8,128)(2,1)S(1)}, bf16[128,768]{1,0:T(8,128)(2,1)S(1)}, u32[]{:S(2)}, u32[]{:S(2)}) collective-permute-start(bf16[128,768]{1,0:T(8,128)(2,1)S(1)} %shard_map.118.other_in), channel_id=1, source_target_pairs={{0,4},{1,5},{4,8},{5,9},{6,2},{7,3},{8,12},{9,13},{10,6},{11,7},{1... | collective-permute-start | bytes 589832 | tf_op jit(solution)/shard_map/ppermute | solution.py:57
  52.4 3.5 %collective-permute-start.18 = (bf16[128,768]{1,0:T(8,128)(2,1)S(1)}, bf16[128,768]{1,0:T(8,128)(2,1)S(1)}, u32[]{:S(2)}, u32[]{:S(2)}) collective-permute-start(bf16[128,768]{1,0:T(8,128)(2,1)S(1)} %get-tuple-element.48), channel_id=1, source_target_pairs={{0,1},{1,0},{2,3},{3,2},{4,5},{5,4},{6,7},{7,6},{8,9},{9,8},{10,11... | collective-permute-start | bytes 589832 | tf_op jit(solution)/shard_map/ppermute | solution.py:61

commit v11 on v9

--- a/solution.py
+++ b/solution.py
@@ -31,15 +31,6 @@
     )(*args)
 
 
-def copy_body(*refs):
-    refs[-1][...] = refs[0][...]
-
-
-def gate(value, *after):
-    specs = [VMEM] * (1 + len(after))
-    return call(copy_body, [(value.shape, value.dtype)], specs, (value, *after), 0)[0]
-
-
 def device_pairs(target):
     lat_count = lax.axis_size("lat")
     pairs = []
@@ -85,7 +76,7 @@
 
 def pack_body(*refs, weights):
     tokens, bias, gain = refs[:3]
-    message, raw, out_own, bias_here, gain_here, rows, sems = refs[-7:]
+    message, wide, raw, out_own, bias_here, gain_here, rows, sems = refs[-8:]
     count = tokens.shape[0]
     heads, bias_width = bias.shape
     core = lax.axis_index("lon")
@@ -106,12 +97,17 @@
         fetch.wait()
     message[count : count + heads, :bias_width] = bias_here[...]
     message[:count, :] = norm_rows(raw[...].astype(F32), gain_here[...][None])
+    wide[: count + 16, :] = message[...]
+    wide[count + 16 : 2 * count + 16, :] = raw[...]
     for fetch in fetches[3:]:
         fetch.wait()
     if weights:
         side = lax.rem(lax.axis_index("lat"), 2)
         cross = pick_columns(rows, 1 - side, tokens.shape[1] // 4)
-        message[count + 16 :, : cross.shape[1]] = cross
+        wide[2 * count + 16 :, : cross.shape[1]] = cross
+        wide[2 * count + 16 :, cross.shape[1] :] = jnp.zeros(
+            (rows.shape[0], tokens.shape[1] - cross.shape[1]), BF16
+        )
 
 
 def columns_body(w_qkv, w_out, own, out_own):
@@ -123,29 +119,35 @@
 
 
 def arrived_body(
-    own, by_x, by_y, out_own, out1, out2, out3, bundle, x_block, outs
+    own, by_x, by_y, out_own, out1, out2, out3, bundle, x_block, raw_x, outs
 ):
     del by_y
     side = lax.rem(lax.axis_index("lat"), 2)
     rows, width = x_block.shape[0], own.shape[1]
     bundle[side] = own[...]
-    bundle[1 - side] = by_x[rows:, :width]
+    count = raw_x.shape[0]
+    bundle[1 - side] = by_x[rows + count :, :width]
+    raw_x[...] = by_x[rows : rows + count, :]
     x_block[...] = by_x[:rows, :]
     for at, block in enumerate((out_own, out1, out2, out3)):
         outs[at] = block[...]
 
 
 def complete_body(
-    bundle, level1, level2, level3, message, x_block, by_y, by_xy, outs, crossed, gains, *results
+    bundle, level1, level2, level3, message, x_block, by_y, by_xy, crossed, gains, *results
 ):
-    del gains
-    weights, near, both = results
+    del crossed, gains
+    weights, near = results
     rows = x_block.shape[0]
     for at, block in enumerate((bundle, level1, level2, level3)):
         weights[at] = block[...]
     for at, block in enumerate((message, x_block, by_y, by_xy)):
         near[at] = block[:rows, :]
-    both[0] = outs[...]
+
+
+def pair_body(mine, crossed, after, both):
+    del after
+    both[0] = mine[...]
     both[1] = crossed[...]
 
 
@@ -410,10 +412,11 @@
 
     direct = half % 16 == 0 and lat_count == 8
     rows = count + 16
-    message, raw_tokens, out_own = call(
+    message, wide, raw_tokens, out_own = call(
         functools.partial(pack_body, weights=direct),
         [
-            ((rows + (half if direct else 0), width), BF16),
+            ((rows, width), BF16),
+            ((rows + count + (half if direct else 0), width), BF16),
             ((count, width), BF16),
             ((half, width), BF16),
         ],
@@ -429,8 +432,8 @@
         limit=56,
     )
 
-    by_x, by_y = flip_chips(message, 1, 0), flip_chips(message, 0, 1)
-    x_block = by_x
+    by_x, by_y = flip_chips(wide, 1, 0), flip_chips(message, 0, 1)
+    x_block, other_tokens = by_x[:rows], by_x[rows : rows + count]
     if direct:
         levels = flip_levels(out_own)
         qkv_own, out_own = call(
@@ -440,11 +443,12 @@
             (w_qkv, w_out),
             0,
         )
-        bundle, x_block, outs = call(
+        bundle, x_block, other_tokens, outs = call(
             arrived_body,
             [
                 ((2, half, 3 * quarter), BF16),
                 ((rows, width), BF16),
+                ((count, width), BF16),
                 ((4, half, width), BF16),
             ],
             [VMEM] * 7,
@@ -464,14 +468,14 @@
         0,
     )
     if direct:
-        qkv_mine, near, out_mine = call(
+        crossed = flip_chips(outs, 1, 0)
+        qkv_mine, near = call(
             complete_body,
             [
                 ((4, 2, half, 3 * quarter), BF16),
                 ((4, rows, width), BF16),
-                ((2, 4, half, width), BF16),
             ],
-            [VMEM] * 11,
+            [VMEM] * 10,
             (
                 bundle,
                 *flip_levels(bundle),
@@ -479,22 +483,19 @@
                 x_block,
                 by_y,
                 flip_chips(x_block, 0, 1),
-                outs,
-                flip_chips(outs, 1, 0),
+                crossed,
                 gains,
             ),
             0,
         )
-        qkv_other, out_other = swap_cores(qkv_mine), swap_cores(out_mine)
+        qkv_other = swap_cores(qkv_mine)
         join = join_columns
     else:
-        near = jnp.stack([message, by_x, by_y, flip_chips(by_x, 0, 1)])
+        near = jnp.stack([message, x_block, by_y, flip_chips(x_block, 0, 1)])
         qkv_mine, qkv_other = gather_plain(w_qkv, 3 * quarter)
         out_mine, out_other = gather_plain(w_out, width)
         join = join_bundles
     far = swap_cores(near)
-    raw_tokens = gate(raw_tokens, qkv_mine)
-    other_tokens = flip_chips(raw_tokens, 1, 0)
 
     pieces = call(
         attend_body,
@@ -512,6 +513,15 @@
     back = [pieces[0]] + [
         flip_chips(piece, flip, sample) for piece, (flip, sample) in zip(pieces[1:], FLIPS)
     ]
+    if direct:
+        (out_mine,) = call(
+            pair_body,
+            [((2, 4, half, width), BF16)],
+            [VMEM] * 3,
+            (outs, crossed, pieces[0]),
+            0,
+        )
+        out_other = swap_cores(out_mine)
     (full_out,) = call(
         join, [((width, width), BF16)], [VMEM] * 2, (out_mine, out_other), 0
     )

time: 56.3 us -> 59.3 us (1.053)
  waiting for transfers between devices: 18.9 us -> 22.8 us
  starting transfers between devices: 22.2 us -> 21.1 us
    ppermute x15 -> x14, waiting for transfers between devices: 15.9 us -> 19.1 us  [move(): return lax.ppermute(values, AXES, device_pairs(target))]
    ppermute x4, waiting for transfers between devices: 2.95 us -> 3.75 us  [swap_cores(): return lax.ppermute(values, 'lon', [(0, 1), (1, 0)])]
    ppermute x4, starting transfers between devices: 7.54 us -> 6.81 us  [swap_cores(): return lax.ppermute(values, 'lon', [(0, 1), (1, 0)])]
    ppermute x15 -> x14, starting transfers between devices: 14.7 us -> 14.3 us  [move(): return lax.ppermute(values, AXES, device_pairs(target))]
  transfers between devices with their start and end apart: 19 -> 18, of which waited for: 8 -> 10; matrix products, arithmetic and copies ran while one was open for 1% -> 1% of each run, Pallas kernels for 11% -> 5%
where the time goes in v11:
time: 59.3 us; the launch traced here: 58.6 us
  waiting for transfers between devices  22.8 us (38%)
  starting transfers between devices  21.1 us (36%)
  Pallas kernels  9.65 us (16%)
  local copies, waits for them, and re-layouts  2.26 us (4%)
  between operations  2.12 us (4%)
  other arithmetic  0.71 us (1%)
    ppermute x14, waiting for transfers between devices, move(): return lax.ppermute(values, AXES, device_pairs(target))  19.1 us
    ppermute x14, starting transfers between devices, move(): return lax.ppermute(values, AXES, device_pairs(target))  14.3 us
    pallas_call x11, Pallas kernels, call(): pl.pallas_call(body, out_shape=outs, in_specs=specs, out_specs=tuple((VME...  9.65 us
    ppermute x4, starting transfers between devices, swap_cores(): return lax.ppermute(values, 'lon', [(0, 1), (1, 0)])  6.81 us
    ppermute x4, waiting for transfers between devices, swap_cores(): return lax.ppermute(values, 'lon', [(0, 1), (1, 0)])  3.75 us
    unnamed x16, local copies, waits for them, and re-layouts  2.25 us
  transfers between devices with their start and end apart: 18, of which 10 were waited for; matrix products, arithmetic and copies ran while one was open for 1% of the time, Pallas kernels for 5%

profile of v11, /device:TPU:3, one launch (start us, length us, event | category | flops | bytes accessed | tf_op | source)
XLA Modules:
  0.0 58.6 jit_solution(654783583992338425)
XLA Ops:
  0.0 2.3 %shard_map.110 = (bf16[144,768]{1,0:T(8,128)(2,1)}, bf16[320,768]{1,0:T(8,128)(2,1)}, bf16[128,768]{1,0:T(8,128)(2,1)}, bf16[48,768]{1,0:T(8,128)(2,1)}) custom-call(bf16[128,768]{1,0:T(8,128)(2,1)} %bitcast.4, bf16[12,128]{1,0:T(8,128)(2,1)} %bitcast.5, f32[768]{0:T(1024)} %refs_2_.1, bf16[96,2304]{1,0:T(8,128)(2,1)} %refs_3_.1, bf16[96,768]{1,0:T(8,128)(2,1)} %refs_4_.1), custom_call_target="tpu_custom_call" | custom-call | flops 983040 | bytes 792576 | tf_op jit(solution)/shard_map/pallas_call | solution.py:23
  2.3 0.0 copy-start.6
  2.3 0.1 collective-permute-start
  2.4 1.5 %collective-permute-start.1 = (bf16[144,768]{1,0:T(8,128)(2,1)}, bf16[144,768]{1,0:T(8,128)(2,1)S(1)}, u32[]{:S(2)}, u32[]{:S(2)}) collective-permute-start(bf16[144,768]{1,0:T(8,128)(2,1)} %get-tuple-element.30.message), channel_id=1, source_target_pairs={{0,16},{1,17},{2,18},{3,19},{4,20},{5,21},{6,22},{7,23},{8,24},{9,... | collective-permute-start | bytes 663560 | tf_op jit(solution)/shard_map/ppermute | solution.py:48
  3.9 1.3 %collective-permute-start.2 = (bf16[48,768]{1,0:T(8,128)(2,1)}, bf16[48,768]{1,0:T(8,128)(2,1)S(1)}, u32[]{:S(2)}, u32[]{:S(2)}) collective-permute-start(bf16[48,768]{1,0:T(8,128)(2,1)} %get-tuple-element.32), channel_id=1, source_target_pairs={{0,4},{1,5},{2,6},{3,7},{4,0},{5,1},{6,2},{7,3},{8,12},{9,13},{10,... | collective-permute-start | bytes 221192 | tf_op jit(solution)/shard_map/ppermute | solution.py:48
  5.2 2.3 %collective-permute-start.3 = (bf16[48,768]{1,0:T(8,128)(2,1)}, bf16[48,768]{1,0:T(8,128)(2,1)S(1)}, u32[]{:S(2)}, u32[]{:S(2)}) collective-permute-start(bf16[48,768]{1,0:T(8,128)(2,1)} %get-tuple-element.32), channel_id=1, source_target_pairs={{0,8},{1,9},{2,10},{3,11},{4,12},{5,13},{6,14},{7,15},{8,0},{9,1},... | collective-permute-start | bytes 221192 | tf_op jit(solution)/shard_map/ppermute | solution.py:48
  7.5 0.0 collective-permute-start.4
  7.5 1.0 %copy-done = bf16[96,2304]{1,0:T(8,128)(2,1)S(1)} copy-done((bf16[96,2304]{1,0:T(8,128)(2,1)S(1)}, bf16[96,2304]{1,0:T(8,128)(2,1)}, u32[]{:S(2)}) %copy-start) | copy-done | bytes 442392
  8.5 0.9 %copy-done.1 = bf16[96,768]{1,0:T(8,128)(2,1)S(1)} copy-done((bf16[96,768]{1,0:T(8,128)(2,1)S(1)}, bf16[96,768]{1,0:T(8,128)(2,1)}, u32[]{:S(2)}) %copy-start.1) | copy-done | bytes 147480
  9.4 0.2 shard_map.109
  9.6 0.0 collective-permute-done.2.out1
  9.6 0.7 %collective-permute-done.3.out2 = bf16[48,768]{1,0:T(8,128)(2,1)S(1)} collective-permute-done((bf16[48,768]{1,0:T(8,128)(2,1)}, bf16[48,768]{1,0:T(8,128)(2,1)S(1)}, u32[]{:S(2)}, u32[]{:S(2)}) %collective-permute-start.3) | collective-permute-done | bytes 73760 | tf_op jit(solution)/shard_map/ppermute | solution.py:48
  10.3 2.4 %collective-permute-done.4.out3 = bf16[48,768]{1,0:T(8,128)(2,1)S(1)} collective-permute-done((bf16[48,768]{1,0:T(8,128)(2,1)}, bf16[48,768]{1,0:T(8,128)(2,1)S(1)}, u32[]{:S(2)}, u32[]{:S(2)}) %collective-permute-start.4) | collective-permute-done | bytes 73760 | tf_op jit(solution)/shard_map/ppermute | solution.py:48
  12.7 0.0 collective-permute-done.1.by_y
  12.7 2.0 %collective-permute-done.by_x = bf16[320,768]{1,0:T(8,128)(2,1)S(1)} collective-permute-done((bf16[320,768]{1,0:T(8,128)(2,1)}, bf16[320,768]{1,0:T(8,128)(2,1)S(1)}, u32[]{:S(2)}, u32[]{:S(2)}) %collective-permute-start) | collective-permute-done | bytes 491552 | tf_op jit(solution)/shard_map/ppermute | solution.py:48
  14.7 0.1 shard_map.111
  14.7 0.4 collective-permute-start.9
  15.1 1.2 %collective-permute-start.8 = (bf16[144,768]{1,0:T(8,128)(2,1)S(1)}, bf16[144,768]{1,0:T(8,128)(2,1)S(1)}, u32[]{:S(2)}, u32[]{:S(2)}) collective-permute-start(bf16[144,768]{1,0:T(8,128)(2,1)S(1)} %get-tuple-element.33.message.x_block), channel_id=1, source_target_pairs={{0,16},{1,17},{2,18},{3,19},{4,20},{5,21},{6,22},{7,23},{8,24},{9,... | collective-permute-start | bytes 663560 | tf_op jit(solution)/shard_map/ppermute | solution.py:48
  16.3 1.3 %collective-permute-start.5 = (bf16[2,48,576]{2,1,0:T(8,128)(2,1)S(1)}, bf16[2,48,576]{2,1,0:T(8,128)(2,1)S(1)}, u32[]{:S(2)}, u32[]{:S(2)}) collective-permute-start(bf16[2,48,576]{2,1,0:T(8,128)(2,1)S(1)} %get-tuple-element.35.bundle), channel_id=1, source_target_pairs={{0,4},{1,5},{2,6},{3,7},{4,0},{5,1},{6,2},{7,3},{8,12},{9,13},{10,... | collective-permute-start | bytes 331784 | tf_op jit(solution)/shard_map/ppermute | solution.py:48
  17.6 2.3 %collective-permute-start.6 = (bf16[2,48,576]{2,1,0:T(8,128)(2,1)S(1)}, bf16[2,48,576]{2,1,0:T(8,128)(2,1)S(1)}, u32[]{:S(2)}, u32[]{:S(2)}) collective-permute-start(bf16[2,48,576]{2,1,0:T(8,128)(2,1)S(1)} %get-tuple-element.35.bundle), channel_id=1, source_target_pairs={{0,8},{1,9},{2,10},{3,11},{4,12},{5,13},{6,14},{7,15},{8,0},{9,1},... | collective-permute-start | bytes 331784 | tf_op jit(solution)/shard_map/ppermute | solution.py:48
  19.9 0.0 collective-permute-start.7
  19.9 0.2 copy.13.w_conv
  20.1 0.1 copy.12.taps
  22.2 1.0 %shard_map.112 = (bf16[2,3,256,256]{3,2,1,0:T(8,128)(2,1)S(1)}, bf16[256,512]{1,0:T(8,128)(2,1)S(1)}, f32[8,128]{1,0:T(8,128)S(1)}) custom-call(s32[1]{0:T(128)S(6)} %copy.14.lon_half, s32[1]{0:T(128)S(6)} %copy.15.lat_half, s32[1]{0:T(128)S(6)} %copy.16.quad_off, f32[16,2]{1,0:T(8,128)S(1)} %copy.12.taps, bf16[2,768,64]{2,1,0:T(8,128)(2,1)S(1)} %copy.13.w_conv, ...), custom_call_target="tpu_custom_call" | custom-call | bytes 417932 | tf_op jit(solution)/shard_map/pallas_call | solution.py:23
  23.2 0.3 collective-permute-done.6.level2
  23.5 3.2 %collective-permute-done.7.level3 = bf16[2,48,576]{2,1,0:T(8,128)(2,1)S(1)} collective-permute-done((bf16[2,48,576]{2,1,0:T(8,128)(2,1)S(1)}, bf16[2,48,576]{2,1,0:T(8,128)(2,1)S(1)}, u32[]{:S(2)}, u32[]{:S(2)}) %collective-permute-start.7) | collective-permute-done | bytes 110624 | tf_op jit(solution)/shard_map/ppermute | solution.py:48
  26.7 0.1 shard_map.113
  26.8 4.2 %collective-permute-start.10 = (bf16[4,144,768]{2,1,0:T(8,128)(2,1)S(1)}, bf16[4,144,768]{2,1,0:T(8,128)(2,1)S(1)}, u32[]{:S(2)}, u32[]{:S(2)}) collective-permute-start(bf16[4,144,768]{2,1,0:T(8,128)(2,1)S(1)} %get-tuple-element.37.refs_0_), channel_id=1, source_target_pairs={{0,1},{1,0},{2,3},{3,2},{4,5},{5,4},{6,7},{7,6},{8,9},{9,8},{10,11... | collective-permute-start | bytes 2654216 | tf_op jit(solution)/shard_map/ppermute | solution.py:52
  31.0 0.1 collective-permute-start.11
  31.1 2.7 %collective-permute-done.11.refs_3_ = bf16[4,2,48,576]{3,2,1,0:T(8,128)(2,1)S(1)} collective-permute-done((bf16[4,2,48,576]{3,2,1,0:T(8,128)(2,1)S(1)}, bf16[4,2,48,576]{3,2,1,0:T(8,128)(2,1)S(1)}, u32[]{:S(2)}, u32[]{:S(2)}) %collective-permute-start.11) | collective-permute-done | bytes 442400 | tf_op jit(solution)/shard_map/ppermute | solution.py:52
  33.8 3.3 %shard_map.114 = (bf16[2,128,192]{2,1,0:T(8,128)(2,1)S(1)}, bf16[2,128,192]{2,1,0:T(8,128)(2,1)S(1)}, bf16[2,128,192]{2,1,0:T(8,128)(2,1)S(1)}, bf16[2,128,192]{2,1,0:T(8,128)(2,1)S(1)}) custom-call(bf16[4,144,768]{2,1,0:T(8,128)(2,1)S(1)} %get-tuple-element.37.refs_0_, bf16[4,144,768]{2,1,0:T(8,128)(2,1)S(1)} %collective-permute-done.10.refs_1_, ...), custom_call_target="tpu_custom_call" | custom-call | flops 905969664 | bytes 2654208 | tf_op jit(solution)/shard_map/pallas_call | solution.py:23
  37.0 0.0 copy-start.5
  37.1 0.4 collective-permute-start.15
  37.5 1.2 %collective-permute-start.12 = (bf16[2,128,192]{2,1,0:T(8,128)(2,1)S(1)}, bf16[2,128,192]{2,1,0:T(8,128)(2,1)S(1)}, u32[]{:S(2)}, u32[]{:S(2)}) collective-permute-start(bf16[2,128,192]{2,1,0:T(8,128)(2,1)S(1)} %get-tuple-element.40), channel_id=1, source_target_pairs={{0,2},{1,3},{2,0},{3,1},{4,6},{5,7},{6,4},{7,5},{8,10},{9,11},{10,... | collective-permute-start | bytes 294920 | tf_op jit(solution)/shard_map/ppermute | solution.py:48
  38.8 0.2 collective-permute-start.13
  39.0 1.2 %collective-permute-start.14 = (bf16[2,128,192]{2,1,0:T(8,128)(2,1)S(1)}, bf16[2,128,192]{2,1,0:T(8,128)(2,1)S(1)}, u32[]{:S(2)}, u32[]{:S(2)}) collective-permute-start(bf16[2,128,192]{2,1,0:T(8,128)(2,1)S(1)} %get-tuple-element.42), channel_id=1, source_target_pairs={{0,18},{1,19},{2,16},{3,17},{4,22},{5,23},{6,20},{7,21},{8,26},{9,... | collective-permute-start | bytes 294920 | tf_op jit(solution)/shard_map/ppermute | solution.py:48
  40.2 0.1 shard_map.116.weights
  40.3 0.0 copy-start.3
  40.3 2.2 %collective-permute-done.12.piece1 = bf16[2,128,192]{2,1,0:T(8,128)(2,1)S(1)} collective-permute-done((bf16[2,128,192]{2,1,0:T(8,128)(2,1)S(1)}, bf16[2,128,192]{2,1,0:T(8,128)(2,1)S(1)}, u32[]{:S(2)}, u32[]{:S(2)}) %collective-permute-start.12) | collective-permute-done | bytes 98336 | tf_op jit(solution)/shard_map/ppermute | solution.py:48
  42.5 3.7 %collective-permute-done.13.piece2 = bf16[2,128,192]{2,1,0:T(8,128)(2,1)S(1)} collective-permute-done((bf16[2,128,192]{2,1,0:T(8,128)(2,1)S(1)}, bf16[2,128,192]{2,1,0:T(8,128)(2,1)S(1)}, u32[]{:S(2)}, u32[]{:S(2)}) %collective-permute-start.13) | collective-permute-done | bytes 98336 | tf_op jit(solution)/shard_map/ppermute | solution.py:48
  46.2 0.6 shard_map.117.other_in
  46.8 1.3 %collective-permute-start.16 = (bf16[128,768]{1,0:T(8,128)(2,1)S(1)}, bf16[128,768]{1,0:T(8,128)(2,1)S(1)}, u32[]{:S(2)}, u32[]{:S(2)}) collective-permute-start(bf16[128,768]{1,0:T(8,128)(2,1)S(1)} %shard_map.117.other_in), channel_id=1, source_target_pairs={{0,4},{1,5},{4,8},{5,9},{6,2},{7,3},{8,12},{9,13},{10,6},{11,7},{1... | collective-permute-start | bytes 589832 | tf_op jit(solution)/shard_map/ppermute | solution.py:48
  48.1 1.4 %shard_map.118 = (bf16[128,768]{1,0:T(8,128)(2,1)S(1)}, f32[256,768]{1,0:T(8,128)S(1)}) custom-call(f32[8,128]{1,0:T(8,128)S(1)} %get-tuple-element.34.gains, f32[1,768]{1,0:T(1,128)S(1)} %broadcast_in_dim.6.gain, bf16[2,128,192]{2,1,0:T(8,128)(2,1)S(1)} %get-tuple-element.39.after.piece0, bf16[2,128,192]{2,1,0:T(8,128)(2,1)S(1)} %collective-permute-done.12.piece1, ...), custom_call_target="tpu_custom_call" | custom-call | flops 452984832 | bytes 3021824 | tf_op jit(solution)/shard_map/pallas_call | solution.py:23
  49.5 4.6 %collective-permute-done.16.halo = bf16[128,768]{1,0:T(8,128)(2,1)S(1)} collective-permute-done((bf16[128,768]{1,0:T(8,128)(2,1)S(1)}, bf16[128,768]{1,0:T(8,128)(2,1)S(1)}, u32[]{:S(2)}, u32[]{:S(2)}) %collective-permute-start.16) | collective-permute-done | bytes 196640 | tf_op jit(solution)/shard_map/ppermute | solution.py:48
  54.1 0.7 %shard_map.119 = (f32[128,768]{1,0:T(8,128)S(1)}, bf16[128,768]{1,0:T(8,128)(2,1)S(1)}) custom-call(f32[8,128]{1,0:T(8,128)S(1)} %get-tuple-element.34.gains, bf16[128,768]{1,0:T(8,128)(2,1)S(1)} %collective-permute-done.16.halo, bf16[2,3,256,256]{3,2,1,0:T(8,128)(2,1)S(1)} %get-tuple-element.44.blocks, bf16[256,512]{1,0:T(8,128)(2,1)S(1)} %get-tuple-element.45.coeffs, ...), custom_call_target="tpu_custom_call" | custom-call | flops 100663296 | bytes 2232320 | tf_op jit(solution)/shard_map/pallas_call | solution.py:23
  54.7 2.1 %collective-permute-start.17 = (bf16[128,768]{1,0:T(8,128)(2,1)S(1)}, bf16[128,768]{1,0:T(8,128)(2,1)S(1)}, u32[]{:S(2)}, u32[]{:S(2)}) collective-permute-start(bf16[128,768]{1,0:T(8,128)(2,1)S(1)} %get-tuple-element.50), channel_id=1, source_target_pairs={{0,1},{1,0},{2,3},{3,2},{4,5},{5,4},{6,7},{7,6},{8,9},{9,8},{10,11... | collective-permute-start | bytes 589832 | tf_op jit(solution)/shard_map/ppermute | solution.py:52
  56.9 1.1 %collective-permute-done.17 = bf16[128,768]{1,0:T(8,128)(2,1)S(1)} collective-permute-done((bf16[128,768]{1,0:T(8,128)(2,1)S(1)}, bf16[128,768]{1,0:T(8,128)(2,1)S(1)}, u32[]{:S(2)}, u32[]{:S(2)}) %collective-permute-start.17) | collective-permute-done | bytes 196640 | tf_op jit(solution)/shard_map/ppermute | solution.py:52
  57.9 0.7 %fusion = bf16[1,128,768]{2,1,0:T(8,128)(2,1)} fusion(f32[128,768]{1,0:T(8,128)S(1)} %get-tuple-element.49, bf16[128,768]{1,0:T(8,128)(2,1)S(1)} %collective-permute-done.17), kind=kLoop, calls=%fused_computation.1 | loop fusion | flops 294912 | bytes 786432 | tf_op jit(solution)/shard_map/broadcast_in_dim | solution.py:552
  (17 shorter events, 0.1 us)
Async XLA Ops:
  0.0 19.9 %copy-start.4 = (bf16[2,768,64]{1,2,0:T(8,128)(2,1)S(1)}, bf16[2,768,64]{1,2,0:T(8,128)(2,1)}, u32[]{:S(2)}) copy-start(bf16[2,768,64]{1,2,0:T(8,128)(2,1)} %param.17) | copy-start | bytes 589828
  2.3 17.8 %copy-start.6 = (f32[16,2]{0,1:T(2,128)S(1)}, f32[16,2]{0,1:T(2,128)}, u32[]{:S(2)}) copy-start(f32[16,2]{0,1:T(2,128)} %param.18) | copy-start | bytes 388
  2.3 12.4 %collective-permute-start = (bf16[320,768]{1,0:T(8,128)(2,1)}, bf16[320,768]{1,0:T(8,128)(2,1)S(1)}, u32[]{:S(2)}, u32[]{:S(2)}) collective-permute-start(bf16[320,768]{1,0:T(8,128)(2,1)} %get-tuple-element.29), channel_id=1, source_target_pairs={{0,2},{1,3},{2,0},{3,1},{4,6},{5,7},{6,4},{7,5},{8,10},{9,11},{10,... | collective-permute-start | bytes 1474568 | tf_op jit(solution)/shard_map/ppermute | solution.py:48
  2.4 10.3 %collective-permute-start.1 = (bf16[144,768]{1,0:T(8,128)(2,1)}, bf16[144,768]{1,0:T(8,128)(2,1)S(1)}, u32[]{:S(2)}, u32[]{:S(2)}) collective-permute-start(bf16[144,768]{1,0:T(8,128)(2,1)} %get-tuple-element.30.message), channel_id=1, source_target_pairs={{0,16},{1,17},{2,18},{3,19},{4,20},{5,21},{6,22},{7,23},{8,24},{9,... | collective-permute-start | bytes 663560 | tf_op jit(solution)/shard_map/ppermute | solution.py:48
  3.9 5.7 %collective-permute-start.2 = (bf16[48,768]{1,0:T(8,128)(2,1)}, bf16[48,768]{1,0:T(8,128)(2,1)S(1)}, u32[]{:S(2)}, u32[]{:S(2)}) collective-permute-start(bf16[48,768]{1,0:T(8,128)(2,1)} %get-tuple-element.32), channel_id=1, source_target_pairs={{0,4},{1,5},{2,6},{3,7},{4,0},{5,1},{6,2},{7,3},{8,12},{9,13},{10,... | collective-permute-start | bytes 221192 | tf_op jit(solution)/shard_map/ppermute | solution.py:48
  5.2 5.1 %collective-permute-start.3 = (bf16[48,768]{1,0:T(8,128)(2,1)}, bf16[48,768]{1,0:T(8,128)(2,1)S(1)}, u32[]{:S(2)}, u32[]{:S(2)}) collective-permute-start(bf16[48,768]{1,0:T(8,128)(2,1)} %get-tuple-element.32), channel_id=1, source_target_pairs={{0,8},{1,9},{2,10},{3,11},{4,12},{5,13},{6,14},{7,15},{8,0},{9,1},... | collective-permute-start | bytes 221192 | tf_op jit(solution)/shard_map/ppermute | solution.py:48
  7.5 5.2 %collective-permute-start.4 = (bf16[48,768]{1,0:T(8,128)(2,1)}, bf16[48,768]{1,0:T(8,128)(2,1)S(1)}, u32[]{:S(2)}, u32[]{:S(2)}) collective-permute-start(bf16[48,768]{1,0:T(8,128)(2,1)} %get-tuple-element.32), channel_id=1, source_target_pairs={{0,12},{1,13},{2,14},{3,15},{4,8},{5,9},{6,10},{7,11},{8,4},{9,5},... | collective-permute-start | bytes 221192 | tf_op jit(solution)/shard_map/ppermute | solution.py:48
  7.5 1.0 %copy-start = (bf16[96,2304]{1,0:T(8,128)(2,1)S(1)}, bf16[96,2304]{1,0:T(8,128)(2,1)}, u32[]{:S(2)}) copy-start(bf16[96,2304]{1,0:T(8,128)(2,1)} %refs_3_.1) | copy-start | bytes 1327108
  8.5 0.9 %copy-start.1 = (bf16[96,768]{1,0:T(8,128)(2,1)S(1)}, bf16[96,768]{1,0:T(8,128)(2,1)}, u32[]{:S(2)}) copy-start(bf16[96,768]{1,0:T(8,128)(2,1)} %refs_4_.1) | copy-start | bytes 442372
  9.6 17.2 %copy-start.2 = (bf16[144,768]{1,0:T(8,128)(2,1)S(1)}, bf16[144,768]{1,0:T(8,128)(2,1)}, u32[]{:S(2)}) copy-start(bf16[144,768]{1,0:T(8,128)(2,1)} %get-tuple-element.30.message) | copy-start | bytes 663556
  14.7 12.0 %collective-permute-start.9 = (bf16[4,48,768]{2,1,0:T(8,128)(2,1)S(1)}, bf16[4,48,768]{2,1,0:T(8,128)(2,1)S(1)}, u32[]{:S(2)}, u32[]{:S(2)}) collective-permute-start(bf16[4,48,768]{2,1,0:T(8,128)(2,1)S(1)} %get-tuple-element.36.mine), channel_id=1, source_target_pairs={{0,2},{1,3},{2,0},{3,1},{4,6},{5,7},{6,4},{7,5},{8,10},{9,11},{10,... | collective-permute-start | bytes 884744 | tf_op jit(solution)/shard_map/ppermute | solution.py:48
  15.1 11.6 %collective-permute-start.8 = (bf16[144,768]{1,0:T(8,128)(2,1)S(1)}, bf16[144,768]{1,0:T(8,128)(2,1)S(1)}, u32[]{:S(2)}, u32[]{:S(2)}) collective-permute-start(bf16[144,768]{1,0:T(8,128)(2,1)S(1)} %get-tuple-element.33.message.x_block), channel_id=1, source_target_pairs={{0,16},{1,17},{2,18},{3,19},{4,20},{5,21},{6,22},{7,23},{8,24},{9,... | collective-permute-start | bytes 663560 | tf_op jit(solution)/shard_map/ppermute | solution.py:48
  16.3 6.9 %collective-permute-start.5 = (bf16[2,48,576]{2,1,0:T(8,128)(2,1)S(1)}, bf16[2,48,576]{2,1,0:T(8,128)(2,1)S(1)}, u32[]{:S(2)}, u32[]{:S(2)}) collective-permute-start(bf16[2,48,576]{2,1,0:T(8,128)(2,1)S(1)} %get-tuple-element.35.bundle), channel_id=1, source_target_pairs={{0,4},{1,5},{2,6},{3,7},{4,0},{5,1},{6,2},{7,3},{8,12},{9,13},{10,... | collective-permute-start | bytes 331784 | tf_op jit(solution)/shard_map/ppermute | solution.py:48
  17.6 5.9 %collective-permute-start.6 = (bf16[2,48,576]{2,1,0:T(8,128)(2,1)S(1)}, bf16[2,48,576]{2,1,0:T(8,128)(2,1)S(1)}, u32[]{:S(2)}, u32[]{:S(2)}) collective-permute-start(bf16[2,48,576]{2,1,0:T(8,128)(2,1)S(1)} %get-tuple-element.35.bundle), channel_id=1, source_target_pairs={{0,8},{1,9},{2,10},{3,11},{4,12},{5,13},{6,14},{7,15},{8,0},{9,1},... | collective-permute-start | bytes 331784 | tf_op jit(solution)/shard_map/ppermute | solution.py:48
  19.9 6.8 %collective-permute-start.7 = (bf16[2,48,576]{2,1,0:T(8,128)(2,1)S(1)}, bf16[2,48,576]{2,1,0:T(8,128)(2,1)S(1)}, u32[]{:S(2)}, u32[]{:S(2)}) collective-permute-start(bf16[2,48,576]{2,1,0:T(8,128)(2,1)S(1)} %get-tuple-element.35.bundle), channel_id=1, source_target_pairs={{0,12},{1,13},{2,14},{3,15},{4,8},{5,9},{6,10},{7,11},{8,4},{9,5},... | collective-permute-start | bytes 331784 | tf_op jit(solution)/shard_map/ppermute | solution.py:48
  26.8 6.9 %collective-permute-start.10 = (bf16[4,144,768]{2,1,0:T(8,128)(2,1)S(1)}, bf16[4,144,768]{2,1,0:T(8,128)(2,1)S(1)}, u32[]{:S(2)}, u32[]{:S(2)}) collective-permute-start(bf16[4,144,768]{2,1,0:T(8,128)(2,1)S(1)} %get-tuple-element.37.refs_0_), channel_id=1, source_target_pairs={{0,1},{1,0},{2,3},{3,2},{4,5},{5,4},{6,7},{7,6},{8,9},{9,8},{10,11... | collective-permute-start | bytes 2654216 | tf_op jit(solution)/shard_map/ppermute | solution.py:52
  31.0 2.8 %collective-permute-start.11 = (bf16[4,2,48,576]{3,2,1,0:T(8,128)(2,1)S(1)}, bf16[4,2,48,576]{3,2,1,0:T(8,128)(2,1)S(1)}, u32[]{:S(2)}, u32[]{:S(2)}) collective-permute-start(bf16[4,2,48,576]{3,2,1,0:T(8,128)(2,1)S(1)} %get-tuple-element.38.refs_2_), channel_id=1, source_target_pairs={{0,1},{1,0},{2,3},{3,2},{4,5},{5,4},{6,7},{7,6},{8,9},{9,8},{10,11... | collective-permute-start | bytes 1327112 | tf_op jit(solution)/shard_map/ppermute | solution.py:52
  37.0 3.1 %copy-start.5 = (f32[768]{0:T(1024)S(1)}, f32[768]{0:T(1024)}, u32[]{:S(2)}) copy-start(f32[768]{0:T(1024)} %param.16) | copy-start | bytes 9220
  37.1 3.1 %collective-permute-start.15 = (bf16[2,4,48,768]{3,2,1,0:T(8,128)(2,1)S(1)}, bf16[2,4,48,768]{3,2,1,0:T(8,128)(2,1)S(1)}, u32[]{:S(2)}, u32[]{:S(2)}) collective-permute-start(bf16[2,4,48,768]{3,2,1,0:T(8,128)(2,1)S(1)} %shard_map.115.mine), channel_id=1, source_target_pairs={{0,1},{1,0},{2,3},{3,2},{4,5},{5,4},{6,7},{7,6},{8,9},{9,8},{10,11... | collective-permute-start | bytes 1769480 | tf_op jit(solution)/shard_map/ppermute | solution.py:52
  37.5 5.0 %collective-permute-start.12 = (bf16[2,128,192]{2,1,0:T(8,128)(2,1)S(1)}, bf16[2,128,192]{2,1,0:T(8,128)(2,1)S(1)}, u32[]{:S(2)}, u32[]{:S(2)}) collective-permute-start(bf16[2,128,192]{2,1,0:T(8,128)(2,1)S(1)} %get-tuple-element.40), channel_id=1, source_target_pairs={{0,2},{1,3},{2,0},{3,1},{4,6},{5,7},{6,4},{7,5},{8,10},{9,11},{10,... | collective-permute-start | bytes 294920 | tf_op jit(solution)/shard_map/ppermute | solution.py:48
  38.8 7.5 %collective-permute-start.13 = (bf16[2,128,192]{2,1,0:T(8,128)(2,1)S(1)}, bf16[2,128,192]{2,1,0:T(8,128)(2,1)S(1)}, u32[]{:S(2)}, u32[]{:S(2)}) collective-permute-start(bf16[2,128,192]{2,1,0:T(8,128)(2,1)S(1)} %get-tuple-element.41), channel_id=1, source_target_pairs={{0,16},{1,17},{2,18},{3,19},{4,20},{5,21},{6,22},{7,23},{8,24},{9,... | collective-permute-start | bytes 294920 | tf_op jit(solution)/shard_map/ppermute | solution.py:48
  39.0 7.2 %collective-permute-start.14 = (bf16[2,128,192]{2,1,0:T(8,128)(2,1)S(1)}, bf16[2,128,192]{2,1,0:T(8,128)(2,1)S(1)}, u32[]{:S(2)}, u32[]{:S(2)}) collective-permute-start(bf16[2,128,192]{2,1,0:T(8,128)(2,1)S(1)} %get-tuple-element.42), channel_id=1, source_target_pairs={{0,18},{1,19},{2,16},{3,17},{4,22},{5,23},{6,20},{7,21},{8,26},{9,... | collective-permute-start | bytes 294920 | tf_op jit(solution)/shard_map/ppermute | solution.py:48
  40.3 7.8 %copy-start.3 = (bf16[128,768]{1,0:T(8,128)(2,1)S(1)}, bf16[128,768]{1,0:T(8,128)(2,1)}, u32[]{:S(2)}) copy-start(bf16[128,768]{1,0:T(8,128)(2,1)} %get-tuple-element.46.tokens) | copy-start | bytes 589828
  46.8 7.3 %collective-permute-start.16 = (bf16[128,768]{1,0:T(8,128)(2,1)S(1)}, bf16[128,768]{1,0:T(8,128)(2,1)S(1)}, u32[]{:S(2)}, u32[]{:S(2)}) collective-permute-start(bf16[128,768]{1,0:T(8,128)(2,1)S(1)} %shard_map.117.other_in), channel_id=1, source_target_pairs={{0,4},{1,5},{4,8},{5,9},{6,2},{7,3},{8,12},{9,13},{10,6},{11,7},{1... | collective-permute-start | bytes 589832 | tf_op jit(solution)/shard_map/ppermute | solution.py:48
  54.7 3.2 %collective-permute-start.17 = (bf16[128,768]{1,0:T(8,128)(2,1)S(1)}, bf16[128,768]{1,0:T(8,128)(2,1)S(1)}, u32[]{:S(2)}, u32[]{:S(2)}) collective-permute-start(bf16[128,768]{1,0:T(8,128)(2,1)S(1)} %get-tuple-element.50), channel_id=1, source_target_pairs={{0,1},{1,0},{2,3},{3,2},{4,5},{5,4},{6,7},{7,6},{8,9},{9,8},{10,11... | collective-permute-start | bytes 589832 | tf_op jit(solution)/shard_map/ppermute | solution.py:52

commit v12 on v9

--- a/solution.py
+++ b/solution.py
@@ -123,7 +123,7 @@
 
 
 def arrived_body(
-    own, by_x, by_y, out_own, out1, out2, out3, bundle, x_block, outs
+    own, by_x, by_y, out_own, out3, out2, out1, bundle, x_block, outs
 ):
     del by_y
     side = lax.rem(lax.axis_index("lat"), 2)
@@ -136,7 +136,7 @@
 
 
 def complete_body(
-    bundle, level1, level2, level3, message, x_block, by_y, by_xy, outs, crossed, gains, *results
+    bundle, level3, level2, level1, message, x_block, by_y, by_xy, outs, crossed, gains, *results
 ):
     del gains
     weights, near, both = results
@@ -238,7 +238,7 @@
     return middle, norm_rows(middle.astype(F32), gain)
 
 
-def other_body(gain, piece0, piece1, piece2, piece3, weights, tokens, other_in):
+def other_body(gain, piece3, piece2, piece1, piece0, weights, tokens, other_in):
     pieces = (piece0, piece1, piece2, piece3)
     other_in[...] = project_out(1, pieces, weights, tokens[...], gain[...])[1]
 
@@ -307,10 +307,10 @@
 def own_body(
     gains,
     gain,
+    piece3,
+    piece2,
+    piece1,
     piece0,
-    piece1,
-    piece2,
-    piece3,
     weights,
     tokens,
     other_in,
@@ -385,7 +385,8 @@
 
 
 def flip_levels(bundle):
-    return [move(bundle, lambda g, l, c: (g, l ^ (2 * flip), c)) for flip in (1, 2, 3)]
+    moved = [move(bundle, lambda g, l, c: (g, l ^ (2 * flip), c)) for flip in (3, 2, 1)]
+    return moved[::-1]
 
 
 def per_device(
@@ -448,7 +449,7 @@
                 ((4, half, width), BF16),
             ],
             [VMEM] * 7,
-            (qkv_own, by_x, by_y, out_own, *levels),
+            (qkv_own, by_x, by_y, out_own, *levels[::-1]),
             0,
         )
     size = 4 * w_conv.shape[2]
@@ -474,7 +475,7 @@
             [VMEM] * 11,
             (
                 bundle,
-                *flip_levels(bundle),
+                *flip_levels(bundle)[::-1],
                 message,
                 x_block,
                 by_y,
@@ -509,9 +510,10 @@
             pltpu.VMEM((4 * count, width), BF16),
         ],
     )
-    back = [pieces[0]] + [
-        flip_chips(piece, flip, sample) for piece, (flip, sample) in zip(pieces[1:], FLIPS)
+    back = [
+        flip_chips(piece, flip, sample) for piece, (flip, sample) in zip(pieces[:0:-1], FLIPS[::-1])
     ]
+    back = [pieces[0]] + back[::-1]
     (full_out,) = call(
         join, [((width, width), BF16)], [VMEM] * 2, (out_mine, out_other), 0
     )
@@ -519,7 +521,7 @@
         other_body,
         [((count, width), BF16)],
         [VMEM] * 7,
-        (gain_conv, *back, full_out, other_tokens),
+        (gain_conv, *back[::-1], full_out, other_tokens),
         2 * count * width * width,
     )
     halo = move(other_in, lambda g, l, c: (g, l + 2 - 4 * (l % 2), c))
@@ -527,7 +529,7 @@
         own_body,
         [((count, width), BF16), ((2 * count, width), F32)],
         [VMEM] * 11,
-        (gains, gain_conv, *back, full_out, raw_tokens, other_in, diagonal, coeffs),
+        (gains, gain_conv, *back[::-1], full_out, raw_tokens, other_in, diagonal, coeffs),
         2 * count * width * width * 3,
     )
     kept, sent = call(

time: 56.3 us -> 56.3 us (level)
  waiting for transfers between devices: 18.9 us -> 22.3 us
  starting transfers between devices: 22.2 us -> 19.1 us
    ppermute x15, waiting for transfers between devices: 15.9 us -> 19.3 us  [move(): return lax.ppermute(values, AXES, device_pairs(target))]
    ppermute x4, starting transfers between devices: 7.54 us -> 4.58 us  [swap_cores(): return lax.ppermute(values, 'lon', [(0, 1), (1, 0)])]
  transfers between devices with their start and end apart: 19 -> 19, of which waited for: 8 -> 7; matrix products, arithmetic and copies ran while one was open for 1% -> 1% of each run, Pallas kernels for 11% -> 11%
where the time goes in v12:
time: 56.3 us; the launch traced here: 56 us
  waiting for transfers between devices  22.3 us (40%)
  starting transfers between devices  19.1 us (34%)
  Pallas kernels  9.51 us (17%)
  local copies, waits for them, and re-layouts  2.25 us (4%)
  between operations  2.12 us (4%)
  other arithmetic  0.71 us (1%)
    ppermute x15, waiting for transfers between devices, move(): return lax.ppermute(values, AXES, device_pairs(target))  19.3 us
    ppermute x15, starting transfers between devices, move(): return lax.ppermute(values, AXES, device_pairs(target))  14.5 us
    pallas_call x11, Pallas kernels, call(): pl.pallas_call(body, out_shape=outs, in_specs=specs, out_specs=tuple((VME...  9.51 us
    ppermute x4, starting transfers between devices, swap_cores(): return lax.ppermute(values, 'lon', [(0, 1), (1, 0)])  4.58 us
    ppermute x4, waiting for transfers between devices, swap_cores(): return lax.ppermute(values, 'lon', [(0, 1), (1, 0)])  2.95 us
    unnamed x16, local copies, waits for them, and re-layouts  2.25 us
  transfers between devices with their start and end apart: 19, of which 7 were waited for; matrix products, arithmetic and copies ran while one was open for 1% of the time, Pallas kernels for 11%

profile of v12, /device:TPU:3, one launch (start us, length us, event | category | flops | bytes accessed | tf_op | source)
XLA Modules:
  0.0 56.0 jit_solution(10686220398955941988)
XLA Ops:
  0.0 2.1 %shard_map.110 = (bf16[192,768]{1,0:T(8,128)(2,1)}, bf16[128,768]{1,0:T(8,128)(2,1)}, bf16[48,768]{1,0:T(8,128)(2,1)}) custom-call(bf16[128,768]{1,0:T(8,128)(2,1)} %bitcast.4, bf16[12,128]{1,0:T(8,128)(2,1)} %bitcast.5, f32[768]{0:T(1024)} %refs_2_.1, bf16[96,2304]{1,0:T(8,128)(2,1)} %refs_3_.1, bf16[96,768]{1,0:T(8,128)(2,1)} %refs_4_.1), custom_call_target="tpu_custom_call" | custom-call | flops 983040 | bytes 792576 | tf_op jit(solution)/shard_map/pallas_call | solution.py:23
  2.1 0.1 collective-permute-start
  2.2 1.5 %collective-permute-start.1 = (bf16[192,768]{1,0:T(8,128)(2,1)}, bf16[192,768]{1,0:T(8,128)(2,1)S(1)}, u32[]{:S(2)}, u32[]{:S(2)}) collective-permute-start(bf16[192,768]{1,0:T(8,128)(2,1)} %get-tuple-element.28.message), channel_id=1, source_target_pairs={{0,16},{1,17},{2,18},{3,19},{4,20},{5,21},{6,22},{7,23},{8,24},{9,... | collective-permute-start | bytes 884744 | tf_op jit(solution)/shard_map/ppermute | solution.py:57
  3.7 3.3 %collective-permute-start.2 = (bf16[48,768]{1,0:T(8,128)(2,1)}, bf16[48,768]{1,0:T(8,128)(2,1)S(1)}, u32[]{:S(2)}, u32[]{:S(2)}) collective-permute-start(bf16[48,768]{1,0:T(8,128)(2,1)} %get-tuple-element.30), channel_id=1, source_target_pairs={{0,12},{1,13},{2,14},{3,15},{4,8},{5,9},{6,10},{7,11},{8,4},{9,5},... | collective-permute-start | bytes 221192 | tf_op jit(solution)/shard_map/ppermute | solution.py:57
  7.0 0.0 collective-permute-start.3
  7.0 0.3 collective-permute-start.4
  7.3 1.0 %copy-done = bf16[96,2304]{1,0:T(8,128)(2,1)S(1)} copy-done((bf16[96,2304]{1,0:T(8,128)(2,1)S(1)}, bf16[96,2304]{1,0:T(8,128)(2,1)}, u32[]{:S(2)}) %copy-start) | copy-done | bytes 442392
  8.3 0.9 %copy-done.1 = bf16[96,768]{1,0:T(8,128)(2,1)S(1)} copy-done((bf16[96,768]{1,0:T(8,128)(2,1)S(1)}, bf16[96,768]{1,0:T(8,128)(2,1)}, u32[]{:S(2)}) %copy-start.1) | copy-done | bytes 147480
  9.2 0.2 shard_map.109
  9.4 0.0 collective-permute-done.2.out3
  9.4 4.1 %collective-permute-done.3.out2 = bf16[48,768]{1,0:T(8,128)(2,1)S(1)} collective-permute-done((bf16[48,768]{1,0:T(8,128)(2,1)}, bf16[48,768]{1,0:T(8,128)(2,1)S(1)}, u32[]{:S(2)}, u32[]{:S(2)}) %collective-permute-start.3) | collective-permute-done | bytes 73760 | tf_op jit(solution)/shard_map/ppermute | solution.py:57
  13.5 0.0 collective-permute-done.4.out1
  13.5 0.0 collective-permute-done.by_x
  13.5 0.1 shard_map.111
  13.6 1.3 %collective-permute-start.9 = (bf16[4,48,768]{2,1,0:T(8,128)(2,1)S(1)}, bf16[4,48,768]{2,1,0:T(8,128)(2,1)S(1)}, u32[]{:S(2)}, u32[]{:S(2)}) collective-permute-start(bf16[4,48,768]{2,1,0:T(8,128)(2,1)S(1)} %get-tuple-element.34.outs), channel_id=1, source_target_pairs={{0,2},{1,3},{2,0},{3,1},{4,6},{5,7},{6,4},{7,5},{8,10},{9,11},{10,... | collective-permute-start | bytes 884744 | tf_op jit(solution)/shard_map/ppermute | solution.py:57
  14.9 0.2 collective-permute-start.8
  15.1 1.0 %collective-permute-start.5 = (bf16[2,48,576]{2,1,0:T(8,128)(2,1)S(1)}, bf16[2,48,576]{2,1,0:T(8,128)(2,1)S(1)}, u32[]{:S(2)}, u32[]{:S(2)}) collective-permute-start(bf16[2,48,576]{2,1,0:T(8,128)(2,1)S(1)} %get-tuple-element.33.bundle), channel_id=1, source_target_pairs={{0,12},{1,13},{2,14},{3,15},{4,8},{5,9},{6,10},{7,11},{8,4},{9,5},... | collective-permute-start | bytes 331784 | tf_op jit(solution)/shard_map/ppermute | solution.py:57
  16.1 2.5 %collective-permute-start.7 = (bf16[2,48,576]{2,1,0:T(8,128)(2,1)S(1)}, bf16[2,48,576]{2,1,0:T(8,128)(2,1)S(1)}, u32[]{:S(2)}, u32[]{:S(2)}) collective-permute-start(bf16[2,48,576]{2,1,0:T(8,128)(2,1)S(1)} %get-tuple-element.33.bundle), channel_id=1, source_target_pairs={{0,4},{1,5},{2,6},{3,7},{4,0},{5,1},{6,2},{7,3},{8,12},{9,13},{10,... | collective-permute-start | bytes 331784 | tf_op jit(solution)/shard_map/ppermute | solution.py:57
  20.6 0.1 copy.12.taps
  20.7 0.2 copy.13.w_conv
  20.9 1.0 %shard_map.112 = (bf16[2,3,256,256]{3,2,1,0:T(8,128)(2,1)S(1)}, bf16[256,512]{1,0:T(8,128)(2,1)S(1)}, f32[8,128]{1,0:T(8,128)S(1)}) custom-call(s32[1]{0:T(128)S(6)} %copy.14.lon_half, s32[1]{0:T(128)S(6)} %copy.15.lat_half, s32[1]{0:T(128)S(6)} %copy.16.quad_off, f32[16,2]{1,0:T(8,128)S(1)} %copy.12.taps, bf16[2,768,64]{2,1,0:T(8,128)(2,1)S(1)} %copy.13.w_conv, ...), custom_call_target="tpu_custom_call" | custom-call | bytes 417932 | tf_op jit(solution)/shard_map/pallas_call | solution.py:23
  21.9 0.0 copy-start.3
  21.9 0.0 collective-permute-done.5.level3
  21.9 5.2 %collective-permute-done.6.level2 = bf16[2,48,576]{2,1,0:T(8,128)(2,1)S(1)} collective-permute-done((bf16[2,48,576]{2,1,0:T(8,128)(2,1)S(1)}, bf16[2,48,576]{2,1,0:T(8,128)(2,1)S(1)}, u32[]{:S(2)}, u32[]{:S(2)}) %collective-permute-start.6) | collective-permute-done | bytes 110624 | tf_op jit(solution)/shard_map/ppermute | solution.py:57
  27.2 0.1 shard_map.113
  27.3 2.1 %collective-permute-start.10 = (bf16[4,144,768]{2,1,0:T(8,128)(2,1)S(1)}, bf16[4,144,768]{2,1,0:T(8,128)(2,1)S(1)}, u32[]{:S(2)}, u32[]{:S(2)}) collective-permute-start(bf16[4,144,768]{2,1,0:T(8,128)(2,1)S(1)} %get-tuple-element.35.refs_0_), channel_id=1, source_target_pairs={{0,1},{1,0},{2,3},{3,2},{4,5},{5,4},{6,7},{7,6},{8,9},{9,8},{10,11... | collective-permute-start | bytes 2654216 | tf_op jit(solution)/shard_map/ppermute | solution.py:61
  29.4 0.1 collective-permute-start.11
  29.5 0.4 collective-permute-start.15
  30.0 0.0 copy-start.5
  30.0 0.3 collective-permute-start.16
  30.3 1.9 %collective-permute-done.11.refs_3_ = bf16[4,2,48,576]{3,2,1,0:T(8,128)(2,1)S(1)} collective-permute-done((bf16[4,2,48,576]{3,2,1,0:T(8,128)(2,1)S(1)}, bf16[4,2,48,576]{3,2,1,0:T(8,128)(2,1)S(1)}, u32[]{:S(2)}, u32[]{:S(2)}) %collective-permute-start.11) | collective-permute-done | bytes 442400 | tf_op jit(solution)/shard_map/ppermute | solution.py:61
  32.2 3.3 %shard_map.114 = (bf16[2,128,192]{2,1,0:T(8,128)(2,1)S(1)}, bf16[2,128,192]{2,1,0:T(8,128)(2,1)S(1)}, bf16[2,128,192]{2,1,0:T(8,128)(2,1)S(1)}, bf16[2,128,192]{2,1,0:T(8,128)(2,1)S(1)}) custom-call(bf16[4,144,768]{2,1,0:T(8,128)(2,1)S(1)} %get-tuple-element.35.refs_0_, bf16[4,144,768]{2,1,0:T(8,128)(2,1)S(1)} %collective-permute-done.10.refs_1_, ...), custom_call_target="tpu_custom_call" | custom-call | flops 905969664 | bytes 2654208 | tf_op jit(solution)/shard_map/pallas_call | solution.py:23
  35.5 0.5 collective-permute-start.12
  36.0 1.0 %collective-permute-start.13 = (bf16[2,128,192]{2,1,0:T(8,128)(2,1)S(1)}, bf16[2,128,192]{2,1,0:T(8,128)(2,1)S(1)}, u32[]{:S(2)}, u32[]{:S(2)}) collective-permute-start(bf16[2,128,192]{2,1,0:T(8,128)(2,1)S(1)} %get-tuple-element.38), channel_id=1, source_target_pairs={{0,16},{1,17},{2,18},{3,19},{4,20},{5,21},{6,22},{7,23},{8,24},{9,... | collective-permute-start | bytes 294920 | tf_op jit(solution)/shard_map/ppermute | solution.py:57
  37.0 1.2 %collective-permute-start.14 = (bf16[2,128,192]{2,1,0:T(8,128)(2,1)S(1)}, bf16[2,128,192]{2,1,0:T(8,128)(2,1)S(1)}, u32[]{:S(2)}, u32[]{:S(2)}) collective-permute-start(bf16[2,128,192]{2,1,0:T(8,128)(2,1)S(1)} %get-tuple-element.39), channel_id=1, source_target_pairs={{0,2},{1,3},{2,0},{3,1},{4,6},{5,7},{6,4},{7,5},{8,10},{9,11},{10,... | collective-permute-start | bytes 294920 | tf_op jit(solution)/shard_map/ppermute | solution.py:57
  38.2 0.0 collective-permute-done.15.other
  38.2 0.1 shard_map.115.weights
  38.3 0.0 collective-permute-done.16.tokens
  38.3 2.9 %collective-permute-done.12.piece3 = bf16[2,128,192]{2,1,0:T(8,128)(2,1)S(1)} collective-permute-done((bf16[2,128,192]{2,1,0:T(8,128)(2,1)S(1)}, bf16[2,128,192]{2,1,0:T(8,128)(2,1)S(1)}, u32[]{:S(2)}, u32[]{:S(2)}) %collective-permute-start.12) | collective-permute-done | bytes 98336 | tf_op jit(solution)/shard_map/ppermute | solution.py:57
  41.2 2.5 %collective-permute-done.13.piece2 = bf16[2,128,192]{2,1,0:T(8,128)(2,1)S(1)} collective-permute-done((bf16[2,128,192]{2,1,0:T(8,128)(2,1)S(1)}, bf16[2,128,192]{2,1,0:T(8,128)(2,1)S(1)}, u32[]{:S(2)}, u32[]{:S(2)}) %collective-permute-start.13) | collective-permute-done | bytes 98336 | tf_op jit(solution)/shard_map/ppermute | solution.py:57
  43.7 0.6 shard_map.117.other_in
  44.3 1.3 %collective-permute-start.17 = (bf16[128,768]{1,0:T(8,128)(2,1)S(1)}, bf16[128,768]{1,0:T(8,128)(2,1)S(1)}, u32[]{:S(2)}, u32[]{:S(2)}) collective-permute-start(bf16[128,768]{1,0:T(8,128)(2,1)S(1)} %shard_map.117.other_in), channel_id=1, source_target_pairs={{0,4},{1,5},{4,8},{5,9},{6,2},{7,3},{8,12},{9,13},{10,6},{11,7},{1... | collective-permute-start | bytes 589832 | tf_op jit(solution)/shard_map/ppermute | solution.py:57
  45.6 1.4 %shard_map.118 = (bf16[128,768]{1,0:T(8,128)(2,1)S(1)}, f32[256,768]{1,0:T(8,128)S(1)}) custom-call(f32[8,128]{1,0:T(8,128)S(1)} %get-tuple-element.32.gains, f32[1,768]{1,0:T(1,128)S(1)} %broadcast_in_dim.6.gain, bf16[2,128,192]{2,1,0:T(8,128)(2,1)S(1)} %collective-permute-done.12.piece3, bf16[2,128,192]{2,1,0:T(8,128)(2,1)S(1)} %collective-permute-done.13.piece2, ...), custom_call_target="tpu_custom_call" | custom-call | flops 452984832 | bytes 3021824 | tf_op jit(solution)/shard_map/pallas_call | solution.py:23
  47.0 4.6 %collective-permute-done.17.halo = bf16[128,768]{1,0:T(8,128)(2,1)S(1)} collective-permute-done((bf16[128,768]{1,0:T(8,128)(2,1)S(1)}, bf16[128,768]{1,0:T(8,128)(2,1)S(1)}, u32[]{:S(2)}, u32[]{:S(2)}) %collective-permute-start.17) | collective-permute-done | bytes 196640 | tf_op jit(solution)/shard_map/ppermute | solution.py:57
  51.6 0.7 %shard_map.119 = (f32[128,768]{1,0:T(8,128)S(1)}, bf16[128,768]{1,0:T(8,128)(2,1)S(1)}) custom-call(f32[8,128]{1,0:T(8,128)S(1)} %get-tuple-element.32.gains, bf16[128,768]{1,0:T(8,128)(2,1)S(1)} %collective-permute-done.17.halo, bf16[2,3,256,256]{3,2,1,0:T(8,128)(2,1)S(1)} %get-tuple-element.43.blocks, bf16[256,512]{1,0:T(8,128)(2,1)S(1)} %get-tuple-element.44.coeffs, ...), custom_call_target="tpu_custom_call" | custom-call | flops 100663296 | bytes 2232320 | tf_op jit(solution)/shard_map/pallas_call | solution.py:23
  52.3 2.0 %collective-permute-start.18 = (bf16[128,768]{1,0:T(8,128)(2,1)S(1)}, bf16[128,768]{1,0:T(8,128)(2,1)S(1)}, u32[]{:S(2)}, u32[]{:S(2)}) collective-permute-start(bf16[128,768]{1,0:T(8,128)(2,1)S(1)} %get-tuple-element.48), channel_id=1, source_target_pairs={{0,1},{1,0},{2,3},{3,2},{4,5},{5,4},{6,7},{7,6},{8,9},{9,8},{10,11... | collective-permute-start | bytes 589832 | tf_op jit(solution)/shard_map/ppermute | solution.py:61
  54.2 1.1 %collective-permute-done.18 = bf16[128,768]{1,0:T(8,128)(2,1)S(1)} collective-permute-done((bf16[128,768]{1,0:T(8,128)(2,1)S(1)}, bf16[128,768]{1,0:T(8,128)(2,1)S(1)}, u32[]{:S(2)}, u32[]{:S(2)}) %collective-permute-start.18) | collective-permute-done | bytes 196640 | tf_op jit(solution)/shard_map/ppermute | solution.py:61
  55.3 0.7 %fusion = bf16[1,128,768]{2,1,0:T(8,128)(2,1)} fusion(f32[128,768]{1,0:T(8,128)S(1)} %get-tuple-element.47, bf16[128,768]{1,0:T(8,128)(2,1)S(1)} %collective-permute-done.18), kind=kLoop, calls=%fused_computation.1 | loop fusion | flops 294912 | bytes 786432 | tf_op jit(solution)/shard_map/broadcast_in_dim | solution.py:544
  (19 shorter events, 0.1 us)
Async XLA Ops:
  0.0 20.6 %copy-start.6 = (f32[16,2]{0,1:T(2,128)S(1)}, f32[16,2]{0,1:T(2,128)}, u32[]{:S(2)}) copy-start(f32[16,2]{0,1:T(2,128)} %param.18) | copy-start | bytes 388
  0.0 20.7 %copy-start.4 = (bf16[2,768,64]{1,2,0:T(8,128)(2,1)S(1)}, bf16[2,768,64]{1,2,0:T(8,128)(2,1)}, u32[]{:S(2)}) copy-start(bf16[2,768,64]{1,2,0:T(8,128)(2,1)} %param.17) | copy-start | bytes 589828
  2.1 11.4 %collective-permute-start = (bf16[192,768]{1,0:T(8,128)(2,1)}, bf16[192,768]{1,0:T(8,128)(2,1)S(1)}, u32[]{:S(2)}, u32[]{:S(2)}) collective-permute-start(bf16[192,768]{1,0:T(8,128)(2,1)} %get-tuple-element.28.message), channel_id=1, source_target_pairs={{0,2},{1,3},{2,0},{3,1},{4,6},{5,7},{6,4},{7,5},{8,10},{9,11},{10,... | collective-permute-start | bytes 884744 | tf_op jit(solution)/shard_map/ppermute | solution.py:57
  2.2 11.3 %collective-permute-start.1 = (bf16[192,768]{1,0:T(8,128)(2,1)}, bf16[192,768]{1,0:T(8,128)(2,1)S(1)}, u32[]{:S(2)}, u32[]{:S(2)}) collective-permute-start(bf16[192,768]{1,0:T(8,128)(2,1)} %get-tuple-element.28.message), channel_id=1, source_target_pairs={{0,16},{1,17},{2,18},{3,19},{4,20},{5,21},{6,22},{7,23},{8,24},{9,... | collective-permute-start | bytes 884744 | tf_op jit(solution)/shard_map/ppermute | solution.py:57
  3.7 5.7 %collective-permute-start.2 = (bf16[48,768]{1,0:T(8,128)(2,1)}, bf16[48,768]{1,0:T(8,128)(2,1)S(1)}, u32[]{:S(2)}, u32[]{:S(2)}) collective-permute-start(bf16[48,768]{1,0:T(8,128)(2,1)} %get-tuple-element.30), channel_id=1, source_target_pairs={{0,12},{1,13},{2,14},{3,15},{4,8},{5,9},{6,10},{7,11},{8,4},{9,5},... | collective-permute-start | bytes 221192 | tf_op jit(solution)/shard_map/ppermute | solution.py:57
  7.0 6.5 %collective-permute-start.3 = (bf16[48,768]{1,0:T(8,128)(2,1)}, bf16[48,768]{1,0:T(8,128)(2,1)S(1)}, u32[]{:S(2)}, u32[]{:S(2)}) collective-permute-start(bf16[48,768]{1,0:T(8,128)(2,1)} %get-tuple-element.30), channel_id=1, source_target_pairs={{0,8},{1,9},{2,10},{3,11},{4,12},{5,13},{6,14},{7,15},{8,0},{9,1},... | collective-permute-start | bytes 221192 | tf_op jit(solution)/shard_map/ppermute | solution.py:57
  7.0 6.5 %collective-permute-start.4 = (bf16[48,768]{1,0:T(8,128)(2,1)}, bf16[48,768]{1,0:T(8,128)(2,1)S(1)}, u32[]{:S(2)}, u32[]{:S(2)}) collective-permute-start(bf16[48,768]{1,0:T(8,128)(2,1)} %get-tuple-element.30), channel_id=1, source_target_pairs={{0,4},{1,5},{2,6},{3,7},{4,0},{5,1},{6,2},{7,3},{8,12},{9,13},{10,... | collective-permute-start | bytes 221192 | tf_op jit(solution)/shard_map/ppermute | solution.py:57
  7.3 1.0 %copy-start = (bf16[96,2304]{1,0:T(8,128)(2,1)S(1)}, bf16[96,2304]{1,0:T(8,128)(2,1)}, u32[]{:S(2)}) copy-start(bf16[96,2304]{1,0:T(8,128)(2,1)} %refs_3_.1) | copy-start | bytes 1327108
  8.3 0.9 %copy-start.1 = (bf16[96,768]{1,0:T(8,128)(2,1)S(1)}, bf16[96,768]{1,0:T(8,128)(2,1)}, u32[]{:S(2)}) copy-start(bf16[96,768]{1,0:T(8,128)(2,1)} %refs_4_.1) | copy-start | bytes 442372
  9.4 17.8 %copy-start.2 = (bf16[192,768]{1,0:T(8,128)(2,1)S(1)}, bf16[192,768]{1,0:T(8,128)(2,1)}, u32[]{:S(2)}) copy-start(bf16[192,768]{1,0:T(8,128)(2,1)} %get-tuple-element.28.message) | copy-start | bytes 884740
  13.6 13.6 %collective-permute-start.9 = (bf16[4,48,768]{2,1,0:T(8,128)(2,1)S(1)}, bf16[4,48,768]{2,1,0:T(8,128)(2,1)S(1)}, u32[]{:S(2)}, u32[]{:S(2)}) collective-permute-start(bf16[4,48,768]{2,1,0:T(8,128)(2,1)S(1)} %get-tuple-element.34.outs), channel_id=1, source_target_pairs={{0,2},{1,3},{2,0},{3,1},{4,6},{5,7},{6,4},{7,5},{8,10},{9,11},{10,... | collective-permute-start | bytes 884744 | tf_op jit(solution)/shard_map/ppermute | solution.py:57
  14.9 12.3 %collective-permute-start.8 = (bf16[144,768]{1,0:T(8,128)(2,1)S(1)}, bf16[144,768]{1,0:T(8,128)(2,1)S(1)}, u32[]{:S(2)}, u32[]{:S(2)}) collective-permute-start(bf16[144,768]{1,0:T(8,128)(2,1)S(1)} %get-tuple-element.31.message.x_block), channel_id=1, source_target_pairs={{0,16},{1,17},{2,18},{3,19},{4,20},{5,21},{6,22},{7,23},{8,24},{9,... | collective-permute-start | bytes 663560 | tf_op jit(solution)/shard_map/ppermute | solution.py:57
  15.1 6.9 %collective-permute-start.5 = (bf16[2,48,576]{2,1,0:T(8,128)(2,1)S(1)}, bf16[2,48,576]{2,1,0:T(8,128)(2,1)S(1)}, u32[]{:S(2)}, u32[]{:S(2)}) collective-permute-start(bf16[2,48,576]{2,1,0:T(8,128)(2,1)S(1)} %get-tuple-element.33.bundle), channel_id=1, source_target_pairs={{0,12},{1,13},{2,14},{3,15},{4,8},{5,9},{6,10},{7,11},{8,4},{9,5},... | collective-permute-start | bytes 331784 | tf_op jit(solution)/shard_map/ppermute | solution.py:57
  16.1 11.0 %collective-permute-start.6 = (bf16[2,48,576]{2,1,0:T(8,128)(2,1)S(1)}, bf16[2,48,576]{2,1,0:T(8,128)(2,1)S(1)}, u32[]{:S(2)}, u32[]{:S(2)}) collective-permute-start(bf16[2,48,576]{2,1,0:T(8,128)(2,1)S(1)} %get-tuple-element.33.bundle), channel_id=1, source_target_pairs={{0,8},{1,9},{2,10},{3,11},{4,12},{5,13},{6,14},{7,15},{8,0},{9,1},... | collective-permute-start | bytes 331784 | tf_op jit(solution)/shard_map/ppermute | solution.py:57
  16.1 11.0 %collective-permute-start.7 = (bf16[2,48,576]{2,1,0:T(8,128)(2,1)S(1)}, bf16[2,48,576]{2,1,0:T(8,128)(2,1)S(1)}, u32[]{:S(2)}, u32[]{:S(2)}) collective-permute-start(bf16[2,48,576]{2,1,0:T(8,128)(2,1)S(1)} %get-tuple-element.33.bundle), channel_id=1, source_target_pairs={{0,4},{1,5},{2,6},{3,7},{4,0},{5,1},{6,2},{7,3},{8,12},{9,13},{10,... | collective-permute-start | bytes 331784 | tf_op jit(solution)/shard_map/ppermute | solution.py:57
  21.9 8.0 %copy-start.3 = (bf16[128,768]{1,0:T(8,128)(2,1)S(1)}, bf16[128,768]{1,0:T(8,128)(2,1)}, u32[]{:S(2)}) copy-start(bf16[128,768]{1,0:T(8,128)(2,1)} %get-tuple-element.42.refs_0_) | copy-start | bytes 589828
  27.3 4.9 %collective-permute-start.10 = (bf16[4,144,768]{2,1,0:T(8,128)(2,1)S(1)}, bf16[4,144,768]{2,1,0:T(8,128)(2,1)S(1)}, u32[]{:S(2)}, u32[]{:S(2)}) collective-permute-start(bf16[4,144,768]{2,1,0:T(8,128)(2,1)S(1)} %get-tuple-element.35.refs_0_), channel_id=1, source_target_pairs={{0,1},{1,0},{2,3},{3,2},{4,5},{5,4},{6,7},{7,6},{8,9},{9,8},{10,11... | collective-permute-start | bytes 2654216 | tf_op jit(solution)/shard_map/ppermute | solution.py:61
  29.4 2.8 %collective-permute-start.11 = (bf16[4,2,48,576]{3,2,1,0:T(8,128)(2,1)S(1)}, bf16[4,2,48,576]{3,2,1,0:T(8,128)(2,1)S(1)}, u32[]{:S(2)}, u32[]{:S(2)}) collective-permute-start(bf16[4,2,48,576]{3,2,1,0:T(8,128)(2,1)S(1)} %get-tuple-element.36.refs_2_.refs_1_), channel_id=1, source_target_pairs={{0,1},{1,0},{2,3},{3,2},{4,5},{5,4},{6,7},{7,6},{8,9},{9,8},{10,11... | collective-permute-start | bytes 1327112 | tf_op jit(solution)/shard_map/ppermute | solution.py:61
  29.5 8.7 %collective-permute-start.15 = (bf16[2,4,48,768]{3,2,1,0:T(8,128)(2,1)S(1)}, bf16[2,4,48,768]{3,2,1,0:T(8,128)(2,1)S(1)}, u32[]{:S(2)}, u32[]{:S(2)}) collective-permute-start(bf16[2,4,48,768]{3,2,1,0:T(8,128)(2,1)S(1)} %get-tuple-element.41.mine), channel_id=1, source_target_pairs={{0,1},{1,0},{2,3},{3,2},{4,5},{5,4},{6,7},{7,6},{8,9},{9,8},{10,11... | collective-permute-start | bytes 1769480 | tf_op jit(solution)/shard_map/ppermute | solution.py:61
  30.0 8.2 %copy-start.5 = (f32[768]{0:T(1024)S(1)}, f32[768]{0:T(1024)}, u32[]{:S(2)}) copy-start(f32[768]{0:T(1024)} %param.16) | copy-start | bytes 9220
  30.0 8.3 %collective-permute-start.16 = (bf16[128,768]{1,0:T(8,128)(2,1)S(1)}, bf16[128,768]{1,0:T(8,128)(2,1)S(1)}, u32[]{:S(2)}, u32[]{:S(2)}) collective-permute-start(bf16[128,768]{1,0:T(8,128)(2,1)S(1)} %shard_map.116.tokens), channel_id=1, source_target_pairs={{0,2},{1,3},{2,0},{3,1},{4,6},{5,7},{6,4},{7,5},{8,10},{9,11},{10,... | collective-permute-start | bytes 589832 | tf_op jit(solution)/shard_map/ppermute | solution.py:57
  35.5 5.7 %collective-permute-start.12 = (bf16[2,128,192]{2,1,0:T(8,128)(2,1)S(1)}, bf16[2,128,192]{2,1,0:T(8,128)(2,1)S(1)}, u32[]{:S(2)}, u32[]{:S(2)}) collective-permute-start(bf16[2,128,192]{2,1,0:T(8,128)(2,1)S(1)} %get-tuple-element.37), channel_id=1, source_target_pairs={{0,18},{1,19},{2,16},{3,17},{4,22},{5,23},{6,20},{7,21},{8,26},{9,... | collective-permute-start | bytes 294920 | tf_op jit(solution)/shard_map/ppermute | solution.py:57
  36.0 7.7 %collective-permute-start.13 = (bf16[2,128,192]{2,1,0:T(8,128)(2,1)S(1)}, bf16[2,128,192]{2,1,0:T(8,128)(2,1)S(1)}, u32[]{:S(2)}, u32[]{:S(2)}) collective-permute-start(bf16[2,128,192]{2,1,0:T(8,128)(2,1)S(1)} %get-tuple-element.38), channel_id=1, source_target_pairs={{0,16},{1,17},{2,18},{3,19},{4,20},{5,21},{6,22},{7,23},{8,24},{9,... | collective-permute-start | bytes 294920 | tf_op jit(solution)/shard_map/ppermute | solution.py:57
  37.0 6.7 %collective-permute-start.14 = (bf16[2,128,192]{2,1,0:T(8,128)(2,1)S(1)}, bf16[2,128,192]{2,1,0:T(8,128)(2,1)S(1)}, u32[]{:S(2)}, u32[]{:S(2)}) collective-permute-start(bf16[2,128,192]{2,1,0:T(8,128)(2,1)S(1)} %get-tuple-element.39), channel_id=1, source_target_pairs={{0,2},{1,3},{2,0},{3,1},{4,6},{5,7},{6,4},{7,5},{8,10},{9,11},{10,... | collective-permute-start | bytes 294920 | tf_op jit(solution)/shard_map/ppermute | solution.py:57
  44.3 7.3 %collective-permute-start.17 = (bf16[128,768]{1,0:T(8,128)(2,1)S(1)}, bf16[128,768]{1,0:T(8,128)(2,1)S(1)}, u32[]{:S(2)}, u32[]{:S(2)}) collective-permute-start(bf16[128,768]{1,0:T(8,128)(2,1)S(1)} %shard_map.117.other_in), channel_id=1, source_target_pairs={{0,4},{1,5},{4,8},{5,9},{6,2},{7,3},{8,12},{9,13},{10,6},{11,7},{1... | collective-permute-start | bytes 589832 | tf_op jit(solution)/shard_map/ppermute | solution.py:57
  52.3 3.0 %collective-permute-start.18 = (bf16[128,768]{1,0:T(8,128)(2,1)S(1)}, bf16[128,768]{1,0:T(8,128)(2,1)S(1)}, u32[]{:S(2)}, u32[]{:S(2)}) collective-permute-start(bf16[128,768]{1,0:T(8,128)(2,1)S(1)} %get-tuple-element.48), channel_id=1, source_target_pairs={{0,1},{1,0},{2,3},{3,2},{4,5},{5,4},{6,7},{7,6},{8,9},{9,8},{10,11... | collective-permute-start | bytes 589832 | tf_op jit(solution)/shard_map/ppermute | solution.py:61

commit v13 on v12

--- a/solution.py
+++ b/solution.py
@@ -29,15 +29,6 @@
         compiler_params=pltpu.CompilerParams(vmem_limit_bytes=limit * 1024 * 1024),
         cost_estimate=pl.CostEstimate(flops=flops, bytes_accessed=moved, transcendentals=0),
     )(*args)
-
-
-def copy_body(*refs):
-    refs[-1][...] = refs[0][...]
-
-
-def gate(value, *after):
-    specs = [VMEM] * (1 + len(after))
-    return call(copy_body, [(value.shape, value.dtype)], specs, (value, *after), 0)[0]
 
 
 def device_pairs(target):
@@ -123,7 +114,7 @@
 
 
 def arrived_body(
-    own, by_x, by_y, out_own, out3, out2, out1, bundle, x_block, outs
+    own, by_x, by_y, out_own, out3, out2, out1, raw, bundle, x_block, cargo
 ):
     del by_y
     side = lax.rem(lax.axis_index("lat"), 2)
@@ -131,22 +122,27 @@
     bundle[side] = own[...]
     bundle[1 - side] = by_x[rows:, :width]
     x_block[...] = by_x[:rows, :]
+    half = out_own.shape[0]
     for at, block in enumerate((out_own, out1, out2, out3)):
-        outs[at] = block[...]
+        cargo[at * half : (at + 1) * half, :] = block[...]
+    cargo[4 * half :, :] = raw[...]
 
 
 def complete_body(
-    bundle, level3, level2, level1, message, x_block, by_y, by_xy, outs, crossed, gains, *results
+    bundle, level3, level2, level1, message, x_block, by_y, by_xy, cargo, crossed, gains, *results
 ):
     del gains
-    weights, near, both = results
+    weights, near, both, raw_x = results
     rows = x_block.shape[0]
     for at, block in enumerate((bundle, level1, level2, level3)):
         weights[at] = block[...]
     for at, block in enumerate((message, x_block, by_y, by_xy)):
         near[at] = block[:rows, :]
-    both[0] = outs[...]
-    both[1] = crossed[...]
+    half = both.shape[2]
+    for at in range(4):
+        both[0, at] = cargo[at * half : (at + 1) * half, :]
+        both[1, at] = crossed[at * half : (at + 1) * half, :]
+    raw_x[...] = crossed[4 * half :, :]
 
 
 def pair_away(flip):
@@ -441,15 +437,15 @@
             (w_qkv, w_out),
             0,
         )
-        bundle, x_block, outs = call(
+        bundle, x_block, cargo = call(
             arrived_body,
             [
                 ((2, half, 3 * quarter), BF16),
                 ((rows, width), BF16),
-                ((4, half, width), BF16),
+                ((4 * half + count, width), BF16),
             ],
-            [VMEM] * 7,
-            (qkv_own, by_x, by_y, out_own, *levels[::-1]),
+            [VMEM] * 8,
+            (qkv_own, by_x, by_y, out_own, *levels[::-1], raw_tokens),
             0,
         )
     size = 4 * w_conv.shape[2]
@@ -465,12 +461,13 @@
         0,
     )
     if direct:
-        qkv_mine, near, out_mine = call(
+        qkv_mine, near, out_mine, other_tokens = call(
             complete_body,
             [
                 ((4, 2, half, 3 * quarter), BF16),
                 ((4, rows, width), BF16),
                 ((2, 4, half, width), BF16),
+                ((count, width), BF16),
             ],
             [VMEM] * 11,
             (
@@ -480,8 +477,8 @@
                 x_block,
                 by_y,
                 flip_chips(x_block, 0, 1),
-                outs,
-                flip_chips(outs, 1, 0),
+                cargo,
+                flip_chips(cargo, 1, 0),
                 gains,
             ),
             0,
@@ -490,12 +487,11 @@
         join = join_columns
     else:
         near = jnp.stack([message, by_x, by_y, flip_chips(by_x, 0, 1)])
+        other_tokens = flip_chips(raw_tokens, 1, 0)
         qkv_mine, qkv_other = gather_plain(w_qkv, 3 * quarter)
         out_mine, out_other = gather_plain(w_out, width)
         join = join_bundles
     far = swap_cores(near)
-    raw_tokens = gate(raw_tokens, qkv_mine)
-    other_tokens = flip_chips(raw_tokens, 1, 0)
 
     pieces = call(
         attend_body,

time: 56.3 us -> 57.4 us (1.020)
  local copies, waits for them, and re-layouts: 2.25 us -> 3.18 us
    unnamed x16 -> x18, local copies, waits for them, and re-layouts: 2.25 us -> 3.17 us
    ppermute x4, starting transfers between devices: 4.58 us -> 5.19 us  [swap_cores(): return lax.ppermute(values, 'lon', [(0, 1), (1, 0)])]
    ppermute x15 -> x14, waiting for transfers between devices: 19.3 us -> 18.9 us  [move(): return lax.ppermute(values, AXES, device_pairs(target))]
    ppermute x15 -> x14, starting transfers between devices: 14.5 us -> 14.2 us  [move(): return lax.ppermute(values, AXES, device_pairs(target))]
    pallas_call x11 -> x10, Pallas kernels: 9.51 us -> 9.51 us  [call(): pl.pallas_call(body, out_shape=outs, in_specs=specs, out_specs=tuple((VME...]
  transfers between devices with their start and end apart: 19 -> 18, of which waited for: 7 -> 8; matrix products, arithmetic and copies ran while one was open for 1% -> 1% of each run, Pallas kernels for 11% -> 10%
where the time goes in v13:
time: 57.4 us; the launch traced here: 57.2 us
  waiting for transfers between devices  22.3 us (39%)
  starting transfers between devices  19.4 us (34%)
  Pallas kernels  9.51 us (17%)
  local copies, waits for them, and re-layouts  3.18 us (6%)
  between operations  2.1 us (4%)
  other arithmetic  0.71 us (1%)
    ppermute x14, waiting for transfers between devices, move(): return lax.ppermute(values, AXES, device_pairs(target))  18.9 us
    ppermute x14, starting transfers between devices, move(): return lax.ppermute(values, AXES, device_pairs(target))  14.2 us
    pallas_call x10, Pallas kernels, call(): pl.pallas_call(body, out_shape=outs, in_specs=specs, out_specs=tuple((VME...  9.51 us
    ppermute x4, starting transfers between devices, swap_cores(): return lax.ppermute(values, 'lon', [(0, 1), (1, 0)])  5.19 us
    ppermute x4, waiting for transfers between devices, swap_cores(): return lax.ppermute(values, 'lon', [(0, 1), (1, 0)])  3.32 us
    unnamed x18, local copies, waits for them, and re-layouts  3.17 us
  transfers between devices with their start and end apart: 18, of which 8 were waited for; matrix products, arithmetic and copies ran while one was open for 1% of the time, Pallas kernels for 10%

profile of v13, /device:TPU:3, one launch (start us, length us, event | category | flops | bytes accessed | tf_op | source)
XLA Modules:
  0.0 57.2 jit_solution(15232959114389429269)
XLA Ops:
  0.0 2.1 %shard_map.110 = (bf16[192,768]{1,0:T(8,128)(2,1)}, bf16[128,768]{1,0:T(8,128)(2,1)}, bf16[48,768]{1,0:T(8,128)(2,1)}) custom-call(bf16[128,768]{1,0:T(8,128)(2,1)} %bitcast.4, bf16[12,128]{1,0:T(8,128)(2,1)} %bitcast.5, f32[768]{0:T(1024)} %refs_2_.1, bf16[96,2304]{1,0:T(8,128)(2,1)} %refs_3_.1, bf16[96,768]{1,0:T(8,128)(2,1)} %refs_4_.1), custom_call_target="tpu_custom_call" | custom-call | flops 983040 | bytes 792576 | tf_op jit(solution)/shard_map/pallas_call | solution.py:23
  2.1 0.0 copy-start.7
  2.2 1.3 %collective-permute-start.1 = (bf16[192,768]{1,0:T(8,128)(2,1)}, bf16[192,768]{1,0:T(8,128)(2,1)S(1)}, u32[]{:S(2)}, u32[]{:S(2)}) collective-permute-start(bf16[192,768]{1,0:T(8,128)(2,1)} %get-tuple-element.29.message), channel_id=1, source_target_pairs={{0,16},{1,17},{2,18},{3,19},{4,20},{5,21},{6,22},{7,23},{8,24},{9,... | collective-permute-start | bytes 884744 | tf_op jit(solution)/shard_map/ppermute | solution.py:48
  3.5 0.3 collective-permute-start
  3.7 3.3 %collective-permute-start.2 = (bf16[48,768]{1,0:T(8,128)(2,1)}, bf16[48,768]{1,0:T(8,128)(2,1)S(1)}, u32[]{:S(2)}, u32[]{:S(2)}) collective-permute-start(bf16[48,768]{1,0:T(8,128)(2,1)} %get-tuple-element.31), channel_id=1, source_target_pairs={{0,12},{1,13},{2,14},{3,15},{4,8},{5,9},{6,10},{7,11},{8,4},{9,5},... | collective-permute-start | bytes 221192 | tf_op jit(solution)/shard_map/ppermute | solution.py:48
  7.0 0.0 collective-permute-start.3
  7.0 0.3 collective-permute-start.4
  7.3 1.0 %copy-done = bf16[96,2304]{1,0:T(8,128)(2,1)S(1)} copy-done((bf16[96,2304]{1,0:T(8,128)(2,1)S(1)}, bf16[96,2304]{1,0:T(8,128)(2,1)}, u32[]{:S(2)}) %copy-start) | copy-done | bytes 442392
  8.3 0.9 %copy-done.3 = bf16[96,768]{1,0:T(8,128)(2,1)S(1)} copy-done((bf16[96,768]{1,0:T(8,128)(2,1)S(1)}, bf16[96,768]{1,0:T(8,128)(2,1)}, u32[]{:S(2)}) %copy-start.3) | copy-done | bytes 147480
  9.3 0.2 shard_map.109
  9.4 0.0 collective-permute-done.2.out3
  9.4 4.1 %collective-permute-done.3.out2 = bf16[48,768]{1,0:T(8,128)(2,1)S(1)} collective-permute-done((bf16[48,768]{1,0:T(8,128)(2,1)}, bf16[48,768]{1,0:T(8,128)(2,1)S(1)}, u32[]{:S(2)}, u32[]{:S(2)}) %collective-permute-start.3) | collective-permute-done | bytes 73760 | tf_op jit(solution)/shard_map/ppermute | solution.py:48
  13.5 0.0 collective-permute-done.4.out1
  13.5 0.0 collective-permute-done.1.by_y
  13.5 0.0 copy-start.1
  13.5 0.9 %copy-done.1 = bf16[128,768]{1,0:T(8,128)(2,1)S(1)} copy-done((bf16[128,768]{1,0:T(8,128)(2,1)S(1)}, bf16[128,768]{1,0:T(8,128)(2,1)}, u32[]{:S(2)}) %copy-start.1) | copy-done | bytes 196632
  14.5 0.1 shard_map.111
  14.5 1.3 %collective-permute-start.9 = (bf16[320,768]{1,0:T(8,128)(2,1)S(1)}, bf16[320,768]{1,0:T(8,128)(2,1)S(1)}, u32[]{:S(2)}, u32[]{:S(2)}) collective-permute-start(bf16[320,768]{1,0:T(8,128)(2,1)S(1)} %get-tuple-element.36.cargo), channel_id=1, source_target_pairs={{0,2},{1,3},{2,0},{3,1},{4,6},{5,7},{6,4},{7,5},{8,10},{9,11},{10,... | collective-permute-start | bytes 1474568 | tf_op jit(solution)/shard_map/ppermute | solution.py:48
  15.8 0.2 collective-permute-start.8
  16.0 0.2 collective-permute-start.5
  16.2 0.5 collective-permute-start.6
  16.7 2.9 %collective-permute-start.7 = (bf16[2,48,576]{2,1,0:T(8,128)(2,1)S(1)}, bf16[2,48,576]{2,1,0:T(8,128)(2,1)S(1)}, u32[]{:S(2)}, u32[]{:S(2)}) collective-permute-start(bf16[2,48,576]{2,1,0:T(8,128)(2,1)S(1)} %get-tuple-element.35.bundle), channel_id=1, source_target_pairs={{0,4},{1,5},{2,6},{3,7},{4,0},{5,1},{6,2},{7,3},{8,12},{9,13},{10,... | collective-permute-start | bytes 331784 | tf_op jit(solution)/shard_map/ppermute | solution.py:48
  19.6 0.2 copy.13.w_conv
  19.8 0.1 copy.12.taps
  21.8 1.0 %shard_map.112 = (bf16[2,3,256,256]{3,2,1,0:T(8,128)(2,1)S(1)}, bf16[256,512]{1,0:T(8,128)(2,1)S(1)}, f32[8,128]{1,0:T(8,128)S(1)}) custom-call(s32[1]{0:T(128)S(6)} %copy.14.lon_half, s32[1]{0:T(128)S(6)} %copy.15.lat_half, s32[1]{0:T(128)S(6)} %copy.16.quad_off, f32[16,2]{1,0:T(8,128)S(1)} %copy.12.taps, bf16[2,768,64]{2,1,0:T(8,128)(2,1)S(1)} %copy.13.w_conv, ...), custom_call_target="tpu_custom_call" | custom-call | bytes 417932 | tf_op jit(solution)/shard_map/pallas_call | solution.py:23
  22.9 2.5 %collective-permute-done.6.level2 = bf16[2,48,576]{2,1,0:T(8,128)(2,1)S(1)} collective-permute-done((bf16[2,48,576]{2,1,0:T(8,128)(2,1)S(1)}, bf16[2,48,576]{2,1,0:T(8,128)(2,1)S(1)}, u32[]{:S(2)}, u32[]{:S(2)}) %collective-permute-start.6) | collective-permute-done | bytes 110624 | tf_op jit(solution)/shard_map/ppermute | solution.py:48
  25.4 0.8 %collective-permute-done.9.crossed = bf16[320,768]{1,0:T(8,128)(2,1)S(1)} collective-permute-done((bf16[320,768]{1,0:T(8,128)(2,1)S(1)}, bf16[320,768]{1,0:T(8,128)(2,1)S(1)}, u32[]{:S(2)}, u32[]{:S(2)}) %collective-permute-start.9) | collective-permute-done | bytes 491552 | tf_op jit(solution)/shard_map/ppermute | solution.py:48
  26.2 0.1 shard_map.113
  26.4 3.3 %collective-permute-start.10 = (bf16[4,144,768]{2,1,0:T(8,128)(2,1)S(1)}, bf16[4,144,768]{2,1,0:T(8,128)(2,1)S(1)}, u32[]{:S(2)}, u32[]{:S(2)}) collective-permute-start(bf16[4,144,768]{2,1,0:T(8,128)(2,1)S(1)} %get-tuple-element.37.refs_0_), channel_id=1, source_target_pairs={{0,1},{1,0},{2,3},{3,2},{4,5},{5,4},{6,7},{7,6},{8,9},{9,8},{10,11... | collective-permute-start | bytes 2654216 | tf_op jit(solution)/shard_map/ppermute | solution.py:52
  29.7 0.1 collective-permute-start.11
  29.7 0.4 collective-permute-start.15
  30.2 2.2 %collective-permute-done.11.refs_3_ = bf16[4,2,48,576]{3,2,1,0:T(8,128)(2,1)S(1)} collective-permute-done((bf16[4,2,48,576]{3,2,1,0:T(8,128)(2,1)S(1)}, bf16[4,2,48,576]{3,2,1,0:T(8,128)(2,1)S(1)}, u32[]{:S(2)}, u32[]{:S(2)}) %collective-permute-start.11) | collective-permute-done | bytes 442400 | tf_op jit(solution)/shard_map/ppermute | solution.py:52
  32.4 3.3 %shard_map.114 = (bf16[2,128,192]{2,1,0:T(8,128)(2,1)S(1)}, bf16[2,128,192]{2,1,0:T(8,128)(2,1)S(1)}, bf16[2,128,192]{2,1,0:T(8,128)(2,1)S(1)}, bf16[2,128,192]{2,1,0:T(8,128)(2,1)S(1)}) custom-call(bf16[4,144,768]{2,1,0:T(8,128)(2,1)S(1)} %get-tuple-element.37.refs_0_, bf16[4,144,768]{2,1,0:T(8,128)(2,1)S(1)} %collective-permute-done.10.refs_1_, ...), custom_call_target="tpu_custom_call" | custom-call | flops 905969664 | bytes 2654208 | tf_op jit(solution)/shard_map/pallas_call | solution.py:23
  35.7 2.0 %collective-permute-start.12 = (bf16[2,128,192]{2,1,0:T(8,128)(2,1)S(1)}, bf16[2,128,192]{2,1,0:T(8,128)(2,1)S(1)}, u32[]{:S(2)}, u32[]{:S(2)}) collective-permute-start(bf16[2,128,192]{2,1,0:T(8,128)(2,1)S(1)} %get-tuple-element.39), channel_id=1, source_target_pairs={{0,18},{1,19},{2,16},{3,17},{4,22},{5,23},{6,20},{7,21},{8,26},{9,... | collective-permute-start | bytes 294920 | tf_op jit(solution)/shard_map/ppermute | solution.py:48
  37.7 0.2 collective-permute-start.13
  37.9 0.5 collective-permute-start.14
  38.4 0.1 shard_map.115.weights
  38.5 0.0 copy-start.2
  38.6 2.8 %collective-permute-done.12.piece3 = bf16[2,128,192]{2,1,0:T(8,128)(2,1)S(1)} collective-permute-done((bf16[2,128,192]{2,1,0:T(8,128)(2,1)S(1)}, bf16[2,128,192]{2,1,0:T(8,128)(2,1)S(1)}, u32[]{:S(2)}, u32[]{:S(2)}) %collective-permute-start.12) | collective-permute-done | bytes 98336 | tf_op jit(solution)/shard_map/ppermute | solution.py:48
  41.4 3.5 %collective-permute-done.13.piece2 = bf16[2,128,192]{2,1,0:T(8,128)(2,1)S(1)} collective-permute-done((bf16[2,128,192]{2,1,0:T(8,128)(2,1)S(1)}, bf16[2,128,192]{2,1,0:T(8,128)(2,1)S(1)}, u32[]{:S(2)}, u32[]{:S(2)}) %collective-permute-start.13) | collective-permute-done | bytes 98336 | tf_op jit(solution)/shard_map/ppermute | solution.py:48
  44.9 0.6 shard_map.116.other_in
  45.5 1.3 %collective-permute-start.16 = (bf16[128,768]{1,0:T(8,128)(2,1)S(1)}, bf16[128,768]{1,0:T(8,128)(2,1)S(1)}, u32[]{:S(2)}, u32[]{:S(2)}) collective-permute-start(bf16[128,768]{1,0:T(8,128)(2,1)S(1)} %shard_map.116.other_in), channel_id=1, source_target_pairs={{0,4},{1,5},{4,8},{5,9},{6,2},{7,3},{8,12},{9,13},{10,6},{11,7},{1... | collective-permute-start | bytes 589832 | tf_op jit(solution)/shard_map/ppermute | solution.py:48
  46.8 1.4 %shard_map.117 = (bf16[128,768]{1,0:T(8,128)(2,1)S(1)}, f32[256,768]{1,0:T(8,128)S(1)}) custom-call(f32[8,128]{1,0:T(8,128)S(1)} %get-tuple-element.34.gains, f32[1,768]{1,0:T(1,128)S(1)} %broadcast_in_dim.6.gain, bf16[2,128,192]{2,1,0:T(8,128)(2,1)S(1)} %collective-permute-done.12.piece3, bf16[2,128,192]{2,1,0:T(8,128)(2,1)S(1)} %collective-permute-done.13.piece2, ...), custom_call_target="tpu_custom_call" | custom-call | flops 452984832 | bytes 3021824 | tf_op jit(solution)/shard_map/pallas_call | solution.py:23
  48.2 5.1 %collective-permute-done.16.halo = bf16[128,768]{1,0:T(8,128)(2,1)S(1)} collective-permute-done((bf16[128,768]{1,0:T(8,128)(2,1)S(1)}, bf16[128,768]{1,0:T(8,128)(2,1)S(1)}, u32[]{:S(2)}, u32[]{:S(2)}) %collective-permute-start.16) | collective-permute-done | bytes 196640 | tf_op jit(solution)/shard_map/ppermute | solution.py:48
  53.3 0.7 %shard_map.118 = (f32[128,768]{1,0:T(8,128)S(1)}, bf16[128,768]{1,0:T(8,128)(2,1)S(1)}) custom-call(f32[8,128]{1,0:T(8,128)S(1)} %get-tuple-element.34.gains, bf16[128,768]{1,0:T(8,128)(2,1)S(1)} %collective-permute-done.16.halo, bf16[2,3,256,256]{3,2,1,0:T(8,128)(2,1)S(1)} %get-tuple-element.45.blocks, bf16[256,512]{1,0:T(8,128)(2,1)S(1)} %get-tuple-element.46.coeffs, ...), custom_call_target="tpu_custom_call" | custom-call | flops 100663296 | bytes 2232320 | tf_op jit(solution)/shard_map/pallas_call | solution.py:23
  54.0 1.4 %collective-permute-start.17 = (bf16[128,768]{1,0:T(8,128)(2,1)S(1)}, bf16[128,768]{1,0:T(8,128)(2,1)S(1)}, u32[]{:S(2)}, u32[]{:S(2)}) collective-permute-start(bf16[128,768]{1,0:T(8,128)(2,1)S(1)} %get-tuple-element.50), channel_id=1, source_target_pairs={{0,1},{1,0},{2,3},{3,2},{4,5},{5,4},{6,7},{7,6},{8,9},{9,8},{10,11... | collective-permute-start | bytes 589832 | tf_op jit(solution)/shard_map/ppermute | solution.py:52
  55.4 1.1 %collective-permute-done.17 = bf16[128,768]{1,0:T(8,128)(2,1)S(1)} collective-permute-done((bf16[128,768]{1,0:T(8,128)(2,1)S(1)}, bf16[128,768]{1,0:T(8,128)(2,1)S(1)}, u32[]{:S(2)}, u32[]{:S(2)}) %collective-permute-start.17) | collective-permute-done | bytes 196640 | tf_op jit(solution)/shard_map/ppermute | solution.py:52
  56.5 0.7 %fusion = bf16[1,128,768]{2,1,0:T(8,128)(2,1)} fusion(f32[128,768]{1,0:T(8,128)S(1)} %get-tuple-element.49, bf16[128,768]{1,0:T(8,128)(2,1)S(1)} %collective-permute-done.17), kind=kLoop, calls=%fused_computation.1 | loop fusion | flops 294912 | bytes 786432 | tf_op jit(solution)/shard_map/broadcast_in_dim | solution.py:540
  (18 shorter events, 0.0 us)
Async XLA Ops:
  0.0 19.6 %copy-start.5 = (bf16[2,768,64]{1,2,0:T(8,128)(2,1)S(1)}, bf16[2,768,64]{1,2,0:T(8,128)(2,1)}, u32[]{:S(2)}) copy-start(bf16[2,768,64]{1,2,0:T(8,128)(2,1)} %param.17) | copy-start | bytes 589828
  2.1 17.7 %copy-start.7 = (f32[16,2]{0,1:T(2,128)S(1)}, f32[16,2]{0,1:T(2,128)}, u32[]{:S(2)}) copy-start(f32[16,2]{0,1:T(2,128)} %param.18) | copy-start | bytes 388
  2.2 11.4 %collective-permute-start.1 = (bf16[192,768]{1,0:T(8,128)(2,1)}, bf16[192,768]{1,0:T(8,128)(2,1)S(1)}, u32[]{:S(2)}, u32[]{:S(2)}) collective-permute-start(bf16[192,768]{1,0:T(8,128)(2,1)} %get-tuple-element.29.message), channel_id=1, source_target_pairs={{0,16},{1,17},{2,18},{3,19},{4,20},{5,21},{6,22},{7,23},{8,24},{9,... | collective-permute-start | bytes 884744 | tf_op jit(solution)/shard_map/ppermute | solution.py:48
  3.5 10.1 %collective-permute-start = (bf16[192,768]{1,0:T(8,128)(2,1)}, bf16[192,768]{1,0:T(8,128)(2,1)S(1)}, u32[]{:S(2)}, u32[]{:S(2)}) collective-permute-start(bf16[192,768]{1,0:T(8,128)(2,1)} %get-tuple-element.29.message), channel_id=1, source_target_pairs={{0,2},{1,3},{2,0},{3,1},{4,6},{5,7},{6,4},{7,5},{8,10},{9,11},{10,... | collective-permute-start | bytes 884744 | tf_op jit(solution)/shard_map/ppermute | solution.py:48
  3.7 5.7 %collective-permute-start.2 = (bf16[48,768]{1,0:T(8,128)(2,1)}, bf16[48,768]{1,0:T(8,128)(2,1)S(1)}, u32[]{:S(2)}, u32[]{:S(2)}) collective-permute-start(bf16[48,768]{1,0:T(8,128)(2,1)} %get-tuple-element.31), channel_id=1, source_target_pairs={{0,12},{1,13},{2,14},{3,15},{4,8},{5,9},{6,10},{7,11},{8,4},{9,5},... | collective-permute-start | bytes 221192 | tf_op jit(solution)/shard_map/ppermute | solution.py:48
  7.0 6.5 %collective-permute-start.3 = (bf16[48,768]{1,0:T(8,128)(2,1)}, bf16[48,768]{1,0:T(8,128)(2,1)S(1)}, u32[]{:S(2)}, u32[]{:S(2)}) collective-permute-start(bf16[48,768]{1,0:T(8,128)(2,1)} %get-tuple-element.31), channel_id=1, source_target_pairs={{0,8},{1,9},{2,10},{3,11},{4,12},{5,13},{6,14},{7,15},{8,0},{9,1},... | collective-permute-start | bytes 221192 | tf_op jit(solution)/shard_map/ppermute | solution.py:48
  7.0 6.5 %collective-permute-start.4 = (bf16[48,768]{1,0:T(8,128)(2,1)}, bf16[48,768]{1,0:T(8,128)(2,1)S(1)}, u32[]{:S(2)}, u32[]{:S(2)}) collective-permute-start(bf16[48,768]{1,0:T(8,128)(2,1)} %get-tuple-element.31), channel_id=1, source_target_pairs={{0,4},{1,5},{2,6},{3,7},{4,0},{5,1},{6,2},{7,3},{8,12},{9,13},{10,... | collective-permute-start | bytes 221192 | tf_op jit(solution)/shard_map/ppermute | solution.py:48
  7.3 1.0 %copy-start = (bf16[96,2304]{1,0:T(8,128)(2,1)S(1)}, bf16[96,2304]{1,0:T(8,128)(2,1)}, u32[]{:S(2)}) copy-start(bf16[96,2304]{1,0:T(8,128)(2,1)} %refs_3_.1) | copy-start | bytes 1327108
  8.3 0.9 %copy-start.3 = (bf16[96,768]{1,0:T(8,128)(2,1)S(1)}, bf16[96,768]{1,0:T(8,128)(2,1)}, u32[]{:S(2)}) copy-start(bf16[96,768]{1,0:T(8,128)(2,1)} %refs_4_.1) | copy-start | bytes 442372
  13.5 0.9 %copy-start.1 = (bf16[128,768]{1,0:T(8,128)(2,1)S(1)}, bf16[128,768]{1,0:T(8,128)(2,1)}, u32[]{:S(2)}) copy-start(bf16[128,768]{1,0:T(8,128)(2,1)} %get-tuple-element.32.raw.tokens) | copy-start | bytes 589828
  14.5 11.8 %copy-start.4 = (bf16[192,768]{1,0:T(8,128)(2,1)S(1)}, bf16[192,768]{1,0:T(8,128)(2,1)}, u32[]{:S(2)}) copy-start(bf16[192,768]{1,0:T(8,128)(2,1)} %get-tuple-element.29.message) | copy-start | bytes 884740
  14.5 11.7 %collective-permute-start.9 = (bf16[320,768]{1,0:T(8,128)(2,1)S(1)}, bf16[320,768]{1,0:T(8,128)(2,1)S(1)}, u32[]{:S(2)}, u32[]{:S(2)}) collective-permute-start(bf16[320,768]{1,0:T(8,128)(2,1)S(1)} %get-tuple-element.36.cargo), channel_id=1, source_target_pairs={{0,2},{1,3},{2,0},{3,1},{4,6},{5,7},{6,4},{7,5},{8,10},{9,11},{10,... | collective-permute-start | bytes 1474568 | tf_op jit(solution)/shard_map/ppermute | solution.py:48
  15.8 9.6 %collective-permute-start.8 = (bf16[144,768]{1,0:T(8,128)(2,1)S(1)}, bf16[144,768]{1,0:T(8,128)(2,1)S(1)}, u32[]{:S(2)}, u32[]{:S(2)}) collective-permute-start(bf16[144,768]{1,0:T(8,128)(2,1)S(1)} %get-tuple-element.33.message.x_block), channel_id=1, source_target_pairs={{0,16},{1,17},{2,18},{3,19},{4,20},{5,21},{6,22},{7,23},{8,24},{9,... | collective-permute-start | bytes 663560 | tf_op jit(solution)/shard_map/ppermute | solution.py:48
  16.0 6.8 %collective-permute-start.5 = (bf16[2,48,576]{2,1,0:T(8,128)(2,1)S(1)}, bf16[2,48,576]{2,1,0:T(8,128)(2,1)S(1)}, u32[]{:S(2)}, u32[]{:S(2)}) collective-permute-start(bf16[2,48,576]{2,1,0:T(8,128)(2,1)S(1)} %get-tuple-element.35.bundle), channel_id=1, source_target_pairs={{0,12},{1,13},{2,14},{3,15},{4,8},{5,9},{6,10},{7,11},{8,4},{9,5},... | collective-permute-start | bytes 331784 | tf_op jit(solution)/shard_map/ppermute | solution.py:48
  16.2 9.2 %collective-permute-start.6 = (bf16[2,48,576]{2,1,0:T(8,128)(2,1)S(1)}, bf16[2,48,576]{2,1,0:T(8,128)(2,1)S(1)}, u32[]{:S(2)}, u32[]{:S(2)}) collective-permute-start(bf16[2,48,576]{2,1,0:T(8,128)(2,1)S(1)} %get-tuple-element.35.bundle), channel_id=1, source_target_pairs={{0,8},{1,9},{2,10},{3,11},{4,12},{5,13},{6,14},{7,15},{8,0},{9,1},... | collective-permute-start | bytes 331784 | tf_op jit(solution)/shard_map/ppermute | solution.py:48
  16.7 8.7 %collective-permute-start.7 = (bf16[2,48,576]{2,1,0:T(8,128)(2,1)S(1)}, bf16[2,48,576]{2,1,0:T(8,128)(2,1)S(1)}, u32[]{:S(2)}, u32[]{:S(2)}) collective-permute-start(bf16[2,48,576]{2,1,0:T(8,128)(2,1)S(1)} %get-tuple-element.35.bundle), channel_id=1, source_target_pairs={{0,4},{1,5},{2,6},{3,7},{4,0},{5,1},{6,2},{7,3},{8,12},{9,13},{10,... | collective-permute-start | bytes 331784 | tf_op jit(solution)/shard_map/ppermute | solution.py:48
  26.4 6.0 %collective-permute-start.10 = (bf16[4,144,768]{2,1,0:T(8,128)(2,1)S(1)}, bf16[4,144,768]{2,1,0:T(8,128)(2,1)S(1)}, u32[]{:S(2)}, u32[]{:S(2)}) collective-permute-start(bf16[4,144,768]{2,1,0:T(8,128)(2,1)S(1)} %get-tuple-element.37.refs_0_), channel_id=1, source_target_pairs={{0,1},{1,0},{2,3},{3,2},{4,5},{5,4},{6,7},{7,6},{8,9},{9,8},{10,11... | collective-permute-start | bytes 2654216 | tf_op jit(solution)/shard_map/ppermute | solution.py:52
  29.7 2.8 %collective-permute-start.11 = (bf16[4,2,48,576]{3,2,1,0:T(8,128)(2,1)S(1)}, bf16[4,2,48,576]{3,2,1,0:T(8,128)(2,1)S(1)}, u32[]{:S(2)}, u32[]{:S(2)}) collective-permute-start(bf16[4,2,48,576]{3,2,1,0:T(8,128)(2,1)S(1)} %get-tuple-element.38.refs_2_), channel_id=1, source_target_pairs={{0,1},{1,0},{2,3},{3,2},{4,5},{5,4},{6,7},{7,6},{8,9},{9,8},{10,11... | collective-permute-start | bytes 1327112 | tf_op jit(solution)/shard_map/ppermute | solution.py:52
  29.7 8.7 %copy-start.6 = (f32[768]{0:T(1024)S(1)}, f32[768]{0:T(1024)}, u32[]{:S(2)}) copy-start(f32[768]{0:T(1024)} %param.16) | copy-start | bytes 9220
  29.7 8.7 %collective-permute-start.15 = (bf16[2,4,48,768]{3,2,1,0:T(8,128)(2,1)S(1)}, bf16[2,4,48,768]{3,2,1,0:T(8,128)(2,1)S(1)}, u32[]{:S(2)}, u32[]{:S(2)}) collective-permute-start(bf16[2,4,48,768]{3,2,1,0:T(8,128)(2,1)S(1)} %get-tuple-element.43.mine), channel_id=1, source_target_pairs={{0,1},{1,0},{2,3},{3,2},{4,5},{5,4},{6,7},{7,6},{8,9},{9,8},{10,11... | collective-permute-start | bytes 1769480 | tf_op jit(solution)/shard_map/ppermute | solution.py:52
  35.7 5.7 %collective-permute-start.12 = (bf16[2,128,192]{2,1,0:T(8,128)(2,1)S(1)}, bf16[2,128,192]{2,1,0:T(8,128)(2,1)S(1)}, u32[]{:S(2)}, u32[]{:S(2)}) collective-permute-start(bf16[2,128,192]{2,1,0:T(8,128)(2,1)S(1)} %get-tuple-element.39), channel_id=1, source_target_pairs={{0,18},{1,19},{2,16},{3,17},{4,22},{5,23},{6,20},{7,21},{8,26},{9,... | collective-permute-start | bytes 294920 | tf_op jit(solution)/shard_map/ppermute | solution.py:48
  37.7 7.2 %collective-permute-start.13 = (bf16[2,128,192]{2,1,0:T(8,128)(2,1)S(1)}, bf16[2,128,192]{2,1,0:T(8,128)(2,1)S(1)}, u32[]{:S(2)}, u32[]{:S(2)}) collective-permute-start(bf16[2,128,192]{2,1,0:T(8,128)(2,1)S(1)} %get-tuple-element.40), channel_id=1, source_target_pairs={{0,16},{1,17},{2,18},{3,19},{4,20},{5,21},{6,22},{7,23},{8,24},{9,... | collective-permute-start | bytes 294920 | tf_op jit(solution)/shard_map/ppermute | solution.py:48
  37.9 7.0 %collective-permute-start.14 = (bf16[2,128,192]{2,1,0:T(8,128)(2,1)S(1)}, bf16[2,128,192]{2,1,0:T(8,128)(2,1)S(1)}, u32[]{:S(2)}, u32[]{:S(2)}) collective-permute-start(bf16[2,128,192]{2,1,0:T(8,128)(2,1)S(1)} %get-tuple-element.41), channel_id=1, source_target_pairs={{0,2},{1,3},{2,0},{3,1},{4,6},{5,7},{6,4},{7,5},{8,10},{9,11},{10,... | collective-permute-start | bytes 294920 | tf_op jit(solution)/shard_map/ppermute | solution.py:48
  38.5 8.2 %copy-start.2 = (bf16[128,768]{1,0:T(8,128)(2,1)S(1)}, bf16[128,768]{1,0:T(8,128)(2,1)}, u32[]{:S(2)}) copy-start(bf16[128,768]{1,0:T(8,128)(2,1)} %get-tuple-element.32.raw.tokens) | copy-start | bytes 589828
  45.5 7.9 %collective-permute-start.16 = (bf16[128,768]{1,0:T(8,128)(2,1)S(1)}, bf16[128,768]{1,0:T(8,128)(2,1)S(1)}, u32[]{:S(2)}, u32[]{:S(2)}) collective-permute-start(bf16[128,768]{1,0:T(8,128)(2,1)S(1)} %shard_map.116.other_in), channel_id=1, source_target_pairs={{0,4},{1,5},{4,8},{5,9},{6,2},{7,3},{8,12},{9,13},{10,6},{11,7},{1... | collective-permute-start | bytes 589832 | tf_op jit(solution)/shard_map/ppermute | solution.py:48
  54.0 2.5 %collective-permute-start.17 = (bf16[128,768]{1,0:T(8,128)(2,1)S(1)}, bf16[128,768]{1,0:T(8,128)(2,1)S(1)}, u32[]{:S(2)}, u32[]{:S(2)}) collective-permute-start(bf16[128,768]{1,0:T(8,128)(2,1)S(1)} %get-tuple-element.50), channel_id=1, source_target_pairs={{0,1},{1,0},{2,3},{3,2},{4,5},{5,4},{6,7},{7,6},{8,9},{9,8},{10,11... | collective-permute-start | bytes 589832 | tf_op jit(solution)/shard_map/ppermute | solution.py:52

commit v14 on v12

--- a/solution.py
+++ b/solution.py
@@ -486,7 +486,7 @@
             ),
             0,
         )
-        qkv_other, out_other = swap_cores(qkv_mine), swap_cores(out_mine)
+        qkv_other = swap_cores(qkv_mine)
         join = join_columns
     else:
         near = jnp.stack([message, by_x, by_y, flip_chips(by_x, 0, 1)])
@@ -514,6 +514,9 @@
         flip_chips(piece, flip, sample) for piece, (flip, sample) in zip(pieces[:0:-1], FLIPS[::-1])
     ]
     back = [pieces[0]] + back[::-1]
+    if direct:
+        out_mine = gate(out_mine, pieces[0])
+        out_other = swap_cores(out_mine)
     (full_out,) = call(
         join, [((width, width), BF16)], [VMEM] * 2, (out_mine, out_other), 0
     )

time: 56.3 us -> 60.1 us (1.067)
  starting transfers between devices: 19.1 us -> 22 us
    ppermute x4, starting transfers between devices: 4.58 us -> 6.77 us  [swap_cores(): return lax.ppermute(values, 'lon', [(0, 1), (1, 0)])]
    ppermute x4, waiting for transfers between devices: 2.95 us -> 3.75 us  [swap_cores(): return lax.ppermute(values, 'lon', [(0, 1), (1, 0)])]
    ppermute x15, starting transfers between devices: 14.5 us -> 15.2 us  [move(): return lax.ppermute(values, AXES, device_pairs(target))]
    pallas_call x11 -> x12, Pallas kernels: 9.51 us -> 9.56 us  [call(): pl.pallas_call(body, out_shape=outs, in_specs=specs, out_specs=tuple((VME...]
  transfers between devices with their start and end apart: 19 -> 19, of which waited for: 7 -> 8; matrix products, arithmetic and copies ran while one was open for 1% -> 1% of each run, Pallas kernels for 11% -> 4%
where the time goes in v14:
time: 60.1 us; the launch traced here: 59.8 us
  waiting for transfers between devices  22.8 us (38%)
  starting transfers between devices  22 us (37%)
  Pallas kernels  9.56 us (16%)
  local copies, waits for them, and re-layouts  2.68 us (4%)
  between operations  2.12 us (4%)
  other arithmetic  0.72 us (1%)
    ppermute x15, waiting for transfers between devices, move(): return lax.ppermute(values, AXES, device_pairs(target))  19 us
    ppermute x15, starting transfers between devices, move(): return lax.ppermute(values, AXES, device_pairs(target))  15.2 us
    pallas_call x12, Pallas kernels, call(): pl.pallas_call(body, out_shape=outs, in_specs=specs, out_specs=tuple((VME...  9.56 us
    ppermute x4, starting transfers between devices, swap_cores(): return lax.ppermute(values, 'lon', [(0, 1), (1, 0)])  6.77 us
    ppermute x4, waiting for transfers between devices, swap_cores(): return lax.ppermute(values, 'lon', [(0, 1), (1, 0)])  3.75 us
    unnamed x16, local copies, waits for them, and re-layouts  2.68 us
  transfers between devices with their start and end apart: 19, of which 8 were waited for; matrix products, arithmetic and copies ran while one was open for 1% of the time, Pallas kernels for 4%

profile of v14, /device:TPU:3, one launch (start us, length us, event | category | flops | bytes accessed | tf_op | source)
XLA Modules:
  0.0 59.8 jit_solution(16706080686464994273)
XLA Ops:
  0.0 2.1 %shard_map.110 = (bf16[192,768]{1,0:T(8,128)(2,1)}, bf16[128,768]{1,0:T(8,128)(2,1)}, bf16[48,768]{1,0:T(8,128)(2,1)}) custom-call(bf16[128,768]{1,0:T(8,128)(2,1)} %bitcast.4, bf16[12,128]{1,0:T(8,128)(2,1)} %bitcast.5, f32[768]{0:T(1024)} %refs_2_.1, bf16[96,2304]{1,0:T(8,128)(2,1)} %refs_3_.1, bf16[96,768]{1,0:T(8,128)(2,1)} %refs_4_.1), custom_call_target="tpu_custom_call" | custom-call | flops 983040 | bytes 792576 | tf_op jit(solution)/shard_map/pallas_call | solution.py:23
  2.1 0.0 copy-start.6
  2.2 1.3 %collective-permute-start.1 = (bf16[192,768]{1,0:T(8,128)(2,1)}, bf16[192,768]{1,0:T(8,128)(2,1)S(1)}, u32[]{:S(2)}, u32[]{:S(2)}) collective-permute-start(bf16[192,768]{1,0:T(8,128)(2,1)} %get-tuple-element.28.message), channel_id=1, source_target_pairs={{0,16},{1,17},{2,18},{3,19},{4,20},{5,21},{6,22},{7,23},{8,24},{9,... | collective-permute-start | bytes 884744 | tf_op jit(solution)/shard_map/ppermute | solution.py:57
  3.5 0.3 collective-permute-start
  3.7 3.3 %collective-permute-start.2 = (bf16[48,768]{1,0:T(8,128)(2,1)}, bf16[48,768]{1,0:T(8,128)(2,1)S(1)}, u32[]{:S(2)}, u32[]{:S(2)}) collective-permute-start(bf16[48,768]{1,0:T(8,128)(2,1)} %get-tuple-element.30), channel_id=1, source_target_pairs={{0,12},{1,13},{2,14},{3,15},{4,8},{5,9},{6,10},{7,11},{8,4},{9,5},... | collective-permute-start | bytes 221192 | tf_op jit(solution)/shard_map/ppermute | solution.py:57
  7.0 0.0 collective-permute-start.3
  7.0 0.3 collective-permute-start.4
  7.3 1.0 %copy-done = bf16[96,2304]{1,0:T(8,128)(2,1)S(1)} copy-done((bf16[96,2304]{1,0:T(8,128)(2,1)S(1)}, bf16[96,2304]{1,0:T(8,128)(2,1)}, u32[]{:S(2)}) %copy-start) | copy-done | bytes 442392
  8.3 0.9 %copy-done.1 = bf16[96,768]{1,0:T(8,128)(2,1)S(1)} copy-done((bf16[96,768]{1,0:T(8,128)(2,1)S(1)}, bf16[96,768]{1,0:T(8,128)(2,1)}, u32[]{:S(2)}) %copy-start.1) | copy-done | bytes 147480
  9.3 0.2 shard_map.109
  9.4 0.0 collective-permute-done.2.out3
  9.4 4.1 %collective-permute-done.3.out2 = bf16[48,768]{1,0:T(8,128)(2,1)S(1)} collective-permute-done((bf16[48,768]{1,0:T(8,128)(2,1)}, bf16[48,768]{1,0:T(8,128)(2,1)S(1)}, u32[]{:S(2)}, u32[]{:S(2)}) %collective-permute-start.3) | collective-permute-done | bytes 73760 | tf_op jit(solution)/shard_map/ppermute | solution.py:57
  13.5 0.0 collective-permute-done.4.out1
  13.5 0.1 shard_map.111
  13.6 1.3 %collective-permute-start.9 = (bf16[4,48,768]{2,1,0:T(8,128)(2,1)S(1)}, bf16[4,48,768]{2,1,0:T(8,128)(2,1)S(1)}, u32[]{:S(2)}, u32[]{:S(2)}) collective-permute-start(bf16[4,48,768]{2,1,0:T(8,128)(2,1)S(1)} %get-tuple-element.34.outs), channel_id=1, source_target_pairs={{0,2},{1,3},{2,0},{3,1},{4,6},{5,7},{6,4},{7,5},{8,10},{9,11},{10,... | collective-permute-start | bytes 884744 | tf_op jit(solution)/shard_map/ppermute | solution.py:57
  14.9 0.2 collective-permute-start.8
  15.1 0.2 collective-permute-start.5
  15.2 0.5 collective-permute-start.6
  15.8 2.9 %collective-permute-start.7 = (bf16[2,48,576]{2,1,0:T(8,128)(2,1)S(1)}, bf16[2,48,576]{2,1,0:T(8,128)(2,1)S(1)}, u32[]{:S(2)}, u32[]{:S(2)}) collective-permute-start(bf16[2,48,576]{2,1,0:T(8,128)(2,1)S(1)} %get-tuple-element.33.bundle), channel_id=1, source_target_pairs={{0,4},{1,5},{2,6},{3,7},{4,0},{5,1},{6,2},{7,3},{8,12},{9,13},{10,... | collective-permute-start | bytes 331784 | tf_op jit(solution)/shard_map/ppermute | solution.py:57
  18.6 0.2 copy.13.w_conv
  18.9 0.1 copy.12.taps
  20.9 1.0 %shard_map.112 = (bf16[2,3,256,256]{3,2,1,0:T(8,128)(2,1)S(1)}, bf16[256,512]{1,0:T(8,128)(2,1)S(1)}, f32[8,128]{1,0:T(8,128)S(1)}) custom-call(s32[1]{0:T(128)S(6)} %copy.14.lon_half, s32[1]{0:T(128)S(6)} %copy.15.lat_half, s32[1]{0:T(128)S(6)} %copy.16.quad_off, f32[16,2]{1,0:T(8,128)S(1)} %copy.12.taps, bf16[2,768,64]{2,1,0:T(8,128)(2,1)S(1)} %copy.13.w_conv, ...), custom_call_target="tpu_custom_call" | custom-call | bytes 417932 | tf_op jit(solution)/shard_map/pallas_call | solution.py:23
  21.9 2.5 %collective-permute-done.6.level2 = bf16[2,48,576]{2,1,0:T(8,128)(2,1)S(1)} collective-permute-done((bf16[2,48,576]{2,1,0:T(8,128)(2,1)S(1)}, bf16[2,48,576]{2,1,0:T(8,128)(2,1)S(1)}, u32[]{:S(2)}, u32[]{:S(2)}) %collective-permute-start.6) | collective-permute-done | bytes 110624 | tf_op jit(solution)/shard_map/ppermute | solution.py:57
  24.5 0.1 shard_map.113
  24.6 4.1 %collective-permute-start.10 = (bf16[4,144,768]{2,1,0:T(8,128)(2,1)S(1)}, bf16[4,144,768]{2,1,0:T(8,128)(2,1)S(1)}, u32[]{:S(2)}, u32[]{:S(2)}) collective-permute-start(bf16[4,144,768]{2,1,0:T(8,128)(2,1)S(1)} %get-tuple-element.35.refs_0_), channel_id=1, source_target_pairs={{0,1},{1,0},{2,3},{3,2},{4,5},{5,4},{6,7},{7,6},{8,9},{9,8},{10,11... | collective-permute-start | bytes 2654216 | tf_op jit(solution)/shard_map/ppermute | solution.py:61
  28.7 0.1 collective-permute-start.11
  28.8 2.7 %collective-permute-done.11.refs_3_ = bf16[4,2,48,576]{3,2,1,0:T(8,128)(2,1)S(1)} collective-permute-done((bf16[4,2,48,576]{3,2,1,0:T(8,128)(2,1)S(1)}, bf16[4,2,48,576]{3,2,1,0:T(8,128)(2,1)S(1)}, u32[]{:S(2)}, u32[]{:S(2)}) %collective-permute-start.11) | collective-permute-done | bytes 442400 | tf_op jit(solution)/shard_map/ppermute | solution.py:61
  31.5 3.3 %shard_map.114 = (bf16[2,128,192]{2,1,0:T(8,128)(2,1)S(1)}, bf16[2,128,192]{2,1,0:T(8,128)(2,1)S(1)}, bf16[2,128,192]{2,1,0:T(8,128)(2,1)S(1)}, bf16[2,128,192]{2,1,0:T(8,128)(2,1)S(1)}) custom-call(bf16[4,144,768]{2,1,0:T(8,128)(2,1)S(1)} %get-tuple-element.35.refs_0_, bf16[4,144,768]{2,1,0:T(8,128)(2,1)S(1)} %collective-permute-done.10.refs_1_, ...), custom_call_target="tpu_custom_call" | custom-call | flops 905969664 | bytes 2654208 | tf_op jit(solution)/shard_map/pallas_call | solution.py:23
  34.8 0.0 copy-start.3
  34.8 0.0 copy-start.5
  34.8 0.4 collective-permute-start.15
  35.3 0.4 copy-done.3
  35.7 1.0 %collective-permute-start.16 = (bf16[128,768]{1,0:T(8,128)(2,1)S(1)}, bf16[128,768]{1,0:T(8,128)(2,1)S(1)}, u32[]{:S(2)}, u32[]{:S(2)}) collective-permute-start(bf16[128,768]{1,0:T(8,128)(2,1)S(1)} %shard_map.117.tokens), channel_id=1, source_target_pairs={{0,2},{1,3},{2,0},{3,1},{4,6},{5,7},{6,4},{7,5},{8,10},{9,11},{10,... | collective-permute-start | bytes 589832 | tf_op jit(solution)/shard_map/ppermute | solution.py:57
  36.7 1.3 %collective-permute-start.12 = (bf16[2,128,192]{2,1,0:T(8,128)(2,1)S(1)}, bf16[2,128,192]{2,1,0:T(8,128)(2,1)S(1)}, u32[]{:S(2)}, u32[]{:S(2)}) collective-permute-start(bf16[2,128,192]{2,1,0:T(8,128)(2,1)S(1)} %get-tuple-element.37), channel_id=1, source_target_pairs={{0,18},{1,19},{2,16},{3,17},{4,22},{5,23},{6,20},{7,21},{8,26},{9,... | collective-permute-start | bytes 294920 | tf_op jit(solution)/shard_map/ppermute | solution.py:57
  38.1 0.3 collective-permute-start.13
  38.4 1.0 %collective-permute-start.14 = (bf16[2,128,192]{2,1,0:T(8,128)(2,1)S(1)}, bf16[2,128,192]{2,1,0:T(8,128)(2,1)S(1)}, u32[]{:S(2)}, u32[]{:S(2)}) collective-permute-start(bf16[2,128,192]{2,1,0:T(8,128)(2,1)S(1)} %get-tuple-element.39), channel_id=1, source_target_pairs={{0,2},{1,3},{2,0},{3,1},{4,6},{5,7},{6,4},{7,5},{8,10},{9,11},{10,... | collective-permute-start | bytes 294920 | tf_op jit(solution)/shard_map/ppermute | solution.py:57
  39.4 0.1 shard_map.116.weights
  39.5 2.4 %collective-permute-done.16.tokens = bf16[128,768]{1,0:T(8,128)(2,1)S(1)} collective-permute-done((bf16[128,768]{1,0:T(8,128)(2,1)S(1)}, bf16[128,768]{1,0:T(8,128)(2,1)S(1)}, u32[]{:S(2)}, u32[]{:S(2)}) %collective-permute-start.16) | collective-permute-done | bytes 196640 | tf_op jit(solution)/shard_map/ppermute | solution.py:57
  41.9 3.6 %collective-permute-done.12.piece3 = bf16[2,128,192]{2,1,0:T(8,128)(2,1)S(1)} collective-permute-done((bf16[2,128,192]{2,1,0:T(8,128)(2,1)S(1)}, bf16[2,128,192]{2,1,0:T(8,128)(2,1)S(1)}, u32[]{:S(2)}, u32[]{:S(2)}) %collective-permute-start.12) | collective-permute-done | bytes 98336 | tf_op jit(solution)/shard_map/ppermute | solution.py:57
  45.5 2.0 %collective-permute-done.14.piece1 = bf16[2,128,192]{2,1,0:T(8,128)(2,1)S(1)} collective-permute-done((bf16[2,128,192]{2,1,0:T(8,128)(2,1)S(1)}, bf16[2,128,192]{2,1,0:T(8,128)(2,1)S(1)}, u32[]{:S(2)}, u32[]{:S(2)}) %collective-permute-start.14) | collective-permute-done | bytes 98336 | tf_op jit(solution)/shard_map/ppermute | solution.py:57
  47.5 0.6 shard_map.118.other_in
  48.1 1.3 %collective-permute-start.17 = (bf16[128,768]{1,0:T(8,128)(2,1)S(1)}, bf16[128,768]{1,0:T(8,128)(2,1)S(1)}, u32[]{:S(2)}, u32[]{:S(2)}) collective-permute-start(bf16[128,768]{1,0:T(8,128)(2,1)S(1)} %shard_map.118.other_in), channel_id=1, source_target_pairs={{0,4},{1,5},{4,8},{5,9},{6,2},{7,3},{8,12},{9,13},{10,6},{11,7},{1... | collective-permute-start | bytes 589832 | tf_op jit(solution)/shard_map/ppermute | solution.py:57
  49.4 1.4 %shard_map.119 = (bf16[128,768]{1,0:T(8,128)(2,1)S(1)}, f32[256,768]{1,0:T(8,128)S(1)}) custom-call(f32[8,128]{1,0:T(8,128)S(1)} %get-tuple-element.32.gains, f32[1,768]{1,0:T(1,128)S(1)} %broadcast_in_dim.6.gain, bf16[2,128,192]{2,1,0:T(8,128)(2,1)S(1)} %collective-permute-done.12.piece3, bf16[2,128,192]{2,1,0:T(8,128)(2,1)S(1)} %collective-permute-done.13.piece2, ...), custom_call_target="tpu_custom_call" | custom-call | flops 452984832 | bytes 3021824 | tf_op jit(solution)/shard_map/pallas_call | solution.py:23
  50.8 4.4 %collective-permute-done.17.halo = bf16[128,768]{1,0:T(8,128)(2,1)S(1)} collective-permute-done((bf16[128,768]{1,0:T(8,128)(2,1)S(1)}, bf16[128,768]{1,0:T(8,128)(2,1)S(1)}, u32[]{:S(2)}, u32[]{:S(2)}) %collective-permute-start.17) | collective-permute-done | bytes 196640 | tf_op jit(solution)/shard_map/ppermute | solution.py:57
  55.2 0.7 %shard_map.120 = (f32[128,768]{1,0:T(8,128)S(1)}, bf16[128,768]{1,0:T(8,128)(2,1)S(1)}) custom-call(f32[8,128]{1,0:T(8,128)S(1)} %get-tuple-element.32.gains, bf16[128,768]{1,0:T(8,128)(2,1)S(1)} %collective-permute-done.17.halo, bf16[2,3,256,256]{3,2,1,0:T(8,128)(2,1)S(1)} %get-tuple-element.43.blocks, bf16[256,512]{1,0:T(8,128)(2,1)S(1)} %get-tuple-element.44.coeffs, ...), custom_call_target="tpu_custom_call" | custom-call | flops 100663296 | bytes 2232320 | tf_op jit(solution)/shard_map/pallas_call | solution.py:23
  55.8 2.2 %collective-permute-start.18 = (bf16[128,768]{1,0:T(8,128)(2,1)S(1)}, bf16[128,768]{1,0:T(8,128)(2,1)S(1)}, u32[]{:S(2)}, u32[]{:S(2)}) collective-permute-start(bf16[128,768]{1,0:T(8,128)(2,1)S(1)} %get-tuple-element.48), channel_id=1, source_target_pairs={{0,1},{1,0},{2,3},{3,2},{4,5},{5,4},{6,7},{7,6},{8,9},{9,8},{10,11... | collective-permute-start | bytes 589832 | tf_op jit(solution)/shard_map/ppermute | solution.py:61
  58.0 1.1 %collective-permute-done.18 = bf16[128,768]{1,0:T(8,128)(2,1)S(1)} collective-permute-done((bf16[128,768]{1,0:T(8,128)(2,1)S(1)}, bf16[128,768]{1,0:T(8,128)(2,1)S(1)}, u32[]{:S(2)}, u32[]{:S(2)}) %collective-permute-start.18) | collective-permute-done | bytes 196640 | tf_op jit(solution)/shard_map/ppermute | solution.py:61
  59.1 0.7 %fusion = bf16[1,128,768]{2,1,0:T(8,128)(2,1)} fusion(f32[128,768]{1,0:T(8,128)S(1)} %get-tuple-element.47, bf16[128,768]{1,0:T(8,128)(2,1)S(1)} %collective-permute-done.18), kind=kLoop, calls=%fused_computation.1 | loop fusion | flops 294912 | bytes 786432 | tf_op jit(solution)/shard_map/broadcast_in_dim | solution.py:547
  (20 shorter events, 0.1 us)
Async XLA Ops:
  0.0 18.6 %copy-start.4 = (bf16[2,768,64]{1,2,0:T(8,128)(2,1)S(1)}, bf16[2,768,64]{1,2,0:T(8,128)(2,1)}, u32[]{:S(2)}) copy-start(bf16[2,768,64]{1,2,0:T(8,128)(2,1)} %param.17) | copy-start | bytes 589828
  2.1 16.7 %copy-start.6 = (f32[16,2]{0,1:T(2,128)S(1)}, f32[16,2]{0,1:T(2,128)}, u32[]{:S(2)}) copy-start(f32[16,2]{0,1:T(2,128)} %param.18) | copy-start | bytes 388
  2.2 11.4 %collective-permute-start.1 = (bf16[192,768]{1,0:T(8,128)(2,1)}, bf16[192,768]{1,0:T(8,128)(2,1)S(1)}, u32[]{:S(2)}, u32[]{:S(2)}) collective-permute-start(bf16[192,768]{1,0:T(8,128)(2,1)} %get-tuple-element.28.message), channel_id=1, source_target_pairs={{0,16},{1,17},{2,18},{3,19},{4,20},{5,21},{6,22},{7,23},{8,24},{9,... | collective-permute-start | bytes 884744 | tf_op jit(solution)/shard_map/ppermute | solution.py:57
  3.5 10.1 %collective-permute-start = (bf16[192,768]{1,0:T(8,128)(2,1)}, bf16[192,768]{1,0:T(8,128)(2,1)S(1)}, u32[]{:S(2)}, u32[]{:S(2)}) collective-permute-start(bf16[192,768]{1,0:T(8,128)(2,1)} %get-tuple-element.28.message), channel_id=1, source_target_pairs={{0,2},{1,3},{2,0},{3,1},{4,6},{5,7},{6,4},{7,5},{8,10},{9,11},{10,... | collective-permute-start | bytes 884744 | tf_op jit(solution)/shard_map/ppermute | solution.py:57
  3.7 5.7 %collective-permute-start.2 = (bf16[48,768]{1,0:T(8,128)(2,1)}, bf16[48,768]{1,0:T(8,128)(2,1)S(1)}, u32[]{:S(2)}, u32[]{:S(2)}) collective-permute-start(bf16[48,768]{1,0:T(8,128)(2,1)} %get-tuple-element.30), channel_id=1, source_target_pairs={{0,12},{1,13},{2,14},{3,15},{4,8},{5,9},{6,10},{7,11},{8,4},{9,5},... | collective-permute-start | bytes 221192 | tf_op jit(solution)/shard_map/ppermute | solution.py:57
  7.0 6.5 %collective-permute-start.3 = (bf16[48,768]{1,0:T(8,128)(2,1)}, bf16[48,768]{1,0:T(8,128)(2,1)S(1)}, u32[]{:S(2)}, u32[]{:S(2)}) collective-permute-start(bf16[48,768]{1,0:T(8,128)(2,1)} %get-tuple-element.30), channel_id=1, source_target_pairs={{0,8},{1,9},{2,10},{3,11},{4,12},{5,13},{6,14},{7,15},{8,0},{9,1},... | collective-permute-start | bytes 221192 | tf_op jit(solution)/shard_map/ppermute | solution.py:57
  7.0 6.5 %collective-permute-start.4 = (bf16[48,768]{1,0:T(8,128)(2,1)}, bf16[48,768]{1,0:T(8,128)(2,1)S(1)}, u32[]{:S(2)}, u32[]{:S(2)}) collective-permute-start(bf16[48,768]{1,0:T(8,128)(2,1)} %get-tuple-element.30), channel_id=1, source_target_pairs={{0,4},{1,5},{2,6},{3,7},{4,0},{5,1},{6,2},{7,3},{8,12},{9,13},{10,... | collective-permute-start | bytes 221192 | tf_op jit(solution)/shard_map/ppermute | solution.py:57
  7.3 1.0 %copy-start = (bf16[96,2304]{1,0:T(8,128)(2,1)S(1)}, bf16[96,2304]{1,0:T(8,128)(2,1)}, u32[]{:S(2)}) copy-start(bf16[96,2304]{1,0:T(8,128)(2,1)} %refs_3_.1) | copy-start | bytes 1327108
  8.3 0.9 %copy-start.1 = (bf16[96,768]{1,0:T(8,128)(2,1)S(1)}, bf16[96,768]{1,0:T(8,128)(2,1)}, u32[]{:S(2)}) copy-start(bf16[96,768]{1,0:T(8,128)(2,1)} %refs_4_.1) | copy-start | bytes 442372
  9.4 15.1 %copy-start.2 = (bf16[192,768]{1,0:T(8,128)(2,1)S(1)}, bf16[192,768]{1,0:T(8,128)(2,1)}, u32[]{:S(2)}) copy-start(bf16[192,768]{1,0:T(8,128)(2,1)} %get-tuple-element.28.message) | copy-start | bytes 884740
  13.6 10.9 %collective-permute-start.9 = (bf16[4,48,768]{2,1,0:T(8,128)(2,1)S(1)}, bf16[4,48,768]{2,1,0:T(8,128)(2,1)S(1)}, u32[]{:S(2)}, u32[]{:S(2)}) collective-permute-start(bf16[4,48,768]{2,1,0:T(8,128)(2,1)S(1)} %get-tuple-element.34.outs), channel_id=1, source_target_pairs={{0,2},{1,3},{2,0},{3,1},{4,6},{5,7},{6,4},{7,5},{8,10},{9,11},{10,... | collective-permute-start | bytes 884744 | tf_op jit(solution)/shard_map/ppermute | solution.py:57
  14.9 9.6 %collective-permute-start.8 = (bf16[144,768]{1,0:T(8,128)(2,1)S(1)}, bf16[144,768]{1,0:T(8,128)(2,1)S(1)}, u32[]{:S(2)}, u32[]{:S(2)}) collective-permute-start(bf16[144,768]{1,0:T(8,128)(2,1)S(1)} %get-tuple-element.31.message.x_block), channel_id=1, source_target_pairs={{0,16},{1,17},{2,18},{3,19},{4,20},{5,21},{6,22},{7,23},{8,24},{9,... | collective-permute-start | bytes 663560 | tf_op jit(solution)/shard_map/ppermute | solution.py:57
  15.1 6.8 %collective-permute-start.5 = (bf16[2,48,576]{2,1,0:T(8,128)(2,1)S(1)}, bf16[2,48,576]{2,1,0:T(8,128)(2,1)S(1)}, u32[]{:S(2)}, u32[]{:S(2)}) collective-permute-start(bf16[2,48,576]{2,1,0:T(8,128)(2,1)S(1)} %get-tuple-element.33.bundle), channel_id=1, source_target_pairs={{0,12},{1,13},{2,14},{3,15},{4,8},{5,9},{6,10},{7,11},{8,4},{9,5},... | collective-permute-start | bytes 331784 | tf_op jit(solution)/shard_map/ppermute | solution.py:57
  15.2 9.2 %collective-permute-start.6 = (bf16[2,48,576]{2,1,0:T(8,128)(2,1)S(1)}, bf16[2,48,576]{2,1,0:T(8,128)(2,1)S(1)}, u32[]{:S(2)}, u32[]{:S(2)}) collective-permute-start(bf16[2,48,576]{2,1,0:T(8,128)(2,1)S(1)} %get-tuple-element.33.bundle), channel_id=1, source_target_pairs={{0,8},{1,9},{2,10},{3,11},{4,12},{5,13},{6,14},{7,15},{8,0},{9,1},... | collective-permute-start | bytes 331784 | tf_op jit(solution)/shard_map/ppermute | solution.py:57
  15.8 8.7 %collective-permute-start.7 = (bf16[2,48,576]{2,1,0:T(8,128)(2,1)S(1)}, bf16[2,48,576]{2,1,0:T(8,128)(2,1)S(1)}, u32[]{:S(2)}, u32[]{:S(2)}) collective-permute-start(bf16[2,48,576]{2,1,0:T(8,128)(2,1)S(1)} %get-tuple-element.33.bundle), channel_id=1, source_target_pairs={{0,4},{1,5},{2,6},{3,7},{4,0},{5,1},{6,2},{7,3},{8,12},{9,13},{10,... | collective-permute-start | bytes 331784 | tf_op jit(solution)/shard_map/ppermute | solution.py:57
  24.6 6.8 %collective-permute-start.10 = (bf16[4,144,768]{2,1,0:T(8,128)(2,1)S(1)}, bf16[4,144,768]{2,1,0:T(8,128)(2,1)S(1)}, u32[]{:S(2)}, u32[]{:S(2)}) collective-permute-start(bf16[4,144,768]{2,1,0:T(8,128)(2,1)S(1)} %get-tuple-element.35.refs_0_), channel_id=1, source_target_pairs={{0,1},{1,0},{2,3},{3,2},{4,5},{5,4},{6,7},{7,6},{8,9},{9,8},{10,11... | collective-permute-start | bytes 2654216 | tf_op jit(solution)/shard_map/ppermute | solution.py:61
  28.7 2.8 %collective-permute-start.11 = (bf16[4,2,48,576]{3,2,1,0:T(8,128)(2,1)S(1)}, bf16[4,2,48,576]{3,2,1,0:T(8,128)(2,1)S(1)}, u32[]{:S(2)}, u32[]{:S(2)}) collective-permute-start(bf16[4,2,48,576]{3,2,1,0:T(8,128)(2,1)S(1)} %get-tuple-element.36.refs_2_.refs_1_), channel_id=1, source_target_pairs={{0,1},{1,0},{2,3},{3,2},{4,5},{5,4},{6,7},{7,6},{8,9},{9,8},{10,11... | collective-permute-start | bytes 1327112 | tf_op jit(solution)/shard_map/ppermute | solution.py:61
  34.8 0.9 %copy-start.3 = (bf16[128,768]{1,0:T(8,128)(2,1)S(1)}, bf16[128,768]{1,0:T(8,128)(2,1)}, u32[]{:S(2)}) copy-start(bf16[128,768]{1,0:T(8,128)(2,1)} %get-tuple-element.42.refs_0_) | copy-start | bytes 589828
  34.8 4.6 %copy-start.5 = (f32[768]{0:T(1024)S(1)}, f32[768]{0:T(1024)}, u32[]{:S(2)}) copy-start(f32[768]{0:T(1024)} %param.16) | copy-start | bytes 9220
  34.8 4.6 %collective-permute-start.15 = (bf16[2,4,48,768]{3,2,1,0:T(8,128)(2,1)S(1)}, bf16[2,4,48,768]{3,2,1,0:T(8,128)(2,1)S(1)}, u32[]{:S(2)}, u32[]{:S(2)}) collective-permute-start(bf16[2,4,48,768]{3,2,1,0:T(8,128)(2,1)S(1)} %shard_map.115.mine), channel_id=1, source_target_pairs={{0,1},{1,0},{2,3},{3,2},{4,5},{5,4},{6,7},{7,6},{8,9},{9,8},{10,11... | collective-permute-start | bytes 1769480 | tf_op jit(solution)/shard_map/ppermute | solution.py:61
  35.7 6.2 %collective-permute-start.16 = (bf16[128,768]{1,0:T(8,128)(2,1)S(1)}, bf16[128,768]{1,0:T(8,128)(2,1)S(1)}, u32[]{:S(2)}, u32[]{:S(2)}) collective-permute-start(bf16[128,768]{1,0:T(8,128)(2,1)S(1)} %shard_map.117.tokens), channel_id=1, source_target_pairs={{0,2},{1,3},{2,0},{3,1},{4,6},{5,7},{6,4},{7,5},{8,10},{9,11},{10,... | collective-permute-start | bytes 589832 | tf_op jit(solution)/shard_map/ppermute | solution.py:57
  36.7 8.8 %collective-permute-start.12 = (bf16[2,128,192]{2,1,0:T(8,128)(2,1)S(1)}, bf16[2,128,192]{2,1,0:T(8,128)(2,1)S(1)}, u32[]{:S(2)}, u32[]{:S(2)}) collective-permute-start(bf16[2,128,192]{2,1,0:T(8,128)(2,1)S(1)} %get-tuple-element.37), channel_id=1, source_target_pairs={{0,18},{1,19},{2,16},{3,17},{4,22},{5,23},{6,20},{7,21},{8,26},{9,... | collective-permute-start | bytes 294920 | tf_op jit(solution)/shard_map/ppermute | solution.py:57
  38.1 7.4 %collective-permute-start.13 = (bf16[2,128,192]{2,1,0:T(8,128)(2,1)S(1)}, bf16[2,128,192]{2,1,0:T(8,128)(2,1)S(1)}, u32[]{:S(2)}, u32[]{:S(2)}) collective-permute-start(bf16[2,128,192]{2,1,0:T(8,128)(2,1)S(1)} %get-tuple-element.38), channel_id=1, source_target_pairs={{0,16},{1,17},{2,18},{3,19},{4,20},{5,21},{6,22},{7,23},{8,24},{9,... | collective-permute-start | bytes 294920 | tf_op jit(solution)/shard_map/ppermute | solution.py:57
  38.4 9.1 %collective-permute-start.14 = (bf16[2,128,192]{2,1,0:T(8,128)(2,1)S(1)}, bf16[2,128,192]{2,1,0:T(8,128)(2,1)S(1)}, u32[]{:S(2)}, u32[]{:S(2)}) collective-permute-start(bf16[2,128,192]{2,1,0:T(8,128)(2,1)S(1)} %get-tuple-element.39), channel_id=1, source_target_pairs={{0,2},{1,3},{2,0},{3,1},{4,6},{5,7},{6,4},{7,5},{8,10},{9,11},{10,... | collective-permute-start | bytes 294920 | tf_op jit(solution)/shard_map/ppermute | solution.py:57
  48.1 7.1 %collective-permute-start.17 = (bf16[128,768]{1,0:T(8,128)(2,1)S(1)}, bf16[128,768]{1,0:T(8,128)(2,1)S(1)}, u32[]{:S(2)}, u32[]{:S(2)}) collective-permute-start(bf16[128,768]{1,0:T(8,128)(2,1)S(1)} %shard_map.118.other_in), channel_id=1, source_target_pairs={{0,4},{1,5},{4,8},{5,9},{6,2},{7,3},{8,12},{9,13},{10,6},{11,7},{1... | collective-permute-start | bytes 589832 | tf_op jit(solution)/shard_map/ppermute | solution.py:57
  55.8 3.3 %collective-permute-start.18 = (bf16[128,768]{1,0:T(8,128)(2,1)S(1)}, bf16[128,768]{1,0:T(8,128)(2,1)S(1)}, u32[]{:S(2)}, u32[]{:S(2)}) collective-permute-start(bf16[128,768]{1,0:T(8,128)(2,1)S(1)} %get-tuple-element.48), channel_id=1, source_target_pairs={{0,1},{1,0},{2,3},{3,2},{4,5},{5,4},{6,7},{7,6},{8,9},{9,8},{10,11... | collective-permute-start | bytes 589832 | tf_op jit(solution)/shard_map/ppermute | solution.py:61
